TPU v7x, 32 devices: a whole 2x2x4 slice. The times are simulated.
32 devices in a mesh: groups: 1, req: 32 (over z, y, x, core).
Axes of the slice: x: 2, y: 2, z: 4, core: 2. Of those that a mesh axis runs over, the one named last changes fastest.
Arguments:
- hidden: bfloat16 [2, 512, 2880], P(None, ('groups', 'req')), may hold values from -6 to 6
- norm_gain: bfloat16 [2880], replicated, may hold values from 0.099609375 to 1.8984375
- w_gate: bfloat16 [2880, 23040], P(None, 'req'), may hold values from -0.109375 to 0.109375
- w_up: bfloat16 [2880, 23040], P(None, 'req'), may hold values from -0.109375 to 0.109375
- w_down: bfloat16 [23040, 2880], P('req'), may hold values from -0.109375 to 0.109375
- expert_ids: int32 [2, 512, 4], P(None, ('groups', 'req')), may hold values from 0 to 7, as said below
- route_weight: float32 [2, 512, 4], P(None, ('groups', 'req')), may hold values from 0.1 to 1
Outputs:
- mixed: bfloat16 [2, 512, 2880], P(None, ('groups', 'req'))
Inputs may be any that keep to these rules, and one draw needn't show every extreme that they name: `expert_ids`: each token names 4 different experts. In each micro-batch the 16 tokens of one device name any one expert at most 12 times, and every expert is named exactly 12 times by the tokens of some device.
All inputs are finite; a program needn't handle non-finite values.
Results may differ from a plain program's by a relative error of at most 0.0058.
Values may be sent and summed in bfloat16 or wider, within the bound.
No kernel may reach another device: no remote copies, remote signals or barrier semaphores. Data moves between devices by JAX's collectives and lax.ppermute only.
A program may use at most 128 MiB of HBM per device.

v0:
```python
import jax
import jax.numpy as jnp
from jax import lax
from jax.sharding import PartitionSpec as P

HSPLIT = 4


epsilon = 1e-05
swish_scale = 1.702


def swapped(block, axis, apart):
    count = lax.axis_size(axis)
    route = []
    for low in range(count):
        high = low | 1 << apart
        if high != low and high < count:
            route += [(low, high), (high, low)]
    return lax.ppermute(block, axis, route)


def local(hidden, norm_gain, w_gate, w_up, w_down, expert_ids, route_weight):
    micro_count, tokens, model_width = hidden.shape
    top_count = expert_ids.shape[2]
    devices = lax.axis_size("req")
    experts = devices // HSPLIT
    rounded = HSPLIT * (
        (3 * tokens * top_count + 2 * experts * HSPLIT - 1) // (2 * experts * HSPLIT)
    )
    capacity = min(tokens, max(HSPLIT, rounded))
    quarter = capacity // HSPLIT
    levels = HSPLIT.bit_length() - 1
    position = lax.axis_index("req")
    gain_f32 = norm_gain.astype(jnp.float32)
    results = []
    for batch_index in range(micro_count):
        residual = hidden[batch_index].astype(jnp.float32)
        normed = (
            residual
            * lax.rsqrt(jnp.mean(residual * residual, axis=-1, keepdims=True) + epsilon)
            * gain_f32
        ).astype(jnp.bfloat16)
        flat_ids = expert_ids[batch_index].reshape(-1)
        onehot = (flat_ids[:, None] == jnp.arange(experts, dtype=jnp.int32)[None, :]).astype(
            jnp.int32
        )
        slot_index = jnp.sum((jnp.cumsum(onehot, axis=0) - onehot) * onehot, axis=1)
        target = flat_ids * capacity + slot_index
        placing = (
            target[:, None] == jnp.arange(experts * capacity, dtype=jnp.int32)[None, :]
        ).reshape(tokens, top_count, experts * capacity)
        selector = jnp.any(placing, axis=1).astype(jnp.bfloat16)
        outgoing = jnp.dot(selector.T, normed, preferred_element_type=jnp.float32).astype(
            jnp.bfloat16
        )
        copies = jnp.broadcast_to(
            outgoing.reshape(experts, 1, capacity, model_width),
            (experts, HSPLIT, capacity, model_width),
        ).reshape(devices, capacity, model_width)
        received = lax.all_to_all(copies, "req", split_axis=0, concat_axis=0, tiled=True)
        count = received.shape[1]
        slot_rows = received.reshape(-1, model_width)
        gate = jnp.dot(slot_rows, w_gate, preferred_element_type=jnp.float32)
        upward = jnp.dot(slot_rows, w_up, preferred_element_type=jnp.float32)
        act = ((upward + 1.0) * gate * jax.nn.sigmoid(swish_scale * gate)).astype(jnp.bfloat16)
        source_form = jnp.dot(act, w_down, preferred_element_type=jnp.float32).reshape(
            devices, count, model_width
        )
        shard_form = source_form.reshape(devices, HSPLIT, quarter, model_width).transpose(
            1, 0, 2, 3
        )
        folded = shard_form
        for bit_index in reversed(range(levels)):
            halfway = folded.shape[0] // 2
            upper_side = position >> bit_index & 1 == 1
            kept_part = jnp.where(upper_side, folded[halfway:], folded[:halfway])
            given_part = jnp.where(upper_side, folded[:halfway], folded[halfway:])
            folded = kept_part + swapped(given_part, "req", bit_index)
        own_rows = folded[0].astype(jnp.bfloat16)
        expert_out = lax.all_to_all(
            own_rows, "req", split_axis=0, concat_axis=0, tiled=True
        ).reshape(experts * capacity, model_width)
        weigh_table = jnp.sum(
            placing.astype(jnp.float32) * route_weight[batch_index][:, :, None], axis=1
        )
        mixture = jnp.dot(
            weigh_table, expert_out.astype(jnp.float32), precision=lax.Precision.HIGHEST
        )
        results.append((residual + mixture).astype(jnp.bfloat16))
    return jnp.stack(results, axis=0)


def solution(mesh):
    return jax.shard_map(
        local,
        mesh=mesh,
        in_specs=(
            P(None, ("groups", "req"), None),
            P(),
            P(None, "req"),
            P(None, "req"),
            P("req", None),
            P(None, ("groups", "req"), None),
            P(None, ("groups", "req"), None),
        ),
        out_specs=P(None, ("groups", "req"), None),
        check_vma=False,
    )
```

profile of v0, /device:TPU:0, one launch (start us, length us, event | category | flops | bytes accessed | tf_op | source)
XLA Modules:
  0.0 300.5 jit_solution(10818462330565919077)
XLA Ops:
  0.0 0.7 fusion.42
  1.0 0.2 select_reduce_fusion.3
  1.8 0.2 select_reduce_fusion.1
  2.1 1.1 fusion.18
  3.2 0.7 convert_element_type.66
  3.9 0.7 bitcast_add_fusion.1
  4.7 1.3 convolution_convert_fusion
  6.1 1.8 broadcast_in_dim.11
  8.0 7.3 %all-to-all-start.2 = ((bf16[32,12,2880]{2,1,0:T(8,128)(2,1)}), bf16[32,12,2880]{2,1,0:T(8,128)(2,1)S(1)}, u32[]{:S(2)}, u32[]{:S(2)}) async-start(bf16[32,12,2880]{2,1,0:T(8,128)(2,1)} %bitcast.63), calls=%async_computation.2 | async-start | bytes 6029312 | tf_op jit(solution)/shard_map/all_to_all | solution.py:61
  15.3 1.2 convolution_convert_fusion.1
  16.4 2.1 broadcast_in_dim.8
  18.5 65.4 %all-to-all-done.2 = bf16[32,12,2880]{2,1,0:T(8,128)(2,1)S(1)} async-done(((bf16[32,12,2880]{2,1,0:T(8,128)(2,1)}), bf16[32,12,2880]{2,1,0:T(8,128)(2,1)S(1)}, u32[]{:S(2)}, u32[]{:S(2)}) %all-to-all-start.2) | async-done | bytes 2211872 | tf_op jit(solution)/shard_map/all_to_all | solution.py:61
  83.9 2.9 broadcast_in_dim.9
  86.8 4.0 %all-to-all-start = ((bf16[32,12,2880]{2,1,0:T(8,128)(2,1)}), bf16[32,12,2880]{2,1,0:T(8,128)(2,1)}, u32[]{:S(2)}, u32[]{:S(2)}) async-start(bf16[32,12,2880]{2,1,0:T(8,128)(2,1)} %bitcast.62), calls=%async_computation | async-start | bytes 6029312 | tf_op jit(solution)/shard_map/all_to_all | solution.py:61
  90.9 2.5 reshape.93
  93.4 6.5 %fusion.44 = f32[384,720]{0,1:T(8,128)} fusion(bf16[384,2880]{1,0:T(8,128)(2,1)} %reshape.93, bf16[2880,720]{0,1:T(8,128)(2,1)} %param.9), kind=kOutput, calls=%fused_computation.77 | convolution fusion | flops 1592524800 | bytes 7464960 | tf_op jit(solution)/shard_map/dot_general | solution.py:64
  99.8 10.3 %fusion.10 = f32[384,2880]{1,0:T(8,128)} fusion(bf16[720,2880]{1,0:T(8,128)(2,1)} %param.11, f32[384,720]{0,1:T(8,128)} %fusion.44, bf16[384,2880]{1,0:T(8,128)(2,1)S(1)} %copy-done.2, bf16[2880,720]{0,1:T(8,128)(2,1)} %param.10), kind=kOutput, calls=%fused_computation.26 | convolution fusion | flops 3187261440 | bytes 16035840 | tf_op jit(solution)/shard_map/dot_general | solution.py:67
  110.2 7.1 %reshape_reshape.7 = f32[32,4,3,2880]{3,2,1,0:T(4,128)} reshape(f32[384,2880]{1,0:T(8,128)} %fusion.10) | data formatting | bytes 8847360 | tf_op jit(solution)/shard_map/reshape;reshape | solution.py:70
  117.3 4.2 %copy.84 = f32[32,4,3,2880]{3,0,2,1:T(8,128)S(1)} copy(f32[32,4,3,2880]{3,2,1,0:T(4,128)} %reshape_reshape.7) | data formatting | bytes 8847360 | tf_op jit(solution)/shard_map/reshape;reshape | solution.py:70
  121.5 1.8 slice_select_fusion
  123.3 1.0 copy-done
  124.3 1.7 collective-permute-start.2
  126.0 33.7 %all-to-all-done = bf16[32,12,2880]{2,1,0:T(8,128)(2,1)} async-done(((bf16[32,12,2880]{2,1,0:T(8,128)(2,1)}), bf16[32,12,2880]{2,1,0:T(8,128)(2,1)}, u32[]{:S(2)}, u32[]{:S(2)}) %all-to-all-start) | async-done | bytes 2211872 | tf_op jit(solution)/shard_map/all_to_all | solution.py:61
  159.7 4.4 %reshape.90 = bf16[384,2880]{1,0:T(8,128)(2,1)} reshape(bf16[32,12,2880]{2,1,0:T(8,128)(2,1)} %all-to-all-done) | data formatting | bytes 4423680 | tf_op jit(solution)/shard_map/reshape | solution.py:63
  164.1 6.4 %fusion.43 = f32[384,720]{0,1:T(8,128)} fusion(bf16[384,2880]{1,0:T(8,128)(2,1)} %reshape.90, bf16[2880,720]{0,1:T(8,128)(2,1)} %param.9), kind=kOutput, calls=%fused_computation.76 | convolution fusion | flops 1592524800 | bytes 7464960 | tf_op jit(solution)/shard_map/dot_general | solution.py:64
  170.5 11.1 %fusion.11 = f32[384,2880]{1,0:T(8,128)} fusion(bf16[720,2880]{1,0:T(8,128)(2,1)} %param.11, f32[384,720]{0,1:T(8,128)} %fusion.43, bf16[384,2880]{1,0:T(8,128)(2,1)} %reshape.90, bf16[2880,720]{0,1:T(8,128)(2,1)} %param.10), kind=kOutput, calls=%fused_computation.27 | convolution fusion | flops 3187261440 | bytes 16035840 | tf_op jit(solution)/shard_map/dot_general | solution.py:67
  181.5 7.1 %reshape_reshape.6 = f32[32,4,3,2880]{3,2,1,0:T(4,128)} reshape(f32[384,2880]{1,0:T(8,128)} %fusion.11) | data formatting | bytes 8847360 | tf_op jit(solution)/shard_map/reshape;reshape | solution.py:70
  188.7 4.2 %copy.85 = f32[32,4,3,2880]{3,0,2,1:T(8,128)S(1)} copy(f32[32,4,3,2880]{3,2,1,0:T(4,128)} %reshape_reshape.6) | data formatting | bytes 8847360 | tf_op jit(solution)/shard_map/reshape;reshape | solution.py:70
  192.8 1.9 slice_select_fusion.1
  194.7 0.9 copy-done.1
  195.6 1.2 collective-permute-start
  196.7 2.8 select_add_fusion
  199.8 46.8 %collective-permute-done = f32[2,32,3,2880]{3,1,2,0:T(8,128)} collective-permute-done((f32[2,32,3,2880]{3,1,2,0:T(8,128)}, f32[2,32,3,2880]{3,1,2,0:T(8,128)}, u32[]{:S(2)}, u32[]{:S(2)}) %collective-permute-start) | collective-permute-done | bytes 2211872 | tf_op jit(solution)/shard_map/ppermute | solution.py:20
  246.6 2.0 select_add_fusion.1
  248.6 1.1 slice_select_fusion.3
  249.7 0.2 fusion.13
  249.8 1.3 copy.79
  251.1 4.4 %all-to-all-start.3 = ((bf16[32,3,2880]{2,1,0:T(4,128)(2,1)}), bf16[32,3,2880]{2,1,0:T(4,128)(2,1)S(1)}, u32[]{:S(2)}, u32[]{:S(2)}) async-start(bf16[32,3,2880]{2,1,0:T(4,128)(2,1)} %copy.79), calls=%async_computation.3 | async-start | bytes 1507328 | tf_op jit(solution)/shard_map/all_to_all | solution.py:81
  255.5 1.4 fusion.12
  256.9 1.3 copy.74
  258.2 17.2 %all-to-all-done.3 = bf16[32,3,2880]{2,1,0:T(4,128)(2,1)S(1)} async-done(((bf16[32,3,2880]{2,1,0:T(4,128)(2,1)}), bf16[32,3,2880]{2,1,0:T(4,128)(2,1)S(1)}, u32[]{:S(2)}, u32[]{:S(2)}) %all-to-all-start.3) | async-done | bytes 552992 | tf_op jit(solution)/shard_map/all_to_all | solution.py:81
  275.4 3.6 %all-to-all-start.1 = ((bf16[32,3,2880]{2,1,0:T(4,128)(2,1)}), bf16[32,3,2880]{2,1,0:T(4,128)(2,1)S(1)}, u32[]{:S(2)}, u32[]{:S(2)}) async-start(bf16[32,3,2880]{2,1,0:T(4,128)(2,1)} %copy.74), calls=%async_computation.1 | async-start | bytes 1507328 | tf_op jit(solution)/shard_map/all_to_all | solution.py:81
  279.1 0.5 reshape.94
  279.6 0.3 fusion.2
  280.0 19.0 %all-to-all-done.1 = bf16[32,3,2880]{2,1,0:T(4,128)(2,1)S(1)} async-done(((bf16[32,3,2880]{2,1,0:T(4,128)(2,1)}), bf16[32,3,2880]{2,1,0:T(4,128)(2,1)S(1)}, u32[]{:S(2)}, u32[]{:S(2)}) %all-to-all-start.1) | async-done | bytes 552992 | tf_op jit(solution)/shard_map/all_to_all | solution.py:81
  298.9 0.5 reshape.91
  299.4 0.3 fusion.3
  299.8 0.7 pad_maximum_fusion
  (36 shorter events, 1.6 us)
Async XLA Ops:
  8.0 7.3 %copy-start.3 = (bf16[2,16,2880]{2,1,0:T(8,128)(2,1)S(1)}, bf16[2,16,2880]{2,1,0:T(8,128)(2,1)}, u32[]{:S(2)}) copy-start(bf16[2,16,2880]{2,1,0:T(8,128)(2,1)} %param.7) | copy-start | bytes 552964
  8.0 76.0 %all-to-all-start.2 = ((bf16[32,12,2880]{2,1,0:T(8,128)(2,1)}), bf16[32,12,2880]{2,1,0:T(8,128)(2,1)S(1)}, u32[]{:S(2)}, u32[]{:S(2)}) async-start(bf16[32,12,2880]{2,1,0:T(8,128)(2,1)} %bitcast.63), calls=%async_computation.2 | async-start | bytes 6029312 | tf_op jit(solution)/shard_map/all_to_all | solution.py:61
  86.8 72.8 %all-to-all-start = ((bf16[32,12,2880]{2,1,0:T(8,128)(2,1)}), bf16[32,12,2880]{2,1,0:T(8,128)(2,1)}, u32[]{:S(2)}, u32[]{:S(2)}) async-start(bf16[32,12,2880]{2,1,0:T(8,128)(2,1)} %bitcast.62), calls=%async_computation | async-start | bytes 6029312 | tf_op jit(solution)/shard_map/all_to_all | solution.py:61
  93.3 6.5 %copy-start.2 = (bf16[384,2880]{1,0:T(8,128)(2,1)S(1)}, bf16[384,2880]{1,0:T(8,128)(2,1)}, u32[]{:S(2)}) copy-start(bf16[384,2880]{1,0:T(8,128)(2,1)} %reshape.93) | copy-start | bytes 6635524
  121.5 2.8 copy-start
  124.3 72.5 %collective-permute-start.2 = (f32[2,32,3,2880]{3,1,2,0:T(8,128)}, f32[2,32,3,2880]{3,1,2,0:T(8,128)S(1)}, u32[]{:S(2)}, u32[]{:S(2)}) collective-permute-start(f32[2,32,3,2880]{3,1,2,0:T(8,128)} %slice_select_fusion), channel_id=1, source_target_pairs={{0,2},{2,0},{1,3},{3,1},{4,6},{6,4},{5,7},{7,5},{8,10},{10,8},{9,1... | collective-permute-start | bytes 6635528 | tf_op jit(solution)/shard_map/ppermute | solution.py:20
  192.8 2.8 copy-start.1
  195.6 51.0 %collective-permute-start = (f32[2,32,3,2880]{3,1,2,0:T(8,128)}, f32[2,32,3,2880]{3,1,2,0:T(8,128)}, u32[]{:S(2)}, u32[]{:S(2)}) collective-permute-start(f32[2,32,3,2880]{3,1,2,0:T(8,128)} %slice_select_fusion.1), channel_id=1, source_target_pairs={{0,2},{2,0},{1,3},{3,1},{4,6},{6,4},{5,7},{7,5},{8,10},{10,8},{9,1... | collective-permute-start | bytes 6635528 | tf_op jit(solution)/shard_map/ppermute | solution.py:20
  196.7 49.9 %slice-start = ((s8[4521984]{0:T(1024)(128)(4,1)}), s8[327680]{0:T(1024)(128)(4,1)S(1)}, s32[]{:S(2)}) async-start(s8[4521984]{0:T(1024)(128)(4,1)} %bitcast.59), calls=%async_computation.4 | async-start | bytes 655360
  196.7 49.9 %slice-start.1 = ((s8[4521984]{0:T(1024)(128)(4,1)}), s8[4194304]{0:T(1024)(128)(4,1)S(1)}, s32[]{:S(2)}) async-start(s8[4521984]{0:T(1024)(128)(4,1)} %bitcast.59), calls=%async_computation.5 | async-start | bytes 8388608
  199.7 50.0 %collective-permute-start.3 = (f32[1,32,3,2880]{3,1,2,0:T(8,128)S(1)}, f32[1,32,3,2880]{3,1,2,0:T(8,128)S(1)}, u32[]{:S(2)}, u32[]{:S(2)}) collective-permute-start(f32[1,32,3,2880]{3,1,2,0:T(8,128)S(1)} %slice_select_fusion.2), channel_id=1, source_target_pairs={{0,1},{1,0},{2,3},{3,2},{4,5},{5,4},{6,7},{7,6},{8,9},{9,8},{10,11... | collective-permute-start | bytes 3317768 | tf_op jit(solution)/shard_map/ppermute | solution.py:20
  249.7 5.8 %collective-permute-start.1 = (f32[1,32,3,2880]{3,1,2,0:T(8,128)}, f32[1,32,3,2880]{3,1,2,0:T(8,128)}, u32[]{:S(2)}, u32[]{:S(2)}) collective-permute-start(f32[1,32,3,2880]{3,1,2,0:T(8,128)} %slice_select_fusion.3), channel_id=1, source_target_pairs={{0,1},{1,0},{2,3},{3,2},{4,5},{5,4},{6,7},{7,6},{8,9},{9,8},{10,11... | collective-permute-start | bytes 3317768 | tf_op jit(solution)/shard_map/ppermute | solution.py:20
  251.1 24.3 %all-to-all-start.3 = ((bf16[32,3,2880]{2,1,0:T(4,128)(2,1)}), bf16[32,3,2880]{2,1,0:T(4,128)(2,1)S(1)}, u32[]{:S(2)}, u32[]{:S(2)}) async-start(bf16[32,3,2880]{2,1,0:T(4,128)(2,1)} %copy.79), calls=%async_computation.3 | async-start | bytes 1507328 | tf_op jit(solution)/shard_map/all_to_all | solution.py:81
  256.9 22.1 %copy-start.4 = (f32[2,16,4]{1,2,0:T(4,128)S(1)}, f32[2,16,4]{1,2,0:T(4,128)}, u32[]{:S(2)}) copy-start(f32[2,16,4]{1,2,0:T(4,128)} %param.13) | copy-start | bytes 1540
  275.4 23.5 %all-to-all-start.1 = ((bf16[32,3,2880]{2,1,0:T(4,128)(2,1)}), bf16[32,3,2880]{2,1,0:T(4,128)(2,1)S(1)}, u32[]{:S(2)}, u32[]{:S(2)}) async-start(bf16[32,3,2880]{2,1,0:T(4,128)(2,1)} %copy.74), calls=%async_computation.1 | async-start | bytes 1507328 | tf_op jit(solution)/shard_map/all_to_all | solution.py:81
where the time goes:
time: 302 us; the launch traced here: 300 us
  waiting for transfers between devices  182 us (60%)
  local copies, waits for them, and re-layouts  43.1 us (14%)
  matrix products  37.4 us (12%)
  starting transfers between devices  22.3 us (7%)
  other arithmetic  15.3 us (5%)
    all_to_all x2, waiting for transfers between devices, local(): lax.all_to_all(copies, 'req', split_axis=0, concat_axis=0, tiled=True)  99.1 us
    ppermute x4, waiting for transfers between devices, swapped(): return lax.ppermute(block, axis, route)  46.8 us
    all_to_all x2, waiting for transfers between devices, local(): lax.all_to_all(own_rows, 'req', split_axis=0, concat_axis=0, tiled=True)  36.2 us
    another operation x4, local copies, waits for them, and re-layouts, local(): source_form.reshape(devices, HSPLIT, quarter, model_width)  22.6 us
    dot_general x2, matrix products, local(): jnp.dot(act, w_down, preferred_element_type=jnp.float32)  21.4 us
    dot_general x2, matrix products, local(): gate = jnp.dot(slot_rows, w_gate, preferred_element_type=jnp.float32)  12.9 us
    all_to_all x2, starting transfers between devices, local(): lax.all_to_all(copies, 'req', split_axis=0, concat_axis=0, tiled=True)  11.3 us
    all_to_all x2, starting transfers between devices, local(): lax.all_to_all(own_rows, 'req', split_axis=0, concat_axis=0, tiled=True)  8.01 us
  transfers between devices with their start and end apart: 8, of which 5 were waited for; matrix products, arithmetic and copies ran while one was open for 27% of the time, Pallas kernels for 0%

commit v1 on v0

v1 whole, which is shorter than its diff:
```python
import functools

import jax
import jax.numpy as jnp
from jax import lax
from jax.experimental import pallas as pl
from jax.experimental.pallas import tpu as pltpu
from jax.sharding import PartitionSpec as P

HSPLIT = 4
LANES = 128

epsilon = 1e-05
swish_scale = 1.702


def split_widths(width):
    first = width // 2 // LANES * LANES
    second = width - first
    held = -(-(second + 32) // LANES) * LANES
    return first, second, held


def moved(block, partner):
    count = lax.axis_size("req")
    return lax.ppermute(block, "req", [(i, partner(i)) for i in range(count)])


def other_core(i):
    return i ^ 1


def first_axis(i):
    return i ^ (2 if i & 1 else 4)


def second_axis(i):
    return i ^ (4 if i & 1 else 2)


def far(step):
    return lambda i: i ^ (step << 3)


def ffn_body(
    width, core_ref, expert_ref, mine_ref, other_ref, gate_hbm, up_hbm, down_hbm,
    keep_ref, send_ref, gate_v, up_v, down_v, swap_v, gate_acc, up_acc, act_v, sems,
):
    first, second, held = split_widths(width)
    quads, rows, _ = mine_ref.shape
    total = quads * rows
    hidden = gate_v.shape[1]
    copies = []
    parts = [(0, first), (first, second)]
    for place, (start, size) in enumerate(parts):
        for index, (source, target) in enumerate(((gate_hbm, gate_v), (up_hbm, up_v))):
            copies.append(
                pltpu.make_async_copy(
                    source.at[pl.ds(start, size)], target.at[pl.ds(start, size)], sems.at[2 * place + index]
                )
            )
    copies.append(pltpu.make_async_copy(down_hbm, down_v, sems.at[4]))

    @pl.when(pl.program_id(0) == 0)
    def _():
        for copy in copies:
            copy.start()

    order = (0, 2, 1, 3)
    for place, source in enumerate(order):
        swap_v[pl.ds(place * rows, rows), :] = other_ref[source]

    tile = mine_ref[:, :, held - LANES :].reshape(total, LANES).astype(jnp.float32)
    lane = lax.broadcasted_iota(jnp.int32, (total, LANES), 1)
    chosen = (lane >= LANES - 32) & (lane < LANES - 16) & (tile == expert_ref[0].astype(jnp.float32))
    weight = jnp.sum(
        jnp.where(chosen, pltpu.roll(tile, LANES - 16, 1), 0.0), axis=1, keepdims=True
    )

    def run(first_rows, second_rows, first_is_mine):
        def ready(index):
            @pl.when(pl.program_id(0) == 0)
            def _():
                copies[index].wait()

        ready(0)
        gate_acc[...] = jnp.dot(first_rows(), gate_v[:first, :], preferred_element_type=jnp.float32)
        ready(1)
        up_acc[...] = jnp.dot(first_rows(), up_v[:first, :], preferred_element_type=jnp.float32)
        ready(2)
        gate_acc[...] += jnp.dot(second_rows(), gate_v[first:, :], preferred_element_type=jnp.float32)
        ready(3)
        up_acc[...] += jnp.dot(second_rows(), up_v[first:, :], preferred_element_type=jnp.float32)
        gate = gate_acc[...]
        act_v[...] = ((up_acc[...] + 1.0) * gate * jax.nn.sigmoid(swish_scale * gate)).astype(jnp.bfloat16)
        ready(4)
        for is_first, (start, size) in zip((True, False), parts):
            result = (
                weight * jnp.dot(act_v[...], down_v[:, start : start + size], preferred_element_type=jnp.float32)
            ).astype(jnp.bfloat16)
            if is_first == first_is_mine:
                keep_ref[:, :, :size] = result.reshape(quads, rows, size)
                if size < held:
                    keep_ref[:, :, size:] = jnp.zeros((quads, rows, held - size), jnp.bfloat16)
            else:
                for place, source in enumerate(order):
                    send_ref[place, :, :size] = result[source * rows : (source + 1) * rows]
                if size < held:
                    send_ref[:, :, size:] = jnp.zeros((quads, rows, held - size), jnp.bfloat16)

    @pl.when(core_ref[0] == 0)
    def _():
        run(
            lambda: mine_ref[:, :, :first].reshape(total, first),
            lambda: swap_v[:, :second],
            True,
        )

    @pl.when(core_ref[0] != 0)
    def _():
        run(
            lambda: swap_v[:, :first],
            lambda: mine_ref[:, :, :second].reshape(total, second),
            False,
        )


def ffn(core, expert, mine, other, w_gate, w_up, w_down):
    quads, rows, held = mine.shape
    width, hidden = w_gate.shape
    block = min(rows, 128)
    total = quads * block
    spec = pl.BlockSpec((quads, block, held), lambda step, *_: (0, step, 0))
    hbm = pl.BlockSpec(memory_space=pl.ANY)
    return pl.pallas_call(
        functools.partial(ffn_body, width),
        out_shape=[jax.ShapeDtypeStruct(mine.shape, jnp.bfloat16)] * 2,
        grid_spec=pltpu.PrefetchScalarGridSpec(
            num_scalar_prefetch=2,
            grid=(rows // block,),
            in_specs=[spec, spec, hbm, hbm, hbm],
            out_specs=[spec, spec],
            scratch_shapes=[
                pltpu.VMEM((width, hidden), jnp.bfloat16),
                pltpu.VMEM((width, hidden), jnp.bfloat16),
                pltpu.VMEM((hidden, width), jnp.bfloat16),
                pltpu.VMEM((total, held), jnp.bfloat16),
                pltpu.VMEM((total, hidden), jnp.float32),
                pltpu.VMEM((total, hidden), jnp.float32),
                pltpu.VMEM((total, hidden), jnp.bfloat16),
                pltpu.SemaphoreType.DMA((5,)),
            ],
        ),
        compiler_params=pltpu.CompilerParams(vmem_limit_bytes=48 * 2**20),
        cost_estimate=pl.CostEstimate(
            flops=6 * quads * rows * width * hidden,
            bytes_accessed=6 * width * hidden + 8 * quads * rows * held,
            transcendentals=quads * rows * hidden,
        ),
    )(core, expert, mine, other, w_gate, w_up, w_down)


def local(hidden, norm_gain, w_gate, w_up, w_down, expert_ids, route_weight):
    micro_count, tokens, width = hidden.shape
    top_count = expert_ids.shape[2]
    devices = lax.axis_size("req")
    distant = devices // 8
    first, second, held = split_widths(width)
    position = lax.axis_index("req")
    core = position & 1
    lower = core == 0
    core_scalar = core.astype(jnp.int32).reshape(1)
    expert_scalar = (position // HSPLIT).astype(jnp.int32).reshape(1)
    gain_f32 = norm_gain.astype(jnp.float32)

    def join(a, b):
        return jnp.concatenate([a, b], axis=0)

    def spread(batch_index):
        residual = hidden[batch_index].astype(jnp.float32)
        normed = (
            residual
            * lax.rsqrt(jnp.mean(residual * residual, axis=-1, keepdims=True) + epsilon)
            * gain_f32
        ).astype(jnp.bfloat16)
        weights = route_weight[batch_index]
        high = lax.reduce_precision(weights, 8, 7)
        middle = lax.reduce_precision(weights - high, 8, 7)
        low = weights - high - middle
        ids = expert_ids[batch_index].astype(jnp.float32)
        gap = jnp.full((tokens, 16 - 3 * top_count), -1.0, jnp.float32)
        routing = jnp.concatenate([ids, ids, ids, gap, high, middle, low, gap], axis=1).astype(jnp.bfloat16)

        def padded(part):
            blank = jnp.zeros((tokens, held - 32 - part.shape[1]), jnp.bfloat16)
            return jnp.concatenate([part, blank, routing], axis=1)

        low_half, high_half = padded(normed[:, :first]), padded(normed[:, first:])
        mine = jnp.where(lower, low_half, high_half)
        theirs = moved(jnp.where(lower, high_half, low_half), other_core)
        pair = join(jnp.where(lower, mine, theirs), jnp.where(lower, theirs, mine))
        column = jnp.concatenate([pair] + [moved(pair, far(j)) for j in range(1, distant)], axis=0)
        half_plane = join(column, moved(column, first_axis))
        plane = join(half_plane, moved(half_plane, second_axis))
        rows = column.shape[0]
        mine = plane.reshape(4, rows, held)
        return residual, mine, moved(plane, other_core).reshape(4, rows, held)

    def add(a, b):
        return (a.astype(jnp.float32) + b.astype(jnp.float32)).astype(jnp.bfloat16)

    def collect(residual, keep, send):
        total = add(keep, moved(send, other_core))
        total = add(total[:2], moved(total[2:], second_axis))
        total = add(total[0], moved(total[1], first_axis))
        total = total.reshape(distant, 2 * tokens, held)
        summed = total[0].astype(jnp.float32)
        for j in range(1, distant):
            summed = summed + moved(total[j], far(j)).astype(jnp.float32)
        own = jnp.where(lower, summed[:tokens], summed[tokens:])
        give = jnp.where(lower, summed[tokens:], summed[:tokens]).astype(jnp.bfloat16)
        taken = moved(give, other_core).astype(jnp.float32)
        mixture = jnp.concatenate(
            [
                jnp.where(lower, own, taken)[:, :first],
                jnp.where(lower, taken, own)[:, :second],
            ],
            axis=1,
        )
        return (residual + mixture).astype(jnp.bfloat16)

    gathered = [spread(b) for b in range(micro_count)]
    results = []
    for residual, mine, other in gathered:
        keep, send = ffn(core_scalar, expert_scalar, mine, other, w_gate, w_up, w_down)
        results.append(collect(residual, keep, send))
    return jnp.stack(results, axis=0)


def solution(mesh):
    return jax.shard_map(
        local,
        mesh=mesh,
        in_specs=(
            P(None, ("groups", "req"), None),
            P(),
            P(None, "req"),
            P(None, "req"),
            P("req", None),
            P(None, ("groups", "req"), None),
            P(None, ("groups", "req"), None),
        ),
        out_specs=P(None, ("groups", "req"), None),
        check_vma=False,
    )
```

time: 302 us -> 155 us (0.51)
  waiting for transfers between devices: 182 us -> 59.3 us
  matrix products: 37.4 us -> 0 us
  Pallas kernels: 0 us -> 27.6 us
  local copies, waits for them, and re-layouts: 43.1 us -> 16.9 us
  starting transfers between devices: 22.3 us -> 41.1 us
  other arithmetic: 15.3 us -> 8.59 us
    all_to_all x4 -> x0, waiting for transfers between devices: 135 us -> none  [the longest x2 99.1 us: local(): lax.all_to_all(copies, 'req', split_axis=0, concat_axis=0, tiled=True)]
    ppermute x4 -> x28, starting transfers between devices: 2.93 us -> 41.1 us  [moved(): return lax.ppermute(block, 'req', [(i, partner(i)) for i in range(count)])]
    dot_general x8 -> x0, matrix products: 37.4 us -> none  [the longest x2 21.4 us: local(): jnp.dot(act, w_down, preferred_element_type=jnp.float32)]
    pallas_call x0 -> x2, Pallas kernels: none -> 27.6 us  [ffn(): pl.pallas_call(functools.partial(ffn_body, width), out_shape=[jax.ShapeDt...]
    another operation x4 -> x5, local copies, waits for them, and re-layouts: 22.6 us -> 0.2 us  [local(): source_form.reshape(devices, HSPLIT, quarter, model_width)]
    all_to_all x4 -> x0, starting transfers between devices: 19.4 us -> none  [the longest x2 11.3 us: local(): lax.all_to_all(copies, 'req', split_axis=0, concat_axis=0, tiled=True)]
    ppermute x4 -> x28, waiting for transfers between devices: 46.8 us -> 59.3 us  [moved(): return lax.ppermute(block, 'req', [(i, partner(i)) for i in range(count)])]
    unnamed x14 -> x16, local copies, waits for them, and re-layouts: 1.88 us -> 13.9 us
  transfers between devices with their start and end apart: 8 -> 28, of which waited for: 5 -> 12; matrix products, arithmetic and copies ran while one was open for 27% -> 13% of each run, Pallas kernels for 0% -> 18%
where the time goes in v1:
time: 155 us; the launch traced here: 154 us
  waiting for transfers between devices  59.3 us (38%)
  starting transfers between devices  41.1 us (27%)
  Pallas kernels  27.6 us (18%)
  local copies, waits for them, and re-layouts  16.9 us (11%)
  other arithmetic  8.59 us (6%)
    ppermute x28, waiting for transfers between devices, moved(): return lax.ppermute(block, 'req', [(i, partner(i)) for i in range(count)])  59.3 us
    ppermute x28, starting transfers between devices, moved(): return lax.ppermute(block, 'req', [(i, partner(i)) for i in range(count)])  41.1 us
    pallas_call x2, Pallas kernels, ffn(): pl.pallas_call(functools.partial(ffn_body, width), out_shape=[jax.ShapeDt...  27.6 us
    unnamed x16, local copies, waits for them, and re-layouts  13.9 us
    convert_element_type x6, other arithmetic, add(): return (a.astype(jnp.float32) + b.astype(jnp.float32)).astype(jnp.bfloat16)  3.93 us
  transfers between devices with their start and end apart: 28, of which 12 were waited for; matrix products, arithmetic and copies ran while one was open for 13% of the time, Pallas kernels for 18%

profile of v1, /device:TPU:0, one launch (start us, length us, event | category | flops | bytes accessed | tf_op | source)
XLA Modules:
  0.0 153.9 jit_solution(17542952660207897121)
XLA Ops:
  0.0 0.7 fusion.22
  0.7 0.7 slice_bitcast_fusion.5
  1.4 1.1 fusion.6
  2.5 0.7 convert_element_type.148
  3.2 1.1 fusion.8
  4.4 0.7 fusion.20
  5.5 0.5 collective-permute-start.14
  6.6 0.3 collective-permute-done.14
  7.0 3.0 %collective-permute-start.15 = (bf16[32,1536]{1,0:T(8,128)(2,1)S(1)}, bf16[32,1536]{1,0:T(8,128)(2,1)S(1)}, u32[]{:S(2)}, u32[]{:S(2)}) collective-permute-start(bf16[32,1536]{1,0:T(8,128)(2,1)S(1)} %pad_maximum_fusion.2), channel_id=1, source_target_pairs={{0,8},{1,9},{2,10},{3,11},{4,12},{5,13},{6,14},{7,15},{8,0},{9,1},... | collective-permute-start | bytes 294920 | tf_op jit(solution)/shard_map/ppermute | solution.py:26
  10.0 2.6 %collective-permute-start.16 = (bf16[32,1536]{1,0:T(8,128)(2,1)S(1)}, bf16[32,1536]{1,0:T(8,128)(2,1)S(1)}, u32[]{:S(2)}, u32[]{:S(2)}) collective-permute-start(bf16[32,1536]{1,0:T(8,128)(2,1)S(1)} %pad_maximum_fusion.2), channel_id=1, source_target_pairs={{0,16},{1,17},{2,18},{3,19},{4,20},{5,21},{6,22},{7,23},{8,24},{9,... | collective-permute-start | bytes 294920 | tf_op jit(solution)/shard_map/ppermute | solution.py:26
  12.6 1.0 collective-permute-start.1
  13.6 3.5 %collective-permute-start.2 = (bf16[32,1536]{1,0:T(8,128)(2,1)S(1)}, bf16[32,1536]{1,0:T(8,128)(2,1)S(1)}, u32[]{:S(2)}, u32[]{:S(2)}) collective-permute-start(bf16[32,1536]{1,0:T(8,128)(2,1)S(1)} %pad_maximum_fusion.1), channel_id=1, source_target_pairs={{0,16},{1,17},{2,18},{3,19},{4,20},{5,21},{6,22},{7,23},{8,24},{9,... | collective-permute-start | bytes 294920 | tf_op jit(solution)/shard_map/ppermute | solution.py:26
  17.1 0.8 collective-permute-start.3
  17.9 2.7 %collective-permute-done.16 = bf16[32,1536]{1,0:T(8,128)(2,1)S(1)} collective-permute-done((bf16[32,1536]{1,0:T(8,128)(2,1)S(1)}, bf16[32,1536]{1,0:T(8,128)(2,1)S(1)}, u32[]{:S(2)}, u32[]{:S(2)}) %collective-permute-start.16) | collective-permute-done | bytes 98336 | tf_op jit(solution)/shard_map/ppermute | solution.py:26
  20.7 1.6 %collective-permute-start.18 = (bf16[128,1536]{1,0:T(8,128)(2,1)S(1)}, bf16[128,1536]{1,0:T(8,128)(2,1)S(1)}, u32[]{:S(2)}, u32[]{:S(2)}) collective-permute-start(bf16[128,1536]{1,0:T(8,128)(2,1)S(1)} %get-tuple-element.48), channel_id=1, source_target_pairs={{0,4},{1,3},{2,6},{3,1},{4,0},{5,7},{6,2},{7,5},{8,12},{9,11},{10,... | collective-permute-start | bytes 1179656 | tf_op jit(solution)/shard_map/ppermute | solution.py:26
  22.3 6.7 %collective-permute-done.2 = bf16[32,1536]{1,0:T(8,128)(2,1)S(1)} collective-permute-done((bf16[32,1536]{1,0:T(8,128)(2,1)S(1)}, bf16[32,1536]{1,0:T(8,128)(2,1)S(1)}, u32[]{:S(2)}, u32[]{:S(2)}) %collective-permute-start.2) | collective-permute-done | bytes 98336 | tf_op jit(solution)/shard_map/ppermute | solution.py:26
  29.1 1.6 %collective-permute-start.19 = (bf16[256,1536]{1,0:T(8,128)(2,1)S(1)}, bf16[256,1536]{1,0:T(8,128)(2,1)S(1)}, u32[]{:S(2)}, u32[]{:S(2)}) collective-permute-start(bf16[256,1536]{1,0:T(8,128)(2,1)S(1)} %get-tuple-element.31), channel_id=1, source_target_pairs={{0,2},{1,5},{2,0},{3,7},{4,6},{5,1},{6,4},{7,3},{8,10},{9,13},{10,... | collective-permute-start | bytes 2359304 | tf_op jit(solution)/shard_map/ppermute | solution.py:26
  30.7 1.6 %collective-permute-start.4 = (bf16[128,1536]{1,0:T(8,128)(2,1)S(1)}, bf16[128,1536]{1,0:T(8,128)(2,1)S(1)}, u32[]{:S(2)}, u32[]{:S(2)}) collective-permute-start(bf16[128,1536]{1,0:T(8,128)(2,1)S(1)} %get-tuple-element.39), channel_id=1, source_target_pairs={{0,4},{1,3},{2,6},{3,1},{4,0},{5,7},{6,2},{7,5},{8,12},{9,11},{10,... | collective-permute-start | bytes 1179656 | tf_op jit(solution)/shard_map/ppermute | solution.py:26
  32.3 10.5 %collective-permute-done.4 = bf16[128,1536]{1,0:T(8,128)(2,1)S(1)} collective-permute-done((bf16[128,1536]{1,0:T(8,128)(2,1)S(1)}, bf16[128,1536]{1,0:T(8,128)(2,1)S(1)}, u32[]{:S(2)}, u32[]{:S(2)}) %collective-permute-start.4) | collective-permute-done | bytes 393248 | tf_op jit(solution)/shard_map/ppermute | solution.py:26
  42.9 0.6 collective-permute-start.5
  43.5 0.5 collective-permute-done.19
  44.2 10.8 %collective-permute-done.5 = bf16[256,1536]{1,0:T(8,128)(2,1)S(1)} collective-permute-done((bf16[256,1536]{1,0:T(8,128)(2,1)S(1)}, bf16[256,1536]{1,0:T(8,128)(2,1)S(1)}, u32[]{:S(2)}, u32[]{:S(2)}) %collective-permute-start.5) | collective-permute-done | bytes 786464 | tf_op jit(solution)/shard_map/ppermute | solution.py:26
  55.1 6.5 %copy.37.gate_hbm = bf16[2880,720]{1,0:T(8,128)(2,1)} copy(bf16[2880,720]{0,1:T(8,128)(2,1)} %param.9) | data formatting | bytes 8294400 | tf_op args[2]
  61.6 6.6 %copy.38.up_hbm = bf16[2880,720]{1,0:T(8,128)(2,1)} copy(bf16[2880,720]{0,1:T(8,128)(2,1)} %param.10) | data formatting | bytes 8294400 | tf_op args[3]
  68.2 13.2 %shard_map.74 = (bf16[4,128,1536]{2,1,0:T(8,128)(2,1)S(1)}, bf16[4,128,1536]{2,1,0:T(8,128)(2,1)S(1)}) custom-call(s32[1]{0:T(128)} %bitcast.core_ref, s32[1]{0:T(128)} %bitcast.1.expert_ref, bf16[4,128,1536]{2,1,0:T(8,128)(2,1)S(1)} %bitcast.64, bf16[4,128,1536]{2,1,0:T(8,128)(2,1)} %bitcast.15.other_ref, bf16[2880,720]{1,0:T(8,128)(2,1)} %copy.37.gate_hbm, ...), custom_call_target="tpu_custom_call" | custom-call | flops 6370099200 | bytes 18733056 | tf_op jit(solution)/shard_map/pallas_call | solution.py:135
  81.4 0.4 collective-permute-start.21
  81.8 14.4 %shard_map.73 = (bf16[4,128,1536]{2,1,0:T(8,128)(2,1)S(1)}, bf16[4,128,1536]{2,1,0:T(8,128)(2,1)}) custom-call(s32[1]{0:T(128)} %bitcast.core_ref, s32[1]{0:T(128)} %bitcast.1.expert_ref, bf16[4,128,1536]{2,1,0:T(8,128)(2,1)S(1)} %bitcast.65, bf16[4,128,1536]{2,1,0:T(8,128)(2,1)} %bitcast.6.other_ref, bf16[2880,720]{1,0:T(8,128)(2,1)} %copy.37.gate_hbm, ...), custom_call_target="tpu_custom_call" | custom-call | flops 6370099200 | bytes 18733056 | tf_op jit(solution)/shard_map/pallas_call | solution.py:135
  96.1 0.3 collective-permute-start.7
  96.4 0.4 add_convert_fusion
  96.8 0.9 slice.167
  97.8 0.5 collective-permute-start.22
  98.3 1.7 %collective-permute-done.7 = bf16[4,128,1536]{2,1,0:T(8,128)(2,1)} collective-permute-done((bf16[4,128,1536]{2,1,0:T(8,128)(2,1)}, bf16[4,128,1536]{2,1,0:T(8,128)(2,1)}, u32[]{:S(2)}, u32[]{:S(2)}) %collective-permute-start.7) | collective-permute-done | bytes 1572896 | tf_op jit(solution)/shard_map/ppermute | solution.py:26
  100.0 1.8 %add_convert_fusion.1 = bf16[4,128,1536]{2,1,0:T(8,128)(2,1)S(1)} fusion(bf16[4,128,1536]{2,1,0:T(8,128)(2,1)} %collective-permute-done.7, bf16[4,128,1536]{2,1,0:T(8,128)(2,1)S(1)} %get-tuple-element.9), kind=kLoop, calls=%fused_computation.1 | loop fusion | flops 3145728 | bytes 4718592 | tf_op jit(solution)/shard_map/convert_element_type | solution.py:210
  101.8 0.6 collective-permute-start.8
  102.4 7.6 %collective-permute-done.22 = bf16[2,128,1536]{2,1,0:T(8,128)(2,1)} collective-permute-done((bf16[2,128,1536]{2,1,0:T(8,128)(2,1)}, bf16[2,128,1536]{2,1,0:T(8,128)(2,1)}, u32[]{:S(2)}, u32[]{:S(2)}) %collective-permute-start.22) | collective-permute-done | bytes 786464 | tf_op jit(solution)/shard_map/ppermute | solution.py:26
  110.1 1.3 add_convert_fusion.2
  111.4 1.6 %collective-permute-start.23 = (bf16[128,1536]{1,0:T(8,128)(2,1)S(1)}, bf16[128,1536]{1,0:T(8,128)(2,1)S(1)}, u32[]{:S(2)}, u32[]{:S(2)}) collective-permute-start(bf16[128,1536]{1,0:T(8,128)(2,1)S(1)} %slice_bitcast_fusion), channel_id=1, source_target_pairs={{0,4},{1,3},{2,6},{3,1},{4,0},{5,7},{6,2},{7,5},{8,12},{9,11},{10,... | collective-permute-start | bytes 1179656 | tf_op jit(solution)/shard_map/ppermute | solution.py:26
  113.0 9.6 %collective-permute-done.8 = bf16[2,128,1536]{2,1,0:T(8,128)(2,1)S(1)} collective-permute-done((bf16[2,128,1536]{2,1,0:T(8,128)(2,1)S(1)}, bf16[2,128,1536]{2,1,0:T(8,128)(2,1)S(1)}, u32[]{:S(2)}, u32[]{:S(2)}) %collective-permute-start.8) | collective-permute-done | bytes 786464 | tf_op jit(solution)/shard_map/ppermute | solution.py:26
  122.6 0.2 add_convert_fusion.3
  122.9 1.6 %collective-permute-start.9 = (bf16[128,1536]{1,0:T(8,128)(2,1)S(1)}, bf16[128,1536]{1,0:T(8,128)(2,1)S(1)}, u32[]{:S(2)}, u32[]{:S(2)}) collective-permute-start(bf16[128,1536]{1,0:T(8,128)(2,1)S(1)} %slice_bitcast_fusion.2), channel_id=1, source_target_pairs={{0,4},{1,3},{2,6},{3,1},{4,0},{5,7},{6,2},{7,5},{8,12},{9,11},{10,... | collective-permute-start | bytes 1179656 | tf_op jit(solution)/shard_map/ppermute | solution.py:26
  124.6 10.6 %collective-permute-start.24 = (bf16[32,1536]{1,0:T(8,128)(2,1)S(1)}, bf16[32,1536]{1,0:T(8,128)(2,1)S(1)}, u32[]{:S(2)}, u32[]{:S(2)}) collective-permute-start(bf16[32,1536]{1,0:T(8,128)(2,1)S(1)} %get-tuple-element.28), channel_id=1, source_target_pairs={{0,8},{1,9},{2,10},{3,11},{4,12},{5,13},{6,14},{7,15},{8,0},{9,1},... | collective-permute-start | bytes 294920 | tf_op jit(solution)/shard_map/ppermute | solution.py:26
  135.2 2.4 %collective-permute-start.26 = (bf16[32,1536]{1,0:T(8,128)(2,1)S(1)}, bf16[32,1536]{1,0:T(8,128)(2,1)S(1)}, u32[]{:S(2)}, u32[]{:S(2)}) collective-permute-start(bf16[32,1536]{1,0:T(8,128)(2,1)S(1)} %get-tuple-element.29), channel_id=1, source_target_pairs={{0,24},{1,25},{2,26},{3,27},{4,28},{5,29},{6,30},{7,31},{8,16},{9,... | collective-permute-start | bytes 294920 | tf_op jit(solution)/shard_map/ppermute | solution.py:26
  137.7 3.7 %collective-permute-start.10 = (bf16[32,1536]{1,0:T(8,128)(2,1)S(1)}, bf16[32,1536]{1,0:T(8,128)(2,1)S(1)}, u32[]{:S(2)}, u32[]{:S(2)}) collective-permute-start(bf16[32,1536]{1,0:T(8,128)(2,1)S(1)} %get-tuple-element.23), channel_id=1, source_target_pairs={{0,8},{1,9},{2,10},{3,11},{4,12},{5,13},{6,14},{7,15},{8,0},{9,1},... | collective-permute-start | bytes 294920 | tf_op jit(solution)/shard_map/ppermute | solution.py:26
  141.4 2.4 %collective-permute-start.12 = (bf16[32,1536]{1,0:T(8,128)(2,1)S(1)}, bf16[32,1536]{1,0:T(8,128)(2,1)S(1)}, u32[]{:S(2)}, u32[]{:S(2)}) collective-permute-start(bf16[32,1536]{1,0:T(8,128)(2,1)S(1)} %get-tuple-element.24), channel_id=1, source_target_pairs={{0,24},{1,25},{2,26},{3,27},{4,28},{5,29},{6,30},{7,31},{8,16},{9,... | collective-permute-start | bytes 294920 | tf_op jit(solution)/shard_map/ppermute | solution.py:26
  143.9 4.0 %collective-permute-done.25 = bf16[32,1536]{1,0:T(8,128)(2,1)S(1)} collective-permute-done((bf16[32,1536]{1,0:T(8,128)(2,1)S(1)}, bf16[32,1536]{1,0:T(8,128)(2,1)S(1)}, u32[]{:S(2)}, u32[]{:S(2)}) %collective-permute-start.25) | collective-permute-done | bytes 98336 | tf_op jit(solution)/shard_map/ppermute | solution.py:26
  148.1 3.6 %collective-permute-done.11 = bf16[32,1536]{1,0:T(8,128)(2,1)S(1)} collective-permute-done((bf16[32,1536]{1,0:T(8,128)(2,1)S(1)}, bf16[32,1536]{1,0:T(8,128)(2,1)S(1)}, u32[]{:S(2)}, u32[]{:S(2)}) %collective-permute-start.11) | collective-permute-done | bytes 98336 | tf_op jit(solution)/shard_map/ppermute | solution.py:26
  151.9 1.1 collective-permute-done.13
  153.2 0.7 copy-done.1
  (90 shorter events, 2.5 us)
Async XLA Ops:
  5.5 1.4 collective-permute-start.14
  6.5 6.1 %collective-permute-start = (bf16[16,1536]{1,0:T(8,128)(2,1)S(1)}, bf16[16,1536]{1,0:T(8,128)(2,1)S(1)}, u32[]{:S(2)}, u32[]{:S(2)}) collective-permute-start(bf16[16,1536]{1,0:T(8,128)(2,1)S(1)} %broadcast_select_fusion.6), channel_id=1, source_target_pairs={{0,1},{1,0},{2,3},{3,2},{4,5},{5,4},{6,7},{7,6},{8,9},{9,8},{10,11... | collective-permute-start | bytes 147464 | tf_op jit(solution)/shard_map/ppermute | solution.py:26
  7.0 10.1 %collective-permute-start.15 = (bf16[32,1536]{1,0:T(8,128)(2,1)S(1)}, bf16[32,1536]{1,0:T(8,128)(2,1)S(1)}, u32[]{:S(2)}, u32[]{:S(2)}) collective-permute-start(bf16[32,1536]{1,0:T(8,128)(2,1)S(1)} %pad_maximum_fusion.2), channel_id=1, source_target_pairs={{0,8},{1,9},{2,10},{3,11},{4,12},{5,13},{6,14},{7,15},{8,0},{9,1},... | collective-permute-start | bytes 294920 | tf_op jit(solution)/shard_map/ppermute | solution.py:26
  10.0 10.6 %collective-permute-start.16 = (bf16[32,1536]{1,0:T(8,128)(2,1)S(1)}, bf16[32,1536]{1,0:T(8,128)(2,1)S(1)}, u32[]{:S(2)}, u32[]{:S(2)}) collective-permute-start(bf16[32,1536]{1,0:T(8,128)(2,1)S(1)} %pad_maximum_fusion.2), channel_id=1, source_target_pairs={{0,16},{1,17},{2,18},{3,19},{4,20},{5,21},{6,22},{7,23},{8,24},{9,... | collective-permute-start | bytes 294920 | tf_op jit(solution)/shard_map/ppermute | solution.py:26
  12.5 8.1 %collective-permute-start.17 = (bf16[32,1536]{1,0:T(8,128)(2,1)S(1)}, bf16[32,1536]{1,0:T(8,128)(2,1)S(1)}, u32[]{:S(2)}, u32[]{:S(2)}) collective-permute-start(bf16[32,1536]{1,0:T(8,128)(2,1)S(1)} %pad_maximum_fusion.2), channel_id=1, source_target_pairs={{0,24},{1,25},{2,26},{3,27},{4,28},{5,29},{6,30},{7,31},{8,16},{9,... | collective-permute-start | bytes 294920 | tf_op jit(solution)/shard_map/ppermute | solution.py:26
  12.6 9.6 %collective-permute-start.1 = (bf16[32,1536]{1,0:T(8,128)(2,1)S(1)}, bf16[32,1536]{1,0:T(8,128)(2,1)S(1)}, u32[]{:S(2)}, u32[]{:S(2)}) collective-permute-start(bf16[32,1536]{1,0:T(8,128)(2,1)S(1)} %pad_maximum_fusion.1), channel_id=1, source_target_pairs={{0,8},{1,9},{2,10},{3,11},{4,12},{5,13},{6,14},{7,15},{8,0},{9,1},... | collective-permute-start | bytes 294920 | tf_op jit(solution)/shard_map/ppermute | solution.py:26
  13.6 15.4 %collective-permute-start.2 = (bf16[32,1536]{1,0:T(8,128)(2,1)S(1)}, bf16[32,1536]{1,0:T(8,128)(2,1)S(1)}, u32[]{:S(2)}, u32[]{:S(2)}) collective-permute-start(bf16[32,1536]{1,0:T(8,128)(2,1)S(1)} %pad_maximum_fusion.1), channel_id=1, source_target_pairs={{0,16},{1,17},{2,18},{3,19},{4,20},{5,21},{6,22},{7,23},{8,24},{9,... | collective-permute-start | bytes 294920 | tf_op jit(solution)/shard_map/ppermute | solution.py:26
  17.1 13.6 %collective-permute-start.3 = (bf16[32,1536]{1,0:T(8,128)(2,1)S(1)}, bf16[32,1536]{1,0:T(8,128)(2,1)S(1)}, u32[]{:S(2)}, u32[]{:S(2)}) collective-permute-start(bf16[32,1536]{1,0:T(8,128)(2,1)S(1)} %pad_maximum_fusion.1), channel_id=1, source_target_pairs={{0,24},{1,25},{2,26},{3,27},{4,28},{5,29},{6,30},{7,31},{8,16},{9,... | collective-permute-start | bytes 294920 | tf_op jit(solution)/shard_map/ppermute | solution.py:26
  20.7 8.4 %collective-permute-start.18 = (bf16[128,1536]{1,0:T(8,128)(2,1)S(1)}, bf16[128,1536]{1,0:T(8,128)(2,1)S(1)}, u32[]{:S(2)}, u32[]{:S(2)}) collective-permute-start(bf16[128,1536]{1,0:T(8,128)(2,1)S(1)} %get-tuple-element.48), channel_id=1, source_target_pairs={{0,4},{1,3},{2,6},{3,1},{4,0},{5,7},{6,2},{7,5},{8,12},{9,11},{10,... | collective-permute-start | bytes 1179656 | tf_op jit(solution)/shard_map/ppermute | solution.py:26
  29.1 14.9 %collective-permute-start.19 = (bf16[256,1536]{1,0:T(8,128)(2,1)S(1)}, bf16[256,1536]{1,0:T(8,128)(2,1)S(1)}, u32[]{:S(2)}, u32[]{:S(2)}) collective-permute-start(bf16[256,1536]{1,0:T(8,128)(2,1)S(1)} %get-tuple-element.31), channel_id=1, source_target_pairs={{0,2},{1,5},{2,0},{3,7},{4,6},{5,1},{6,4},{7,3},{8,10},{9,13},{10,... | collective-permute-start | bytes 2359304 | tf_op jit(solution)/shard_map/ppermute | solution.py:26
  30.7 12.1 %collective-permute-start.4 = (bf16[128,1536]{1,0:T(8,128)(2,1)S(1)}, bf16[128,1536]{1,0:T(8,128)(2,1)S(1)}, u32[]{:S(2)}, u32[]{:S(2)}) collective-permute-start(bf16[128,1536]{1,0:T(8,128)(2,1)S(1)} %get-tuple-element.39), channel_id=1, source_target_pairs={{0,4},{1,3},{2,6},{3,1},{4,0},{5,7},{6,2},{7,5},{8,12},{9,11},{10,... | collective-permute-start | bytes 1179656 | tf_op jit(solution)/shard_map/ppermute | solution.py:26
  42.9 12.1 %collective-permute-start.5 = (bf16[256,1536]{1,0:T(8,128)(2,1)S(1)}, bf16[256,1536]{1,0:T(8,128)(2,1)S(1)}, u32[]{:S(2)}, u32[]{:S(2)}) collective-permute-start(bf16[256,1536]{1,0:T(8,128)(2,1)S(1)} %get-tuple-element.26), channel_id=1, source_target_pairs={{0,2},{1,5},{2,0},{3,7},{4,6},{5,1},{6,4},{7,3},{8,10},{9,13},{10,... | collective-permute-start | bytes 2359304 | tf_op jit(solution)/shard_map/ppermute | solution.py:26
  44.1 24.1 %collective-permute-start.20 = (bf16[512,1536]{1,0:T(8,128)(2,1)S(1)}, bf16[512,1536]{1,0:T(8,128)(2,1)}, u32[]{:S(2)}, u32[]{:S(2)}) collective-permute-start(bf16[512,1536]{1,0:T(8,128)(2,1)S(1)} %constant_dynamic-update-slice_fusion.29), channel_id=1, source_target_pairs={{0,1},{1,0},{2,3},{3,2},{4,5},{5,4},{6,7},{7,6},{8,9},{9,8},{10,11... | collective-permute-start | bytes 4718600 | tf_op jit(solution)/shard_map/ppermute | solution.py:26
  55.0 26.8 %collective-permute-start.6 = (bf16[512,1536]{1,0:T(8,128)(2,1)S(1)}, bf16[512,1536]{1,0:T(8,128)(2,1)}, u32[]{:S(2)}, u32[]{:S(2)}) collective-permute-start(bf16[512,1536]{1,0:T(8,128)(2,1)S(1)} %constant_dynamic-update-slice_fusion.11), channel_id=1, source_target_pairs={{0,1},{1,0},{2,3},{3,2},{4,5},{5,4},{6,7},{7,6},{8,9},{9,8},{10,11... | collective-permute-start | bytes 4718600 | tf_op jit(solution)/shard_map/ppermute | solution.py:26
  81.4 15.1 %collective-permute-start.21 = (bf16[4,128,1536]{2,1,0:T(8,128)(2,1)S(1)}, bf16[4,128,1536]{2,1,0:T(8,128)(2,1)S(1)}, u32[]{:S(2)}, u32[]{:S(2)}) collective-permute-start(bf16[4,128,1536]{2,1,0:T(8,128)(2,1)S(1)} %get-tuple-element.12), channel_id=1, source_target_pairs={{0,1},{1,0},{2,3},{3,2},{4,5},{5,4},{6,7},{7,6},{8,9},{9,8},{10,11... | collective-permute-start | bytes 4718600 | tf_op jit(solution)/shard_map/ppermute | solution.py:26
  96.1 3.8 %collective-permute-start.7 = (bf16[4,128,1536]{2,1,0:T(8,128)(2,1)}, bf16[4,128,1536]{2,1,0:T(8,128)(2,1)}, u32[]{:S(2)}, u32[]{:S(2)}) collective-permute-start(bf16[4,128,1536]{2,1,0:T(8,128)(2,1)} %get-tuple-element.10), channel_id=1, source_target_pairs={{0,1},{1,0},{2,3},{3,2},{4,5},{5,4},{6,7},{7,6},{8,9},{9,8},{10,11... | collective-permute-start | bytes 4718600 | tf_op jit(solution)/shard_map/ppermute | solution.py:26
  97.8 12.3 %collective-permute-start.22 = (bf16[2,128,1536]{2,1,0:T(8,128)(2,1)}, bf16[2,128,1536]{2,1,0:T(8,128)(2,1)}, u32[]{:S(2)}, u32[]{:S(2)}) collective-permute-start(bf16[2,128,1536]{2,1,0:T(8,128)(2,1)} %slice.167), channel_id=1, source_target_pairs={{0,2},{1,5},{2,0},{3,7},{4,6},{5,1},{6,4},{7,3},{8,10},{9,13},{10,... | collective-permute-start | bytes 2359304 | tf_op jit(solution)/shard_map/ppermute | solution.py:26
  101.8 20.8 %collective-permute-start.8 = (bf16[2,128,1536]{2,1,0:T(8,128)(2,1)S(1)}, bf16[2,128,1536]{2,1,0:T(8,128)(2,1)S(1)}, u32[]{:S(2)}, u32[]{:S(2)}) collective-permute-start(bf16[2,128,1536]{2,1,0:T(8,128)(2,1)S(1)} %slice.151), channel_id=1, source_target_pairs={{0,2},{1,5},{2,0},{3,7},{4,6},{5,1},{6,4},{7,3},{8,10},{9,13},{10,... | collective-permute-start | bytes 2359304 | tf_op jit(solution)/shard_map/ppermute | solution.py:26
  111.4 13.0 %collective-permute-start.23 = (bf16[128,1536]{1,0:T(8,128)(2,1)S(1)}, bf16[128,1536]{1,0:T(8,128)(2,1)S(1)}, u32[]{:S(2)}, u32[]{:S(2)}) collective-permute-start(bf16[128,1536]{1,0:T(8,128)(2,1)S(1)} %slice_bitcast_fusion), channel_id=1, source_target_pairs={{0,4},{1,3},{2,6},{3,1},{4,0},{5,7},{6,2},{7,5},{8,12},{9,11},{10,... | collective-permute-start | bytes 1179656 | tf_op jit(solution)/shard_map/ppermute | solution.py:26
  122.9 14.7 %collective-permute-start.9 = (bf16[128,1536]{1,0:T(8,128)(2,1)S(1)}, bf16[128,1536]{1,0:T(8,128)(2,1)S(1)}, u32[]{:S(2)}, u32[]{:S(2)}) collective-permute-start(bf16[128,1536]{1,0:T(8,128)(2,1)S(1)} %slice_bitcast_fusion.2), channel_id=1, source_target_pairs={{0,4},{1,3},{2,6},{3,1},{4,0},{5,7},{6,2},{7,5},{8,12},{9,11},{10,... | collective-permute-start | bytes 1179656 | tf_op jit(solution)/shard_map/ppermute | solution.py:26
  124.6 16.8 %collective-permute-start.24 = (bf16[32,1536]{1,0:T(8,128)(2,1)S(1)}, bf16[32,1536]{1,0:T(8,128)(2,1)S(1)}, u32[]{:S(2)}, u32[]{:S(2)}) collective-permute-start(bf16[32,1536]{1,0:T(8,128)(2,1)S(1)} %get-tuple-element.28), channel_id=1, source_target_pairs={{0,8},{1,9},{2,10},{3,11},{4,12},{5,13},{6,14},{7,15},{8,0},{9,1},... | collective-permute-start | bytes 294920 | tf_op jit(solution)/shard_map/ppermute | solution.py:26
  135.2 12.7 %collective-permute-start.25 = (bf16[32,1536]{1,0:T(8,128)(2,1)S(1)}, bf16[32,1536]{1,0:T(8,128)(2,1)S(1)}, u32[]{:S(2)}, u32[]{:S(2)}) collective-permute-start(bf16[32,1536]{1,0:T(8,128)(2,1)S(1)} %get-tuple-element.30), channel_id=1, source_target_pairs={{0,16},{1,17},{2,18},{3,19},{4,20},{5,21},{6,22},{7,23},{8,24},{9,... | collective-permute-start | bytes 294920 | tf_op jit(solution)/shard_map/ppermute | solution.py:26
  135.2 12.7 %collective-permute-start.26 = (bf16[32,1536]{1,0:T(8,128)(2,1)S(1)}, bf16[32,1536]{1,0:T(8,128)(2,1)S(1)}, u32[]{:S(2)}, u32[]{:S(2)}) collective-permute-start(bf16[32,1536]{1,0:T(8,128)(2,1)S(1)} %get-tuple-element.29), channel_id=1, source_target_pairs={{0,24},{1,25},{2,26},{3,27},{4,28},{5,29},{6,30},{7,31},{8,16},{9,... | collective-permute-start | bytes 294920 | tf_op jit(solution)/shard_map/ppermute | solution.py:26
  137.7 10.4 %collective-permute-start.10 = (bf16[32,1536]{1,0:T(8,128)(2,1)S(1)}, bf16[32,1536]{1,0:T(8,128)(2,1)S(1)}, u32[]{:S(2)}, u32[]{:S(2)}) collective-permute-start(bf16[32,1536]{1,0:T(8,128)(2,1)S(1)} %get-tuple-element.23), channel_id=1, source_target_pairs={{0,8},{1,9},{2,10},{3,11},{4,12},{5,13},{6,14},{7,15},{8,0},{9,1},... | collective-permute-start | bytes 294920 | tf_op jit(solution)/shard_map/ppermute | solution.py:26
  141.4 10.3 %collective-permute-start.11 = (bf16[32,1536]{1,0:T(8,128)(2,1)S(1)}, bf16[32,1536]{1,0:T(8,128)(2,1)S(1)}, u32[]{:S(2)}, u32[]{:S(2)}) collective-permute-start(bf16[32,1536]{1,0:T(8,128)(2,1)S(1)} %get-tuple-element.25), channel_id=1, source_target_pairs={{0,16},{1,17},{2,18},{3,19},{4,20},{5,21},{6,22},{7,23},{8,24},{9,... | collective-permute-start | bytes 294920 | tf_op jit(solution)/shard_map/ppermute | solution.py:26
  141.4 10.3 %collective-permute-start.12 = (bf16[32,1536]{1,0:T(8,128)(2,1)S(1)}, bf16[32,1536]{1,0:T(8,128)(2,1)S(1)}, u32[]{:S(2)}, u32[]{:S(2)}) collective-permute-start(bf16[32,1536]{1,0:T(8,128)(2,1)S(1)} %get-tuple-element.24), channel_id=1, source_target_pairs={{0,24},{1,25},{2,26},{3,27},{4,28},{5,29},{6,30},{7,31},{8,16},{9,... | collective-permute-start | bytes 294920 | tf_op jit(solution)/shard_map/ppermute | solution.py:26
  148.0 5.2 %copy-start = (bf16[2,16,2880]{2,1,0:T(8,128)(2,1)S(1)}, bf16[2,16,2880]{2,1,0:T(8,128)(2,1)}, u32[]{:S(2)}) copy-start(bf16[2,16,2880]{2,1,0:T(8,128)(2,1)} %param.7) | copy-start | bytes 552964
  148.0 3.9 %collective-permute-start.27 = (bf16[16,1536]{1,0:T(8,128)(2,1)S(1)}, bf16[16,1536]{1,0:T(8,128)(2,1)S(1)}, u32[]{:S(2)}, u32[]{:S(2)}) collective-permute-start(bf16[16,1536]{1,0:T(8,128)(2,1)S(1)} %select_convert_fusion), channel_id=1, source_target_pairs={{0,1},{1,0},{2,3},{3,2},{4,5},{5,4},{6,7},{7,6},{8,9},{9,8},{10,11... | collective-permute-start | bytes 147464 | tf_op jit(solution)/shard_map/ppermute | solution.py:26
  151.8 1.3 collective-permute-start.13
  153.2 0.7 copy-start.1

commit v2 on v0

v2 whole, which is shorter than its diff:
```python
import functools

import jax
import jax.numpy as jnp
from jax import lax
from jax.experimental import pallas as pl
from jax.experimental.pallas import tpu as pltpu
from jax.sharding import PartitionSpec as P

HSPLIT = 4
LANES = 128
ROUTING = 32

epsilon = 1e-05
swish_scale = 1.702

across = (((1,), (1,)), ((), ()))
downward = (((0,), (0,)), ((), ()))


def split_widths(width):
    first = width // 2 // LANES * LANES
    second = width - first
    held = -(-(second + ROUTING) // LANES) * LANES
    return first, second, held


def moved(block, partner):
    count = lax.axis_size("req")
    return lax.ppermute(block, "req", [(i, partner(i)) for i in range(count)])


def other_core(i):
    return i ^ 1


def first_axis(i):
    return i ^ (2 if i & 1 else 4)


def second_axis(i):
    return i ^ (4 if i & 1 else 2)


def far(step):
    return lambda i: i ^ (step << 3)


def whole_arrays(count):
    return [pl.BlockSpec(memory_space=pltpu.VMEM)] * count


SCALARS = pl.BlockSpec(memory_space=pltpu.SMEM)


def select_body(tokens, capacity, places_ref, near_ref, next_ref, own_ref, send_ref, slots_ref):
    rows = near_ref.shape[0]
    held = near_ref.shape[1]
    total = 2 * rows
    compact = own_ref.shape[0]
    tile = jnp.concatenate([near_ref[:, held - LANES :], next_ref[:, held - LANES :]], axis=0).astype(jnp.float32)
    lane = lax.broadcasted_iota(jnp.int32, (total, LANES), 1)
    row = lax.broadcasted_iota(jnp.int32, (total, LANES), 0)
    listed = (lane >= LANES - ROUTING) & (lane < LANES - ROUTING // 2)

    def named(expert):
        return jnp.max(jnp.where(listed & (tile == expert.astype(jnp.float32)), 1.0, 0.0), axis=1, keepdims=True)

    mine, theirs = named(places_ref[1]), named(places_ref[2])
    marks = jnp.where(lane == 0, mine, jnp.where(lane == 1, theirs, 0.0))
    left = lax.broadcasted_iota(jnp.int32, (total, total), 0)
    right = lax.broadcasted_iota(jnp.int32, (total, total), 1)
    earlier = ((right < left) & (left // tokens == right // tokens)).astype(jnp.float32).astype(jnp.bfloat16)
    ahead = jnp.dot(earlier, marks.astype(jnp.bfloat16), preferred_element_type=jnp.float32)
    slots = jnp.where(marks > 0.0, ahead + (row // tokens * capacity).astype(jnp.float32), -1.0)
    slots_ref[...] = slots
    column = lax.broadcasted_iota(jnp.int32, (total, compact), 1).astype(jnp.float32)
    for index, target in enumerate((own_ref, send_ref)):
        picks = (slots[:, index : index + 1] == column).astype(jnp.float32).astype(jnp.bfloat16)
        target[...] = (
            lax.dot_general(picks[:rows], near_ref[...], downward, preferred_element_type=jnp.float32)
            + lax.dot_general(picks[rows:], next_ref[...], downward, preferred_element_type=jnp.float32)
        ).astype(jnp.bfloat16)


def select(tokens, capacity, places, near, following):
    rows, held = near.shape
    compact = 2 * rows // tokens * capacity
    block = jax.ShapeDtypeStruct((compact, held), jnp.bfloat16)
    return pl.pallas_call(
        functools.partial(select_body, tokens, capacity),
        out_shape=[block, block, jax.ShapeDtypeStruct((2 * rows, LANES), jnp.float32)],
        in_specs=[SCALARS] + whole_arrays(2),
        out_specs=whole_arrays(3),
        compiler_params=pltpu.CompilerParams(vmem_limit_bytes=40 * 2**20),
        cost_estimate=pl.CostEstimate(flops=8 * rows * compact * held, bytes_accessed=8 * rows * held, transcendentals=0),
    )(places, near, following)


def merge_body(slots_ref, keep_ref, taken_ref, arrived_ref, near_ref, next_ref):
    rows = near_ref.shape[0]
    total = 2 * rows
    compact = keep_ref.shape[0]
    slots = slots_ref[...]
    column = lax.broadcasted_iota(jnp.int32, (total, compact), 1).astype(jnp.float32)
    summed = keep_ref[...] + taken_ref[...].astype(jnp.float32)
    high = summed.astype(jnp.bfloat16)
    result = jnp.zeros((total, keep_ref.shape[1]), jnp.float32)
    for index, source in enumerate((high, arrived_ref[...])):
        picks = (slots[:, index : index + 1] == column).astype(jnp.float32).astype(jnp.bfloat16)
        result += jnp.dot(picks, source, preferred_element_type=jnp.float32)
    near_ref[...] = result[:rows]
    next_ref[...] = result[rows:].astype(jnp.bfloat16)


def merge(slots, keep, taken, arrived):
    rows = slots.shape[0] // 2
    compact, held = keep.shape
    return pl.pallas_call(
        merge_body,
        out_shape=[
            jax.ShapeDtypeStruct((rows, held), jnp.float32),
            jax.ShapeDtypeStruct((rows, held), jnp.bfloat16),
        ],
        in_specs=whole_arrays(4),
        out_specs=whole_arrays(2),
        compiler_params=pltpu.CompilerParams(vmem_limit_bytes=40 * 2**20),
        cost_estimate=pl.CostEstimate(flops=8 * rows * compact * held, bytes_accessed=8 * rows * held, transcendentals=0),
    )(slots, keep, taken, arrived)


def ffn_body(
    places_ref, mine_near_ref, mine_far_ref, other_near_ref, other_far_ref, gate_hbm, up_hbm, down_hbm,
    keep_near_ref, keep_far_ref, send_near_ref, send_far_ref, gate_v, up_v, down_v, rows_v, act_v, sems,
):
    hidden, width = gate_v.shape
    first, second, held = split_widths(width)
    pair = mine_near_ref.shape[0]
    quad = pair // 2
    chunk = hidden // 3
    copies = []
    for part in range(3):
        for place, (source, target) in enumerate(((gate_hbm, gate_v), (up_hbm, up_v))):
            there = pl.ds(part * chunk, chunk)
            copies.append(pltpu.make_async_copy(source.at[there], target.at[there], sems.at[2 * part + place]))
    copies.append(pltpu.make_async_copy(down_hbm, down_v, sems.at[6]))
    for copy in copies:
        copy.start()

    def lay(near, far_ref, swapped, start, size):
        for place in range(4):
            if swapped:
                source, block = (near, far_ref)[place % 2], place // 2
            else:
                source, block = (near, far_ref)[place // 2], place % 2
            rows_v[pl.ds(place * quad, quad), start : start + size] = source[pl.ds(block * quad, quad), :size]

    lower = places_ref[0] == 0

    @pl.when(lower)
    def _():
        lay(mine_near_ref, mine_far_ref, False, 0, first)
        lay(other_near_ref, other_far_ref, True, first, second)

    @pl.when(jnp.logical_not(lower))
    def _():
        lay(other_near_ref, other_far_ref, True, 0, first)
        lay(mine_near_ref, mine_far_ref, False, first, second)

    tile = jnp.concatenate([mine_near_ref[:, held - LANES :], mine_far_ref[:, held - LANES :]], axis=0)
    tile = tile.astype(jnp.float32)
    lane = lax.broadcasted_iota(jnp.int32, (2 * pair, LANES), 1)
    listed = (lane >= LANES - ROUTING) & (lane < LANES - ROUTING // 2)
    chosen = listed & (tile == places_ref[1].astype(jnp.float32))
    weight = jnp.sum(
        jnp.where(chosen, pltpu.roll(tile, LANES - ROUTING // 2, 1), 0.0), axis=1, keepdims=True
    )

    for part in range(3):
        there = slice(part * chunk, (part + 1) * chunk)
        copies[2 * part].wait()
        gate = lax.dot_general(rows_v[...], gate_v[there, :], across, preferred_element_type=jnp.float32)
        copies[2 * part + 1].wait()
        up = lax.dot_general(rows_v[...], up_v[there, :], across, preferred_element_type=jnp.float32)
        act_v[:, there] = ((up + 1.0) * gate * jax.nn.sigmoid(swish_scale * gate)).astype(jnp.bfloat16)
    copies[6].wait()

    def keep_half(result, size):
        keep_near_ref[:, :size] = result[:pair]
        keep_far_ref[:, :size] = result[pair:]
        if size < held:
            keep_near_ref[:, size:] = jnp.zeros((pair, held - size), jnp.float32)
            keep_far_ref[:, size:] = jnp.zeros((pair, held - size), jnp.float32)

    def send_half(result, size):
        result = result.astype(jnp.bfloat16)
        for place in range(4):
            target, block = (send_near_ref, send_far_ref)[place % 2], place // 2
            target[pl.ds(block * quad, quad), :size] = result[place * quad : (place + 1) * quad]
        if size < held:
            send_near_ref[:, size:] = jnp.zeros((pair, held - size), jnp.bfloat16)
            send_far_ref[:, size:] = jnp.zeros((pair, held - size), jnp.bfloat16)

    low = weight * jnp.dot(act_v[...], down_v[:, :first], preferred_element_type=jnp.float32)

    @pl.when(lower)
    def _():
        keep_half(low, first)

    @pl.when(jnp.logical_not(lower))
    def _():
        send_half(low, first)

    high = weight * jnp.dot(act_v[...], down_v[:, first:], preferred_element_type=jnp.float32)

    @pl.when(lower)
    def _():
        send_half(high, second)

    @pl.when(jnp.logical_not(lower))
    def _():
        keep_half(high, second)


def ffn(places, mine_near, mine_far, other_near, other_far, gate_t, up_t, w_down):
    pair, held = mine_near.shape
    hidden, width = gate_t.shape
    total = 2 * pair
    hbm = pl.BlockSpec(memory_space=pl.ANY)
    return pl.pallas_call(
        ffn_body,
        out_shape=[jax.ShapeDtypeStruct((pair, held), jnp.float32)] * 2
        + [jax.ShapeDtypeStruct((pair, held), jnp.bfloat16)] * 2,
        in_specs=[SCALARS] + whole_arrays(4) + [hbm] * 3,
        out_specs=whole_arrays(4),
        scratch_shapes=[
            pltpu.VMEM((hidden, width), jnp.bfloat16),
            pltpu.VMEM((hidden, width), jnp.bfloat16),
            pltpu.VMEM((hidden, width), jnp.bfloat16),
            pltpu.VMEM((total, width), jnp.bfloat16),
            pltpu.VMEM((total, hidden), jnp.bfloat16),
            pltpu.SemaphoreType.DMA((7,)),
        ],
        compiler_params=pltpu.CompilerParams(vmem_limit_bytes=48 * 2**20),
        cost_estimate=pl.CostEstimate(
            flops=6 * total * width * hidden,
            bytes_accessed=6 * width * hidden + 8 * total * held,
            transcendentals=total * hidden,
        ),
    )(places, mine_near, mine_far, other_near, other_far, gate_t, up_t, w_down)


def local(hidden, norm_gain, w_gate, w_up, w_down, expert_ids, route_weight):
    micro_count, tokens, width = hidden.shape
    top_count = expert_ids.shape[2]
    devices = lax.axis_size("req")
    experts = devices // HSPLIT
    rounded = HSPLIT * ((3 * tokens * top_count + 2 * experts * HSPLIT - 1) // (2 * experts * HSPLIT))
    capacity = min(tokens, max(HSPLIT, rounded))
    distant = devices // 8
    first, second, held = split_widths(width)
    position = lax.axis_index("req")
    core = position & 1
    lower = core == 0
    expert = position // HSPLIT
    places = jnp.stack([core, expert, expert ^ core]).astype(jnp.int32)
    gate_t, up_t = w_gate.T, w_up.T

    def join(*blocks):
        return jnp.concatenate(blocks, axis=0)

    residual = hidden.astype(jnp.float32)
    normed = (
        residual
        * lax.rsqrt(jnp.mean(residual * residual, axis=-1, keepdims=True) + epsilon)
        * norm_gain.astype(jnp.float32)
    ).astype(jnp.bfloat16)
    high = lax.reduce_precision(route_weight, 8, 7)
    middle = lax.reduce_precision(route_weight - high, 8, 7)
    low = route_weight - high - middle
    ids = expert_ids.astype(jnp.float32)
    gap = jnp.full((micro_count, tokens, ROUTING // 2 - 3 * top_count), -1.0, jnp.float32)
    routing = jnp.concatenate([ids, ids, ids, gap, high, middle, low, gap], axis=2).astype(jnp.bfloat16)

    def padded(part):
        blank = jnp.zeros((micro_count, tokens, held - ROUTING - part.shape[2]), jnp.bfloat16)
        return jnp.concatenate([part, blank, routing], axis=2)

    low_half, high_half = padded(normed[:, :, :first]), padded(normed[:, :, first:])
    mine = jnp.where(lower, low_half, high_half)
    theirs = moved(jnp.where(lower, high_half, low_half), other_core)
    pairs = [
        join(jnp.where(lower, mine[b], theirs[b]), jnp.where(lower, theirs[b], mine[b]))
        for b in range(micro_count)
    ]

    def column_of(pair):
        return join(pair, *[moved(pair, far(j)) for j in range(1, distant)])

    def tied(*arrays):
        return lax.optimization_barrier(arrays)

    held_state = []
    last = None
    for b in range(micro_count):
        pair = pairs[b]
        if last is not None:
            pair, _ = tied(pair, last["column"])
        column = column_of(pair)
        following = moved(column, first_axis)
        own, send, slots = select(tokens, capacity, places, column, following)
        if last is not None:
            send, last["arrived"] = tied(send, last["arrived"])
        arrived = moved(send, second_axis)
        last = {"column": column, "own": own, "slots": slots, "arrived": arrived}
        held_state.append(last)

    outputs = []
    before = None
    for b in range(micro_count):
        state = held_state[b]
        own, arrived = state["own"], state["arrived"]
        if before is not None:
            arrived, *before = tied(arrived, *before)
            outputs[-1] = before
        before = ffn(
            places, own, arrived, moved(own, other_core), moved(arrived, other_core), gate_t, up_t, w_down
        )
        outputs.append(before)

    def collect(state, keep_near, keep_far, send_near, send_far):
        give = (keep_far + moved(send_far, other_core).astype(jnp.float32)).astype(jnp.bfloat16)
        arrived = moved(give, second_axis)
        near, following = merge(state["slots"], keep_near, moved(send_near, other_core), arrived)
        near = near + moved(following, first_axis).astype(jnp.float32)
        near = near.reshape(distant, 2 * tokens, held)
        summed = near[0]
        for j in range(1, distant):
            summed = summed + moved(near[j].astype(jnp.bfloat16), far(j)).astype(jnp.float32)
        return summed

    sums = jnp.stack([collect(state, *out) for state, out in zip(held_state, outputs)])
    own = jnp.where(lower, sums[:, :tokens], sums[:, tokens:])
    give = jnp.where(lower, sums[:, tokens:], sums[:, :tokens]).astype(jnp.bfloat16)
    taken = moved(give, other_core).astype(jnp.float32)
    mixture = jnp.concatenate(
        [jnp.where(lower, own, taken)[:, :, :first], jnp.where(lower, taken, own)[:, :, :second]], axis=2
    )
    return (residual + mixture).astype(jnp.bfloat16)


def solution(mesh):
    return jax.shard_map(
        local,
        mesh=mesh,
        in_specs=(
            P(None, ("groups", "req"), None),
            P(),
            P(None, "req"),
            P(None, "req"),
            P("req", None),
            P(None, ("groups", "req"), None),
            P(None, ("groups", "req"), None),
        ),
        out_specs=P(None, ("groups", "req"), None),
        check_vma=False,
    )
```

time: 302 us -> 117 us (0.39)
  waiting for transfers between devices: 182 us -> 49.6 us
  local copies, waits for them, and re-layouts: 43.1 us -> 1.97 us
  matrix products: 37.4 us -> 0 us
  Pallas kernels: 0 us -> 30.4 us
  other arithmetic: 15.3 us -> 5.03 us
  starting transfers between devices: 22.3 us -> 29.3 us
    all_to_all x4 -> x0, waiting for transfers between devices: 135 us -> none  [the longest x2 99.1 us: local(): lax.all_to_all(copies, 'req', split_axis=0, concat_axis=0, tiled=True)]
    dot_general x8 -> x0, matrix products: 37.4 us -> none  [the longest x2 21.4 us: local(): jnp.dot(act, w_down, preferred_element_type=jnp.float32)]
    pallas_call x0 -> x6, Pallas kernels: none -> 30.4 us  [the longest x2 25.8 us: ffn(): pl.pallas_call(ffn_body, out_shape=[jax.ShapeDtypeStruct((pair, held), jn...]
    ppermute x4 -> x30, starting transfers between devices: 2.93 us -> 29.3 us  [moved(): return lax.ppermute(block, 'req', [(i, partner(i)) for i in range(count)])]
    another operation x4 -> x0, local copies, waits for them, and re-layouts: 22.6 us -> none  [local(): source_form.reshape(devices, HSPLIT, quarter, model_width)]
    all_to_all x4 -> x0, starting transfers between devices: 19.4 us -> none  [the longest x2 11.3 us: local(): lax.all_to_all(copies, 'req', split_axis=0, concat_axis=0, tiled=True)]
    reshape x4 -> x0, local copies, waits for them, and re-layouts: 7.83 us -> none  [the longest x2 6.88 us: local(): slot_rows = received.reshape(-1, model_width)]
    broadcast_in_dim x4 -> x3, local copies, waits for them, and re-layouts: 6.95 us -> 0.01 us  [the longest x2 0.01 us: padded(): jnp.zeros((micro_count, tokens, held - ROUTING - part.shape[2]), jnp.bflo...]
  transfers between devices with their start and end apart: 8 -> 30, of which waited for: 5 -> 17; matrix products, arithmetic and copies ran while one was open for 27% -> 1% of each run, Pallas kernels for 0% -> 26%
where the time goes in v2:
time: 117 us
  waiting for transfers between devices  49.6 us (42%)
  Pallas kernels  30.4 us (26%)
  starting transfers between devices  29.3 us (25%)
  other arithmetic  5.03 us (4%)
  local copies, waits for them, and re-layouts  1.97 us (2%)
    ppermute x30, waiting for transfers between devices, moved(): return lax.ppermute(block, 'req', [(i, partner(i)) for i in range(count)])  49.6 us
    ppermute x30, starting transfers between devices, moved(): return lax.ppermute(block, 'req', [(i, partner(i)) for i in range(count)])  29.3 us
    pallas_call x2, Pallas kernels, ffn(): pl.pallas_call(ffn_body, out_shape=[jax.ShapeDtypeStruct((pair, held), jn...  25.8 us
    pallas_call x2, Pallas kernels, select(): pl.pallas_call(functools.partial(select_body, tokens, capacity), out_shap...  3.41 us
  transfers between devices with their start and end apart: 30, of which 17 were waited for; matrix products, arithmetic and copies ran while one was open for 1% of the time, Pallas kernels for 26%

profile of v2, /device:TPU:0, one launch (start us, length us, event | category | flops | bytes accessed | tf_op | source)
XLA Modules:
  0.0 116.7 jit_solution(4486477436311091145)
XLA Ops:
  0.0 0.7 reduce_precision.6
  0.7 0.8 copy.13
  1.5 0.7 convert_element_type.65
  2.2 1.0 fusion
  3.2 1.1 fusion.2
  4.4 0.8 copy.11
  5.5 0.5 collective-permute-start
  6.1 0.9 collective-permute-done
  7.0 3.0 %collective-permute-start.1 = (bf16[32,1536]{1,0:T(8,128)(2,1)S(1)}, bf16[32,1536]{1,0:T(8,128)(2,1)S(1)}, u32[]{:S(2)}, u32[]{:S(2)}) collective-permute-start(bf16[32,1536]{1,0:T(8,128)(2,1)S(1)} %pad_maximum_fusion.1), channel_id=1, source_target_pairs={{0,8},{1,9},{2,10},{3,11},{4,12},{5,13},{6,14},{7,15},{8,0},{9,1},... | collective-permute-start | bytes 294920 | tf_op jit(solution)/shard_map/ppermute | solution.py:30
  10.0 2.6 %collective-permute-start.2 = (bf16[32,1536]{1,0:T(8,128)(2,1)S(1)}, bf16[32,1536]{1,0:T(8,128)(2,1)S(1)}, u32[]{:S(2)}, u32[]{:S(2)}) collective-permute-start(bf16[32,1536]{1,0:T(8,128)(2,1)S(1)} %pad_maximum_fusion.1), channel_id=1, source_target_pairs={{0,16},{1,17},{2,18},{3,19},{4,20},{5,21},{6,22},{7,23},{8,24},{9,... | collective-permute-start | bytes 294920 | tf_op jit(solution)/shard_map/ppermute | solution.py:30
  12.6 0.5 collective-permute-done.1
  13.1 7.5 %collective-permute-done.2 = bf16[32,1536]{1,0:T(8,128)(2,1)S(1)} collective-permute-done((bf16[32,1536]{1,0:T(8,128)(2,1)S(1)}, bf16[32,1536]{1,0:T(8,128)(2,1)S(1)}, u32[]{:S(2)}, u32[]{:S(2)}) %collective-permute-start.2) | collective-permute-done | bytes 98336 | tf_op jit(solution)/shard_map/ppermute | solution.py:30
  20.7 1.6 %collective-permute-start.4 = (bf16[128,1536]{1,0:T(8,128)(2,1)S(1)}, bf16[128,1536]{1,0:T(8,128)(2,1)S(1)}, u32[]{:S(2)}, u32[]{:S(2)}) collective-permute-start(bf16[128,1536]{1,0:T(8,128)(2,1)S(1)} %constant_dynamic-update-slice_fusion.near_ref), channel_id=1, source_target_pairs={{0,4},{1,3},{2,6},{3,1},{4,0},{5,7},{6,2},{7,5},{8,12},{9,11},{10,... | collective-permute-start | bytes 1179656 | tf_op jit(solution)/shard_map/ppermute | solution.py:30
  22.3 1.7 %collective-permute-start.5 = (bf16[32,1536]{1,0:T(8,128)(2,1)S(1)}, bf16[32,1536]{1,0:T(8,128)(2,1)S(1)}, u32[]{:S(2)}, u32[]{:S(2)}) collective-permute-start(bf16[32,1536]{1,0:T(8,128)(2,1)S(1)} %pad_maximum_fusion.2), channel_id=1, source_target_pairs={{0,8},{1,9},{2,10},{3,11},{4,12},{5,13},{6,14},{7,15},{8,0},{9,1},... | collective-permute-start | bytes 294920 | tf_op jit(solution)/shard_map/ppermute | solution.py:30
  24.0 1.5 %collective-permute-start.6 = (bf16[32,1536]{1,0:T(8,128)(2,1)S(1)}, bf16[32,1536]{1,0:T(8,128)(2,1)S(1)}, u32[]{:S(2)}, u32[]{:S(2)}) collective-permute-start(bf16[32,1536]{1,0:T(8,128)(2,1)S(1)} %pad_maximum_fusion.2), channel_id=1, source_target_pairs={{0,16},{1,17},{2,18},{3,19},{4,20},{5,21},{6,22},{7,23},{8,24},{9,... | collective-permute-start | bytes 294920 | tf_op jit(solution)/shard_map/ppermute | solution.py:30
  25.5 1.2 %collective-permute-start.7 = (bf16[32,1536]{1,0:T(8,128)(2,1)S(1)}, bf16[32,1536]{1,0:T(8,128)(2,1)S(1)}, u32[]{:S(2)}, u32[]{:S(2)}) collective-permute-start(bf16[32,1536]{1,0:T(8,128)(2,1)S(1)} %pad_maximum_fusion.2), channel_id=1, source_target_pairs={{0,24},{1,25},{2,26},{3,27},{4,28},{5,29},{6,30},{7,31},{8,16},{9,... | collective-permute-start | bytes 294920 | tf_op jit(solution)/shard_map/ppermute | solution.py:30
  26.7 0.7 collective-permute-done.5
  27.4 5.9 %collective-permute-done.6 = bf16[32,1536]{1,0:T(8,128)(2,1)S(1)} collective-permute-done((bf16[32,1536]{1,0:T(8,128)(2,1)S(1)}, bf16[32,1536]{1,0:T(8,128)(2,1)S(1)}, u32[]{:S(2)}, u32[]{:S(2)}) %collective-permute-start.6) | collective-permute-done | bytes 98336 | tf_op jit(solution)/shard_map/ppermute | solution.py:30
  33.3 1.7 %shard_map.73 = (bf16[192,1536]{1,0:T(8,128)(2,1)S(1)}, bf16[192,1536]{1,0:T(8,128)(2,1)S(1)}, f32[256,128]{1,0:T(8,128)S(1)}) custom-call(s32[3]{0:T(128)S(1)} %pad_add_fusion.places_ref, bf16[128,1536]{1,0:T(8,128)(2,1)S(1)} %constant_dynamic-update-slice_fusion.near_ref, bf16[128,1536]{1,0:T(8,128)(2,1)S(1)} %collective-permute-done.4.next_ref), custom_call_target="tpu_custom_call" | custom-call | flops 301989888 | bytes 1572864 | tf_op jit(solution)/shard_map/pallas_call | solution.py:90
  35.0 0.9 collective-permute-start.9
  35.9 1.3 %collective-permute-start.8 = (bf16[128,1536]{1,0:T(8,128)(2,1)S(1)}, bf16[128,1536]{1,0:T(8,128)(2,1)S(1)}, u32[]{:S(2)}, u32[]{:S(2)}) collective-permute-start(bf16[128,1536]{1,0:T(8,128)(2,1)S(1)} %constant_dynamic-update-slice_fusion.5.near_ref), channel_id=1, source_target_pairs={{0,4},{1,3},{2,6},{3,1},{4,0},{5,7},{6,2},{7,5},{8,12},{9,11},{10,... | collective-permute-start | bytes 1179656 | tf_op jit(solution)/shard_map/ppermute | solution.py:30
  37.2 7.4 %collective-permute-done.8.next_ref = bf16[128,1536]{1,0:T(8,128)(2,1)S(1)} collective-permute-done((bf16[128,1536]{1,0:T(8,128)(2,1)S(1)}, bf16[128,1536]{1,0:T(8,128)(2,1)S(1)}, u32[]{:S(2)}, u32[]{:S(2)}) %collective-permute-start.8) | collective-permute-done | bytes 393248 | tf_op jit(solution)/shard_map/ppermute | solution.py:30
  44.6 1.7 %shard_map.74 = (bf16[192,1536]{1,0:T(8,128)(2,1)S(1)}, bf16[192,1536]{1,0:T(8,128)(2,1)S(1)}, f32[256,128]{1,0:T(8,128)S(1)}) custom-call(s32[3]{0:T(128)S(1)} %pad_add_fusion.places_ref, bf16[128,1536]{1,0:T(8,128)(2,1)S(1)} %constant_dynamic-update-slice_fusion.5.near_ref, bf16[128,1536]{1,0:T(8,128)(2,1)S(1)} %collective-permute-done.8.next_ref), custom_call_target="tpu_custom_call" | custom-call | flops 301989888 | bytes 1572864 | tf_op jit(solution)/shard_map/pallas_call | solution.py:90
  46.4 0.5 collective-permute-start.10
  46.8 1.5 %collective-permute-done.12.other_far_ref = bf16[192,1536]{1,0:T(8,128)(2,1)S(1)} collective-permute-done((bf16[192,1536]{1,0:T(8,128)(2,1)S(1)}, bf16[192,1536]{1,0:T(8,128)(2,1)S(1)}, u32[]{:S(2)}, u32[]{:S(2)}) %collective-permute-start.12) | collective-permute-done | bytes 589856 | tf_op jit(solution)/shard_map/ppermute | solution.py:30
  48.4 12.9 %shard_map.75 = (f32[192,1536]{1,0:T(8,128)S(1)}, f32[192,1536]{1,0:T(8,128)S(1)}, bf16[192,1536]{1,0:T(8,128)(2,1)S(1)}, bf16[192,1536]{1,0:T(8,128)(2,1)S(1)}) custom-call(s32[3]{0:T(128)S(1)} %pad_add_fusion.places_ref, bf16[192,1536]{1,0:T(8,128)(2,1)S(1)} %get-tuple-element.36.mine_near_ref, bf16[192,1536]{1,0:T(8,128)(2,1)S(1)} %collective-permute-done.9.mine_far_ref, ...), custom_call_target="tpu_custom_call" | custom-call | flops 4777574400 | bytes 17160192 | tf_op jit(solution)/shard_map/pallas_call | solution.py:230
  62.3 1.0 collective-permute-done.14
  63.4 0.5 collective-permute-start.15
  64.2 0.8 collective-permute-done.21.other_far_ref
  65.0 12.9 %shard_map.77 = (f32[192,1536]{1,0:T(8,128)S(1)}, f32[192,1536]{1,0:T(8,128)S(1)}, bf16[192,1536]{1,0:T(8,128)(2,1)S(1)}, bf16[192,1536]{1,0:T(8,128)(2,1)S(1)}) custom-call(s32[3]{0:T(128)S(1)} %pad_add_fusion.places_ref, bf16[192,1536]{1,0:T(8,128)(2,1)S(1)} %get-tuple-element.49.mine_near_ref, bf16[192,1536]{1,0:T(8,128)(2,1)S(1)} %collective-permute-done.10.mine_far_ref, ...), custom_call_target="tpu_custom_call" | custom-call | flops 4777574400 | bytes 17160192 | tf_op jit(solution)/shard_map/pallas_call | solution.py:230
  78.5 0.6 shard_map.76
  79.1 1.2 %collective-permute-start.16 = (bf16[128,1536]{1,0:T(8,128)(2,1)S(1)}, bf16[128,1536]{1,0:T(8,128)(2,1)S(1)}, u32[]{:S(2)}, u32[]{:S(2)}) collective-permute-start(bf16[128,1536]{1,0:T(8,128)(2,1)S(1)} %get-tuple-element.47), channel_id=1, source_target_pairs={{0,4},{1,3},{2,6},{3,1},{4,0},{5,7},{6,2},{7,5},{8,12},{9,11},{10,... | collective-permute-start | bytes 1179656 | tf_op jit(solution)/shard_map/ppermute | solution.py:30
  80.4 1.1 collective-permute-start.24
  81.5 9.4 %collective-permute-done.16 = bf16[128,1536]{1,0:T(8,128)(2,1)S(1)} collective-permute-done((bf16[128,1536]{1,0:T(8,128)(2,1)S(1)}, bf16[128,1536]{1,0:T(8,128)(2,1)S(1)}, u32[]{:S(2)}, u32[]{:S(2)}) %collective-permute-start.16) | collective-permute-done | bytes 393248 | tf_op jit(solution)/shard_map/ppermute | solution.py:30
  91.1 1.5 %collective-permute-done.24.arrived_ref = bf16[192,1536]{1,0:T(8,128)(2,1)S(1)} collective-permute-done((bf16[192,1536]{1,0:T(8,128)(2,1)S(1)}, bf16[192,1536]{1,0:T(8,128)(2,1)S(1)}, u32[]{:S(2)}, u32[]{:S(2)}) %collective-permute-start.24) | collective-permute-done | bytes 589856 | tf_op jit(solution)/shard_map/ppermute | solution.py:30
  92.5 0.7 shard_map.78
  93.2 1.2 %collective-permute-start.25 = (bf16[128,1536]{1,0:T(8,128)(2,1)S(1)}, bf16[128,1536]{1,0:T(8,128)(2,1)S(1)}, u32[]{:S(2)}, u32[]{:S(2)}) collective-permute-start(bf16[128,1536]{1,0:T(8,128)(2,1)S(1)} %get-tuple-element.56), channel_id=1, source_target_pairs={{0,4},{1,3},{2,6},{3,1},{4,0},{5,7},{6,2},{7,5},{8,12},{9,11},{10,... | collective-permute-start | bytes 1179656 | tf_op jit(solution)/shard_map/ppermute | solution.py:30
  94.4 1.9 %collective-permute-start.17 = (bf16[32,1536]{1,0:T(8,128)(2,1)S(1)}, bf16[32,1536]{1,0:T(8,128)(2,1)S(1)}, u32[]{:S(2)}, u32[]{:S(2)}) collective-permute-start(bf16[32,1536]{1,0:T(8,128)(2,1)S(1)} %get-tuple-element.65), channel_id=1, source_target_pairs={{0,8},{1,9},{2,10},{3,11},{4,12},{5,13},{6,14},{7,15},{8,0},{9,1},... | collective-permute-start | bytes 294920 | tf_op jit(solution)/shard_map/ppermute | solution.py:30
  96.6 2.2 %collective-permute-start.19 = (bf16[32,1536]{1,0:T(8,128)(2,1)S(1)}, bf16[32,1536]{1,0:T(8,128)(2,1)S(1)}, u32[]{:S(2)}, u32[]{:S(2)}) collective-permute-start(bf16[32,1536]{1,0:T(8,128)(2,1)S(1)} %get-tuple-element.66), channel_id=1, source_target_pairs={{0,24},{1,25},{2,26},{3,27},{4,28},{5,29},{6,30},{7,31},{8,16},{9,... | collective-permute-start | bytes 294920 | tf_op jit(solution)/shard_map/ppermute | solution.py:30
  98.8 2.2 %collective-permute-done.25 = bf16[128,1536]{1,0:T(8,128)(2,1)S(1)} collective-permute-done((bf16[128,1536]{1,0:T(8,128)(2,1)S(1)}, bf16[128,1536]{1,0:T(8,128)(2,1)S(1)}, u32[]{:S(2)}, u32[]{:S(2)}) %collective-permute-start.25) | collective-permute-done | bytes 393248 | tf_op jit(solution)/shard_map/ppermute | solution.py:30
  101.2 1.3 %collective-permute-start.26 = (bf16[32,1536]{1,0:T(8,128)(2,1)S(1)}, bf16[32,1536]{1,0:T(8,128)(2,1)S(1)}, u32[]{:S(2)}, u32[]{:S(2)}) collective-permute-start(bf16[32,1536]{1,0:T(8,128)(2,1)S(1)} %get-tuple-element.68), channel_id=1, source_target_pairs={{0,8},{1,9},{2,10},{3,11},{4,12},{5,13},{6,14},{7,15},{8,0},{9,1},... | collective-permute-start | bytes 294920 | tf_op jit(solution)/shard_map/ppermute | solution.py:30
  102.5 1.0 collective-permute-start.27
  103.5 2.1 %collective-permute-start.28 = (bf16[32,1536]{1,0:T(8,128)(2,1)S(1)}, bf16[32,1536]{1,0:T(8,128)(2,1)S(1)}, u32[]{:S(2)}, u32[]{:S(2)}) collective-permute-start(bf16[32,1536]{1,0:T(8,128)(2,1)S(1)} %get-tuple-element.69), channel_id=1, source_target_pairs={{0,24},{1,25},{2,26},{3,27},{4,28},{5,29},{6,30},{7,31},{8,16},{9,... | collective-permute-start | bytes 294920 | tf_op jit(solution)/shard_map/ppermute | solution.py:30
  105.6 1.0 collective-permute-done.18
  106.6 0.8 collective-permute-done.26
  107.5 7.0 %collective-permute-done.27 = bf16[32,1536]{1,0:T(8,128)(2,1)S(1)} collective-permute-done((bf16[32,1536]{1,0:T(8,128)(2,1)S(1)}, bf16[32,1536]{1,0:T(8,128)(2,1)S(1)}, u32[]{:S(2)}, u32[]{:S(2)}) %collective-permute-start.27) | collective-permute-done | bytes 98336 | tf_op jit(solution)/shard_map/ppermute | solution.py:30
  114.6 1.3 %collective-permute-done.29 = bf16[2,16,1536]{2,1,0:T(8,128)(2,1)S(1)} collective-permute-done((bf16[2,16,1536]{2,1,0:T(8,128)(2,1)S(1)}, bf16[2,16,1536]{2,1,0:T(8,128)(2,1)S(1)}, u32[]{:S(2)}, u32[]{:S(2)}) %collective-permute-start.29) | collective-permute-done | bytes 98336 | tf_op jit(solution)/shard_map/ppermute | solution.py:30
  116.0 0.7 fusion.3
  (65 shorter events, 3.7 us)
Async XLA Ops:
  5.5 1.5 %collective-permute-start = (bf16[2,16,1536]{2,1,0:T(8,128)(2,1)S(1)}, bf16[2,16,1536]{2,1,0:T(8,128)(2,1)S(1)}, u32[]{:S(2)}, u32[]{:S(2)}) collective-permute-start(bf16[2,16,1536]{2,1,0:T(8,128)(2,1)S(1)} %get-tuple-element.74), channel_id=1, source_target_pairs={{0,1},{1,0},{2,3},{3,2},{4,5},{5,4},{6,7},{7,6},{8,9},{9,8},{10,11... | collective-permute-start | bytes 294920 | tf_op jit(solution)/shard_map/ppermute | solution.py:30
  7.0 6.1 %collective-permute-start.1 = (bf16[32,1536]{1,0:T(8,128)(2,1)S(1)}, bf16[32,1536]{1,0:T(8,128)(2,1)S(1)}, u32[]{:S(2)}, u32[]{:S(2)}) collective-permute-start(bf16[32,1536]{1,0:T(8,128)(2,1)S(1)} %pad_maximum_fusion.1), channel_id=1, source_target_pairs={{0,8},{1,9},{2,10},{3,11},{4,12},{5,13},{6,14},{7,15},{8,0},{9,1},... | collective-permute-start | bytes 294920 | tf_op jit(solution)/shard_map/ppermute | solution.py:30
  10.0 10.7 %collective-permute-start.2 = (bf16[32,1536]{1,0:T(8,128)(2,1)S(1)}, bf16[32,1536]{1,0:T(8,128)(2,1)S(1)}, u32[]{:S(2)}, u32[]{:S(2)}) collective-permute-start(bf16[32,1536]{1,0:T(8,128)(2,1)S(1)} %pad_maximum_fusion.1), channel_id=1, source_target_pairs={{0,16},{1,17},{2,18},{3,19},{4,20},{5,21},{6,22},{7,23},{8,24},{9,... | collective-permute-start | bytes 294920 | tf_op jit(solution)/shard_map/ppermute | solution.py:30
  12.6 8.1 %collective-permute-start.3 = (bf16[32,1536]{1,0:T(8,128)(2,1)S(1)}, bf16[32,1536]{1,0:T(8,128)(2,1)S(1)}, u32[]{:S(2)}, u32[]{:S(2)}) collective-permute-start(bf16[32,1536]{1,0:T(8,128)(2,1)S(1)} %pad_maximum_fusion.1), channel_id=1, source_target_pairs={{0,24},{1,25},{2,26},{3,27},{4,28},{5,29},{6,30},{7,31},{8,16},{9,... | collective-permute-start | bytes 294920 | tf_op jit(solution)/shard_map/ppermute | solution.py:30
  20.7 12.6 %collective-permute-start.4 = (bf16[128,1536]{1,0:T(8,128)(2,1)S(1)}, bf16[128,1536]{1,0:T(8,128)(2,1)S(1)}, u32[]{:S(2)}, u32[]{:S(2)}) collective-permute-start(bf16[128,1536]{1,0:T(8,128)(2,1)S(1)} %constant_dynamic-update-slice_fusion.near_ref), channel_id=1, source_target_pairs={{0,4},{1,3},{2,6},{3,1},{4,0},{5,7},{6,2},{7,5},{8,12},{9,11},{10,... | collective-permute-start | bytes 1179656 | tf_op jit(solution)/shard_map/ppermute | solution.py:30
  22.3 5.1 %collective-permute-start.5 = (bf16[32,1536]{1,0:T(8,128)(2,1)S(1)}, bf16[32,1536]{1,0:T(8,128)(2,1)S(1)}, u32[]{:S(2)}, u32[]{:S(2)}) collective-permute-start(bf16[32,1536]{1,0:T(8,128)(2,1)S(1)} %pad_maximum_fusion.2), channel_id=1, source_target_pairs={{0,8},{1,9},{2,10},{3,11},{4,12},{5,13},{6,14},{7,15},{8,0},{9,1},... | collective-permute-start | bytes 294920 | tf_op jit(solution)/shard_map/ppermute | solution.py:30
  24.0 9.3 %collective-permute-start.6 = (bf16[32,1536]{1,0:T(8,128)(2,1)S(1)}, bf16[32,1536]{1,0:T(8,128)(2,1)S(1)}, u32[]{:S(2)}, u32[]{:S(2)}) collective-permute-start(bf16[32,1536]{1,0:T(8,128)(2,1)S(1)} %pad_maximum_fusion.2), channel_id=1, source_target_pairs={{0,16},{1,17},{2,18},{3,19},{4,20},{5,21},{6,22},{7,23},{8,24},{9,... | collective-permute-start | bytes 294920 | tf_op jit(solution)/shard_map/ppermute | solution.py:30
  25.5 10.4 %collective-permute-start.7 = (bf16[32,1536]{1,0:T(8,128)(2,1)S(1)}, bf16[32,1536]{1,0:T(8,128)(2,1)S(1)}, u32[]{:S(2)}, u32[]{:S(2)}) collective-permute-start(bf16[32,1536]{1,0:T(8,128)(2,1)S(1)} %pad_maximum_fusion.2), channel_id=1, source_target_pairs={{0,24},{1,25},{2,26},{3,27},{4,28},{5,29},{6,30},{7,31},{8,16},{9,... | collective-permute-start | bytes 294920 | tf_op jit(solution)/shard_map/ppermute | solution.py:30
  35.0 11.3 %collective-permute-start.9 = (bf16[192,1536]{1,0:T(8,128)(2,1)S(1)}, bf16[192,1536]{1,0:T(8,128)(2,1)S(1)}, u32[]{:S(2)}, u32[]{:S(2)}) collective-permute-start(bf16[192,1536]{1,0:T(8,128)(2,1)S(1)} %get-tuple-element.34), channel_id=1, source_target_pairs={{0,2},{1,5},{2,0},{3,7},{4,6},{5,1},{6,4},{7,3},{8,10},{9,13},{10,... | collective-permute-start | bytes 1769480 | tf_op jit(solution)/shard_map/ppermute | solution.py:30
  35.9 8.7 %collective-permute-start.8 = (bf16[128,1536]{1,0:T(8,128)(2,1)S(1)}, bf16[128,1536]{1,0:T(8,128)(2,1)S(1)}, u32[]{:S(2)}, u32[]{:S(2)}) collective-permute-start(bf16[128,1536]{1,0:T(8,128)(2,1)S(1)} %constant_dynamic-update-slice_fusion.5.near_ref), channel_id=1, source_target_pairs={{0,4},{1,3},{2,6},{3,1},{4,0},{5,7},{6,2},{7,5},{8,12},{9,11},{10,... | collective-permute-start | bytes 1179656 | tf_op jit(solution)/shard_map/ppermute | solution.py:30
  37.2 9.7 %collective-permute-start.11 = (bf16[192,1536]{1,0:T(8,128)(2,1)S(1)}, bf16[192,1536]{1,0:T(8,128)(2,1)S(1)}, u32[]{:S(2)}, u32[]{:S(2)}) collective-permute-start(bf16[192,1536]{1,0:T(8,128)(2,1)S(1)} %get-tuple-element.36.mine_near_ref), channel_id=1, source_target_pairs={{0,1},{1,0},{2,3},{3,2},{4,5},{5,4},{6,7},{7,6},{8,9},{9,8},{10,11... | collective-permute-start | bytes 1769480 | tf_op jit(solution)/shard_map/ppermute | solution.py:30
  46.3 2.1 %collective-permute-start.12 = (bf16[192,1536]{1,0:T(8,128)(2,1)S(1)}, bf16[192,1536]{1,0:T(8,128)(2,1)S(1)}, u32[]{:S(2)}, u32[]{:S(2)}) collective-permute-start(bf16[192,1536]{1,0:T(8,128)(2,1)S(1)} %collective-permute-done.9.mine_far_ref), channel_id=1, source_target_pairs={{0,1},{1,0},{2,3},{3,2},{4,5},{5,4},{6,7},{7,6},{8,9},{9,8},{10,11... | collective-permute-start | bytes 1769480 | tf_op jit(solution)/shard_map/ppermute | solution.py:30
  46.4 14.9 %collective-permute-start.10 = (bf16[192,1536]{1,0:T(8,128)(2,1)S(1)}, bf16[192,1536]{1,0:T(8,128)(2,1)S(1)}, u32[]{:S(2)}, u32[]{:S(2)}) collective-permute-start(bf16[192,1536]{1,0:T(8,128)(2,1)S(1)} %get-tuple-element.35), channel_id=1, source_target_pairs={{0,2},{1,5},{2,0},{3,7},{4,6},{5,1},{6,4},{7,3},{8,10},{9,13},{10,... | collective-permute-start | bytes 1769480 | tf_op jit(solution)/shard_map/ppermute | solution.py:30
  61.3 2.1 %collective-permute-start.14 = (bf16[192,1536]{1,0:T(8,128)(2,1)S(1)}, bf16[192,1536]{1,0:T(8,128)(2,1)S(1)}, u32[]{:S(2)}, u32[]{:S(2)}) collective-permute-start(bf16[192,1536]{1,0:T(8,128)(2,1)S(1)} %get-tuple-element.45), channel_id=1, source_target_pairs={{0,1},{1,0},{2,3},{3,2},{4,5},{5,4},{6,7},{7,6},{8,9},{9,8},{10,11... | collective-permute-start | bytes 1769480 | tf_op jit(solution)/shard_map/ppermute | solution.py:30
  61.5 2.7 %collective-permute-start.20 = (bf16[192,1536]{1,0:T(8,128)(2,1)S(1)}, bf16[192,1536]{1,0:T(8,128)(2,1)S(1)}, u32[]{:S(2)}, u32[]{:S(2)}) collective-permute-start(bf16[192,1536]{1,0:T(8,128)(2,1)S(1)} %get-tuple-element.49.mine_near_ref), channel_id=1, source_target_pairs={{0,1},{1,0},{2,3},{3,2},{4,5},{5,4},{6,7},{7,6},{8,9},{9,8},{10,11... | collective-permute-start | bytes 1769480 | tf_op jit(solution)/shard_map/ppermute | solution.py:30
  61.8 3.2 %collective-permute-start.21 = (bf16[192,1536]{1,0:T(8,128)(2,1)S(1)}, bf16[192,1536]{1,0:T(8,128)(2,1)S(1)}, u32[]{:S(2)}, u32[]{:S(2)}) collective-permute-start(bf16[192,1536]{1,0:T(8,128)(2,1)S(1)} %collective-permute-done.10.mine_far_ref), channel_id=1, source_target_pairs={{0,1},{1,0},{2,3},{3,2},{4,5},{5,4},{6,7},{7,6},{8,9},{9,8},{10,11... | collective-permute-start | bytes 1769480 | tf_op jit(solution)/shard_map/ppermute | solution.py:30
  62.0 16.5 %collective-permute-start.13 = (bf16[192,1536]{1,0:T(8,128)(2,1)S(1)}, bf16[192,1536]{1,0:T(8,128)(2,1)S(1)}, u32[]{:S(2)}, u32[]{:S(2)}) collective-permute-start(bf16[192,1536]{1,0:T(8,128)(2,1)S(1)} %get-tuple-element.43), channel_id=1, source_target_pairs={{0,1},{1,0},{2,3},{3,2},{4,5},{5,4},{6,7},{7,6},{8,9},{9,8},{10,11... | collective-permute-start | bytes 1769480 | tf_op jit(solution)/shard_map/ppermute | solution.py:30
  63.4 15.0 %collective-permute-start.15 = (bf16[192,1536]{1,0:T(8,128)(2,1)S(1)}, bf16[192,1536]{1,0:T(8,128)(2,1)S(1)}, u32[]{:S(2)}, u32[]{:S(2)}) collective-permute-start(bf16[192,1536]{1,0:T(8,128)(2,1)S(1)} %add_convert_fusion.1), channel_id=1, source_target_pairs={{0,2},{1,5},{2,0},{3,7},{4,6},{5,1},{6,4},{7,3},{8,10},{9,13},{10,... | collective-permute-start | bytes 1769480 | tf_op jit(solution)/shard_map/ppermute | solution.py:30
  77.9 2.4 %collective-permute-start.23 = (bf16[192,1536]{1,0:T(8,128)(2,1)S(1)}, bf16[192,1536]{1,0:T(8,128)(2,1)S(1)}, u32[]{:S(2)}, u32[]{:S(2)}) collective-permute-start(bf16[192,1536]{1,0:T(8,128)(2,1)S(1)} %get-tuple-element.54), channel_id=1, source_target_pairs={{0,1},{1,0},{2,3},{3,2},{4,5},{5,4},{6,7},{7,6},{8,9},{9,8},{10,11... | collective-permute-start | bytes 1769480 | tf_op jit(solution)/shard_map/ppermute | solution.py:30
  78.2 12.9 %collective-permute-start.22 = (bf16[192,1536]{1,0:T(8,128)(2,1)S(1)}, bf16[192,1536]{1,0:T(8,128)(2,1)S(1)}, u32[]{:S(2)}, u32[]{:S(2)}) collective-permute-start(bf16[192,1536]{1,0:T(8,128)(2,1)S(1)} %get-tuple-element.52), channel_id=1, source_target_pairs={{0,1},{1,0},{2,3},{3,2},{4,5},{5,4},{6,7},{7,6},{8,9},{9,8},{10,11... | collective-permute-start | bytes 1769480 | tf_op jit(solution)/shard_map/ppermute | solution.py:30
  79.1 11.8 %collective-permute-start.16 = (bf16[128,1536]{1,0:T(8,128)(2,1)S(1)}, bf16[128,1536]{1,0:T(8,128)(2,1)S(1)}, u32[]{:S(2)}, u32[]{:S(2)}) collective-permute-start(bf16[128,1536]{1,0:T(8,128)(2,1)S(1)} %get-tuple-element.47), channel_id=1, source_target_pairs={{0,4},{1,3},{2,6},{3,1},{4,0},{5,7},{6,2},{7,5},{8,12},{9,11},{10,... | collective-permute-start | bytes 1179656 | tf_op jit(solution)/shard_map/ppermute | solution.py:30
  80.4 12.1 %collective-permute-start.24 = (bf16[192,1536]{1,0:T(8,128)(2,1)S(1)}, bf16[192,1536]{1,0:T(8,128)(2,1)S(1)}, u32[]{:S(2)}, u32[]{:S(2)}) collective-permute-start(bf16[192,1536]{1,0:T(8,128)(2,1)S(1)} %add_convert_fusion), channel_id=1, source_target_pairs={{0,2},{1,5},{2,0},{3,7},{4,6},{5,1},{6,4},{7,3},{8,10},{9,13},{10,... | collective-permute-start | bytes 1769480 | tf_op jit(solution)/shard_map/ppermute | solution.py:30
  93.2 7.8 %collective-permute-start.25 = (bf16[128,1536]{1,0:T(8,128)(2,1)S(1)}, bf16[128,1536]{1,0:T(8,128)(2,1)S(1)}, u32[]{:S(2)}, u32[]{:S(2)}) collective-permute-start(bf16[128,1536]{1,0:T(8,128)(2,1)S(1)} %get-tuple-element.56), channel_id=1, source_target_pairs={{0,4},{1,3},{2,6},{3,1},{4,0},{5,7},{6,2},{7,5},{8,12},{9,11},{10,... | collective-permute-start | bytes 1179656 | tf_op jit(solution)/shard_map/ppermute | solution.py:30
  94.4 9.1 %collective-permute-start.17 = (bf16[32,1536]{1,0:T(8,128)(2,1)S(1)}, bf16[32,1536]{1,0:T(8,128)(2,1)S(1)}, u32[]{:S(2)}, u32[]{:S(2)}) collective-permute-start(bf16[32,1536]{1,0:T(8,128)(2,1)S(1)} %get-tuple-element.65), channel_id=1, source_target_pairs={{0,8},{1,9},{2,10},{3,11},{4,12},{5,13},{6,14},{7,15},{8,0},{9,1},... | collective-permute-start | bytes 294920 | tf_op jit(solution)/shard_map/ppermute | solution.py:30
  96.3 10.3 %collective-permute-start.18 = (bf16[32,1536]{1,0:T(8,128)(2,1)S(1)}, bf16[32,1536]{1,0:T(8,128)(2,1)S(1)}, u32[]{:S(2)}, u32[]{:S(2)}) collective-permute-start(bf16[32,1536]{1,0:T(8,128)(2,1)S(1)} %get-tuple-element.67), channel_id=1, source_target_pairs={{0,16},{1,17},{2,18},{3,19},{4,20},{5,21},{6,22},{7,23},{8,24},{9,... | collective-permute-start | bytes 294920 | tf_op jit(solution)/shard_map/ppermute | solution.py:30
  96.6 10.0 %collective-permute-start.19 = (bf16[32,1536]{1,0:T(8,128)(2,1)S(1)}, bf16[32,1536]{1,0:T(8,128)(2,1)S(1)}, u32[]{:S(2)}, u32[]{:S(2)}) collective-permute-start(bf16[32,1536]{1,0:T(8,128)(2,1)S(1)} %get-tuple-element.66), channel_id=1, source_target_pairs={{0,24},{1,25},{2,26},{3,27},{4,28},{5,29},{6,30},{7,31},{8,16},{9,... | collective-permute-start | bytes 294920 | tf_op jit(solution)/shard_map/ppermute | solution.py:30
  101.2 6.3 %collective-permute-start.26 = (bf16[32,1536]{1,0:T(8,128)(2,1)S(1)}, bf16[32,1536]{1,0:T(8,128)(2,1)S(1)}, u32[]{:S(2)}, u32[]{:S(2)}) collective-permute-start(bf16[32,1536]{1,0:T(8,128)(2,1)S(1)} %get-tuple-element.68), channel_id=1, source_target_pairs={{0,8},{1,9},{2,10},{3,11},{4,12},{5,13},{6,14},{7,15},{8,0},{9,1},... | collective-permute-start | bytes 294920 | tf_op jit(solution)/shard_map/ppermute | solution.py:30
  102.5 12.0 %collective-permute-start.27 = (bf16[32,1536]{1,0:T(8,128)(2,1)S(1)}, bf16[32,1536]{1,0:T(8,128)(2,1)S(1)}, u32[]{:S(2)}, u32[]{:S(2)}) collective-permute-start(bf16[32,1536]{1,0:T(8,128)(2,1)S(1)} %get-tuple-element.70), channel_id=1, source_target_pairs={{0,16},{1,17},{2,18},{3,19},{4,20},{5,21},{6,22},{7,23},{8,24},{9,... | collective-permute-start | bytes 294920 | tf_op jit(solution)/shard_map/ppermute | solution.py:30
  103.5 10.9 %collective-permute-start.28 = (bf16[32,1536]{1,0:T(8,128)(2,1)S(1)}, bf16[32,1536]{1,0:T(8,128)(2,1)S(1)}, u32[]{:S(2)}, u32[]{:S(2)}) collective-permute-start(bf16[32,1536]{1,0:T(8,128)(2,1)S(1)} %get-tuple-element.69), channel_id=1, source_target_pairs={{0,24},{1,25},{2,26},{3,27},{4,28},{5,29},{6,30},{7,31},{8,16},{9,... | collective-permute-start | bytes 294920 | tf_op jit(solution)/shard_map/ppermute | solution.py:30
  114.5 1.5 %copy-start = (bf16[2,16,2880]{2,1,0:T(8,128)(2,1)S(1)}, bf16[2,16,2880]{2,1,0:T(8,128)(2,1)}, u32[]{:S(2)}) copy-start(bf16[2,16,2880]{2,1,0:T(8,128)(2,1)} %param.7) | copy-start | bytes 552964
  114.5 1.4 %collective-permute-start.29 = (bf16[2,16,1536]{2,1,0:T(8,128)(2,1)S(1)}, bf16[2,16,1536]{2,1,0:T(8,128)(2,1)S(1)}, u32[]{:S(2)}, u32[]{:S(2)}) collective-permute-start(bf16[2,16,1536]{2,1,0:T(8,128)(2,1)S(1)} %select_convert_fusion), channel_id=1, source_target_pairs={{0,1},{1,0},{2,3},{3,2},{4,5},{5,4},{6,7},{7,6},{8,9},{9,8},{10,11... | collective-permute-start | bytes 294920 | tf_op jit(solution)/shard_map/ppermute | solution.py:30

commit v3 on v2

--- a/solution.py
+++ b/solution.py
@@ -53,11 +53,11 @@
 SCALARS = pl.BlockSpec(memory_space=pltpu.SMEM)
 
 
-def select_body(tokens, capacity, places_ref, near_ref, next_ref, own_ref, send_ref, slots_ref):
+def select_body(tokens, capacity, index, places_ref, near_ref, next_ref, rows_ref, *slots_refs):
     rows = near_ref.shape[0]
     held = near_ref.shape[1]
     total = 2 * rows
-    compact = own_ref.shape[0]
+    compact = rows_ref.shape[0]
     tile = jnp.concatenate([near_ref[:, held - LANES :], next_ref[:, held - LANES :]], axis=0).astype(jnp.float32)
     lane = lax.broadcasted_iota(jnp.int32, (total, LANES), 1)
     row = lax.broadcasted_iota(jnp.int32, (total, LANES), 0)
@@ -73,26 +73,26 @@
     earlier = ((right < left) & (left // tokens == right // tokens)).astype(jnp.float32).astype(jnp.bfloat16)
     ahead = jnp.dot(earlier, marks.astype(jnp.bfloat16), preferred_element_type=jnp.float32)
     slots = jnp.where(marks > 0.0, ahead + (row // tokens * capacity).astype(jnp.float32), -1.0)
-    slots_ref[...] = slots
+    for slots_ref in slots_refs:
+        slots_ref[...] = slots
     column = lax.broadcasted_iota(jnp.int32, (total, compact), 1).astype(jnp.float32)
-    for index, target in enumerate((own_ref, send_ref)):
-        picks = (slots[:, index : index + 1] == column).astype(jnp.float32).astype(jnp.bfloat16)
-        target[...] = (
-            lax.dot_general(picks[:rows], near_ref[...], downward, preferred_element_type=jnp.float32)
-            + lax.dot_general(picks[rows:], next_ref[...], downward, preferred_element_type=jnp.float32)
-        ).astype(jnp.bfloat16)
-
-
-def select(tokens, capacity, places, near, following):
+    picks = (slots[:, index : index + 1] == column).astype(jnp.float32).astype(jnp.bfloat16)
+    rows_ref[...] = (
+        lax.dot_general(picks[:rows], near_ref[...], downward, preferred_element_type=jnp.float32)
+        + lax.dot_general(picks[rows:], next_ref[...], downward, preferred_element_type=jnp.float32)
+    ).astype(jnp.bfloat16)
+
+
+def select(tokens, capacity, index, places, near, following):
     rows, held = near.shape
     compact = 2 * rows // tokens * capacity
     block = jax.ShapeDtypeStruct((compact, held), jnp.bfloat16)
     return pl.pallas_call(
-        functools.partial(select_body, tokens, capacity),
-        out_shape=[block, block, jax.ShapeDtypeStruct((2 * rows, LANES), jnp.float32)],
+        functools.partial(select_body, tokens, capacity, index),
+        out_shape=[block] + [jax.ShapeDtypeStruct((2 * rows, LANES), jnp.float32)] * (1 - index),
         in_specs=[SCALARS] + whole_arrays(2),
-        out_specs=whole_arrays(3),
-        compiler_params=pltpu.CompilerParams(vmem_limit_bytes=40 * 2**20),
+        out_specs=whole_arrays(2 - index),
+        compiler_params=pltpu.CompilerParams(vmem_limit_bytes=20 * 2**20),
         cost_estimate=pl.CostEstimate(flops=8 * rows * compact * held, bytes_accessed=8 * rows * held, transcendentals=0),
     )(places, near, following)
 
@@ -124,29 +124,20 @@
         ],
         in_specs=whole_arrays(4),
         out_specs=whole_arrays(2),
-        compiler_params=pltpu.CompilerParams(vmem_limit_bytes=40 * 2**20),
+        compiler_params=pltpu.CompilerParams(vmem_limit_bytes=20 * 2**20),
         cost_estimate=pl.CostEstimate(flops=8 * rows * compact * held, bytes_accessed=8 * rows * held, transcendentals=0),
     )(slots, keep, taken, arrived)
 
 
 def ffn_body(
-    places_ref, mine_near_ref, mine_far_ref, other_near_ref, other_far_ref, gate_hbm, up_hbm, down_hbm,
-    keep_near_ref, keep_far_ref, send_near_ref, send_far_ref, gate_v, up_v, down_v, rows_v, act_v, sems,
+    places_ref, mine_near_ref, mine_far_ref, other_near_ref, other_far_ref, gate_v, up_v, down_v,
+    keep_near_ref, keep_far_ref, send_near_ref, send_far_ref, rows_v, act_v,
 ):
     hidden, width = gate_v.shape
     first, second, held = split_widths(width)
     pair = mine_near_ref.shape[0]
     quad = pair // 2
     chunk = hidden // 3
-    copies = []
-    for part in range(3):
-        for place, (source, target) in enumerate(((gate_hbm, gate_v), (up_hbm, up_v))):
-            there = pl.ds(part * chunk, chunk)
-            copies.append(pltpu.make_async_copy(source.at[there], target.at[there], sems.at[2 * part + place]))
-    copies.append(pltpu.make_async_copy(down_hbm, down_v, sems.at[6]))
-    for copy in copies:
-        copy.start()
-
     def lay(near, far_ref, swapped, start, size):
         for place in range(4):
             if swapped:
@@ -178,12 +169,9 @@
 
     for part in range(3):
         there = slice(part * chunk, (part + 1) * chunk)
-        copies[2 * part].wait()
         gate = lax.dot_general(rows_v[...], gate_v[there, :], across, preferred_element_type=jnp.float32)
-        copies[2 * part + 1].wait()
         up = lax.dot_general(rows_v[...], up_v[there, :], across, preferred_element_type=jnp.float32)
         act_v[:, there] = ((up + 1.0) * gate * jax.nn.sigmoid(swish_scale * gate)).astype(jnp.bfloat16)
-    copies[6].wait()
 
     def keep_half(result, size):
         keep_near_ref[:, :size] = result[:pair]
@@ -226,28 +214,108 @@
     pair, held = mine_near.shape
     hidden, width = gate_t.shape
     total = 2 * pair
-    hbm = pl.BlockSpec(memory_space=pl.ANY)
     return pl.pallas_call(
         ffn_body,
         out_shape=[jax.ShapeDtypeStruct((pair, held), jnp.float32)] * 2
         + [jax.ShapeDtypeStruct((pair, held), jnp.bfloat16)] * 2,
-        in_specs=[SCALARS] + whole_arrays(4) + [hbm] * 3,
+        in_specs=[SCALARS] + whole_arrays(7),
         out_specs=whole_arrays(4),
         scratch_shapes=[
-            pltpu.VMEM((hidden, width), jnp.bfloat16),
-            pltpu.VMEM((hidden, width), jnp.bfloat16),
-            pltpu.VMEM((hidden, width), jnp.bfloat16),
             pltpu.VMEM((total, width), jnp.bfloat16),
             pltpu.VMEM((total, hidden), jnp.bfloat16),
-            pltpu.SemaphoreType.DMA((7,)),
         ],
-        compiler_params=pltpu.CompilerParams(vmem_limit_bytes=48 * 2**20),
+        compiler_params=pltpu.CompilerParams(vmem_limit_bytes=20 * 2**20),
         cost_estimate=pl.CostEstimate(
             flops=6 * total * width * hidden,
             bytes_accessed=6 * width * hidden + 8 * total * held,
             transcendentals=total * hidden,
         ),
     )(places, mine_near, mine_far, other_near, other_far, gate_t, up_t, w_down)
+
+
+def preload_body(_, *refs):
+    count = (len(refs) - 1) // 2
+    sems = refs[-1]
+    copies = [pltpu.make_async_copy(refs[i], refs[count + i], sems.at[i]) for i in range(count)]
+    for copy in copies:
+        copy.start()
+    for copy in copies:
+        copy.wait()
+
+
+def preload(token, *arrays):
+    return pl.pallas_call(
+        preload_body,
+        out_shape=[pltpu.VMEM(a.shape, a.dtype) for a in arrays],
+        in_specs=[pl.BlockSpec(memory_space=pl.ANY)] + [pl.BlockSpec(memory_space=pltpu.HBM)] * len(arrays),
+        out_specs=whole_arrays(len(arrays)),
+        scratch_shapes=[pltpu.SemaphoreType.DMA((len(arrays),))],
+        compiler_params=pltpu.CompilerParams(vmem_limit_bytes=20 * 2**20),
+    )(token, *arrays)
+
+
+def prologue_body(
+    tokens, top_count, places_ref, hidden_ref, gain_ref, ids_ref, weights_ref, mine_ref, give_ref
+):
+    micro_count, _, width = hidden_ref.shape
+    first, second, held = split_widths(width)
+    lane = lax.broadcasted_iota(jnp.int32, (tokens, LANES), 1)
+    here = lane % (ROUTING // 2)
+    on_ids = (lane >= LANES - ROUTING) & (lane < LANES - ROUTING // 2)
+    on_weights = lane >= LANES - ROUTING // 2
+    diagonal = lax.broadcasted_iota(jnp.int32, (tokens, tokens), 0) == lax.broadcasted_iota(
+        jnp.int32, (tokens, tokens), 1
+    )
+
+    def upright(line):
+        return jnp.sum(jnp.where(diagonal, line, 0.0), axis=1, keepdims=True)
+
+    def store(ref, b, part, tile):
+        size = part.shape[1]
+        inside = size // LANES * LANES
+        ref[b, :, :inside] = part[:, :inside].astype(jnp.bfloat16)
+        if inside < size:
+            rest = jnp.concatenate([part[:, inside:], jnp.zeros((tokens, LANES - size + inside), jnp.float32)], axis=1)
+            tile = jnp.where(lane < size - inside, rest, tile)
+        ref[b, :, inside:] = tile.astype(jnp.bfloat16)
+
+    lower = places_ref[0] == 0
+    for b in range(micro_count):
+        residual = hidden_ref[b].astype(jnp.float32)
+        scale = lax.rsqrt(jnp.mean(residual * residual, axis=-1, keepdims=True) + epsilon)
+        normed = residual * scale * gain_ref[...].astype(jnp.float32)
+        tile = jnp.where(on_ids, -1.0, 0.0)
+        for k in range(top_count):
+            number = upright(ids_ref[b, k : k + 1, :].astype(jnp.float32))
+            weight = upright(weights_ref[b, k : k + 1, :])
+            high = weight.astype(jnp.bfloat16).astype(jnp.float32)
+            middle = (weight - high).astype(jnp.bfloat16).astype(jnp.float32)
+            for place, piece in enumerate((high, middle, weight - high - middle)):
+                at = here == place * top_count + k
+                tile = jnp.where(at & on_ids, number, jnp.where(at & on_weights, piece, tile))
+        parts = normed[:, :first], normed[:, first:]
+
+        @pl.when(lower)
+        def _():
+            store(mine_ref, b, parts[0], tile)
+            store(give_ref, b, parts[1], tile)
+
+        @pl.when(jnp.logical_not(lower))
+        def _():
+            store(mine_ref, b, parts[1], tile)
+            store(give_ref, b, parts[0], tile)
+
+
+def prologue(places, hidden, gain, ids, weights):
+    micro_count, tokens, width = hidden.shape
+    held = split_widths(width)[2]
+    return pl.pallas_call(
+        functools.partial(prologue_body, tokens, ids.shape[1]),
+        out_shape=[jax.ShapeDtypeStruct((micro_count, tokens, held), jnp.bfloat16)] * 2,
+        in_specs=[SCALARS] + whole_arrays(4),
+        out_specs=whole_arrays(2),
+        compiler_params=pltpu.CompilerParams(vmem_limit_bytes=20 * 2**20),
+    )(places, hidden, gain, ids, weights)
 
 
 def local(hidden, norm_gain, w_gate, w_up, w_down, expert_ids, route_weight):
@@ -264,56 +332,49 @@
     lower = core == 0
     expert = position // HSPLIT
     places = jnp.stack([core, expert, expert ^ core]).astype(jnp.int32)
-    gate_t, up_t = w_gate.T, w_up.T
 
     def join(*blocks):
         return jnp.concatenate(blocks, axis=0)
 
-    residual = hidden.astype(jnp.float32)
-    normed = (
-        residual
-        * lax.rsqrt(jnp.mean(residual * residual, axis=-1, keepdims=True) + epsilon)
-        * norm_gain.astype(jnp.float32)
-    ).astype(jnp.bfloat16)
-    high = lax.reduce_precision(route_weight, 8, 7)
-    middle = lax.reduce_precision(route_weight - high, 8, 7)
-    low = route_weight - high - middle
-    ids = expert_ids.astype(jnp.float32)
-    gap = jnp.full((micro_count, tokens, ROUTING // 2 - 3 * top_count), -1.0, jnp.float32)
-    routing = jnp.concatenate([ids, ids, ids, gap, high, middle, low, gap], axis=2).astype(jnp.bfloat16)
-
-    def padded(part):
-        blank = jnp.zeros((micro_count, tokens, held - ROUTING - part.shape[2]), jnp.bfloat16)
-        return jnp.concatenate([part, blank, routing], axis=2)
-
-    low_half, high_half = padded(normed[:, :, :first]), padded(normed[:, :, first:])
-    mine = jnp.where(lower, low_half, high_half)
-    theirs = moved(jnp.where(lower, high_half, low_half), other_core)
+    mine, give = prologue(
+        places, hidden, norm_gain.reshape(1, width), expert_ids.transpose(0, 2, 1), route_weight.transpose(0, 2, 1)
+    )
+    theirs = moved(give, other_core)
     pairs = [
         join(jnp.where(lower, mine[b], theirs[b]), jnp.where(lower, theirs[b], mine[b]))
         for b in range(micro_count)
     ]
 
-    def column_of(pair):
-        return join(pair, *[moved(pair, far(j)) for j in range(1, distant)])
-
     def tied(*arrays):
         return lax.optimization_barrier(arrays)
 
-    held_state = []
-    last = None
-    for b in range(micro_count):
-        pair = pairs[b]
-        if last is not None:
-            pair, _ = tied(pair, last["column"])
-        column = column_of(pair)
-        following = moved(column, first_axis)
-        own, send, slots = select(tokens, capacity, places, column, following)
-        if last is not None:
-            send, last["arrived"] = tied(send, last["arrived"])
-        arrived = moved(send, second_axis)
-        last = {"column": column, "own": own, "slots": slots, "arrived": arrived}
-        held_state.append(last)
+    def far_blocks(pair):
+        return [moved(pair, far(j)) for j in range(1, distant)]
+
+    def second_hop(state, earlier):
+        following = moved(state["column"], first_axis)
+        chosen = tokens, capacity
+        (send,) = select(*chosen, 1, places, state["column"], following)
+        if earlier is not None:
+            send, earlier["arrived"] = tied(send, earlier["arrived"])
+        state["arrived"] = moved(send, second_axis)
+        state["own"], state["slots"] = select(*chosen, 0, places, state["column"], following)
+
+    states = []
+    gate_v, up_v, down_v = preload(pairs[0], w_gate.T, w_up.T, w_down)
+    for pair in pairs:
+        if states:
+            last = states[-1]
+            pair, last["column"] = tied(pair, last["column"])
+        blocks = far_blocks(pair)
+        if states:
+            second_hop(last, states[-2] if len(states) > 1 else None)
+            *blocks, last["own"] = tied(*blocks, last["own"])
+        else:
+            blocks[0], gate_v, up_v, down_v = tied(blocks[0], gate_v, up_v, down_v)
+        states.append({"column": join(pair, *blocks)})
+    second_hop(states[-1], states[-2] if len(states) > 1 else None)
+    held_state = states
 
     outputs = []
     before = None
@@ -324,7 +385,7 @@
             arrived, *before = tied(arrived, *before)
             outputs[-1] = before
         before = ffn(
-            places, own, arrived, moved(own, other_core), moved(arrived, other_core), gate_t, up_t, w_down
+            places, own, arrived, moved(own, other_core), moved(arrived, other_core), gate_v, up_v, down_v
         )
         outputs.append(before)
 
@@ -346,7 +407,7 @@
     mixture = jnp.concatenate(
         [jnp.where(lower, own, taken)[:, :, :first], jnp.where(lower, taken, own)[:, :, :second]], axis=2
     )
-    return (residual + mixture).astype(jnp.bfloat16)
+    return (hidden.astype(jnp.float32) + mixture).astype(jnp.bfloat16)
 
 
 def solution(mesh):

time: 117 us -> 105 us (0.90)
  waiting for transfers between devices: 49.6 us -> 36 us
  local copies, waits for them, and re-layouts: 1.97 us -> 9.7 us
  Pallas kernels: 30.4 us -> 23 us
  starting transfers between devices: 29.3 us -> 34.3 us
  other arithmetic: 5.03 us -> 1.52 us
    ppermute x30, waiting for transfers between devices: 49.6 us -> 36 us  [moved(): return lax.ppermute(block, 'req', [(i, partner(i)) for i in range(count)])]
    pallas_call x2, Pallas kernels: 25.8 us -> 14 us  [ffn(): pl.pallas_call(ffn_body, out_shape=[jax.ShapeDtypeStruct((pair, held), jn...]
    unnamed x9 -> x19, local copies, waits for them, and re-layouts: 1.58 us -> 8.94 us
    ppermute x30, starting transfers between devices: 29.3 us -> 34.3 us  [moved(): return lax.ppermute(block, 'req', [(i, partner(i)) for i in range(count)])]
    pallas_call x2 -> x6, Pallas kernels: 3.41 us -> 7.73 us  [the longest x4 5.85 us: select(): pl.pallas_call(functools.partial(select_body, tokens, capacity, index), o...]
    convert_element_type x3 -> x1, other arithmetic: 2.47 us -> 0.73 us  [local(): return (hidden.astype(jnp.float32) + mixture).astype(jnp.bfloat16)]
  transfers between devices with their start and end apart: 30 -> 30, of which waited for: 17 -> 17; matrix products, arithmetic and copies ran while one was open for 1% -> 1% of each run, Pallas kernels for 26% -> 21%
where the time goes in v3:
time: 105 us
  waiting for transfers between devices  36 us (34%)
  starting transfers between devices  34.3 us (33%)
  Pallas kernels  23 us (22%)
  local copies, waits for them, and re-layouts  9.7 us (9%)
  other arithmetic  1.52 us (1%)
    ppermute x30, waiting for transfers between devices, moved(): return lax.ppermute(block, 'req', [(i, partner(i)) for i in range(count)])  36 us
    ppermute x30, starting transfers between devices, moved(): return lax.ppermute(block, 'req', [(i, partner(i)) for i in range(count)])  34.3 us
    pallas_call x2, Pallas kernels, ffn(): pl.pallas_call(ffn_body, out_shape=[jax.ShapeDtypeStruct((pair, held), jn...  14 us
    unnamed x19, local copies, waits for them, and re-layouts  8.94 us
    pallas_call x4, Pallas kernels, select(): pl.pallas_call(functools.partial(select_body, tokens, capacity, index), o...  5.85 us
  transfers between devices with their start and end apart: 30, of which 17 were waited for; matrix products, arithmetic and copies ran while one was open for 1% of the time, Pallas kernels for 21%

profile of v3, /device:TPU:0, one launch (start us, length us, event | category | flops | bytes accessed | tf_op | source)
XLA Modules:
  0.0 104.8 jit_solution(14557967915715798784)
XLA Ops:
  0.0 0.7 reshape.29.gain_ref
  0.8 0.9 copy-done.3
  1.7 0.7 copy-done.5
  2.4 0.7 copy-done.6
  3.1 0.8 shard_map.73
  4.4 0.9 collective-permute-done
  5.4 3.0 %collective-permute-start.1 = (bf16[32,1536]{1,0:T(8,128)(2,1)S(1)}, bf16[32,1536]{1,0:T(8,128)(2,1)S(1)}, u32[]{:S(2)}, u32[]{:S(2)}) collective-permute-start(bf16[32,1536]{1,0:T(8,128)(2,1)S(1)} %pad_maximum_fusion.2._), channel_id=1, source_target_pairs={{0,8},{1,9},{2,10},{3,11},{4,12},{5,13},{6,14},{7,15},{8,0},{9,1},... | collective-permute-start | bytes 294920 | tf_op jit(solution)/shard_map/ppermute | solution.py:30
  8.4 2.6 %collective-permute-start.2 = (bf16[32,1536]{1,0:T(8,128)(2,1)S(1)}, bf16[32,1536]{1,0:T(8,128)(2,1)S(1)}, u32[]{:S(2)}, u32[]{:S(2)}) collective-permute-start(bf16[32,1536]{1,0:T(8,128)(2,1)S(1)} %pad_maximum_fusion.2._), channel_id=1, source_target_pairs={{0,16},{1,17},{2,18},{3,19},{4,20},{5,21},{6,22},{7,23},{8,24},{9,... | collective-permute-start | bytes 294920 | tf_op jit(solution)/shard_map/ppermute | solution.py:30
  11.1 2.2 %copy-done = bf16[2880,720]{0,1:T(8,128)(2,1)S(1)} copy-done((bf16[2880,720]{0,1:T(8,128)(2,1)S(1)}, bf16[2880,720]{0,1:T(8,128)(2,1)}, u32[]{:S(2)}) %copy-start) | copy-done | bytes 4147224
  13.3 2.2 %copy-done.1 = bf16[2880,720]{0,1:T(8,128)(2,1)S(1)} copy-done((bf16[2880,720]{0,1:T(8,128)(2,1)S(1)}, bf16[2880,720]{0,1:T(8,128)(2,1)}, u32[]{:S(2)}) %copy-start.1) | copy-done | bytes 4147224
  15.5 2.2 %copy-done.2 = bf16[720,2880]{1,0:T(8,128)(2,1)S(1)} copy-done((bf16[720,2880]{1,0:T(8,128)(2,1)S(1)}, bf16[720,2880]{1,0:T(8,128)(2,1)}, u32[]{:S(2)}) %copy-start.2) | copy-done | bytes 4147224
  17.7 1.1 %shard_map.74 = (bf16[720,2880]{1,0:T(8,128)(2,1)S(1)}, bf16[720,2880]{1,0:T(8,128)(2,1)S(1)}, bf16[720,2880]{1,0:T(8,128)(2,1)S(1)}) custom-call(bf16[32,1536]{1,0:T(8,128)(2,1)S(1)} %pad_maximum_fusion.2._, bf16[720,2880]{1,0:T(8,128)(2,1)S(1)} %bitcast.21, bf16[720,2880]{1,0:T(8,128)(2,1)S(1)} %bitcast.22, bf16[720,2880]{1,0:T(8,128)(2,1)S(1)} %copy-done.2), custom_call_target="tpu_custom_call" | custom-call | tf_op jit(solution)/shard_map/pallas_call | solution.py:247
  19.1 1.6 %collective-permute-start.4 = (bf16[128,1536]{1,0:T(8,128)(2,1)S(1)}, bf16[128,1536]{1,0:T(8,128)(2,1)S(1)}, u32[]{:S(2)}, u32[]{:S(2)}) collective-permute-start(bf16[128,1536]{1,0:T(8,128)(2,1)S(1)} %constant_dynamic-update-slice_fusion.near_ref), channel_id=1, source_target_pairs={{0,4},{1,3},{2,6},{3,1},{4,0},{5,7},{6,2},{7,5},{8,12},{9,11},{10,... | collective-permute-start | bytes 1179656 | tf_op jit(solution)/shard_map/ppermute | solution.py:30
  20.7 1.7 %collective-permute-start.5 = (bf16[32,1536]{1,0:T(8,128)(2,1)S(1)}, bf16[32,1536]{1,0:T(8,128)(2,1)S(1)}, u32[]{:S(2)}, u32[]{:S(2)}) collective-permute-start(bf16[32,1536]{1,0:T(8,128)(2,1)S(1)} %pad_maximum_fusion.1), channel_id=1, source_target_pairs={{0,8},{1,9},{2,10},{3,11},{4,12},{5,13},{6,14},{7,15},{8,0},{9,1},... | collective-permute-start | bytes 294920 | tf_op jit(solution)/shard_map/ppermute | solution.py:30
  22.4 2.4 %collective-permute-start.6 = (bf16[32,1536]{1,0:T(8,128)(2,1)S(1)}, bf16[32,1536]{1,0:T(8,128)(2,1)S(1)}, u32[]{:S(2)}, u32[]{:S(2)}) collective-permute-start(bf16[32,1536]{1,0:T(8,128)(2,1)S(1)} %pad_maximum_fusion.1), channel_id=1, source_target_pairs={{0,16},{1,17},{2,18},{3,19},{4,20},{5,21},{6,22},{7,23},{8,24},{9,... | collective-permute-start | bytes 294920 | tf_op jit(solution)/shard_map/ppermute | solution.py:30
  25.1 1.9 %collective-permute-done.4.next_ref = bf16[128,1536]{1,0:T(8,128)(2,1)S(1)} collective-permute-done((bf16[128,1536]{1,0:T(8,128)(2,1)S(1)}, bf16[128,1536]{1,0:T(8,128)(2,1)S(1)}, u32[]{:S(2)}, u32[]{:S(2)}) %collective-permute-start.4) | collective-permute-done | bytes 393248 | tf_op jit(solution)/shard_map/ppermute | solution.py:30
  27.0 1.5 %shard_map.77 = bf16[192,1536]{1,0:T(8,128)(2,1)S(1)} custom-call(s32[3]{0:T(128)S(1)} %pad_add_fusion.places_ref, bf16[128,1536]{1,0:T(8,128)(2,1)S(1)} %constant_dynamic-update-slice_fusion.near_ref, bf16[128,1536]{1,0:T(8,128)(2,1)S(1)} %collective-permute-done.4.next_ref), custom_call_target="tpu_custom_call" | custom-call | flops 301989888 | bytes 1572864 | tf_op jit(solution)/shard_map/pallas_call | solution.py:90
  28.4 1.6 %collective-permute-start.9 = (bf16[192,1536]{1,0:T(8,128)(2,1)S(1)}, bf16[192,1536]{1,0:T(8,128)(2,1)S(1)}, u32[]{:S(2)}, u32[]{:S(2)}) collective-permute-start(bf16[192,1536]{1,0:T(8,128)(2,1)S(1)} %shard_map.77), channel_id=1, source_target_pairs={{0,2},{1,5},{2,0},{3,7},{4,6},{5,1},{6,4},{7,3},{8,10},{9,13},{10,... | collective-permute-start | bytes 1769480 | tf_op jit(solution)/shard_map/ppermute | solution.py:30
  30.0 1.5 %shard_map.75 = (bf16[192,1536]{1,0:T(8,128)(2,1)S(1)}, f32[256,128]{1,0:T(8,128)S(1)}) custom-call(s32[3]{0:T(128)S(1)} %pad_add_fusion.places_ref, bf16[128,1536]{1,0:T(8,128)(2,1)S(1)} %constant_dynamic-update-slice_fusion.near_ref, bf16[128,1536]{1,0:T(8,128)(2,1)S(1)} %collective-permute-done.4.next_ref), custom_call_target="tpu_custom_call" | custom-call | flops 301989888 | bytes 1572864 | tf_op jit(solution)/shard_map/pallas_call | solution.py:90
  31.9 1.4 %collective-permute-start.8 = (bf16[128,1536]{1,0:T(8,128)(2,1)S(1)}, bf16[128,1536]{1,0:T(8,128)(2,1)S(1)}, u32[]{:S(2)}, u32[]{:S(2)}) collective-permute-start(bf16[128,1536]{1,0:T(8,128)(2,1)S(1)} %constant_dynamic-update-slice_fusion.5.near_ref), channel_id=1, source_target_pairs={{0,4},{1,3},{2,6},{3,1},{4,0},{5,7},{6,2},{7,5},{8,12},{9,11},{10,... | collective-permute-start | bytes 1179656 | tf_op jit(solution)/shard_map/ppermute | solution.py:30
  33.3 6.7 %collective-permute-done.8.next_ref = bf16[128,1536]{1,0:T(8,128)(2,1)S(1)} collective-permute-done((bf16[128,1536]{1,0:T(8,128)(2,1)S(1)}, bf16[128,1536]{1,0:T(8,128)(2,1)S(1)}, u32[]{:S(2)}, u32[]{:S(2)}) %collective-permute-start.8) | collective-permute-done | bytes 393248 | tf_op jit(solution)/shard_map/ppermute | solution.py:30
  40.0 1.5 %shard_map.76 = bf16[192,1536]{1,0:T(8,128)(2,1)S(1)} custom-call(s32[3]{0:T(128)S(1)} %pad_add_fusion.places_ref, bf16[128,1536]{1,0:T(8,128)(2,1)S(1)} %constant_dynamic-update-slice_fusion.5.near_ref, bf16[128,1536]{1,0:T(8,128)(2,1)S(1)} %collective-permute-done.8.next_ref), custom_call_target="tpu_custom_call" | custom-call | flops 301989888 | bytes 1572864 | tf_op jit(solution)/shard_map/pallas_call | solution.py:90
  41.5 1.1 %collective-permute-done.9.mine_far_ref = bf16[192,1536]{1,0:T(8,128)(2,1)S(1)} collective-permute-done((bf16[192,1536]{1,0:T(8,128)(2,1)S(1)}, bf16[192,1536]{1,0:T(8,128)(2,1)S(1)}, u32[]{:S(2)}, u32[]{:S(2)}) %collective-permute-start.9) | collective-permute-done | bytes 589856 | tf_op jit(solution)/shard_map/ppermute | solution.py:30
  42.6 1.5 %collective-permute-start.10 = (bf16[192,1536]{1,0:T(8,128)(2,1)S(1)}, bf16[192,1536]{1,0:T(8,128)(2,1)S(1)}, u32[]{:S(2)}, u32[]{:S(2)}) collective-permute-start(bf16[192,1536]{1,0:T(8,128)(2,1)S(1)} %shard_map.76), channel_id=1, source_target_pairs={{0,2},{1,5},{2,0},{3,7},{4,6},{5,1},{6,4},{7,3},{8,10},{9,13},{10,... | collective-permute-start | bytes 1769480 | tf_op jit(solution)/shard_map/ppermute | solution.py:30
  44.6 6.9 %shard_map.78 = (f32[192,1536]{1,0:T(8,128)S(1)}, f32[192,1536]{1,0:T(8,128)S(1)}, bf16[192,1536]{1,0:T(8,128)(2,1)S(1)}, bf16[192,1536]{1,0:T(8,128)(2,1)S(1)}) custom-call(s32[3]{0:T(128)S(1)} %pad_add_fusion.places_ref, bf16[192,1536]{1,0:T(8,128)(2,1)S(1)} %get-tuple-element.57.mine_near_ref, bf16[192,1536]{1,0:T(8,128)(2,1)S(1)} %collective-permute-done.9.mine_far_ref, ...), custom_call_target="tpu_custom_call" | custom-call | flops 4777574400 | bytes 17160192 | tf_op jit(solution)/shard_map/pallas_call | solution.py:217
  51.5 1.0 collective-permute-done.10.mine_far_ref
  52.5 1.5 %shard_map.80 = (bf16[192,1536]{1,0:T(8,128)(2,1)S(1)}, f32[256,128]{1,0:T(8,128)S(1)}) custom-call(s32[3]{0:T(128)S(1)} %pad_add_fusion.places_ref, bf16[128,1536]{1,0:T(8,128)(2,1)S(1)} %constant_dynamic-update-slice_fusion.5.near_ref, bf16[128,1536]{1,0:T(8,128)(2,1)S(1)} %collective-permute-done.8.next_ref), custom_call_target="tpu_custom_call" | custom-call | flops 301989888 | bytes 1572864 | tf_op jit(solution)/shard_map/pallas_call | solution.py:90
  54.0 0.6 collective-permute-start.20
  55.2 1.5 %collective-permute-start.15 = (bf16[192,1536]{1,0:T(8,128)(2,1)S(1)}, bf16[192,1536]{1,0:T(8,128)(2,1)S(1)}, u32[]{:S(2)}, u32[]{:S(2)}) collective-permute-start(bf16[192,1536]{1,0:T(8,128)(2,1)S(1)} %add_convert_fusion.1), channel_id=1, source_target_pairs={{0,2},{1,5},{2,0},{3,7},{4,6},{5,1},{6,4},{7,3},{8,10},{9,13},{10,... | collective-permute-start | bytes 1769480 | tf_op jit(solution)/shard_map/ppermute | solution.py:30
  57.0 7.1 %shard_map.81 = (f32[192,1536]{1,0:T(8,128)S(1)}, f32[192,1536]{1,0:T(8,128)S(1)}, bf16[192,1536]{1,0:T(8,128)(2,1)S(1)}, bf16[192,1536]{1,0:T(8,128)(2,1)S(1)}) custom-call(s32[3]{0:T(128)S(1)} %pad_add_fusion.places_ref, bf16[192,1536]{1,0:T(8,128)(2,1)S(1)} %get-tuple-element.73.mine_near_ref, bf16[192,1536]{1,0:T(8,128)(2,1)S(1)} %collective-permute-done.10.mine_far_ref, ...), custom_call_target="tpu_custom_call" | custom-call | flops 4777574400 | bytes 17160192 | tf_op jit(solution)/shard_map/pallas_call | solution.py:217
  65.1 0.6 shard_map.79
  65.8 1.6 %collective-permute-start.16 = (bf16[128,1536]{1,0:T(8,128)(2,1)S(1)}, bf16[128,1536]{1,0:T(8,128)(2,1)S(1)}, u32[]{:S(2)}, u32[]{:S(2)}) collective-permute-start(bf16[128,1536]{1,0:T(8,128)(2,1)S(1)} %get-tuple-element.71), channel_id=1, source_target_pairs={{0,4},{1,3},{2,6},{3,1},{4,0},{5,7},{6,2},{7,5},{8,12},{9,11},{10,... | collective-permute-start | bytes 1179656 | tf_op jit(solution)/shard_map/ppermute | solution.py:30
  67.5 0.9 collective-permute-start.24
  68.3 9.2 %collective-permute-done.16 = bf16[128,1536]{1,0:T(8,128)(2,1)S(1)} collective-permute-done((bf16[128,1536]{1,0:T(8,128)(2,1)S(1)}, bf16[128,1536]{1,0:T(8,128)(2,1)S(1)}, u32[]{:S(2)}, u32[]{:S(2)}) %collective-permute-start.16) | collective-permute-done | bytes 393248 | tf_op jit(solution)/shard_map/ppermute | solution.py:30
  77.6 1.3 %collective-permute-done.24.arrived_ref = bf16[192,1536]{1,0:T(8,128)(2,1)S(1)} collective-permute-done((bf16[192,1536]{1,0:T(8,128)(2,1)S(1)}, bf16[192,1536]{1,0:T(8,128)(2,1)S(1)}, u32[]{:S(2)}, u32[]{:S(2)}) %collective-permute-start.24) | collective-permute-done | bytes 589856 | tf_op jit(solution)/shard_map/ppermute | solution.py:30
  78.9 0.6 shard_map.82
  79.6 1.6 %collective-permute-start.25 = (bf16[128,1536]{1,0:T(8,128)(2,1)S(1)}, bf16[128,1536]{1,0:T(8,128)(2,1)S(1)}, u32[]{:S(2)}, u32[]{:S(2)}) collective-permute-start(bf16[128,1536]{1,0:T(8,128)(2,1)S(1)} %get-tuple-element.80), channel_id=1, source_target_pairs={{0,4},{1,3},{2,6},{3,1},{4,0},{5,7},{6,2},{7,5},{8,12},{9,11},{10,... | collective-permute-start | bytes 1179656 | tf_op jit(solution)/shard_map/ppermute | solution.py:30
  81.2 3.1 %collective-permute-start.17 = (bf16[32,1536]{1,0:T(8,128)(2,1)S(1)}, bf16[32,1536]{1,0:T(8,128)(2,1)S(1)}, u32[]{:S(2)}, u32[]{:S(2)}) collective-permute-start(bf16[32,1536]{1,0:T(8,128)(2,1)S(1)} %get-tuple-element.89), channel_id=1, source_target_pairs={{0,8},{1,9},{2,10},{3,11},{4,12},{5,13},{6,14},{7,15},{8,0},{9,1},... | collective-permute-start | bytes 294920 | tf_op jit(solution)/shard_map/ppermute | solution.py:30
  84.6 2.0 %collective-permute-start.19 = (bf16[32,1536]{1,0:T(8,128)(2,1)S(1)}, bf16[32,1536]{1,0:T(8,128)(2,1)S(1)}, u32[]{:S(2)}, u32[]{:S(2)}) collective-permute-start(bf16[32,1536]{1,0:T(8,128)(2,1)S(1)} %get-tuple-element.90), channel_id=1, source_target_pairs={{0,24},{1,25},{2,26},{3,27},{4,28},{5,29},{6,30},{7,31},{8,16},{9,... | collective-permute-start | bytes 294920 | tf_op jit(solution)/shard_map/ppermute | solution.py:30
  86.7 0.7 collective-permute-done.25
  87.5 2.6 %collective-permute-start.26 = (bf16[32,1536]{1,0:T(8,128)(2,1)S(1)}, bf16[32,1536]{1,0:T(8,128)(2,1)S(1)}, u32[]{:S(2)}, u32[]{:S(2)}) collective-permute-start(bf16[32,1536]{1,0:T(8,128)(2,1)S(1)} %get-tuple-element.92), channel_id=1, source_target_pairs={{0,8},{1,9},{2,10},{3,11},{4,12},{5,13},{6,14},{7,15},{8,0},{9,1},... | collective-permute-start | bytes 294920 | tf_op jit(solution)/shard_map/ppermute | solution.py:30
  90.1 1.6 %collective-permute-start.27 = (bf16[32,1536]{1,0:T(8,128)(2,1)S(1)}, bf16[32,1536]{1,0:T(8,128)(2,1)S(1)}, u32[]{:S(2)}, u32[]{:S(2)}) collective-permute-start(bf16[32,1536]{1,0:T(8,128)(2,1)S(1)} %get-tuple-element.94), channel_id=1, source_target_pairs={{0,16},{1,17},{2,18},{3,19},{4,20},{5,21},{6,22},{7,23},{8,24},{9,... | collective-permute-start | bytes 294920 | tf_op jit(solution)/shard_map/ppermute | solution.py:30
  91.7 0.9 collective-permute-start.28
  92.5 2.4 %collective-permute-done.18 = bf16[32,1536]{1,0:T(8,128)(2,1)S(1)} collective-permute-done((bf16[32,1536]{1,0:T(8,128)(2,1)S(1)}, bf16[32,1536]{1,0:T(8,128)(2,1)S(1)}, u32[]{:S(2)}, u32[]{:S(2)}) %collective-permute-start.18) | collective-permute-done | bytes 98336 | tf_op jit(solution)/shard_map/ppermute | solution.py:30
  95.0 1.0 collective-permute-done.26
  96.1 6.4 %collective-permute-done.27 = bf16[32,1536]{1,0:T(8,128)(2,1)S(1)} collective-permute-done((bf16[32,1536]{1,0:T(8,128)(2,1)S(1)}, bf16[32,1536]{1,0:T(8,128)(2,1)S(1)}, u32[]{:S(2)}, u32[]{:S(2)}) %collective-permute-start.27) | collective-permute-done | bytes 98336 | tf_op jit(solution)/shard_map/ppermute | solution.py:30
  102.7 1.3 %collective-permute-done.29 = bf16[2,16,1536]{2,1,0:T(8,128)(2,1)S(1)} collective-permute-done((bf16[2,16,1536]{2,1,0:T(8,128)(2,1)S(1)}, bf16[2,16,1536]{2,1,0:T(8,128)(2,1)S(1)}, u32[]{:S(2)}, u32[]{:S(2)}) %collective-permute-start.29) | collective-permute-done | bytes 98336 | tf_op jit(solution)/shard_map/ppermute | solution.py:30
  104.1 0.7 fusion
  (64 shorter events, 5.3 us)
Async XLA Ops:
  0.8 0.9 copy-start.3
  1.7 0.7 copy-start.5
  2.4 0.7 copy-start.6
  3.9 1.5 %collective-permute-start = (bf16[2,16,1536]{2,1,0:T(8,128)(2,1)S(1)}, bf16[2,16,1536]{2,1,0:T(8,128)(2,1)S(1)}, u32[]{:S(2)}, u32[]{:S(2)}) collective-permute-start(bf16[2,16,1536]{2,1,0:T(8,128)(2,1)S(1)} %get-tuple-element.44), channel_id=1, source_target_pairs={{0,1},{1,0},{2,3},{3,2},{4,5},{5,4},{6,7},{7,6},{8,9},{9,8},{10,11... | collective-permute-start | bytes 294920 | tf_op jit(solution)/shard_map/ppermute | solution.py:30
  5.4 13.3 %collective-permute-start.1 = (bf16[32,1536]{1,0:T(8,128)(2,1)S(1)}, bf16[32,1536]{1,0:T(8,128)(2,1)S(1)}, u32[]{:S(2)}, u32[]{:S(2)}) collective-permute-start(bf16[32,1536]{1,0:T(8,128)(2,1)S(1)} %pad_maximum_fusion.2._), channel_id=1, source_target_pairs={{0,8},{1,9},{2,10},{3,11},{4,12},{5,13},{6,14},{7,15},{8,0},{9,1},... | collective-permute-start | bytes 294920 | tf_op jit(solution)/shard_map/ppermute | solution.py:30
  8.4 10.7 %collective-permute-start.2 = (bf16[32,1536]{1,0:T(8,128)(2,1)S(1)}, bf16[32,1536]{1,0:T(8,128)(2,1)S(1)}, u32[]{:S(2)}, u32[]{:S(2)}) collective-permute-start(bf16[32,1536]{1,0:T(8,128)(2,1)S(1)} %pad_maximum_fusion.2._), channel_id=1, source_target_pairs={{0,16},{1,17},{2,18},{3,19},{4,20},{5,21},{6,22},{7,23},{8,24},{9,... | collective-permute-start | bytes 294920 | tf_op jit(solution)/shard_map/ppermute | solution.py:30
  11.0 8.1 %collective-permute-start.3 = (bf16[32,1536]{1,0:T(8,128)(2,1)S(1)}, bf16[32,1536]{1,0:T(8,128)(2,1)S(1)}, u32[]{:S(2)}, u32[]{:S(2)}) collective-permute-start(bf16[32,1536]{1,0:T(8,128)(2,1)S(1)} %pad_maximum_fusion.2._), channel_id=1, source_target_pairs={{0,24},{1,25},{2,26},{3,27},{4,28},{5,29},{6,30},{7,31},{8,16},{9,... | collective-permute-start | bytes 294920 | tf_op jit(solution)/shard_map/ppermute | solution.py:30
  11.0 2.2 %copy-start = (bf16[2880,720]{0,1:T(8,128)(2,1)S(1)}, bf16[2880,720]{0,1:T(8,128)(2,1)}, u32[]{:S(2)}) copy-start(bf16[2880,720]{0,1:T(8,128)(2,1)} %param.9) | copy-start | bytes 12441604
  13.3 2.2 %copy-start.1 = (bf16[2880,720]{0,1:T(8,128)(2,1)S(1)}, bf16[2880,720]{0,1:T(8,128)(2,1)}, u32[]{:S(2)}) copy-start(bf16[2880,720]{0,1:T(8,128)(2,1)} %param.10) | copy-start | bytes 12441604
  15.5 2.2 %copy-start.2 = (bf16[720,2880]{1,0:T(8,128)(2,1)S(1)}, bf16[720,2880]{1,0:T(8,128)(2,1)}, u32[]{:S(2)}) copy-start(bf16[720,2880]{1,0:T(8,128)(2,1)} %refs_2_.1) | copy-start | bytes 12441604
  19.1 7.8 %collective-permute-start.4 = (bf16[128,1536]{1,0:T(8,128)(2,1)S(1)}, bf16[128,1536]{1,0:T(8,128)(2,1)S(1)}, u32[]{:S(2)}, u32[]{:S(2)}) collective-permute-start(bf16[128,1536]{1,0:T(8,128)(2,1)S(1)} %constant_dynamic-update-slice_fusion.near_ref), channel_id=1, source_target_pairs={{0,4},{1,3},{2,6},{3,1},{4,0},{5,7},{6,2},{7,5},{8,12},{9,11},{10,... | collective-permute-start | bytes 1179656 | tf_op jit(solution)/shard_map/ppermute | solution.py:30
  20.7 10.8 %collective-permute-start.5 = (bf16[32,1536]{1,0:T(8,128)(2,1)S(1)}, bf16[32,1536]{1,0:T(8,128)(2,1)S(1)}, u32[]{:S(2)}, u32[]{:S(2)}) collective-permute-start(bf16[32,1536]{1,0:T(8,128)(2,1)S(1)} %pad_maximum_fusion.1), channel_id=1, source_target_pairs={{0,8},{1,9},{2,10},{3,11},{4,12},{5,13},{6,14},{7,15},{8,0},{9,1},... | collective-permute-start | bytes 294920 | tf_op jit(solution)/shard_map/ppermute | solution.py:30
  22.4 9.5 %collective-permute-start.6 = (bf16[32,1536]{1,0:T(8,128)(2,1)S(1)}, bf16[32,1536]{1,0:T(8,128)(2,1)S(1)}, u32[]{:S(2)}, u32[]{:S(2)}) collective-permute-start(bf16[32,1536]{1,0:T(8,128)(2,1)S(1)} %pad_maximum_fusion.1), channel_id=1, source_target_pairs={{0,16},{1,17},{2,18},{3,19},{4,20},{5,21},{6,22},{7,23},{8,24},{9,... | collective-permute-start | bytes 294920 | tf_op jit(solution)/shard_map/ppermute | solution.py:30
  24.8 7.1 %collective-permute-start.7 = (bf16[32,1536]{1,0:T(8,128)(2,1)S(1)}, bf16[32,1536]{1,0:T(8,128)(2,1)S(1)}, u32[]{:S(2)}, u32[]{:S(2)}) collective-permute-start(bf16[32,1536]{1,0:T(8,128)(2,1)S(1)} %pad_maximum_fusion.1), channel_id=1, source_target_pairs={{0,24},{1,25},{2,26},{3,27},{4,28},{5,29},{6,30},{7,31},{8,16},{9,... | collective-permute-start | bytes 294920 | tf_op jit(solution)/shard_map/ppermute | solution.py:30
  28.4 14.2 %collective-permute-start.9 = (bf16[192,1536]{1,0:T(8,128)(2,1)S(1)}, bf16[192,1536]{1,0:T(8,128)(2,1)S(1)}, u32[]{:S(2)}, u32[]{:S(2)}) collective-permute-start(bf16[192,1536]{1,0:T(8,128)(2,1)S(1)} %shard_map.77), channel_id=1, source_target_pairs={{0,2},{1,5},{2,0},{3,7},{4,6},{5,1},{6,4},{7,3},{8,10},{9,13},{10,... | collective-permute-start | bytes 1769480 | tf_op jit(solution)/shard_map/ppermute | solution.py:30
  31.9 8.1 %collective-permute-start.8 = (bf16[128,1536]{1,0:T(8,128)(2,1)S(1)}, bf16[128,1536]{1,0:T(8,128)(2,1)S(1)}, u32[]{:S(2)}, u32[]{:S(2)}) collective-permute-start(bf16[128,1536]{1,0:T(8,128)(2,1)S(1)} %constant_dynamic-update-slice_fusion.5.near_ref), channel_id=1, source_target_pairs={{0,4},{1,3},{2,6},{3,1},{4,0},{5,7},{6,2},{7,5},{8,12},{9,11},{10,... | collective-permute-start | bytes 1179656 | tf_op jit(solution)/shard_map/ppermute | solution.py:30
  33.3 10.8 %collective-permute-start.11 = (bf16[192,1536]{1,0:T(8,128)(2,1)S(1)}, bf16[192,1536]{1,0:T(8,128)(2,1)S(1)}, u32[]{:S(2)}, u32[]{:S(2)}) collective-permute-start(bf16[192,1536]{1,0:T(8,128)(2,1)S(1)} %get-tuple-element.57.mine_near_ref), channel_id=1, source_target_pairs={{0,1},{1,0},{2,3},{3,2},{4,5},{5,4},{6,7},{7,6},{8,9},{9,8},{10,11... | collective-permute-start | bytes 1769480 | tf_op jit(solution)/shard_map/ppermute | solution.py:30
  42.6 2.0 %collective-permute-start.12 = (bf16[192,1536]{1,0:T(8,128)(2,1)S(1)}, bf16[192,1536]{1,0:T(8,128)(2,1)S(1)}, u32[]{:S(2)}, u32[]{:S(2)}) collective-permute-start(bf16[192,1536]{1,0:T(8,128)(2,1)S(1)} %collective-permute-done.9.mine_far_ref), channel_id=1, source_target_pairs={{0,1},{1,0},{2,3},{3,2},{4,5},{5,4},{6,7},{7,6},{8,9},{9,8},{10,11... | collective-permute-start | bytes 1769480 | tf_op jit(solution)/shard_map/ppermute | solution.py:30
  42.6 9.9 %collective-permute-start.10 = (bf16[192,1536]{1,0:T(8,128)(2,1)S(1)}, bf16[192,1536]{1,0:T(8,128)(2,1)S(1)}, u32[]{:S(2)}, u32[]{:S(2)}) collective-permute-start(bf16[192,1536]{1,0:T(8,128)(2,1)S(1)} %shard_map.76), channel_id=1, source_target_pairs={{0,2},{1,5},{2,0},{3,7},{4,6},{5,1},{6,4},{7,3},{8,10},{9,13},{10,... | collective-permute-start | bytes 1769480 | tf_op jit(solution)/shard_map/ppermute | solution.py:30
  52.5 2.6 %collective-permute-start.14 = (bf16[192,1536]{1,0:T(8,128)(2,1)S(1)}, bf16[192,1536]{1,0:T(8,128)(2,1)S(1)}, u32[]{:S(2)}, u32[]{:S(2)}) collective-permute-start(bf16[192,1536]{1,0:T(8,128)(2,1)S(1)} %get-tuple-element.69), channel_id=1, source_target_pairs={{0,1},{1,0},{2,3},{3,2},{4,5},{5,4},{6,7},{7,6},{8,9},{9,8},{10,11... | collective-permute-start | bytes 1769480 | tf_op jit(solution)/shard_map/ppermute | solution.py:30
  54.0 2.8 %collective-permute-start.20 = (bf16[192,1536]{1,0:T(8,128)(2,1)S(1)}, bf16[192,1536]{1,0:T(8,128)(2,1)S(1)}, u32[]{:S(2)}, u32[]{:S(2)}) collective-permute-start(bf16[192,1536]{1,0:T(8,128)(2,1)S(1)} %get-tuple-element.73.mine_near_ref), channel_id=1, source_target_pairs={{0,1},{1,0},{2,3},{3,2},{4,5},{5,4},{6,7},{7,6},{8,9},{9,8},{10,11... | collective-permute-start | bytes 1769480 | tf_op jit(solution)/shard_map/ppermute | solution.py:30
  54.5 2.5 %collective-permute-start.21 = (bf16[192,1536]{1,0:T(8,128)(2,1)S(1)}, bf16[192,1536]{1,0:T(8,128)(2,1)S(1)}, u32[]{:S(2)}, u32[]{:S(2)}) collective-permute-start(bf16[192,1536]{1,0:T(8,128)(2,1)S(1)} %collective-permute-done.10.mine_far_ref), channel_id=1, source_target_pairs={{0,1},{1,0},{2,3},{3,2},{4,5},{5,4},{6,7},{7,6},{8,9},{9,8},{10,11... | collective-permute-start | bytes 1769480 | tf_op jit(solution)/shard_map/ppermute | solution.py:30
  54.6 10.1 %collective-permute-start.13 = (bf16[192,1536]{1,0:T(8,128)(2,1)S(1)}, bf16[192,1536]{1,0:T(8,128)(2,1)S(1)}, u32[]{:S(2)}, u32[]{:S(2)}) collective-permute-start(bf16[192,1536]{1,0:T(8,128)(2,1)S(1)} %get-tuple-element.67), channel_id=1, source_target_pairs={{0,1},{1,0},{2,3},{3,2},{4,5},{5,4},{6,7},{7,6},{8,9},{9,8},{10,11... | collective-permute-start | bytes 1769480 | tf_op jit(solution)/shard_map/ppermute | solution.py:30
  55.2 9.9 %collective-permute-start.15 = (bf16[192,1536]{1,0:T(8,128)(2,1)S(1)}, bf16[192,1536]{1,0:T(8,128)(2,1)S(1)}, u32[]{:S(2)}, u32[]{:S(2)}) collective-permute-start(bf16[192,1536]{1,0:T(8,128)(2,1)S(1)} %add_convert_fusion.1), channel_id=1, source_target_pairs={{0,2},{1,5},{2,0},{3,7},{4,6},{5,1},{6,4},{7,3},{8,10},{9,13},{10,... | collective-permute-start | bytes 1769480 | tf_op jit(solution)/shard_map/ppermute | solution.py:30
  64.1 3.2 %collective-permute-start.23 = (bf16[192,1536]{1,0:T(8,128)(2,1)S(1)}, bf16[192,1536]{1,0:T(8,128)(2,1)S(1)}, u32[]{:S(2)}, u32[]{:S(2)}) collective-permute-start(bf16[192,1536]{1,0:T(8,128)(2,1)S(1)} %get-tuple-element.78), channel_id=1, source_target_pairs={{0,1},{1,0},{2,3},{3,2},{4,5},{5,4},{6,7},{7,6},{8,9},{9,8},{10,11... | collective-permute-start | bytes 1769480 | tf_op jit(solution)/shard_map/ppermute | solution.py:30
  64.6 13.0 %collective-permute-start.22 = (bf16[192,1536]{1,0:T(8,128)(2,1)S(1)}, bf16[192,1536]{1,0:T(8,128)(2,1)S(1)}, u32[]{:S(2)}, u32[]{:S(2)}) collective-permute-start(bf16[192,1536]{1,0:T(8,128)(2,1)S(1)} %get-tuple-element.76), channel_id=1, source_target_pairs={{0,1},{1,0},{2,3},{3,2},{4,5},{5,4},{6,7},{7,6},{8,9},{9,8},{10,11... | collective-permute-start | bytes 1769480 | tf_op jit(solution)/shard_map/ppermute | solution.py:30
  65.8 11.7 %collective-permute-start.16 = (bf16[128,1536]{1,0:T(8,128)(2,1)S(1)}, bf16[128,1536]{1,0:T(8,128)(2,1)S(1)}, u32[]{:S(2)}, u32[]{:S(2)}) collective-permute-start(bf16[128,1536]{1,0:T(8,128)(2,1)S(1)} %get-tuple-element.71), channel_id=1, source_target_pairs={{0,4},{1,3},{2,6},{3,1},{4,0},{5,7},{6,2},{7,5},{8,12},{9,11},{10,... | collective-permute-start | bytes 1179656 | tf_op jit(solution)/shard_map/ppermute | solution.py:30
  67.5 11.4 %collective-permute-start.24 = (bf16[192,1536]{1,0:T(8,128)(2,1)S(1)}, bf16[192,1536]{1,0:T(8,128)(2,1)S(1)}, u32[]{:S(2)}, u32[]{:S(2)}) collective-permute-start(bf16[192,1536]{1,0:T(8,128)(2,1)S(1)} %add_convert_fusion), channel_id=1, source_target_pairs={{0,2},{1,5},{2,0},{3,7},{4,6},{5,1},{6,4},{7,3},{8,10},{9,13},{10,... | collective-permute-start | bytes 1769480 | tf_op jit(solution)/shard_map/ppermute | solution.py:30
  79.6 7.8 %collective-permute-start.25 = (bf16[128,1536]{1,0:T(8,128)(2,1)S(1)}, bf16[128,1536]{1,0:T(8,128)(2,1)S(1)}, u32[]{:S(2)}, u32[]{:S(2)}) collective-permute-start(bf16[128,1536]{1,0:T(8,128)(2,1)S(1)} %get-tuple-element.80), channel_id=1, source_target_pairs={{0,4},{1,3},{2,6},{3,1},{4,0},{5,7},{6,2},{7,5},{8,12},{9,11},{10,... | collective-permute-start | bytes 1179656 | tf_op jit(solution)/shard_map/ppermute | solution.py:30
  81.2 10.5 %collective-permute-start.17 = (bf16[32,1536]{1,0:T(8,128)(2,1)S(1)}, bf16[32,1536]{1,0:T(8,128)(2,1)S(1)}, u32[]{:S(2)}, u32[]{:S(2)}) collective-permute-start(bf16[32,1536]{1,0:T(8,128)(2,1)S(1)} %get-tuple-element.89), channel_id=1, source_target_pairs={{0,8},{1,9},{2,10},{3,11},{4,12},{5,13},{6,14},{7,15},{8,0},{9,1},... | collective-permute-start | bytes 294920 | tf_op jit(solution)/shard_map/ppermute | solution.py:30
  84.2 10.8 %collective-permute-start.18 = (bf16[32,1536]{1,0:T(8,128)(2,1)S(1)}, bf16[32,1536]{1,0:T(8,128)(2,1)S(1)}, u32[]{:S(2)}, u32[]{:S(2)}) collective-permute-start(bf16[32,1536]{1,0:T(8,128)(2,1)S(1)} %get-tuple-element.91), channel_id=1, source_target_pairs={{0,16},{1,17},{2,18},{3,19},{4,20},{5,21},{6,22},{7,23},{8,24},{9,... | collective-permute-start | bytes 294920 | tf_op jit(solution)/shard_map/ppermute | solution.py:30
  84.6 10.4 %collective-permute-start.19 = (bf16[32,1536]{1,0:T(8,128)(2,1)S(1)}, bf16[32,1536]{1,0:T(8,128)(2,1)S(1)}, u32[]{:S(2)}, u32[]{:S(2)}) collective-permute-start(bf16[32,1536]{1,0:T(8,128)(2,1)S(1)} %get-tuple-element.90), channel_id=1, source_target_pairs={{0,24},{1,25},{2,26},{3,27},{4,28},{5,29},{6,30},{7,31},{8,16},{9,... | collective-permute-start | bytes 294920 | tf_op jit(solution)/shard_map/ppermute | solution.py:30
  87.5 8.5 %collective-permute-start.26 = (bf16[32,1536]{1,0:T(8,128)(2,1)S(1)}, bf16[32,1536]{1,0:T(8,128)(2,1)S(1)}, u32[]{:S(2)}, u32[]{:S(2)}) collective-permute-start(bf16[32,1536]{1,0:T(8,128)(2,1)S(1)} %get-tuple-element.92), channel_id=1, source_target_pairs={{0,8},{1,9},{2,10},{3,11},{4,12},{5,13},{6,14},{7,15},{8,0},{9,1},... | collective-permute-start | bytes 294920 | tf_op jit(solution)/shard_map/ppermute | solution.py:30
  90.1 12.4 %collective-permute-start.27 = (bf16[32,1536]{1,0:T(8,128)(2,1)S(1)}, bf16[32,1536]{1,0:T(8,128)(2,1)S(1)}, u32[]{:S(2)}, u32[]{:S(2)}) collective-permute-start(bf16[32,1536]{1,0:T(8,128)(2,1)S(1)} %get-tuple-element.94), channel_id=1, source_target_pairs={{0,16},{1,17},{2,18},{3,19},{4,20},{5,21},{6,22},{7,23},{8,24},{9,... | collective-permute-start | bytes 294920 | tf_op jit(solution)/shard_map/ppermute | solution.py:30
  91.7 10.8 %collective-permute-start.28 = (bf16[32,1536]{1,0:T(8,128)(2,1)S(1)}, bf16[32,1536]{1,0:T(8,128)(2,1)S(1)}, u32[]{:S(2)}, u32[]{:S(2)}) collective-permute-start(bf16[32,1536]{1,0:T(8,128)(2,1)S(1)} %get-tuple-element.93), channel_id=1, source_target_pairs={{0,24},{1,25},{2,26},{3,27},{4,28},{5,29},{6,30},{7,31},{8,16},{9,... | collective-permute-start | bytes 294920 | tf_op jit(solution)/shard_map/ppermute | solution.py:30
  102.6 1.5 %copy-start.4 = (bf16[2,16,2880]{2,1,0:T(8,128)(2,1)S(1)}, bf16[2,16,2880]{2,1,0:T(8,128)(2,1)}, u32[]{:S(2)}) copy-start(bf16[2,16,2880]{2,1,0:T(8,128)(2,1)} %hidden_ref.1) | copy-start | bytes 552964
  102.6 1.4 %collective-permute-start.29 = (bf16[2,16,1536]{2,1,0:T(8,128)(2,1)S(1)}, bf16[2,16,1536]{2,1,0:T(8,128)(2,1)S(1)}, u32[]{:S(2)}, u32[]{:S(2)}) collective-permute-start(bf16[2,16,1536]{2,1,0:T(8,128)(2,1)S(1)} %select_convert_fusion), channel_id=1, source_target_pairs={{0,1},{1,0},{2,3},{3,2},{4,5},{5,4},{6,7},{7,6},{8,9},{9,8},{10,11... | collective-permute-start | bytes 294920 | tf_op jit(solution)/shard_map/ppermute | solution.py:30

commit v4 on v3

--- a/solution.py
+++ b/solution.py
@@ -53,12 +53,9 @@
 SCALARS = pl.BlockSpec(memory_space=pltpu.SMEM)
 
 
-def select_body(tokens, capacity, index, places_ref, near_ref, next_ref, rows_ref, *slots_refs):
-    rows = near_ref.shape[0]
-    held = near_ref.shape[1]
-    total = 2 * rows
-    compact = rows_ref.shape[0]
-    tile = jnp.concatenate([near_ref[:, held - LANES :], next_ref[:, held - LANES :]], axis=0).astype(jnp.float32)
+def slots_of(tokens, capacity, base, places_ref, rows_ref):
+    total, held = rows_ref.shape
+    tile = rows_ref[:, held - LANES :].astype(jnp.float32)
     lane = lax.broadcasted_iota(jnp.int32, (total, LANES), 1)
     row = lax.broadcasted_iota(jnp.int32, (total, LANES), 0)
     listed = (lane >= LANES - ROUTING) & (lane < LANES - ROUTING // 2)
@@ -72,61 +69,80 @@
     right = lax.broadcasted_iota(jnp.int32, (total, total), 1)
     earlier = ((right < left) & (left // tokens == right // tokens)).astype(jnp.float32).astype(jnp.bfloat16)
     ahead = jnp.dot(earlier, marks.astype(jnp.bfloat16), preferred_element_type=jnp.float32)
-    slots = jnp.where(marks > 0.0, ahead + (row // tokens * capacity).astype(jnp.float32), -1.0)
-    for slots_ref in slots_refs:
-        slots_ref[...] = slots
-    column = lax.broadcasted_iota(jnp.int32, (total, compact), 1).astype(jnp.float32)
-    picks = (slots[:, index : index + 1] == column).astype(jnp.float32).astype(jnp.bfloat16)
-    rows_ref[...] = (
-        lax.dot_general(picks[:rows], near_ref[...], downward, preferred_element_type=jnp.float32)
-        + lax.dot_general(picks[rows:], next_ref[...], downward, preferred_element_type=jnp.float32)
-    ).astype(jnp.bfloat16)
-
-
-def select(tokens, capacity, index, places, near, following):
+    return jnp.where(marks > 0.0, ahead + (base + row // tokens * capacity).astype(jnp.float32), -1.0)
+
+
+def locate_body(tokens, capacity, places_ref, rows_ref, slots_ref):
+    slots_ref[...] = slots_of(tokens, capacity, 0, places_ref, rows_ref)
+
+
+def locate(tokens, capacity, places, rows):
+    return pl.pallas_call(
+        functools.partial(locate_body, tokens, capacity),
+        out_shape=jax.ShapeDtypeStruct((rows.shape[0], LANES), jnp.float32),
+        in_specs=[SCALARS] + whole_arrays(1),
+        out_specs=pl.BlockSpec(memory_space=pltpu.VMEM),
+        compiler_params=pltpu.CompilerParams(vmem_limit_bytes=20 * 2**20),
+    )(places, rows)
+
+
+def select_body(tokens, capacity, wanted, places_ref, slots_ref, near_ref, next_ref, *out_refs):
+    rows = near_ref.shape[0]
+    compact = out_refs[0].shape[0]
+    slots = slots_ref[...]
+    next_slots = slots_of(tokens, capacity, rows // tokens * capacity, places_ref, next_ref)
+    for next_slots_ref in out_refs[len(wanted) :]:
+        next_slots_ref[...] = next_slots
+    column = lax.broadcasted_iota(jnp.int32, (rows, compact), 1).astype(jnp.float32)
+    for index, rows_ref in zip(wanted, out_refs):
+        result = None
+        for source, at in ((near_ref, slots), (next_ref, next_slots)):
+            picks = (at[:, index : index + 1] == column).astype(jnp.float32).astype(jnp.bfloat16)
+            part = lax.dot_general(picks, source[...], downward, preferred_element_type=jnp.float32)
+            result = part if result is None else result + part
+        rows_ref[...] = result.astype(jnp.bfloat16)
+
+
+def select(tokens, capacity, wanted, places, slots, near, following):
+    with_slots = int(0 in wanted)
     rows, held = near.shape
     compact = 2 * rows // tokens * capacity
     block = jax.ShapeDtypeStruct((compact, held), jnp.bfloat16)
     return pl.pallas_call(
-        functools.partial(select_body, tokens, capacity, index),
-        out_shape=[block] + [jax.ShapeDtypeStruct((2 * rows, LANES), jnp.float32)] * (1 - index),
-        in_specs=[SCALARS] + whole_arrays(2),
-        out_specs=whole_arrays(2 - index),
+        functools.partial(select_body, tokens, capacity, wanted),
+        out_shape=[block] * len(wanted) + [jax.ShapeDtypeStruct((rows, LANES), jnp.float32)] * with_slots,
+        in_specs=[SCALARS] + whole_arrays(3),
+        out_specs=whole_arrays(len(wanted) + with_slots),
         compiler_params=pltpu.CompilerParams(vmem_limit_bytes=20 * 2**20),
         cost_estimate=pl.CostEstimate(flops=8 * rows * compact * held, bytes_accessed=8 * rows * held, transcendentals=0),
-    )(places, near, following)
-
-
-def merge_body(slots_ref, keep_ref, taken_ref, arrived_ref, near_ref, next_ref):
-    rows = near_ref.shape[0]
-    total = 2 * rows
+    )(places, slots, near, following)
+
+
+def merge_body(wanted, near_slots_ref, next_slots_ref, keep_ref, taken_ref, arrived_ref, *out_refs):
+    rows = out_refs[0].shape[0]
     compact = keep_ref.shape[0]
-    slots = slots_ref[...]
-    column = lax.broadcasted_iota(jnp.int32, (total, compact), 1).astype(jnp.float32)
-    summed = keep_ref[...] + taken_ref[...].astype(jnp.float32)
-    high = summed.astype(jnp.bfloat16)
-    result = jnp.zeros((total, keep_ref.shape[1]), jnp.float32)
-    for index, source in enumerate((high, arrived_ref[...])):
-        picks = (slots[:, index : index + 1] == column).astype(jnp.float32).astype(jnp.bfloat16)
-        result += jnp.dot(picks, source, preferred_element_type=jnp.float32)
-    near_ref[...] = result[:rows]
-    next_ref[...] = result[rows:].astype(jnp.bfloat16)
-
-
-def merge(slots, keep, taken, arrived):
-    rows = slots.shape[0] // 2
+    column = lax.broadcasted_iota(jnp.int32, (rows, compact), 1).astype(jnp.float32)
+    high = (keep_ref[...] + taken_ref[...].astype(jnp.float32)).astype(jnp.bfloat16)
+    for part, out_ref in zip(wanted, out_refs):
+        slots = (near_slots_ref, next_slots_ref)[part][...]
+        result = jnp.zeros((rows, keep_ref.shape[1]), jnp.float32)
+        for index, source in enumerate((high, arrived_ref[...])):
+            picks = (slots[:, index : index + 1] == column).astype(jnp.float32).astype(jnp.bfloat16)
+            result += jnp.dot(picks, source, preferred_element_type=jnp.float32)
+        out_ref[...] = result.astype(out_ref.dtype)
+
+
+def merge(wanted, types, slots, keep, taken, arrived):
+    rows = slots[0].shape[0]
     compact, held = keep.shape
     return pl.pallas_call(
-        merge_body,
-        out_shape=[
-            jax.ShapeDtypeStruct((rows, held), jnp.float32),
-            jax.ShapeDtypeStruct((rows, held), jnp.bfloat16),
-        ],
-        in_specs=whole_arrays(4),
-        out_specs=whole_arrays(2),
+        functools.partial(merge_body, wanted),
+        out_shape=[jax.ShapeDtypeStruct((rows, held), kind) for kind in types],
+        in_specs=whole_arrays(5),
+        out_specs=whole_arrays(len(types)),
         compiler_params=pltpu.CompilerParams(vmem_limit_bytes=20 * 2**20),
         cost_estimate=pl.CostEstimate(flops=8 * rows * compact * held, bytes_accessed=8 * rows * held, transcendentals=0),
-    )(slots, keep, taken, arrived)
+    )(*slots, keep, taken, arrived)
 
 
 def ffn_body(
@@ -255,7 +271,7 @@
 
 
 def prologue_body(
-    tokens, top_count, places_ref, hidden_ref, gain_ref, ids_ref, weights_ref, mine_ref, give_ref
+    tokens, top_count, places_ref, hidden_ref, gain_ref, routing_ref, mine_ref, give_ref
 ):
     micro_count, _, width = hidden_ref.shape
     first, second, held = split_widths(width)
@@ -286,8 +302,8 @@
         normed = residual * scale * gain_ref[...].astype(jnp.float32)
         tile = jnp.where(on_ids, -1.0, 0.0)
         for k in range(top_count):
-            number = upright(ids_ref[b, k : k + 1, :].astype(jnp.float32))
-            weight = upright(weights_ref[b, k : k + 1, :])
+            number = upright(routing_ref[b, k : k + 1, :])
+            weight = upright(routing_ref[b, top_count + k : top_count + k + 1, :])
             high = weight.astype(jnp.bfloat16).astype(jnp.float32)
             middle = (weight - high).astype(jnp.bfloat16).astype(jnp.float32)
             for place, piece in enumerate((high, middle, weight - high - middle)):
@@ -306,16 +322,16 @@
             store(give_ref, b, parts[0], tile)
 
 
-def prologue(places, hidden, gain, ids, weights):
+def prologue(places, hidden, gain, routing):
     micro_count, tokens, width = hidden.shape
     held = split_widths(width)[2]
     return pl.pallas_call(
-        functools.partial(prologue_body, tokens, ids.shape[1]),
+        functools.partial(prologue_body, tokens, routing.shape[1] // 2),
         out_shape=[jax.ShapeDtypeStruct((micro_count, tokens, held), jnp.bfloat16)] * 2,
-        in_specs=[SCALARS] + whole_arrays(4),
+        in_specs=[SCALARS] + whole_arrays(3),
         out_specs=whole_arrays(2),
         compiler_params=pltpu.CompilerParams(vmem_limit_bytes=20 * 2**20),
-    )(places, hidden, gain, ids, weights)
+    )(places, hidden, gain, routing)
 
 
 def local(hidden, norm_gain, w_gate, w_up, w_down, expert_ids, route_weight):
@@ -336,9 +352,10 @@
     def join(*blocks):
         return jnp.concatenate(blocks, axis=0)
 
-    mine, give = prologue(
-        places, hidden, norm_gain.reshape(1, width), expert_ids.transpose(0, 2, 1), route_weight.transpose(0, 2, 1)
-    )
+    routing = jnp.concatenate(
+        [expert_ids.transpose(0, 2, 1).astype(jnp.float32), route_weight.transpose(0, 2, 1)], axis=1
+    )
+    mine, give = prologue(places, hidden, norm_gain.reshape(1, width), routing)
     theirs = moved(give, other_core)
     pairs = [
         join(jnp.where(lower, mine[b], theirs[b]), jnp.where(lower, theirs[b], mine[b]))
@@ -351,56 +368,99 @@
     def far_blocks(pair):
         return [moved(pair, far(j)) for j in range(1, distant)]
 
-    def second_hop(state, earlier):
-        following = moved(state["column"], first_axis)
+    def second_hop(state, earlier, apart):
         chosen = tokens, capacity
-        (send,) = select(*chosen, 1, places, state["column"], following)
+        near, following = state["near"], state["next"]
+        slots = state["slots"]
+        if apart:
+            (send,) = select(*chosen, (1,), places, slots, near, following)
+        else:
+            send, state["own"], next_slots = select(*chosen, (1, 0), places, slots, near, following)
         if earlier is not None:
             send, earlier["arrived"] = tied(send, earlier["arrived"])
         state["arrived"] = moved(send, second_axis)
-        state["own"], state["slots"] = select(*chosen, 0, places, state["column"], following)
+        if apart:
+            following, _ = tied(following, send)
+            state["own"], next_slots = select(*chosen, (0,), places, state["twin"], near, following)
+        state["slots"] = slots, next_slots
 
     states = []
     gate_v, up_v, down_v = preload(pairs[0], w_gate.T, w_up.T, w_down)
-    for pair in pairs:
-        if states:
-            last = states[-1]
-            pair, last["column"] = tied(pair, last["column"])
-        blocks = far_blocks(pair)
-        if states:
-            second_hop(last, states[-2] if len(states) > 1 else None)
-            *blocks, last["own"] = tied(*blocks, last["own"])
-        else:
-            blocks[0], gate_v, up_v, down_v = tied(blocks[0], gate_v, up_v, down_v)
-        states.append({"column": join(pair, *blocks)})
-    second_hop(states[-1], states[-2] if len(states) > 1 else None)
-    held_state = states
-
-    outputs = []
-    before = None
-    for b in range(micro_count):
-        state = held_state[b]
+    beside = [moved(pair, first_axis) for pair in pairs[1:]]
+    blocks = far_blocks(pairs[0])
+    blocks[0], gate_v, up_v, down_v, *beside = tied(blocks[0], gate_v, up_v, down_v, *beside)
+    column = join(pairs[0], *blocks)
+    states.append(
+        {"near": column, "next": moved(column, first_axis), "slots": locate(tokens, capacity, places, column)}
+    )
+    side = 2 * tokens
+    for b in range(1, micro_count):
+        last = states[-1]
+        both, last["twin"] = tied(join(pairs[b], beside[b - 1]), moved(last["slots"], other_core))
+        blocks = far_blocks(both)
+        second_hop(last, states[-2] if len(states) > 1 else None, True)
+        *blocks, last["own"] = tied(*blocks, last["own"])
+        blocks = [both] + blocks
+        near, following = join(*[block[:side] for block in blocks]), join(*[block[side:] for block in blocks])
+        states.append({"near": near, "next": following, "slots": locate(tokens, capacity, places, near)})
+    second_hop(states[-1], states[-2] if len(states) > 1 else None, False)
+
+    hops = []
+    for b, state in enumerate(states):
         own, arrived = state["own"], state["arrived"]
-        if before is not None:
-            arrived, *before = tied(arrived, *before)
-            outputs[-1] = before
-        before = ffn(
-            places, own, arrived, moved(own, other_core), moved(arrived, other_core), gate_v, up_v, down_v
+        other_far = moved(arrived, other_core)
+        if b:
+            other_far, hops[-1]["give"] = tied(other_far, hops[-1]["give"])
+        keep_near, keep_far, send_near, send_far = ffn(
+            places, own, arrived, moved(own, other_core), other_far, gate_v, up_v, down_v
         )
-        outputs.append(before)
-
-    def collect(state, keep_near, keep_far, send_near, send_far):
+        if b + 1 < micro_count:
+            send_far, states[b + 1]["arrived"] = tied(send_far, states[b + 1]["arrived"])
+        if b:
+            send_far, hops[-1]["arrived"] = tied(send_far, hops[-1]["arrived"])
         give = (keep_far + moved(send_far, other_core).astype(jnp.float32)).astype(jnp.bfloat16)
-        arrived = moved(give, second_axis)
-        near, following = merge(state["slots"], keep_near, moved(send_near, other_core), arrived)
-        near = near + moved(following, first_axis).astype(jnp.float32)
-        near = near.reshape(distant, 2 * tokens, held)
-        summed = near[0]
-        for j in range(1, distant):
-            summed = summed + moved(near[j].astype(jnp.bfloat16), far(j)).astype(jnp.float32)
-        return summed
-
-    sums = jnp.stack([collect(state, *out) for state, out in zip(held_state, outputs)])
+        hops.append(
+            {"keep": keep_near, "taken": moved(send_near, other_core), "give": give, "arrived": moved(give, second_axis)}
+        )
+
+    def far_sum(block):
+        block = block.reshape(distant, -1, held)
+        arrivals = [moved(block[j].astype(jnp.bfloat16), far(j)) for j in range(1, distant)]
+        return block[0], arrivals
+
+    def total(kept, arrivals):
+        for arrival in arrivals:
+            kept = kept + arrival.astype(jnp.float32)
+        return kept
+
+    count = len(hops)
+    for b in range(1, count):
+        hops[b - 1]["taken"], hops[b]["give"] = tied(hops[b - 1]["taken"], hops[b]["give"])
+    sums = [None] * count
+    waiting = None
+    for b, (state, hop) in enumerate(zip(states, hops)):
+        final = b == count - 1
+        parts = state["slots"], hop["keep"], hop["taken"], hop["arrived"]
+        if final:
+            (following,) = merge((1,), (jnp.bfloat16,), *parts)
+            taken, _ = tied(parts[2], following)
+            (near,) = merge((0,), (jnp.float32,), parts[0], parts[1], taken, parts[3])
+            if waiting is not None:
+                *arrivals, near = tied(*waiting[1], near)
+                waiting = waiting[0], arrivals
+            near = total(near, [moved(following, first_axis)])
+            kept, arrivals = far_sum(near)
+            sums[b] = total(kept, arrivals)
+        if waiting is not None:
+            settled = total(*waiting)
+            sums[b - 1] = total(settled[:side], [moved(settled[side:].astype(jnp.bfloat16), first_axis)])
+            waiting = None
+        if not final:
+            near, following = merge((0, 1), (jnp.float32, jnp.float32), *parts)
+            waiting = far_sum(
+                jnp.concatenate([near.reshape(distant, side, held), following.reshape(distant, side, held)], axis=1)
+            )
+    sums = jnp.stack(sums)
     own = jnp.where(lower, sums[:, :tokens], sums[:, tokens:])
     give = jnp.where(lower, sums[:, tokens:], sums[:, :tokens]).astype(jnp.bfloat16)
     taken = moved(give, other_core).astype(jnp.float32)

time: 105 us -> 108 us (1.029)
  waiting for transfers between devices: 36 us -> 42.4 us
  starting transfers between devices: 34.3 us -> 30.4 us
  other arithmetic: 1.52 us -> 3.02 us
  local copies, waits for them, and re-layouts: 9.7 us -> 8.38 us
    ppermute x30 -> x31, waiting for transfers between devices: 36 us -> 42.4 us  [moved(): return lax.ppermute(block, 'req', [(i, partner(i)) for i in range(count)])]
    ppermute x30 -> x31, starting transfers between devices: 34.3 us -> 30.4 us  [moved(): return lax.ppermute(block, 'req', [(i, partner(i)) for i in range(count)])]
    unnamed x19 -> x12, local copies, waits for them, and re-layouts: 8.94 us -> 7.55 us
    pallas_call x7 -> x9, Pallas kernels: 7.94 us -> 8.24 us  [the longest x3 4.36 us: select(): pl.pallas_call(functools.partial(select_body, tokens, capacity, wanted),...]
  transfers between devices with their start and end apart: 30 -> 31, of which waited for: 17 -> 18; matrix products, arithmetic and copies ran while one was open for 1% -> 1% of each run, Pallas kernels for 21% -> 20%
where the time goes in v4:
time: 108 us
  waiting for transfers between devices  42.4 us (39%)
  starting transfers between devices  30.4 us (28%)
  Pallas kernels  23.3 us (22%)
  local copies, waits for them, and re-layouts  8.38 us (8%)
  other arithmetic  3.02 us (3%)
    ppermute x31, waiting for transfers between devices, moved(): return lax.ppermute(block, 'req', [(i, partner(i)) for i in range(count)])  42.4 us
    ppermute x31, starting transfers between devices, moved(): return lax.ppermute(block, 'req', [(i, partner(i)) for i in range(count)])  30.4 us
    pallas_call x2, Pallas kernels, ffn(): pl.pallas_call(ffn_body, out_shape=[jax.ShapeDtypeStruct((pair, held), jn...  14 us
    unnamed x12, local copies, waits for them, and re-layouts  7.55 us
    pallas_call x3, Pallas kernels, select(): pl.pallas_call(functools.partial(select_body, tokens, capacity, wanted),...  4.36 us
  transfers between devices with their start and end apart: 31, of which 18 were waited for; matrix products, arithmetic and copies ran while one was open for 1% of the time, Pallas kernels for 20%

profile of v4, /device:TPU:0, one launch (start us, length us, event | category | flops | bytes accessed | tf_op | source)
XLA Modules:
  0.0 107.9 jit_solution(4054420432329398545)
XLA Ops:
  0.0 0.7 convert_bitcast_fusion
  0.7 0.7 reshape.29.gain_ref
  1.4 0.7 pad_maximum_fusion.7.routing_ref
  2.2 0.9 copy-done.3
  3.1 0.8 shard_map.73
  4.4 0.9 collective-permute-done
  5.4 2.9 %collective-permute-start.2 = (bf16[32,1536]{1,0:T(8,128)(2,1)S(1)}, bf16[32,1536]{1,0:T(8,128)(2,1)S(1)}, u32[]{:S(2)}, u32[]{:S(2)}) collective-permute-start(bf16[32,1536]{1,0:T(8,128)(2,1)S(1)} %pad_maximum_fusion.6), channel_id=1, source_target_pairs={{0,4},{1,3},{2,6},{3,1},{4,0},{5,7},{6,2},{7,5},{8,12},{9,11},{10,... | collective-permute-start | bytes 294920 | tf_op jit(solution)/shard_map/ppermute | solution.py:30
  8.4 1.6 %collective-permute-start.1 = (bf16[32,1536]{1,0:T(8,128)(2,1)S(1)}, bf16[32,1536]{1,0:T(8,128)(2,1)S(1)}, u32[]{:S(2)}, u32[]{:S(2)}) collective-permute-start(bf16[32,1536]{1,0:T(8,128)(2,1)S(1)} %pad_maximum_fusion.5._), channel_id=1, source_target_pairs={{0,8},{1,9},{2,10},{3,11},{4,12},{5,13},{6,14},{7,15},{8,0},{9,1},... | collective-permute-start | bytes 294920 | tf_op jit(solution)/shard_map/ppermute | solution.py:30
  10.0 2.5 %collective-permute-start.4 = (bf16[32,1536]{1,0:T(8,128)(2,1)S(1)}, bf16[32,1536]{1,0:T(8,128)(2,1)S(1)}, u32[]{:S(2)}, u32[]{:S(2)}) collective-permute-start(bf16[32,1536]{1,0:T(8,128)(2,1)S(1)} %pad_maximum_fusion.5._), channel_id=1, source_target_pairs={{0,24},{1,25},{2,26},{3,27},{4,28},{5,29},{6,30},{7,31},{8,16},{9,... | collective-permute-start | bytes 294920 | tf_op jit(solution)/shard_map/ppermute | solution.py:30
  12.6 2.2 %copy-done = bf16[2880,720]{0,1:T(8,128)(2,1)S(1)} copy-done((bf16[2880,720]{0,1:T(8,128)(2,1)S(1)}, bf16[2880,720]{0,1:T(8,128)(2,1)}, u32[]{:S(2)}) %copy-start) | copy-done | bytes 4147224
  14.8 2.2 %copy-done.1 = bf16[2880,720]{0,1:T(8,128)(2,1)S(1)} copy-done((bf16[2880,720]{0,1:T(8,128)(2,1)S(1)}, bf16[2880,720]{0,1:T(8,128)(2,1)}, u32[]{:S(2)}) %copy-start.1) | copy-done | bytes 4147224
  17.0 2.2 %copy-done.2 = bf16[720,2880]{1,0:T(8,128)(2,1)S(1)} copy-done((bf16[720,2880]{1,0:T(8,128)(2,1)S(1)}, bf16[720,2880]{1,0:T(8,128)(2,1)}, u32[]{:S(2)}) %copy-start.2) | copy-done | bytes 4147224
  19.2 1.1 shard_map.74
  20.3 1.1 %collective-permute-done.3 = bf16[32,1536]{1,0:T(8,128)(2,1)S(1)} collective-permute-done((bf16[32,1536]{1,0:T(8,128)(2,1)S(1)}, bf16[32,1536]{1,0:T(8,128)(2,1)S(1)}, u32[]{:S(2)}, u32[]{:S(2)}) %collective-permute-start.3) | collective-permute-done | bytes 98336 | tf_op jit(solution)/shard_map/ppermute | solution.py:30
  21.5 0.8 shard_map.75.slots_ref.near_slots_ref
  22.3 1.5 %collective-permute-start.6 = (bf16[128,1536]{1,0:T(8,128)(2,1)S(1)}, bf16[128,1536]{1,0:T(8,128)(2,1)S(1)}, u32[]{:S(2)}, u32[]{:S(2)}) collective-permute-start(bf16[128,1536]{1,0:T(8,128)(2,1)S(1)} %constant_dynamic-update-slice_fusion.rows_ref.near_ref), channel_id=1, source_target_pairs={{0,4},{1,3},{2,6},{3,1},{4,0},{5,7},{6,2},{7,5},{8,12},{9,11},{10,... | collective-permute-start | bytes 1179656 | tf_op jit(solution)/shard_map/ppermute | solution.py:30
  23.8 1.2 %collective-permute-done.5.slots_ref = f32[128,128]{1,0:T(8,128)S(1)} collective-permute-done((f32[128,128]{1,0:T(8,128)S(1)}, f32[128,128]{1,0:T(8,128)S(1)}, u32[]{:S(2)}, u32[]{:S(2)}) %collective-permute-start.5) | collective-permute-done | bytes 65568 | tf_op jit(solution)/shard_map/ppermute | solution.py:30
  25.1 2.7 %collective-permute-start.9 = (bf16[64,1536]{1,0:T(8,128)(2,1)S(1)}, bf16[64,1536]{1,0:T(8,128)(2,1)S(1)}, u32[]{:S(2)}, u32[]{:S(2)}) collective-permute-start(bf16[64,1536]{1,0:T(8,128)(2,1)S(1)} %pad_maximum_fusion.4), channel_id=1, source_target_pairs={{0,24},{1,25},{2,26},{3,27},{4,28},{5,29},{6,30},{7,31},{8,16},{9,... | collective-permute-start | bytes 589832 | tf_op jit(solution)/shard_map/ppermute | solution.py:30
  27.7 1.7 %collective-permute-start.7 = (bf16[64,1536]{1,0:T(8,128)(2,1)S(1)}, bf16[64,1536]{1,0:T(8,128)(2,1)S(1)}, u32[]{:S(2)}, u32[]{:S(2)}) collective-permute-start(bf16[64,1536]{1,0:T(8,128)(2,1)S(1)} %pad_maximum_fusion.4), channel_id=1, source_target_pairs={{0,8},{1,9},{2,10},{3,11},{4,12},{5,13},{6,14},{7,15},{8,0},{9,1},... | collective-permute-start | bytes 589832 | tf_op jit(solution)/shard_map/ppermute | solution.py:30
  29.5 0.6 collective-permute-done.6.next_ref
  30.1 1.4 %shard_map.76 = bf16[192,1536]{1,0:T(8,128)(2,1)S(1)} custom-call(s32[3]{0:T(128)S(1)} %pad_add_fusion.places_ref, f32[128,128]{1,0:T(8,128)S(1)} %shard_map.75.slots_ref.near_slots_ref, bf16[128,1536]{1,0:T(8,128)(2,1)S(1)} %constant_dynamic-update-slice_fusion.rows_ref.near_ref, bf16[128,1536]{1,0:T(8,128)(2,1)S(1)} %collective-permute-done.6.next_ref), custom_call_target="tpu_custom_call" | custom-call | flops 301989888 | bytes 1572864 | tf_op jit(solution)/shard_map/pallas_call | solution.py:111
  32.1 1.4 %shard_map.77 = (bf16[192,1536]{1,0:T(8,128)(2,1)S(1)}, f32[128,128]{1,0:T(8,128)S(1)}) custom-call(s32[3]{0:T(128)S(1)} %pad_add_fusion.places_ref, f32[128,128]{1,0:T(8,128)S(1)} %collective-permute-done.5.slots_ref, bf16[128,1536]{1,0:T(8,128)(2,1)S(1)} %constant_dynamic-update-slice_fusion.rows_ref.near_ref, ...), custom_call_target="tpu_custom_call" | custom-call | flops 301989888 | bytes 1572864 | tf_op jit(solution)/shard_map/pallas_call | solution.py:111
  33.4 1.3 %collective-permute-done.9 = bf16[64,1536]{1,0:T(8,128)(2,1)S(1)} collective-permute-done((bf16[64,1536]{1,0:T(8,128)(2,1)S(1)}, bf16[64,1536]{1,0:T(8,128)(2,1)S(1)}, u32[]{:S(2)}, u32[]{:S(2)}) %collective-permute-start.9) | collective-permute-done | bytes 196640 | tf_op jit(solution)/shard_map/ppermute | solution.py:30
  34.7 9.2 %collective-permute-done.8 = bf16[64,1536]{1,0:T(8,128)(2,1)S(1)} collective-permute-done((bf16[64,1536]{1,0:T(8,128)(2,1)S(1)}, bf16[64,1536]{1,0:T(8,128)(2,1)S(1)}, u32[]{:S(2)}, u32[]{:S(2)}) %collective-permute-start.8) | collective-permute-done | bytes 196640 | tf_op jit(solution)/shard_map/ppermute | solution.py:30
  44.1 0.8 shard_map.78.slots_ref.near_slots_ref
  44.9 1.7 %shard_map.79 = (bf16[192,1536]{1,0:T(8,128)(2,1)S(1)}, bf16[192,1536]{1,0:T(8,128)(2,1)S(1)}, f32[128,128]{1,0:T(8,128)S(1)}) custom-call(s32[3]{0:T(128)S(1)} %pad_add_fusion.places_ref, f32[128,128]{1,0:T(8,128)S(1)} %shard_map.78.slots_ref.near_slots_ref, bf16[128,1536]{1,0:T(8,128)(2,1)S(1)} %pad_maximum_fusion.1.rows_ref.near_ref, ...), custom_call_target="tpu_custom_call" | custom-call | flops 301989888 | bytes 1572864 | tf_op jit(solution)/shard_map/pallas_call | solution.py:111
  47.2 1.3 %collective-permute-start.14 = (bf16[192,1536]{1,0:T(8,128)(2,1)S(1)}, bf16[192,1536]{1,0:T(8,128)(2,1)S(1)}, u32[]{:S(2)}, u32[]{:S(2)}) collective-permute-start(bf16[192,1536]{1,0:T(8,128)(2,1)S(1)} %get-tuple-element.75), channel_id=1, source_target_pairs={{0,2},{1,5},{2,0},{3,7},{4,6},{5,1},{6,4},{7,3},{8,10},{9,13},{10,... | collective-permute-start | bytes 1769480 | tf_op jit(solution)/shard_map/ppermute | solution.py:30
  48.8 6.9 %shard_map.80 = (f32[192,1536]{1,0:T(8,128)S(1)}, f32[192,1536]{1,0:T(8,128)S(1)}, bf16[192,1536]{1,0:T(8,128)(2,1)S(1)}, bf16[192,1536]{1,0:T(8,128)(2,1)S(1)}) custom-call(s32[3]{0:T(128)S(1)} %pad_add_fusion.places_ref, bf16[192,1536]{1,0:T(8,128)(2,1)S(1)} %get-tuple-element.62.mine_near_ref, bf16[192,1536]{1,0:T(8,128)(2,1)S(1)} %collective-permute-done.10.mine_far_ref, ...), custom_call_target="tpu_custom_call" | custom-call | flops 4777574400 | bytes 17160192 | tf_op jit(solution)/shard_map/pallas_call | solution.py:233
  55.7 1.3 %collective-permute-done.14.mine_far_ref = bf16[192,1536]{1,0:T(8,128)(2,1)S(1)} collective-permute-done((bf16[192,1536]{1,0:T(8,128)(2,1)S(1)}, bf16[192,1536]{1,0:T(8,128)(2,1)S(1)}, u32[]{:S(2)}, u32[]{:S(2)}) %collective-permute-start.14) | collective-permute-done | bytes 589856 | tf_op jit(solution)/shard_map/ppermute | solution.py:30
  57.5 1.5 %collective-permute-done.17 = bf16[192,1536]{1,0:T(8,128)(2,1)S(1)} collective-permute-done((bf16[192,1536]{1,0:T(8,128)(2,1)S(1)}, bf16[192,1536]{1,0:T(8,128)(2,1)S(1)}, u32[]{:S(2)}, u32[]{:S(2)}) %collective-permute-start.17) | collective-permute-done | bytes 589856 | tf_op jit(solution)/shard_map/ppermute | solution.py:30
  59.2 1.4 %collective-permute-start.18 = (bf16[192,1536]{1,0:T(8,128)(2,1)S(1)}, bf16[192,1536]{1,0:T(8,128)(2,1)S(1)}, u32[]{:S(2)}, u32[]{:S(2)}) collective-permute-start(bf16[192,1536]{1,0:T(8,128)(2,1)S(1)} %add_convert_fusion.1), channel_id=1, source_target_pairs={{0,2},{1,5},{2,0},{3,7},{4,6},{5,1},{6,4},{7,3},{8,10},{9,13},{10,... | collective-permute-start | bytes 1769480 | tf_op jit(solution)/shard_map/ppermute | solution.py:30
  60.7 7.1 %shard_map.81 = (f32[192,1536]{1,0:T(8,128)S(1)}, f32[192,1536]{1,0:T(8,128)S(1)}, bf16[192,1536]{1,0:T(8,128)(2,1)S(1)}, bf16[192,1536]{1,0:T(8,128)(2,1)S(1)}) custom-call(s32[3]{0:T(128)S(1)} %pad_add_fusion.places_ref, bf16[192,1536]{1,0:T(8,128)(2,1)S(1)} %get-tuple-element.73.mine_near_ref, bf16[192,1536]{1,0:T(8,128)(2,1)S(1)} %collective-permute-done.14.mine_far_ref, ...), custom_call_target="tpu_custom_call" | custom-call | flops 4777574400 | bytes 17160192 | tf_op jit(solution)/shard_map/pallas_call | solution.py:233
  67.8 1.3 %collective-permute-done.18.arrived_ref = bf16[192,1536]{1,0:T(8,128)(2,1)S(1)} collective-permute-done((bf16[192,1536]{1,0:T(8,128)(2,1)S(1)}, bf16[192,1536]{1,0:T(8,128)(2,1)S(1)}, u32[]{:S(2)}, u32[]{:S(2)}) %collective-permute-start.18) | collective-permute-done | bytes 589856 | tf_op jit(solution)/shard_map/ppermute | solution.py:30
  69.6 1.5 %collective-permute-done.19 = bf16[192,1536]{1,0:T(8,128)(2,1)S(1)} collective-permute-done((bf16[192,1536]{1,0:T(8,128)(2,1)S(1)}, bf16[192,1536]{1,0:T(8,128)(2,1)S(1)}, u32[]{:S(2)}, u32[]{:S(2)}) %collective-permute-start.19) | collective-permute-done | bytes 589856 | tf_op jit(solution)/shard_map/ppermute | solution.py:30
  71.3 1.4 %collective-permute-start.24 = (bf16[192,1536]{1,0:T(8,128)(2,1)S(1)}, bf16[192,1536]{1,0:T(8,128)(2,1)S(1)}, u32[]{:S(2)}, u32[]{:S(2)}) collective-permute-start(bf16[192,1536]{1,0:T(8,128)(2,1)S(1)} %add_convert_fusion), channel_id=1, source_target_pairs={{0,2},{1,5},{2,0},{3,7},{4,6},{5,1},{6,4},{7,3},{8,10},{9,13},{10,... | collective-permute-start | bytes 1769480 | tf_op jit(solution)/shard_map/ppermute | solution.py:30
  73.5 2.5 %collective-permute-start.22 = (bf16[64,1536]{1,0:T(8,128)(2,1)S(1)}, bf16[64,1536]{1,0:T(8,128)(2,1)S(1)}, u32[]{:S(2)}, u32[]{:S(2)}) collective-permute-start(bf16[64,1536]{1,0:T(8,128)(2,1)S(1)} %get-tuple-element.101), channel_id=1, source_target_pairs={{0,24},{1,25},{2,26},{3,27},{4,28},{5,29},{6,30},{7,31},{8,16},{9,... | collective-permute-start | bytes 589832 | tf_op jit(solution)/shard_map/ppermute | solution.py:30
  76.0 1.9 %collective-permute-start.20 = (bf16[64,1536]{1,0:T(8,128)(2,1)S(1)}, bf16[64,1536]{1,0:T(8,128)(2,1)S(1)}, u32[]{:S(2)}, u32[]{:S(2)}) collective-permute-start(bf16[64,1536]{1,0:T(8,128)(2,1)S(1)} %get-tuple-element.103), channel_id=1, source_target_pairs={{0,8},{1,9},{2,10},{3,11},{4,12},{5,13},{6,14},{7,15},{8,0},{9,1},... | collective-permute-start | bytes 589832 | tf_op jit(solution)/shard_map/ppermute | solution.py:30
  77.9 3.3 %collective-permute-done.24.arrived_ref = bf16[192,1536]{1,0:T(8,128)(2,1)S(1)} collective-permute-done((bf16[192,1536]{1,0:T(8,128)(2,1)S(1)}, bf16[192,1536]{1,0:T(8,128)(2,1)S(1)}, u32[]{:S(2)}, u32[]{:S(2)}) %collective-permute-start.24) | collective-permute-done | bytes 589856 | tf_op jit(solution)/shard_map/ppermute | solution.py:30
  81.7 1.4 %collective-permute-start.26 = (bf16[128,1536]{1,0:T(8,128)(2,1)S(1)}, bf16[128,1536]{1,0:T(8,128)(2,1)S(1)}, u32[]{:S(2)}, u32[]{:S(2)}) collective-permute-start(bf16[128,1536]{1,0:T(8,128)(2,1)S(1)} %shard_map.83), channel_id=1, source_target_pairs={{0,4},{1,3},{2,6},{3,1},{4,0},{5,7},{6,2},{7,5},{8,12},{9,11},{10,... | collective-permute-start | bytes 1179656 | tf_op jit(solution)/shard_map/ppermute | solution.py:30
  83.5 8.4 %collective-permute-done.21 = bf16[64,1536]{1,0:T(8,128)(2,1)S(1)} collective-permute-done((bf16[64,1536]{1,0:T(8,128)(2,1)S(1)}, bf16[64,1536]{1,0:T(8,128)(2,1)S(1)}, u32[]{:S(2)}, u32[]{:S(2)}) %collective-permute-start.21) | collective-permute-done | bytes 196640 | tf_op jit(solution)/shard_map/ppermute | solution.py:30
  92.1 1.0 collective-permute-start.25
  93.3 1.4 %collective-permute-start.29 = (bf16[32,1536]{1,0:T(8,128)(2,1)S(1)}, bf16[32,1536]{1,0:T(8,128)(2,1)S(1)}, u32[]{:S(2)}, u32[]{:S(2)}) collective-permute-start(bf16[32,1536]{1,0:T(8,128)(2,1)S(1)} %get-tuple-element.105), channel_id=1, source_target_pairs={{0,24},{1,25},{2,26},{3,27},{4,28},{5,29},{6,30},{7,31},{8,16},{9,... | collective-permute-start | bytes 294920 | tf_op jit(solution)/shard_map/ppermute | solution.py:30
  94.7 2.1 %collective-permute-start.28 = (bf16[32,1536]{1,0:T(8,128)(2,1)S(1)}, bf16[32,1536]{1,0:T(8,128)(2,1)S(1)}, u32[]{:S(2)}, u32[]{:S(2)}) collective-permute-start(bf16[32,1536]{1,0:T(8,128)(2,1)S(1)} %get-tuple-element.106), channel_id=1, source_target_pairs={{0,16},{1,17},{2,18},{3,19},{4,20},{5,21},{6,22},{7,23},{8,24},{9,... | collective-permute-start | bytes 294920 | tf_op jit(solution)/shard_map/ppermute | solution.py:30
  96.8 2.8 %collective-permute-done.27 = bf16[32,1536]{1,0:T(8,128)(2,1)S(1)} collective-permute-done((bf16[32,1536]{1,0:T(8,128)(2,1)S(1)}, bf16[32,1536]{1,0:T(8,128)(2,1)S(1)}, u32[]{:S(2)}, u32[]{:S(2)}) %collective-permute-start.27) | collective-permute-done | bytes 98336 | tf_op jit(solution)/shard_map/ppermute | solution.py:30
  99.6 1.2 %collective-permute-done.29 = bf16[32,1536]{1,0:T(8,128)(2,1)S(1)} collective-permute-done((bf16[32,1536]{1,0:T(8,128)(2,1)S(1)}, bf16[32,1536]{1,0:T(8,128)(2,1)S(1)}, u32[]{:S(2)}, u32[]{:S(2)}) %collective-permute-start.29) | collective-permute-done | bytes 98336 | tf_op jit(solution)/shard_map/ppermute | solution.py:30
  100.9 4.8 %collective-permute-done.28 = bf16[32,1536]{1,0:T(8,128)(2,1)S(1)} collective-permute-done((bf16[32,1536]{1,0:T(8,128)(2,1)S(1)}, bf16[32,1536]{1,0:T(8,128)(2,1)S(1)}, u32[]{:S(2)}, u32[]{:S(2)}) %collective-permute-start.28) | collective-permute-done | bytes 98336 | tf_op jit(solution)/shard_map/ppermute | solution.py:30
  105.8 1.3 %collective-permute-done.30 = bf16[2,16,1536]{2,1,0:T(8,128)(2,1)S(1)} collective-permute-done((bf16[2,16,1536]{2,1,0:T(8,128)(2,1)S(1)}, bf16[2,16,1536]{2,1,0:T(8,128)(2,1)S(1)}, u32[]{:S(2)}, u32[]{:S(2)}) %collective-permute-start.30) | collective-permute-done | bytes 98336 | tf_op jit(solution)/shard_map/ppermute | solution.py:30
  107.2 0.7 fusion.6
  (70 shorter events, 6.1 us)
Async XLA Ops:
  2.2 0.9 copy-start.3
  3.9 1.5 %collective-permute-start = (bf16[2,16,1536]{2,1,0:T(8,128)(2,1)S(1)}, bf16[2,16,1536]{2,1,0:T(8,128)(2,1)S(1)}, u32[]{:S(2)}, u32[]{:S(2)}) collective-permute-start(bf16[2,16,1536]{2,1,0:T(8,128)(2,1)S(1)} %get-tuple-element.51), channel_id=1, source_target_pairs={{0,1},{1,0},{2,3},{3,2},{4,5},{5,4},{6,7},{7,6},{8,9},{9,8},{10,11... | collective-permute-start | bytes 294920 | tf_op jit(solution)/shard_map/ppermute | solution.py:30
  5.4 14.9 %collective-permute-start.2 = (bf16[32,1536]{1,0:T(8,128)(2,1)S(1)}, bf16[32,1536]{1,0:T(8,128)(2,1)S(1)}, u32[]{:S(2)}, u32[]{:S(2)}) collective-permute-start(bf16[32,1536]{1,0:T(8,128)(2,1)S(1)} %pad_maximum_fusion.6), channel_id=1, source_target_pairs={{0,4},{1,3},{2,6},{3,1},{4,0},{5,7},{6,2},{7,5},{8,12},{9,11},{10,... | collective-permute-start | bytes 294920 | tf_op jit(solution)/shard_map/ppermute | solution.py:30
  8.4 11.9 %collective-permute-start.1 = (bf16[32,1536]{1,0:T(8,128)(2,1)S(1)}, bf16[32,1536]{1,0:T(8,128)(2,1)S(1)}, u32[]{:S(2)}, u32[]{:S(2)}) collective-permute-start(bf16[32,1536]{1,0:T(8,128)(2,1)S(1)} %pad_maximum_fusion.5._), channel_id=1, source_target_pairs={{0,8},{1,9},{2,10},{3,11},{4,12},{5,13},{6,14},{7,15},{8,0},{9,1},... | collective-permute-start | bytes 294920 | tf_op jit(solution)/shard_map/ppermute | solution.py:30
  10.0 11.4 %collective-permute-start.4 = (bf16[32,1536]{1,0:T(8,128)(2,1)S(1)}, bf16[32,1536]{1,0:T(8,128)(2,1)S(1)}, u32[]{:S(2)}, u32[]{:S(2)}) collective-permute-start(bf16[32,1536]{1,0:T(8,128)(2,1)S(1)} %pad_maximum_fusion.5._), channel_id=1, source_target_pairs={{0,24},{1,25},{2,26},{3,27},{4,28},{5,29},{6,30},{7,31},{8,16},{9,... | collective-permute-start | bytes 294920 | tf_op jit(solution)/shard_map/ppermute | solution.py:30
  12.5 9.0 %collective-permute-start.3 = (bf16[32,1536]{1,0:T(8,128)(2,1)S(1)}, bf16[32,1536]{1,0:T(8,128)(2,1)S(1)}, u32[]{:S(2)}, u32[]{:S(2)}) collective-permute-start(bf16[32,1536]{1,0:T(8,128)(2,1)S(1)} %pad_maximum_fusion.5._), channel_id=1, source_target_pairs={{0,16},{1,17},{2,18},{3,19},{4,20},{5,21},{6,22},{7,23},{8,24},{9,... | collective-permute-start | bytes 294920 | tf_op jit(solution)/shard_map/ppermute | solution.py:30
  12.6 2.2 %copy-start = (bf16[2880,720]{0,1:T(8,128)(2,1)S(1)}, bf16[2880,720]{0,1:T(8,128)(2,1)}, u32[]{:S(2)}) copy-start(bf16[2880,720]{0,1:T(8,128)(2,1)} %param.9) | copy-start | bytes 12441604
  14.8 2.2 %copy-start.1 = (bf16[2880,720]{0,1:T(8,128)(2,1)S(1)}, bf16[2880,720]{0,1:T(8,128)(2,1)}, u32[]{:S(2)}) copy-start(bf16[2880,720]{0,1:T(8,128)(2,1)} %param.10) | copy-start | bytes 12441604
  17.0 2.2 %copy-start.2 = (bf16[720,2880]{1,0:T(8,128)(2,1)S(1)}, bf16[720,2880]{1,0:T(8,128)(2,1)}, u32[]{:S(2)}) copy-start(bf16[720,2880]{1,0:T(8,128)(2,1)} %refs_2_.1) | copy-start | bytes 12441604
  22.3 7.8 %collective-permute-start.6 = (bf16[128,1536]{1,0:T(8,128)(2,1)S(1)}, bf16[128,1536]{1,0:T(8,128)(2,1)S(1)}, u32[]{:S(2)}, u32[]{:S(2)}) collective-permute-start(bf16[128,1536]{1,0:T(8,128)(2,1)S(1)} %constant_dynamic-update-slice_fusion.rows_ref.near_ref), channel_id=1, source_target_pairs={{0,4},{1,3},{2,6},{3,1},{4,0},{5,7},{6,2},{7,5},{8,12},{9,11},{10,... | collective-permute-start | bytes 1179656 | tf_op jit(solution)/shard_map/ppermute | solution.py:30
  23.8 1.3 %collective-permute-start.5 = (f32[128,128]{1,0:T(8,128)S(1)}, f32[128,128]{1,0:T(8,128)S(1)}, u32[]{:S(2)}, u32[]{:S(2)}) collective-permute-start(f32[128,128]{1,0:T(8,128)S(1)} %shard_map.75.slots_ref.near_slots_ref), channel_id=1, source_target_pairs={{0,1},{1,0},{2,3},{3,2},{4,5},{5,4},{6,7},{7,6},{8,9},{9,8},{10,11... | collective-permute-start | bytes 196616 | tf_op jit(solution)/shard_map/ppermute | solution.py:30
  25.1 9.7 %collective-permute-start.9 = (bf16[64,1536]{1,0:T(8,128)(2,1)S(1)}, bf16[64,1536]{1,0:T(8,128)(2,1)S(1)}, u32[]{:S(2)}, u32[]{:S(2)}) collective-permute-start(bf16[64,1536]{1,0:T(8,128)(2,1)S(1)} %pad_maximum_fusion.4), channel_id=1, source_target_pairs={{0,24},{1,25},{2,26},{3,27},{4,28},{5,29},{6,30},{7,31},{8,16},{9,... | collective-permute-start | bytes 589832 | tf_op jit(solution)/shard_map/ppermute | solution.py:30
  27.7 16.2 %collective-permute-start.8 = (bf16[64,1536]{1,0:T(8,128)(2,1)S(1)}, bf16[64,1536]{1,0:T(8,128)(2,1)S(1)}, u32[]{:S(2)}, u32[]{:S(2)}) collective-permute-start(bf16[64,1536]{1,0:T(8,128)(2,1)S(1)} %pad_maximum_fusion.4), channel_id=1, source_target_pairs={{0,16},{1,17},{2,18},{3,19},{4,20},{5,21},{6,22},{7,23},{8,24},{9,... | collective-permute-start | bytes 589832 | tf_op jit(solution)/shard_map/ppermute | solution.py:30
  27.7 16.2 %collective-permute-start.7 = (bf16[64,1536]{1,0:T(8,128)(2,1)S(1)}, bf16[64,1536]{1,0:T(8,128)(2,1)S(1)}, u32[]{:S(2)}, u32[]{:S(2)}) collective-permute-start(bf16[64,1536]{1,0:T(8,128)(2,1)S(1)} %pad_maximum_fusion.4), channel_id=1, source_target_pairs={{0,8},{1,9},{2,10},{3,11},{4,12},{5,13},{6,14},{7,15},{8,0},{9,1},... | collective-permute-start | bytes 589832 | tf_op jit(solution)/shard_map/ppermute | solution.py:30
  31.5 15.1 %collective-permute-start.10 = (bf16[192,1536]{1,0:T(8,128)(2,1)S(1)}, bf16[192,1536]{1,0:T(8,128)(2,1)S(1)}, u32[]{:S(2)}, u32[]{:S(2)}) collective-permute-start(bf16[192,1536]{1,0:T(8,128)(2,1)S(1)} %shard_map.76), channel_id=1, source_target_pairs={{0,2},{1,5},{2,0},{3,7},{4,6},{5,1},{6,4},{7,3},{8,10},{9,13},{10,... | collective-permute-start | bytes 1769480 | tf_op jit(solution)/shard_map/ppermute | solution.py:30
  44.8 3.7 %collective-permute-start.11 = (bf16[192,1536]{1,0:T(8,128)(2,1)S(1)}, bf16[192,1536]{1,0:T(8,128)(2,1)S(1)}, u32[]{:S(2)}, u32[]{:S(2)}) collective-permute-start(bf16[192,1536]{1,0:T(8,128)(2,1)S(1)} %get-tuple-element.62.mine_near_ref), channel_id=1, source_target_pairs={{0,1},{1,0},{2,3},{3,2},{4,5},{5,4},{6,7},{7,6},{8,9},{9,8},{10,11... | collective-permute-start | bytes 1769480 | tf_op jit(solution)/shard_map/ppermute | solution.py:30
  46.6 2.2 %collective-permute-start.12 = (bf16[192,1536]{1,0:T(8,128)(2,1)S(1)}, bf16[192,1536]{1,0:T(8,128)(2,1)S(1)}, u32[]{:S(2)}, u32[]{:S(2)}) collective-permute-start(bf16[192,1536]{1,0:T(8,128)(2,1)S(1)} %collective-permute-done.10.mine_far_ref), channel_id=1, source_target_pairs={{0,1},{1,0},{2,3},{3,2},{4,5},{5,4},{6,7},{7,6},{8,9},{9,8},{10,11... | collective-permute-start | bytes 1769480 | tf_op jit(solution)/shard_map/ppermute | solution.py:30
  47.2 9.9 %collective-permute-start.14 = (bf16[192,1536]{1,0:T(8,128)(2,1)S(1)}, bf16[192,1536]{1,0:T(8,128)(2,1)S(1)}, u32[]{:S(2)}, u32[]{:S(2)}) collective-permute-start(bf16[192,1536]{1,0:T(8,128)(2,1)S(1)} %get-tuple-element.75), channel_id=1, source_target_pairs={{0,2},{1,5},{2,0},{3,7},{4,6},{5,1},{6,4},{7,3},{8,10},{9,13},{10,... | collective-permute-start | bytes 1769480 | tf_op jit(solution)/shard_map/ppermute | solution.py:30
  57.0 2.0 %collective-permute-start.17 = (bf16[192,1536]{1,0:T(8,128)(2,1)S(1)}, bf16[192,1536]{1,0:T(8,128)(2,1)S(1)}, u32[]{:S(2)}, u32[]{:S(2)}) collective-permute-start(bf16[192,1536]{1,0:T(8,128)(2,1)S(1)} %get-tuple-element.78), channel_id=1, source_target_pairs={{0,1},{1,0},{2,3},{3,2},{4,5},{5,4},{6,7},{7,6},{8,9},{9,8},{10,11... | collective-permute-start | bytes 1769480 | tf_op jit(solution)/shard_map/ppermute | solution.py:30
  57.0 3.7 %collective-permute-start.15 = (bf16[192,1536]{1,0:T(8,128)(2,1)S(1)}, bf16[192,1536]{1,0:T(8,128)(2,1)S(1)}, u32[]{:S(2)}, u32[]{:S(2)}) collective-permute-start(bf16[192,1536]{1,0:T(8,128)(2,1)S(1)} %get-tuple-element.73.mine_near_ref), channel_id=1, source_target_pairs={{0,1},{1,0},{2,3},{3,2},{4,5},{5,4},{6,7},{7,6},{8,9},{9,8},{10,11... | collective-permute-start | bytes 1769480 | tf_op jit(solution)/shard_map/ppermute | solution.py:30
  57.5 3.2 %collective-permute-start.16 = (bf16[192,1536]{1,0:T(8,128)(2,1)S(1)}, bf16[192,1536]{1,0:T(8,128)(2,1)S(1)}, u32[]{:S(2)}, u32[]{:S(2)}) collective-permute-start(bf16[192,1536]{1,0:T(8,128)(2,1)S(1)} %collective-permute-done.14.mine_far_ref), channel_id=1, source_target_pairs={{0,1},{1,0},{2,3},{3,2},{4,5},{5,4},{6,7},{7,6},{8,9},{9,8},{10,11... | collective-permute-start | bytes 1769480 | tf_op jit(solution)/shard_map/ppermute | solution.py:30
  59.2 9.9 %collective-permute-start.18 = (bf16[192,1536]{1,0:T(8,128)(2,1)S(1)}, bf16[192,1536]{1,0:T(8,128)(2,1)S(1)}, u32[]{:S(2)}, u32[]{:S(2)}) collective-permute-start(bf16[192,1536]{1,0:T(8,128)(2,1)S(1)} %add_convert_fusion.1), channel_id=1, source_target_pairs={{0,2},{1,5},{2,0},{3,7},{4,6},{5,1},{6,4},{7,3},{8,10},{9,13},{10,... | collective-permute-start | bytes 1769480 | tf_op jit(solution)/shard_map/ppermute | solution.py:30
  69.1 2.0 %collective-permute-start.19 = (bf16[192,1536]{1,0:T(8,128)(2,1)S(1)}, bf16[192,1536]{1,0:T(8,128)(2,1)S(1)}, u32[]{:S(2)}, u32[]{:S(2)}) collective-permute-start(bf16[192,1536]{1,0:T(8,128)(2,1)S(1)} %get-tuple-element.82), channel_id=1, source_target_pairs={{0,1},{1,0},{2,3},{3,2},{4,5},{5,4},{6,7},{7,6},{8,9},{9,8},{10,11... | collective-permute-start | bytes 1769480 | tf_op jit(solution)/shard_map/ppermute | solution.py:30
  69.1 3.6 %collective-permute-start.13 = (bf16[192,1536]{1,0:T(8,128)(2,1)S(1)}, bf16[192,1536]{1,0:T(8,128)(2,1)S(1)}, u32[]{:S(2)}, u32[]{:S(2)}) collective-permute-start(bf16[192,1536]{1,0:T(8,128)(2,1)S(1)} %get-tuple-element.72), channel_id=1, source_target_pairs={{0,1},{1,0},{2,3},{3,2},{4,5},{5,4},{6,7},{7,6},{8,9},{9,8},{10,11... | collective-permute-start | bytes 1769480 | tf_op jit(solution)/shard_map/ppermute | solution.py:30
  69.6 8.3 %collective-permute-start.23 = (bf16[192,1536]{1,0:T(8,128)(2,1)S(1)}, bf16[192,1536]{1,0:T(8,128)(2,1)S(1)}, u32[]{:S(2)}, u32[]{:S(2)}) collective-permute-start(bf16[192,1536]{1,0:T(8,128)(2,1)S(1)} %get-tuple-element.89), channel_id=1, source_target_pairs={{0,1},{1,0},{2,3},{3,2},{4,5},{5,4},{6,7},{7,6},{8,9},{9,8},{10,11... | collective-permute-start | bytes 1769480 | tf_op jit(solution)/shard_map/ppermute | solution.py:30
  71.3 9.9 %collective-permute-start.24 = (bf16[192,1536]{1,0:T(8,128)(2,1)S(1)}, bf16[192,1536]{1,0:T(8,128)(2,1)S(1)}, u32[]{:S(2)}, u32[]{:S(2)}) collective-permute-start(bf16[192,1536]{1,0:T(8,128)(2,1)S(1)} %add_convert_fusion), channel_id=1, source_target_pairs={{0,2},{1,5},{2,0},{3,7},{4,6},{5,1},{6,4},{7,3},{8,10},{9,13},{10,... | collective-permute-start | bytes 1769480 | tf_op jit(solution)/shard_map/ppermute | solution.py:30
  73.5 10.1 %collective-permute-start.22 = (bf16[64,1536]{1,0:T(8,128)(2,1)S(1)}, bf16[64,1536]{1,0:T(8,128)(2,1)S(1)}, u32[]{:S(2)}, u32[]{:S(2)}) collective-permute-start(bf16[64,1536]{1,0:T(8,128)(2,1)S(1)} %get-tuple-element.101), channel_id=1, source_target_pairs={{0,24},{1,25},{2,26},{3,27},{4,28},{5,29},{6,30},{7,31},{8,16},{9,... | collective-permute-start | bytes 589832 | tf_op jit(solution)/shard_map/ppermute | solution.py:30
  76.0 16.0 %collective-permute-start.21 = (bf16[64,1536]{1,0:T(8,128)(2,1)S(1)}, bf16[64,1536]{1,0:T(8,128)(2,1)S(1)}, u32[]{:S(2)}, u32[]{:S(2)}) collective-permute-start(bf16[64,1536]{1,0:T(8,128)(2,1)S(1)} %get-tuple-element.102), channel_id=1, source_target_pairs={{0,16},{1,17},{2,18},{3,19},{4,20},{5,21},{6,22},{7,23},{8,24},{9,... | collective-permute-start | bytes 589832 | tf_op jit(solution)/shard_map/ppermute | solution.py:30
  76.0 16.0 %collective-permute-start.20 = (bf16[64,1536]{1,0:T(8,128)(2,1)S(1)}, bf16[64,1536]{1,0:T(8,128)(2,1)S(1)}, u32[]{:S(2)}, u32[]{:S(2)}) collective-permute-start(bf16[64,1536]{1,0:T(8,128)(2,1)S(1)} %get-tuple-element.103), channel_id=1, source_target_pairs={{0,8},{1,9},{2,10},{3,11},{4,12},{5,13},{6,14},{7,15},{8,0},{9,1},... | collective-permute-start | bytes 589832 | tf_op jit(solution)/shard_map/ppermute | solution.py:30
  81.7 11.4 %collective-permute-start.26 = (bf16[128,1536]{1,0:T(8,128)(2,1)S(1)}, bf16[128,1536]{1,0:T(8,128)(2,1)S(1)}, u32[]{:S(2)}, u32[]{:S(2)}) collective-permute-start(bf16[128,1536]{1,0:T(8,128)(2,1)S(1)} %shard_map.83), channel_id=1, source_target_pairs={{0,4},{1,3},{2,6},{3,1},{4,0},{5,7},{6,2},{7,5},{8,12},{9,11},{10,... | collective-permute-start | bytes 1179656 | tf_op jit(solution)/shard_map/ppermute | solution.py:30
  92.1 4.7 %collective-permute-start.25 = (bf16[32,1536]{1,0:T(8,128)(2,1)S(1)}, bf16[32,1536]{1,0:T(8,128)(2,1)S(1)}, u32[]{:S(2)}, u32[]{:S(2)}) collective-permute-start(bf16[32,1536]{1,0:T(8,128)(2,1)S(1)} %slice.194), channel_id=1, source_target_pairs={{0,4},{1,3},{2,6},{3,1},{4,0},{5,7},{6,2},{7,5},{8,12},{9,11},{10,... | collective-permute-start | bytes 294920 | tf_op jit(solution)/shard_map/ppermute | solution.py:30
  93.2 6.4 %collective-permute-start.27 = (bf16[32,1536]{1,0:T(8,128)(2,1)S(1)}, bf16[32,1536]{1,0:T(8,128)(2,1)S(1)}, u32[]{:S(2)}, u32[]{:S(2)}) collective-permute-start(bf16[32,1536]{1,0:T(8,128)(2,1)S(1)} %get-tuple-element.104), channel_id=1, source_target_pairs={{0,8},{1,9},{2,10},{3,11},{4,12},{5,13},{6,14},{7,15},{8,0},{9,1},... | collective-permute-start | bytes 294920 | tf_op jit(solution)/shard_map/ppermute | solution.py:30
  93.3 7.6 %collective-permute-start.29 = (bf16[32,1536]{1,0:T(8,128)(2,1)S(1)}, bf16[32,1536]{1,0:T(8,128)(2,1)S(1)}, u32[]{:S(2)}, u32[]{:S(2)}) collective-permute-start(bf16[32,1536]{1,0:T(8,128)(2,1)S(1)} %get-tuple-element.105), channel_id=1, source_target_pairs={{0,24},{1,25},{2,26},{3,27},{4,28},{5,29},{6,30},{7,31},{8,16},{9,... | collective-permute-start | bytes 294920 | tf_op jit(solution)/shard_map/ppermute | solution.py:30
  94.7 11.0 %collective-permute-start.28 = (bf16[32,1536]{1,0:T(8,128)(2,1)S(1)}, bf16[32,1536]{1,0:T(8,128)(2,1)S(1)}, u32[]{:S(2)}, u32[]{:S(2)}) collective-permute-start(bf16[32,1536]{1,0:T(8,128)(2,1)S(1)} %get-tuple-element.106), channel_id=1, source_target_pairs={{0,16},{1,17},{2,18},{3,19},{4,20},{5,21},{6,22},{7,23},{8,24},{9,... | collective-permute-start | bytes 294920 | tf_op jit(solution)/shard_map/ppermute | solution.py:30
  105.6 1.5 %copy-start.4 = (bf16[2,16,2880]{2,1,0:T(8,128)(2,1)S(1)}, bf16[2,16,2880]{2,1,0:T(8,128)(2,1)}, u32[]{:S(2)}) copy-start(bf16[2,16,2880]{2,1,0:T(8,128)(2,1)} %hidden_ref.1) | copy-start | bytes 552964
  105.7 1.4 %collective-permute-start.30 = (bf16[2,16,1536]{2,1,0:T(8,128)(2,1)S(1)}, bf16[2,16,1536]{2,1,0:T(8,128)(2,1)S(1)}, u32[]{:S(2)}, u32[]{:S(2)}) collective-permute-start(bf16[2,16,1536]{2,1,0:T(8,128)(2,1)S(1)} %select_convert_fusion), channel_id=1, source_target_pairs={{0,1},{1,0},{2,3},{3,2},{4,5},{5,4},{6,7},{7,6},{8,9},{9,8},{10,11... | collective-permute-start | bytes 294920 | tf_op jit(solution)/shard_map/ppermute | solution.py:30

commit v5 on v4

--- a/solution.py
+++ b/solution.py
@@ -72,50 +72,38 @@
     return jnp.where(marks > 0.0, ahead + (base + row // tokens * capacity).astype(jnp.float32), -1.0)
 
 
-def locate_body(tokens, capacity, places_ref, rows_ref, slots_ref):
-    slots_ref[...] = slots_of(tokens, capacity, 0, places_ref, rows_ref)
-
-
-def locate(tokens, capacity, places, rows):
-    return pl.pallas_call(
-        functools.partial(locate_body, tokens, capacity),
-        out_shape=jax.ShapeDtypeStruct((rows.shape[0], LANES), jnp.float32),
-        in_specs=[SCALARS] + whole_arrays(1),
-        out_specs=pl.BlockSpec(memory_space=pltpu.VMEM),
-        compiler_params=pltpu.CompilerParams(vmem_limit_bytes=20 * 2**20),
-    )(places, rows)
-
-
-def select_body(tokens, capacity, wanted, places_ref, slots_ref, near_ref, next_ref, *out_refs):
+def select_body(tokens, capacity, wanted, places_ref, near_ref, next_ref, *out_refs):
     rows = near_ref.shape[0]
     compact = out_refs[0].shape[0]
-    slots = slots_ref[...]
-    next_slots = slots_of(tokens, capacity, rows // tokens * capacity, places_ref, next_ref)
-    for next_slots_ref in out_refs[len(wanted) :]:
-        next_slots_ref[...] = next_slots
+    slots = [
+        slots_of(tokens, capacity, part * (rows // tokens * capacity), places_ref, ref)
+        for part, ref in enumerate((near_ref, next_ref))
+    ]
+    for part, slots_ref in enumerate(out_refs[len(wanted) :]):
+        slots_ref[...] = slots[part]
     column = lax.broadcasted_iota(jnp.int32, (rows, compact), 1).astype(jnp.float32)
     for index, rows_ref in zip(wanted, out_refs):
         result = None
-        for source, at in ((near_ref, slots), (next_ref, next_slots)):
+        for source, at in zip((near_ref, next_ref), slots):
             picks = (at[:, index : index + 1] == column).astype(jnp.float32).astype(jnp.bfloat16)
             part = lax.dot_general(picks, source[...], downward, preferred_element_type=jnp.float32)
             result = part if result is None else result + part
         rows_ref[...] = result.astype(jnp.bfloat16)
 
 
-def select(tokens, capacity, wanted, places, slots, near, following):
-    with_slots = int(0 in wanted)
+def select(tokens, capacity, wanted, places, near, following):
+    located = 2 * int(0 in wanted)
     rows, held = near.shape
     compact = 2 * rows // tokens * capacity
     block = jax.ShapeDtypeStruct((compact, held), jnp.bfloat16)
     return pl.pallas_call(
         functools.partial(select_body, tokens, capacity, wanted),
-        out_shape=[block] * len(wanted) + [jax.ShapeDtypeStruct((rows, LANES), jnp.float32)] * with_slots,
-        in_specs=[SCALARS] + whole_arrays(3),
-        out_specs=whole_arrays(len(wanted) + with_slots),
+        out_shape=[block] * len(wanted) + [jax.ShapeDtypeStruct((rows, LANES), jnp.float32)] * located,
+        in_specs=[SCALARS] + whole_arrays(2),
+        out_specs=whole_arrays(len(wanted) + located),
         compiler_params=pltpu.CompilerParams(vmem_limit_bytes=20 * 2**20),
         cost_estimate=pl.CostEstimate(flops=8 * rows * compact * held, bytes_accessed=8 * rows * held, transcendentals=0),
-    )(places, slots, near, following)
+    )(places, near, following)
 
 
 def merge_body(wanted, near_slots_ref, next_slots_ref, keep_ref, taken_ref, arrived_ref, *out_refs):
@@ -270,21 +258,20 @@
     )(token, *arrays)
 
 
-def prologue_body(
-    tokens, top_count, places_ref, hidden_ref, gain_ref, routing_ref, mine_ref, give_ref
-):
-    micro_count, _, width = hidden_ref.shape
+def prologue_body(top_count, places_ref, hidden_ref, packed_ref, mine_ref, give_ref):
+    micro_count, tokens, width = hidden_ref.shape
     first, second, held = split_widths(width)
+    start = -(-width // LANES) * LANES
     lane = lax.broadcasted_iota(jnp.int32, (tokens, LANES), 1)
+    row = lax.broadcasted_iota(jnp.int32, (tokens, LANES), 0)
     here = lane % (ROUTING // 2)
     on_ids = (lane >= LANES - ROUTING) & (lane < LANES - ROUTING // 2)
     on_weights = lane >= LANES - ROUTING // 2
-    diagonal = lax.broadcasted_iota(jnp.int32, (tokens, tokens), 0) == lax.broadcasted_iota(
-        jnp.int32, (tokens, tokens), 1
-    )
-
-    def upright(line):
-        return jnp.sum(jnp.where(diagonal, line, 0.0), axis=1, keepdims=True)
+
+    def upright(place):
+        at = start + place * tokens
+        line = packed_ref[:, at // LANES * LANES : at // LANES * LANES + LANES]
+        return jnp.sum(jnp.where(lane == row + at % LANES, line, 0.0), axis=1, keepdims=True)
 
     def store(ref, b, part, tile):
         size = part.shape[1]
@@ -299,11 +286,11 @@
     for b in range(micro_count):
         residual = hidden_ref[b].astype(jnp.float32)
         scale = lax.rsqrt(jnp.mean(residual * residual, axis=-1, keepdims=True) + epsilon)
-        normed = residual * scale * gain_ref[...].astype(jnp.float32)
+        normed = residual * scale * packed_ref[:, :width]
         tile = jnp.where(on_ids, -1.0, 0.0)
         for k in range(top_count):
-            number = upright(routing_ref[b, k : k + 1, :])
-            weight = upright(routing_ref[b, top_count + k : top_count + k + 1, :])
+            number = upright(b * top_count + k)
+            weight = upright((micro_count + b) * top_count + k)
             high = weight.astype(jnp.bfloat16).astype(jnp.float32)
             middle = (weight - high).astype(jnp.bfloat16).astype(jnp.float32)
             for place, piece in enumerate((high, middle, weight - high - middle)):
@@ -322,16 +309,25 @@
             store(give_ref, b, parts[0], tile)
 
 
-def prologue(places, hidden, gain, routing):
+def prologue(places, hidden, gain, ids, weights):
     micro_count, tokens, width = hidden.shape
+    top_count = ids.shape[2]
     held = split_widths(width)[2]
+    packed = jnp.concatenate(
+        [
+            jnp.pad(gain.astype(jnp.float32), (0, -width % LANES)),
+            ids.transpose(0, 2, 1).reshape(-1).astype(jnp.float32),
+            weights.transpose(0, 2, 1).reshape(-1),
+        ]
+    )
+    packed = jnp.pad(packed, (0, -packed.shape[0] % LANES)).reshape(1, -1)
     return pl.pallas_call(
-        functools.partial(prologue_body, tokens, routing.shape[1] // 2),
+        functools.partial(prologue_body, top_count),
         out_shape=[jax.ShapeDtypeStruct((micro_count, tokens, held), jnp.bfloat16)] * 2,
-        in_specs=[SCALARS] + whole_arrays(3),
+        in_specs=[SCALARS] + whole_arrays(2),
         out_specs=whole_arrays(2),
         compiler_params=pltpu.CompilerParams(vmem_limit_bytes=20 * 2**20),
-    )(places, hidden, gain, routing)
+    )(places, hidden, packed)
 
 
 def local(hidden, norm_gain, w_gate, w_up, w_down, expert_ids, route_weight):
@@ -352,10 +348,7 @@
     def join(*blocks):
         return jnp.concatenate(blocks, axis=0)
 
-    routing = jnp.concatenate(
-        [expert_ids.transpose(0, 2, 1).astype(jnp.float32), route_weight.transpose(0, 2, 1)], axis=1
-    )
-    mine, give = prologue(places, hidden, norm_gain.reshape(1, width), routing)
+    mine, give = prologue(places, hidden, norm_gain, expert_ids, route_weight)
     theirs = moved(give, other_core)
     pairs = [
         join(jnp.where(lower, mine[b], theirs[b]), jnp.where(lower, theirs[b], mine[b]))
@@ -368,99 +361,98 @@
     def far_blocks(pair):
         return [moved(pair, far(j)) for j in range(1, distant)]
 
-    def second_hop(state, earlier, apart):
-        chosen = tokens, capacity
+    chosen = tokens, capacity
+    states = []
+
+    def second_hop(state, apart):
         near, following = state["near"], state["next"]
-        slots = state["slots"]
         if apart:
-            (send,) = select(*chosen, (1,), places, slots, near, following)
+            (send,) = select(*chosen, (1,), places, near, following)
         else:
-            send, state["own"], next_slots = select(*chosen, (1, 0), places, slots, near, following)
-        if earlier is not None:
-            send, earlier["arrived"] = tied(send, earlier["arrived"])
+            send, state["own"], *state["slots"] = select(*chosen, (1, 0), places, near, following)
+        if len(states) > 1:
+            send, states[-2]["arrived"] = tied(send, states[-2]["arrived"])
         state["arrived"] = moved(send, second_axis)
         if apart:
             following, _ = tied(following, send)
-            state["own"], next_slots = select(*chosen, (0,), places, state["twin"], near, following)
-        state["slots"] = slots, next_slots
-
-    states = []
-    gate_v, up_v, down_v = preload(pairs[0], w_gate.T, w_up.T, w_down)
-    beside = [moved(pair, first_axis) for pair in pairs[1:]]
-    blocks = far_blocks(pairs[0])
-    blocks[0], gate_v, up_v, down_v, *beside = tied(blocks[0], gate_v, up_v, down_v, *beside)
-    column = join(pairs[0], *blocks)
-    states.append(
-        {"near": column, "next": moved(column, first_axis), "slots": locate(tokens, capacity, places, column)}
-    )
-    side = 2 * tokens
-    for b in range(1, micro_count):
+            state["own"], *state["slots"] = select(*chosen, (0,), places, near, following)
+
+    pair = pairs[0]
+    (gate_v,) = preload(pair, w_gate.T)
+    if distant == 4:
+        crossed, beside = moved(pair, far(2)), moved(pair, far(1))
+        crossed, gate_v = tied(crossed, gate_v)
+        (up_v,) = preload(crossed, w_up.T)
+        passed = moved(crossed, far(1))
+        passed, up_v = tied(passed, up_v)
+        blocks = [beside, crossed, passed]
+    else:
+        (up_v,) = preload(pair, w_up.T)
+        blocks = far_blocks(pair)
+    column = join(pair, *blocks)
+    states.append({"near": column, "next": moved(column, first_axis)})
+    down_v = None
+    for pair in pairs[1:]:
         last = states[-1]
-        both, last["twin"] = tied(join(pairs[b], beside[b - 1]), moved(last["slots"], other_core))
-        blocks = far_blocks(both)
-        second_hop(last, states[-2] if len(states) > 1 else None, True)
+        pair, last["near"] = tied(pair, last["near"])
+        blocks = far_blocks(pair)
+        second_hop(last, True)
         *blocks, last["own"] = tied(*blocks, last["own"])
-        blocks = [both] + blocks
-        near, following = join(*[block[:side] for block in blocks]), join(*[block[side:] for block in blocks])
-        states.append({"near": near, "next": following, "slots": locate(tokens, capacity, places, near)})
-    second_hop(states[-1], states[-2] if len(states) > 1 else None, False)
+        column = join(pair, *blocks)
+        following = moved(column, first_axis)
+        if down_v is None:
+            (down_v,) = preload(last["own"], w_down)
+            following, down_v = tied(following, down_v)
+        states.append({"near": column, "next": following})
+    second_hop(states[-1], False)
+    if down_v is None:
+        (down_v,) = preload(states[-1]["own"], w_down)
 
     hops = []
-    for b, state in enumerate(states):
+    before = None
+    for state in states:
         own, arrived = state["own"], state["arrived"]
-        other_far = moved(arrived, other_core)
-        if b:
-            other_far, hops[-1]["give"] = tied(other_far, hops[-1]["give"])
-        keep_near, keep_far, send_near, send_far = ffn(
-            places, own, arrived, moved(own, other_core), other_far, gate_v, up_v, down_v
-        )
-        if b + 1 < micro_count:
-            send_far, states[b + 1]["arrived"] = tied(send_far, states[b + 1]["arrived"])
-        if b:
-            send_far, hops[-1]["arrived"] = tied(send_far, hops[-1]["arrived"])
-        give = (keep_far + moved(send_far, other_core).astype(jnp.float32)).astype(jnp.bfloat16)
-        hops.append(
-            {"keep": keep_near, "taken": moved(send_near, other_core), "give": give, "arrived": moved(give, second_axis)}
-        )
-
-    def far_sum(block):
+        if before is not None:
+            arrived, *before = tied(arrived, *before)
+            hops.append(before)
+        before = ffn(places, own, arrived, moved(own, other_core), moved(arrived, other_core), gate_v, up_v, down_v)
+    hops.append(before)
+
+    def rounded_sum(a, b):
+        return (a + b.astype(jnp.float32)).astype(jnp.bfloat16)
+
+    def far_total(block, earlier):
         block = block.reshape(distant, -1, held)
-        arrivals = [moved(block[j].astype(jnp.bfloat16), far(j)) for j in range(1, distant)]
-        return block[0], arrivals
-
-    def total(kept, arrivals):
+        if distant == 4:
+            if earlier:
+                block, earlier[-1]["crossing"] = tied(block, earlier[-1]["crossing"])
+            through = moved(block[3].astype(jnp.bfloat16), far(1))
+            beside = moved(block[1].astype(jnp.bfloat16), far(1))
+            return {"kept": block[0], "arrivals": [beside], "crossing": rounded_sum(block[2], through)}
+        return {
+            "kept": block[0],
+            "arrivals": [moved(block[j].astype(jnp.bfloat16), far(j)) for j in range(1, distant)],
+            "crossing": None,
+        }
+
+    def settled(total):
+        kept, arrivals = total["kept"], list(total["arrivals"])
+        if total["crossing"] is not None:
+            arrivals.append(moved(total["crossing"], far(2)))
         for arrival in arrivals:
             kept = kept + arrival.astype(jnp.float32)
         return kept
 
-    count = len(hops)
-    for b in range(1, count):
-        hops[b - 1]["taken"], hops[b]["give"] = tied(hops[b - 1]["taken"], hops[b]["give"])
-    sums = [None] * count
-    waiting = None
-    for b, (state, hop) in enumerate(zip(states, hops)):
-        final = b == count - 1
-        parts = state["slots"], hop["keep"], hop["taken"], hop["arrived"]
-        if final:
-            (following,) = merge((1,), (jnp.bfloat16,), *parts)
-            taken, _ = tied(parts[2], following)
-            (near,) = merge((0,), (jnp.float32,), parts[0], parts[1], taken, parts[3])
-            if waiting is not None:
-                *arrivals, near = tied(*waiting[1], near)
-                waiting = waiting[0], arrivals
-            near = total(near, [moved(following, first_axis)])
-            kept, arrivals = far_sum(near)
-            sums[b] = total(kept, arrivals)
-        if waiting is not None:
-            settled = total(*waiting)
-            sums[b - 1] = total(settled[:side], [moved(settled[side:].astype(jnp.bfloat16), first_axis)])
-            waiting = None
-        if not final:
-            near, following = merge((0, 1), (jnp.float32, jnp.float32), *parts)
-            waiting = far_sum(
-                jnp.concatenate([near.reshape(distant, side, held), following.reshape(distant, side, held)], axis=1)
-            )
-    sums = jnp.stack(sums)
+    sums = []
+    for state, (keep_near, keep_far, send_near, send_far) in zip(states, hops):
+        give = rounded_sum(keep_far, moved(send_far, other_core))
+        near, following = merge(
+            (0, 1), (jnp.float32, jnp.bfloat16), state["slots"], keep_near, moved(send_near, other_core),
+            moved(give, second_axis),
+        )
+        near = near + moved(following, first_axis).astype(jnp.float32)
+        sums.append(far_total(near, sums))
+    sums = jnp.stack([settled(total) for total in sums])
     own = jnp.where(lower, sums[:, :tokens], sums[:, tokens:])
     give = jnp.where(lower, sums[:, tokens:], sums[:, :tokens]).astype(jnp.bfloat16)
     taken = moved(give, other_core).astype(jnp.float32)

time: 108 us -> 104 us (0.963)
  local copies, waits for them, and re-layouts: 8.38 us -> 4.09 us
  starting transfers between devices: 30.4 us -> 32.3 us
  Pallas kernels: 23.3 us -> 21.5 us
    unnamed x12 -> x19, local copies, waits for them, and re-layouts: 7.55 us -> 3.19 us
    ppermute x31 -> x30, starting transfers between devices: 30.4 us -> 32.3 us  [moved(): return lax.ppermute(block, 'req', [(i, partner(i)) for i in range(count)])]
    pallas_call x3 -> x1, Pallas kernels: 2.36 us -> 0.82 us  [prologue(): pl.pallas_call(functools.partial(prologue_body, top_count), out_shape=[ja...]
    ppermute x31 -> x30, waiting for transfers between devices: 42.4 us -> 42.7 us  [moved(): return lax.ppermute(block, 'req', [(i, partner(i)) for i in range(count)])]
  transfers between devices with their start and end apart: 31 -> 30, of which waited for: 18 -> 20; matrix products, arithmetic and copies ran while one was open for 1% -> 1% of each run, Pallas kernels for 20% -> 20%
where the time goes in v5:
time: 104 us
  waiting for transfers between devices  42.7 us (41%)
  starting transfers between devices  32.3 us (31%)
  Pallas kernels  21.5 us (21%)
  local copies, waits for them, and re-layouts  4.09 us (4%)
  other arithmetic  3 us (3%)
    ppermute x30, waiting for transfers between devices, moved(): return lax.ppermute(block, 'req', [(i, partner(i)) for i in range(count)])  42.7 us
    ppermute x30, starting transfers between devices, moved(): return lax.ppermute(block, 'req', [(i, partner(i)) for i in range(count)])  32.3 us
    pallas_call x2, Pallas kernels, ffn(): pl.pallas_call(ffn_body, out_shape=[jax.ShapeDtypeStruct((pair, held), jn...  14 us
    pallas_call x3, Pallas kernels, select(): pl.pallas_call(functools.partial(select_body, tokens, capacity, wanted),...  4.33 us
    unnamed x19, local copies, waits for them, and re-layouts  3.19 us
  transfers between devices with their start and end apart: 30, of which 20 were waited for; matrix products, arithmetic and copies ran while one was open for 1% of the time, Pallas kernels for 20%

profile of v5, /device:TPU:0, one launch (start us, length us, event | category | flops | bytes accessed | tf_op | source)
XLA Modules:
  0.0 103.9 jit_solution(1042687693066913422)
XLA Ops:
  0.0 0.7 pad_convert_fusion
  0.7 0.7 convert_bitcast_fusion
  1.5 0.8 reshape.30
  2.4 0.9 copy-done.1
  3.3 0.8 shard_map.73
  4.6 0.9 collective-permute-done
  5.6 4.0 %collective-permute-start.2 = (bf16[32,1536]{1,0:T(8,128)(2,1)S(1)}, bf16[32,1536]{1,0:T(8,128)(2,1)S(1)}, u32[]{:S(2)}, u32[]{:S(2)}) collective-permute-start(bf16[32,1536]{1,0:T(8,128)(2,1)S(1)} %pad_maximum_fusion.2._), channel_id=1, source_target_pairs={{0,16},{1,17},{2,18},{3,19},{4,20},{5,21},{6,22},{7,23},{8,24},{9,... | collective-permute-start | bytes 294920 | tf_op jit(solution)/shard_map/ppermute | solution.py:30
  9.7 1.6 %collective-permute-start.1 = (bf16[32,1536]{1,0:T(8,128)(2,1)S(1)}, bf16[32,1536]{1,0:T(8,128)(2,1)S(1)}, u32[]{:S(2)}, u32[]{:S(2)}) collective-permute-start(bf16[32,1536]{1,0:T(8,128)(2,1)S(1)} %pad_maximum_fusion.2._), channel_id=1, source_target_pairs={{0,8},{1,9},{2,10},{3,11},{4,12},{5,13},{6,14},{7,15},{8,0},{9,1},... | collective-permute-start | bytes 294920 | tf_op jit(solution)/shard_map/ppermute | solution.py:30
  11.3 2.2 %copy-done = bf16[2880,720]{0,1:T(8,128)(2,1)S(1)} copy-done((bf16[2880,720]{0,1:T(8,128)(2,1)S(1)}, bf16[2880,720]{0,1:T(8,128)(2,1)}, u32[]{:S(2)}) %copy-start) | copy-done | bytes 4147224
  13.8 1.2 %collective-permute-done.2._ = bf16[32,1536]{1,0:T(8,128)(2,1)S(1)} collective-permute-done((bf16[32,1536]{1,0:T(8,128)(2,1)S(1)}, bf16[32,1536]{1,0:T(8,128)(2,1)S(1)}, u32[]{:S(2)}, u32[]{:S(2)}) %collective-permute-start.2) | collective-permute-done | bytes 98336 | tf_op jit(solution)/shard_map/ppermute | solution.py:30
  16.0 3.5 %collective-permute-done.3 = bf16[32,1536]{1,0:T(8,128)(2,1)S(1)} collective-permute-done((bf16[32,1536]{1,0:T(8,128)(2,1)S(1)}, bf16[32,1536]{1,0:T(8,128)(2,1)S(1)}, u32[]{:S(2)}, u32[]{:S(2)}) %collective-permute-start.3) | collective-permute-done | bytes 98336 | tf_op jit(solution)/shard_map/ppermute | solution.py:30
  19.6 1.6 %collective-permute-start.4 = (bf16[128,1536]{1,0:T(8,128)(2,1)S(1)}, bf16[128,1536]{1,0:T(8,128)(2,1)S(1)}, u32[]{:S(2)}, u32[]{:S(2)}) collective-permute-start(bf16[128,1536]{1,0:T(8,128)(2,1)S(1)} %get-tuple-element.104), channel_id=1, source_target_pairs={{0,4},{1,3},{2,6},{3,1},{4,0},{5,7},{6,2},{7,5},{8,12},{9,11},{10,... | collective-permute-start | bytes 1179656 | tf_op jit(solution)/shard_map/ppermute | solution.py:30
  21.2 0.7 collective-permute-start.5
  21.9 3.4 %collective-permute-start.6 = (bf16[32,1536]{1,0:T(8,128)(2,1)S(1)}, bf16[32,1536]{1,0:T(8,128)(2,1)S(1)}, u32[]{:S(2)}, u32[]{:S(2)}) collective-permute-start(bf16[32,1536]{1,0:T(8,128)(2,1)S(1)} %get-tuple-element.56), channel_id=1, source_target_pairs={{0,16},{1,17},{2,18},{3,19},{4,20},{5,21},{6,22},{7,23},{8,24},{9,... | collective-permute-start | bytes 294920 | tf_op jit(solution)/shard_map/ppermute | solution.py:30
  25.6 1.8 %collective-permute-done.4.next_ref = bf16[128,1536]{1,0:T(8,128)(2,1)S(1)} collective-permute-done((bf16[128,1536]{1,0:T(8,128)(2,1)S(1)}, bf16[128,1536]{1,0:T(8,128)(2,1)S(1)}, u32[]{:S(2)}, u32[]{:S(2)}) %collective-permute-start.4) | collective-permute-done | bytes 393248 | tf_op jit(solution)/shard_map/ppermute | solution.py:30
  27.5 1.3 %shard_map.76 = bf16[192,1536]{1,0:T(8,128)(2,1)S(1)} custom-call(s32[3]{0:T(128)S(1)} %pad_add_fusion.places_ref, bf16[128,1536]{1,0:T(8,128)(2,1)S(1)} %get-tuple-element.104, bf16[128,1536]{1,0:T(8,128)(2,1)S(1)} %collective-permute-done.4.next_ref), custom_call_target="tpu_custom_call" | custom-call | flops 301989888 | bytes 1572864 | tf_op jit(solution)/shard_map/pallas_call | solution.py:99
  28.8 1.6 %collective-permute-start.9 = (bf16[192,1536]{1,0:T(8,128)(2,1)S(1)}, bf16[192,1536]{1,0:T(8,128)(2,1)S(1)}, u32[]{:S(2)}, u32[]{:S(2)}) collective-permute-start(bf16[192,1536]{1,0:T(8,128)(2,1)S(1)} %shard_map.76), channel_id=1, source_target_pairs={{0,2},{1,5},{2,0},{3,7},{4,6},{5,1},{6,4},{7,3},{8,10},{9,13},{10,... | collective-permute-start | bytes 1769480 | tf_op jit(solution)/shard_map/ppermute | solution.py:30
  30.4 1.3 %shard_map.77 = (bf16[192,1536]{1,0:T(8,128)(2,1)S(1)}, f32[128,128]{1,0:T(8,128)S(1)}, f32[128,128]{1,0:T(8,128)S(1)}) custom-call(s32[3]{0:T(128)S(1)} %pad_add_fusion.places_ref, bf16[128,1536]{1,0:T(8,128)(2,1)S(1)} %get-tuple-element.104, bf16[128,1536]{1,0:T(8,128)(2,1)S(1)} %collective-permute-done.4.next_ref), custom_call_target="tpu_custom_call" | custom-call | flops 301989888 | bytes 1572864 | tf_op jit(solution)/shard_map/pallas_call | solution.py:99
  32.2 1.3 %collective-permute-start.8 = (bf16[128,1536]{1,0:T(8,128)(2,1)S(1)}, bf16[128,1536]{1,0:T(8,128)(2,1)S(1)}, u32[]{:S(2)}, u32[]{:S(2)}) collective-permute-start(bf16[128,1536]{1,0:T(8,128)(2,1)S(1)} %constant_dynamic-update-slice_fusion.5.near_ref), channel_id=1, source_target_pairs={{0,4},{1,3},{2,6},{3,1},{4,0},{5,7},{6,2},{7,5},{8,12},{9,11},{10,... | collective-permute-start | bytes 1179656 | tf_op jit(solution)/shard_map/ppermute | solution.py:30
  33.9 6.2 %collective-permute-done.8.next_ref = bf16[128,1536]{1,0:T(8,128)(2,1)S(1)} collective-permute-done((bf16[128,1536]{1,0:T(8,128)(2,1)S(1)}, bf16[128,1536]{1,0:T(8,128)(2,1)S(1)}, u32[]{:S(2)}, u32[]{:S(2)}) %collective-permute-start.8) | collective-permute-done | bytes 393248 | tf_op jit(solution)/shard_map/ppermute | solution.py:30
  40.1 1.6 %shard_map.79 = (bf16[192,1536]{1,0:T(8,128)(2,1)S(1)}, bf16[192,1536]{1,0:T(8,128)(2,1)S(1)}, f32[128,128]{1,0:T(8,128)S(1)}, f32[128,128]{1,0:T(8,128)S(1)}) custom-call(s32[3]{0:T(128)S(1)} %pad_add_fusion.places_ref, bf16[128,1536]{1,0:T(8,128)(2,1)S(1)} %constant_dynamic-update-slice_fusion.5.near_ref, bf16[128,1536]{1,0:T(8,128)(2,1)S(1)} %collective-permute-done.8.next_ref), custom_call_target="tpu_custom_call" | custom-call | flops 301989888 | bytes 1572864 | tf_op jit(solution)/shard_map/pallas_call | solution.py:99
  41.7 1.2 %collective-permute-done.9.mine_far_ref = bf16[192,1536]{1,0:T(8,128)(2,1)S(1)} collective-permute-done((bf16[192,1536]{1,0:T(8,128)(2,1)S(1)}, bf16[192,1536]{1,0:T(8,128)(2,1)S(1)}, u32[]{:S(2)}, u32[]{:S(2)}) %collective-permute-start.9) | collective-permute-done | bytes 589856 | tf_op jit(solution)/shard_map/ppermute | solution.py:30
  43.0 0.7 collective-permute-start.10
  43.7 1.3 %collective-permute-done.12.other_far_ref = bf16[192,1536]{1,0:T(8,128)(2,1)S(1)} collective-permute-done((bf16[192,1536]{1,0:T(8,128)(2,1)S(1)}, bf16[192,1536]{1,0:T(8,128)(2,1)S(1)}, u32[]{:S(2)}, u32[]{:S(2)}) %collective-permute-start.12) | collective-permute-done | bytes 589856 | tf_op jit(solution)/shard_map/ppermute | solution.py:30
  45.0 6.9 %shard_map.80 = (f32[192,1536]{1,0:T(8,128)S(1)}, f32[192,1536]{1,0:T(8,128)S(1)}, bf16[192,1536]{1,0:T(8,128)(2,1)S(1)}, bf16[192,1536]{1,0:T(8,128)(2,1)S(1)}) custom-call(s32[3]{0:T(128)S(1)} %pad_add_fusion.places_ref, bf16[192,1536]{1,0:T(8,128)(2,1)S(1)} %get-tuple-element.61._.mine_near_ref, ...), custom_call_target="tpu_custom_call" | custom-call | flops 4777574400 | bytes 17160192 | tf_op jit(solution)/shard_map/pallas_call | solution.py:221
  51.9 1.0 collective-permute-done.10.mine_far_ref
  53.9 1.0 collective-permute-done.14
  55.0 0.8 collective-permute-start.15
  55.8 0.8 collective-permute-done.19.other_far_ref
  56.5 7.1 %shard_map.82 = (f32[192,1536]{1,0:T(8,128)S(1)}, f32[192,1536]{1,0:T(8,128)S(1)}, bf16[192,1536]{1,0:T(8,128)(2,1)S(1)}, bf16[192,1536]{1,0:T(8,128)(2,1)S(1)}) custom-call(s32[3]{0:T(128)S(1)} %pad_add_fusion.places_ref, bf16[192,1536]{1,0:T(8,128)(2,1)S(1)} %get-tuple-element.81.mine_near_ref, bf16[192,1536]{1,0:T(8,128)(2,1)S(1)} %collective-permute-done.10.mine_far_ref, ...), custom_call_target="tpu_custom_call" | custom-call | flops 4777574400 | bytes 17160192 | tf_op jit(solution)/shard_map/pallas_call | solution.py:221
  64.2 0.7 collective-permute-done.15.arrived_ref
  64.9 0.7 shard_map.81
  65.6 2.1 %collective-permute-start.16 = (bf16[128,1536]{1,0:T(8,128)(2,1)S(1)}, bf16[128,1536]{1,0:T(8,128)(2,1)S(1)}, u32[]{:S(2)}, u32[]{:S(2)}) collective-permute-start(bf16[128,1536]{1,0:T(8,128)(2,1)S(1)} %get-tuple-element.78), channel_id=1, source_target_pairs={{0,4},{1,3},{2,6},{3,1},{4,0},{5,7},{6,2},{7,5},{8,12},{9,11},{10,... | collective-permute-start | bytes 1179656 | tf_op jit(solution)/shard_map/ppermute | solution.py:30
  67.9 0.7 collective-permute-start.22
  68.5 9.2 %collective-permute-done.16 = bf16[128,1536]{1,0:T(8,128)(2,1)S(1)} collective-permute-done((bf16[128,1536]{1,0:T(8,128)(2,1)S(1)}, bf16[128,1536]{1,0:T(8,128)(2,1)S(1)}, u32[]{:S(2)}, u32[]{:S(2)}) %collective-permute-start.16) | collective-permute-done | bytes 393248 | tf_op jit(solution)/shard_map/ppermute | solution.py:30
  77.8 2.5 %collective-permute-start.24 = (bf16[32,1536]{1,0:T(8,128)(2,1)S(1)}, bf16[32,1536]{1,0:T(8,128)(2,1)S(1)}, u32[]{:S(2)}, u32[]{:S(2)}) collective-permute-start(bf16[32,1536]{1,0:T(8,128)(2,1)S(1)} %get-tuple-element.98), channel_id=1, source_target_pairs={{0,8},{1,9},{2,10},{3,11},{4,12},{5,13},{6,14},{7,15},{8,0},{9,1},... | collective-permute-start | bytes 294920 | tf_op jit(solution)/shard_map/ppermute | solution.py:30
  81.0 1.3 %collective-permute-start.23 = (bf16[128,1536]{1,0:T(8,128)(2,1)S(1)}, bf16[128,1536]{1,0:T(8,128)(2,1)S(1)}, u32[]{:S(2)}, u32[]{:S(2)}) collective-permute-start(bf16[128,1536]{1,0:T(8,128)(2,1)S(1)} %get-tuple-element.88), channel_id=1, source_target_pairs={{0,4},{1,3},{2,6},{3,1},{4,0},{5,7},{6,2},{7,5},{8,12},{9,11},{10,... | collective-permute-start | bytes 1179656 | tf_op jit(solution)/shard_map/ppermute | solution.py:30
  82.9 5.9 %collective-permute-done.23 = bf16[128,1536]{1,0:T(8,128)(2,1)S(1)} collective-permute-done((bf16[128,1536]{1,0:T(8,128)(2,1)S(1)}, bf16[128,1536]{1,0:T(8,128)(2,1)S(1)}, u32[]{:S(2)}, u32[]{:S(2)}) %collective-permute-start.23) | collective-permute-done | bytes 393248 | tf_op jit(solution)/shard_map/ppermute | solution.py:30
  89.5 1.6 %collective-permute-start.17 = (bf16[32,1536]{1,0:T(8,128)(2,1)S(1)}, bf16[32,1536]{1,0:T(8,128)(2,1)S(1)}, u32[]{:S(2)}, u32[]{:S(2)}) collective-permute-start(bf16[32,1536]{1,0:T(8,128)(2,1)S(1)} %get-tuple-element.97), channel_id=1, source_target_pairs={{0,8},{1,9},{2,10},{3,11},{4,12},{5,13},{6,14},{7,15},{8,0},{9,1},... | collective-permute-start | bytes 294920 | tf_op jit(solution)/shard_map/ppermute | solution.py:30
  91.1 1.9 %collective-permute-start.25 = (bf16[32,1536]{1,0:T(8,128)(2,1)S(1)}, bf16[32,1536]{1,0:T(8,128)(2,1)S(1)}, u32[]{:S(2)}, u32[]{:S(2)}) collective-permute-start(bf16[32,1536]{1,0:T(8,128)(2,1)S(1)} %fusion.2), channel_id=1, source_target_pairs={{0,16},{1,17},{2,18},{3,19},{4,20},{5,21},{6,22},{7,23},{8,24},{9,... | collective-permute-start | bytes 294920 | tf_op jit(solution)/shard_map/ppermute | solution.py:30
  92.9 1.4 %collective-permute-start.26 = (bf16[32,1536]{1,0:T(8,128)(2,1)S(1)}, bf16[32,1536]{1,0:T(8,128)(2,1)S(1)}, u32[]{:S(2)}, u32[]{:S(2)}) collective-permute-start(bf16[32,1536]{1,0:T(8,128)(2,1)S(1)} %get-tuple-element.99), channel_id=1, source_target_pairs={{0,8},{1,9},{2,10},{3,11},{4,12},{5,13},{6,14},{7,15},{8,0},{9,1},... | collective-permute-start | bytes 294920 | tf_op jit(solution)/shard_map/ppermute | solution.py:30
  94.4 0.7 collective-permute-done.27
  95.1 1.5 %collective-permute-start.28 = (bf16[32,1536]{1,0:T(8,128)(2,1)S(1)}, bf16[32,1536]{1,0:T(8,128)(2,1)S(1)}, u32[]{:S(2)}, u32[]{:S(2)}) collective-permute-start(bf16[32,1536]{1,0:T(8,128)(2,1)S(1)} %fusion.5), channel_id=1, source_target_pairs={{0,16},{1,17},{2,18},{3,19},{4,20},{5,21},{6,22},{7,23},{8,24},{9,... | collective-permute-start | bytes 294920 | tf_op jit(solution)/shard_map/ppermute | solution.py:30
  96.7 2.3 %collective-permute-done.17 = bf16[32,1536]{1,0:T(8,128)(2,1)S(1)} collective-permute-done((bf16[32,1536]{1,0:T(8,128)(2,1)S(1)}, bf16[32,1536]{1,0:T(8,128)(2,1)S(1)}, u32[]{:S(2)}, u32[]{:S(2)}) %collective-permute-start.17) | collective-permute-done | bytes 98336 | tf_op jit(solution)/shard_map/ppermute | solution.py:30
  99.0 1.8 %collective-permute-done.26 = bf16[32,1536]{1,0:T(8,128)(2,1)S(1)} collective-permute-done((bf16[32,1536]{1,0:T(8,128)(2,1)S(1)}, bf16[32,1536]{1,0:T(8,128)(2,1)S(1)}, u32[]{:S(2)}, u32[]{:S(2)}) %collective-permute-start.26) | collective-permute-done | bytes 98336 | tf_op jit(solution)/shard_map/ppermute | solution.py:30
  100.8 0.9 collective-permute-done.28
  101.9 1.3 %collective-permute-done.29 = bf16[2,16,1536]{2,1,0:T(8,128)(2,1)S(1)} collective-permute-done((bf16[2,16,1536]{2,1,0:T(8,128)(2,1)S(1)}, bf16[2,16,1536]{2,1,0:T(8,128)(2,1)S(1)}, u32[]{:S(2)}, u32[]{:S(2)}) %collective-permute-start.29) | collective-permute-done | bytes 98336 | tf_op jit(solution)/shard_map/ppermute | solution.py:30
  103.2 0.7 fusion
  (74 shorter events, 7.5 us)
Async XLA Ops:
  2.4 0.9 copy-start.1
  3.3 12.4 %slice-start.2 = ((s8[4239360]{0:T(1024)(128)(4,1)}), s8[45056]{0:T(1024)(128)(4,1)S(1)}, s32[]{:S(2)}) async-start(s8[4239360]{0:T(1024)(128)(4,1)} %bitcast.40), calls=%async_computation.2 | async-start | bytes 90112
  4.1 1.5 %collective-permute-start = (bf16[2,16,1536]{2,1,0:T(8,128)(2,1)S(1)}, bf16[2,16,1536]{2,1,0:T(8,128)(2,1)S(1)}, u32[]{:S(2)}, u32[]{:S(2)}) collective-permute-start(bf16[2,16,1536]{2,1,0:T(8,128)(2,1)S(1)} %get-tuple-element.49), channel_id=1, source_target_pairs={{0,1},{1,0},{2,3},{3,2},{4,5},{5,4},{6,7},{7,6},{8,9},{9,8},{10,11... | collective-permute-start | bytes 294920 | tf_op jit(solution)/shard_map/ppermute | solution.py:30
  5.6 9.3 %collective-permute-start.2 = (bf16[32,1536]{1,0:T(8,128)(2,1)S(1)}, bf16[32,1536]{1,0:T(8,128)(2,1)S(1)}, u32[]{:S(2)}, u32[]{:S(2)}) collective-permute-start(bf16[32,1536]{1,0:T(8,128)(2,1)S(1)} %pad_maximum_fusion.2._), channel_id=1, source_target_pairs={{0,16},{1,17},{2,18},{3,19},{4,20},{5,21},{6,22},{7,23},{8,24},{9,... | collective-permute-start | bytes 294920 | tf_op jit(solution)/shard_map/ppermute | solution.py:30
  9.7 6.0 %collective-permute-start.1 = (bf16[32,1536]{1,0:T(8,128)(2,1)S(1)}, bf16[32,1536]{1,0:T(8,128)(2,1)S(1)}, u32[]{:S(2)}, u32[]{:S(2)}) collective-permute-start(bf16[32,1536]{1,0:T(8,128)(2,1)S(1)} %pad_maximum_fusion.2._), channel_id=1, source_target_pairs={{0,8},{1,9},{2,10},{3,11},{4,12},{5,13},{6,14},{7,15},{8,0},{9,1},... | collective-permute-start | bytes 294920 | tf_op jit(solution)/shard_map/ppermute | solution.py:30
  11.2 2.2 %copy-start = (bf16[2880,720]{0,1:T(8,128)(2,1)S(1)}, bf16[2880,720]{0,1:T(8,128)(2,1)}, u32[]{:S(2)}) copy-start(bf16[2880,720]{0,1:T(8,128)(2,1)} %param.9) | copy-start | bytes 12441604
  13.4 2.2 %slice-start.3 = ((s8[4239360]{0:T(1024)(128)(4,1)}), s8[4194304]{0:T(1024)(128)(4,1)S(1)}, s32[]{:S(2)}) async-start(s8[4239360]{0:T(1024)(128)(4,1)} %bitcast.40), calls=%async_computation.3 | async-start | bytes 8388608
  15.0 4.6 %collective-permute-start.3 = (bf16[32,1536]{1,0:T(8,128)(2,1)S(1)}, bf16[32,1536]{1,0:T(8,128)(2,1)S(1)}, u32[]{:S(2)}, u32[]{:S(2)}) collective-permute-start(bf16[32,1536]{1,0:T(8,128)(2,1)S(1)} %collective-permute-done.2._), channel_id=1, source_target_pairs={{0,8},{1,9},{2,10},{3,11},{4,12},{5,13},{6,14},{7,15},{8,0},{9,1},... | collective-permute-start | bytes 294920 | tf_op jit(solution)/shard_map/ppermute | solution.py:30
  15.6 17.9 %slice-start = ((s8[4239360]{0:T(1024)(128)(4,1)}), s8[4194304]{0:T(1024)(128)(4,1)S(1)}, s32[]{:S(2)}) async-start(s8[4239360]{0:T(1024)(128)(4,1)} %bitcast.37), calls=%async_computation | async-start | bytes 8388608
  15.7 17.8 %slice-start.1 = ((s8[4239360]{0:T(1024)(128)(4,1)}), s8[45056]{0:T(1024)(128)(4,1)S(1)}, s32[]{:S(2)}) async-start(s8[4239360]{0:T(1024)(128)(4,1)} %bitcast.37), calls=%async_computation.1 | async-start | bytes 90112
  19.6 7.8 %collective-permute-start.4 = (bf16[128,1536]{1,0:T(8,128)(2,1)S(1)}, bf16[128,1536]{1,0:T(8,128)(2,1)S(1)}, u32[]{:S(2)}, u32[]{:S(2)}) collective-permute-start(bf16[128,1536]{1,0:T(8,128)(2,1)S(1)} %get-tuple-element.104), channel_id=1, source_target_pairs={{0,4},{1,3},{2,6},{3,1},{4,0},{5,7},{6,2},{7,5},{8,12},{9,11},{10,... | collective-permute-start | bytes 1179656 | tf_op jit(solution)/shard_map/ppermute | solution.py:30
  21.2 10.5 %collective-permute-start.5 = (bf16[32,1536]{1,0:T(8,128)(2,1)S(1)}, bf16[32,1536]{1,0:T(8,128)(2,1)S(1)}, u32[]{:S(2)}, u32[]{:S(2)}) collective-permute-start(bf16[32,1536]{1,0:T(8,128)(2,1)S(1)} %get-tuple-element.56), channel_id=1, source_target_pairs={{0,8},{1,9},{2,10},{3,11},{4,12},{5,13},{6,14},{7,15},{8,0},{9,1},... | collective-permute-start | bytes 294920 | tf_op jit(solution)/shard_map/ppermute | solution.py:30
  21.9 10.2 %collective-permute-start.6 = (bf16[32,1536]{1,0:T(8,128)(2,1)S(1)}, bf16[32,1536]{1,0:T(8,128)(2,1)S(1)}, u32[]{:S(2)}, u32[]{:S(2)}) collective-permute-start(bf16[32,1536]{1,0:T(8,128)(2,1)S(1)} %get-tuple-element.56), channel_id=1, source_target_pairs={{0,16},{1,17},{2,18},{3,19},{4,20},{5,21},{6,22},{7,23},{8,24},{9,... | collective-permute-start | bytes 294920 | tf_op jit(solution)/shard_map/ppermute | solution.py:30
  25.3 6.9 %collective-permute-start.7 = (bf16[32,1536]{1,0:T(8,128)(2,1)S(1)}, bf16[32,1536]{1,0:T(8,128)(2,1)S(1)}, u32[]{:S(2)}, u32[]{:S(2)}) collective-permute-start(bf16[32,1536]{1,0:T(8,128)(2,1)S(1)} %get-tuple-element.56), channel_id=1, source_target_pairs={{0,24},{1,25},{2,26},{3,27},{4,28},{5,29},{6,30},{7,31},{8,16},{9,... | collective-permute-start | bytes 294920 | tf_op jit(solution)/shard_map/ppermute | solution.py:30
  28.8 14.2 %collective-permute-start.9 = (bf16[192,1536]{1,0:T(8,128)(2,1)S(1)}, bf16[192,1536]{1,0:T(8,128)(2,1)S(1)}, u32[]{:S(2)}, u32[]{:S(2)}) collective-permute-start(bf16[192,1536]{1,0:T(8,128)(2,1)S(1)} %shard_map.76), channel_id=1, source_target_pairs={{0,2},{1,5},{2,0},{3,7},{4,6},{5,1},{6,4},{7,3},{8,10},{9,13},{10,... | collective-permute-start | bytes 1769480 | tf_op jit(solution)/shard_map/ppermute | solution.py:30
  32.2 7.8 %collective-permute-start.8 = (bf16[128,1536]{1,0:T(8,128)(2,1)S(1)}, bf16[128,1536]{1,0:T(8,128)(2,1)S(1)}, u32[]{:S(2)}, u32[]{:S(2)}) collective-permute-start(bf16[128,1536]{1,0:T(8,128)(2,1)S(1)} %constant_dynamic-update-slice_fusion.5.near_ref), channel_id=1, source_target_pairs={{0,4},{1,3},{2,6},{3,1},{4,0},{5,7},{6,2},{7,5},{8,12},{9,11},{10,... | collective-permute-start | bytes 1179656 | tf_op jit(solution)/shard_map/ppermute | solution.py:30
  33.5 10.2 %collective-permute-start.11 = (bf16[192,1536]{1,0:T(8,128)(2,1)S(1)}, bf16[192,1536]{1,0:T(8,128)(2,1)S(1)}, u32[]{:S(2)}, u32[]{:S(2)}) collective-permute-start(bf16[192,1536]{1,0:T(8,128)(2,1)S(1)} %get-tuple-element.61._.mine_near_ref), channel_id=1, source_target_pairs={{0,1},{1,0},{2,3},{3,2},{4,5},{5,4},{6,7},{7,6},{8,9},{9,8},{10,11... | collective-permute-start | bytes 1769480 | tf_op jit(solution)/shard_map/ppermute | solution.py:30
  43.0 2.0 %collective-permute-start.12 = (bf16[192,1536]{1,0:T(8,128)(2,1)S(1)}, bf16[192,1536]{1,0:T(8,128)(2,1)S(1)}, u32[]{:S(2)}, u32[]{:S(2)}) collective-permute-start(bf16[192,1536]{1,0:T(8,128)(2,1)S(1)} %collective-permute-done.9.mine_far_ref), channel_id=1, source_target_pairs={{0,1},{1,0},{2,3},{3,2},{4,5},{5,4},{6,7},{7,6},{8,9},{9,8},{10,11... | collective-permute-start | bytes 1769480 | tf_op jit(solution)/shard_map/ppermute | solution.py:30
  43.0 9.9 %collective-permute-start.10 = (bf16[192,1536]{1,0:T(8,128)(2,1)S(1)}, bf16[192,1536]{1,0:T(8,128)(2,1)S(1)}, u32[]{:S(2)}, u32[]{:S(2)}) collective-permute-start(bf16[192,1536]{1,0:T(8,128)(2,1)S(1)} %get-tuple-element.64), channel_id=1, source_target_pairs={{0,2},{1,5},{2,0},{3,7},{4,6},{5,1},{6,4},{7,3},{8,10},{9,13},{10,... | collective-permute-start | bytes 1769480 | tf_op jit(solution)/shard_map/ppermute | solution.py:30
  52.9 2.0 %collective-permute-start.14 = (bf16[192,1536]{1,0:T(8,128)(2,1)S(1)}, bf16[192,1536]{1,0:T(8,128)(2,1)S(1)}, u32[]{:S(2)}, u32[]{:S(2)}) collective-permute-start(bf16[192,1536]{1,0:T(8,128)(2,1)S(1)} %get-tuple-element.76), channel_id=1, source_target_pairs={{0,1},{1,0},{2,3},{3,2},{4,5},{5,4},{6,7},{7,6},{8,9},{9,8},{10,11... | collective-permute-start | bytes 1769480 | tf_op jit(solution)/shard_map/ppermute | solution.py:30
  52.9 2.9 %collective-permute-start.18 = (bf16[192,1536]{1,0:T(8,128)(2,1)S(1)}, bf16[192,1536]{1,0:T(8,128)(2,1)S(1)}, u32[]{:S(2)}, u32[]{:S(2)}) collective-permute-start(bf16[192,1536]{1,0:T(8,128)(2,1)S(1)} %get-tuple-element.81.mine_near_ref), channel_id=1, source_target_pairs={{0,1},{1,0},{2,3},{3,2},{4,5},{5,4},{6,7},{7,6},{8,9},{9,8},{10,11... | collective-permute-start | bytes 1769480 | tf_op jit(solution)/shard_map/ppermute | solution.py:30
  53.4 3.2 %collective-permute-start.19 = (bf16[192,1536]{1,0:T(8,128)(2,1)S(1)}, bf16[192,1536]{1,0:T(8,128)(2,1)S(1)}, u32[]{:S(2)}, u32[]{:S(2)}) collective-permute-start(bf16[192,1536]{1,0:T(8,128)(2,1)S(1)} %collective-permute-done.10.mine_far_ref), channel_id=1, source_target_pairs={{0,1},{1,0},{2,3},{3,2},{4,5},{5,4},{6,7},{7,6},{8,9},{9,8},{10,11... | collective-permute-start | bytes 1769480 | tf_op jit(solution)/shard_map/ppermute | solution.py:30
  53.4 10.9 %collective-permute-start.13 = (bf16[192,1536]{1,0:T(8,128)(2,1)S(1)}, bf16[192,1536]{1,0:T(8,128)(2,1)S(1)}, u32[]{:S(2)}, u32[]{:S(2)}) collective-permute-start(bf16[192,1536]{1,0:T(8,128)(2,1)S(1)} %get-tuple-element.74), channel_id=1, source_target_pairs={{0,1},{1,0},{2,3},{3,2},{4,5},{5,4},{6,7},{7,6},{8,9},{9,8},{10,11... | collective-permute-start | bytes 1769480 | tf_op jit(solution)/shard_map/ppermute | solution.py:30
  55.0 9.9 %collective-permute-start.15 = (bf16[192,1536]{1,0:T(8,128)(2,1)S(1)}, bf16[192,1536]{1,0:T(8,128)(2,1)S(1)}, u32[]{:S(2)}, u32[]{:S(2)}) collective-permute-start(bf16[192,1536]{1,0:T(8,128)(2,1)S(1)} %add_convert_fusion.1), channel_id=1, source_target_pairs={{0,2},{1,5},{2,0},{3,7},{4,6},{5,1},{6,4},{7,3},{8,10},{9,13},{10,... | collective-permute-start | bytes 1769480 | tf_op jit(solution)/shard_map/ppermute | solution.py:30
  63.6 4.1 %collective-permute-start.21 = (bf16[192,1536]{1,0:T(8,128)(2,1)S(1)}, bf16[192,1536]{1,0:T(8,128)(2,1)S(1)}, u32[]{:S(2)}, u32[]{:S(2)}) collective-permute-start(bf16[192,1536]{1,0:T(8,128)(2,1)S(1)} %get-tuple-element.86), channel_id=1, source_target_pairs={{0,1},{1,0},{2,3},{3,2},{4,5},{5,4},{6,7},{7,6},{8,9},{9,8},{10,11... | collective-permute-start | bytes 1769480 | tf_op jit(solution)/shard_map/ppermute | solution.py:30
  64.2 16.2 %collective-permute-start.20 = (bf16[192,1536]{1,0:T(8,128)(2,1)S(1)}, bf16[192,1536]{1,0:T(8,128)(2,1)S(1)}, u32[]{:S(2)}, u32[]{:S(2)}) collective-permute-start(bf16[192,1536]{1,0:T(8,128)(2,1)S(1)} %get-tuple-element.84), channel_id=1, source_target_pairs={{0,1},{1,0},{2,3},{3,2},{4,5},{5,4},{6,7},{7,6},{8,9},{9,8},{10,11... | collective-permute-start | bytes 1769480 | tf_op jit(solution)/shard_map/ppermute | solution.py:30
  65.6 12.1 %collective-permute-start.16 = (bf16[128,1536]{1,0:T(8,128)(2,1)S(1)}, bf16[128,1536]{1,0:T(8,128)(2,1)S(1)}, u32[]{:S(2)}, u32[]{:S(2)}) collective-permute-start(bf16[128,1536]{1,0:T(8,128)(2,1)S(1)} %get-tuple-element.78), channel_id=1, source_target_pairs={{0,4},{1,3},{2,6},{3,1},{4,0},{5,7},{6,2},{7,5},{8,12},{9,11},{10,... | collective-permute-start | bytes 1179656 | tf_op jit(solution)/shard_map/ppermute | solution.py:30
  67.9 12.4 %collective-permute-start.22 = (bf16[192,1536]{1,0:T(8,128)(2,1)S(1)}, bf16[192,1536]{1,0:T(8,128)(2,1)S(1)}, u32[]{:S(2)}, u32[]{:S(2)}) collective-permute-start(bf16[192,1536]{1,0:T(8,128)(2,1)S(1)} %add_convert_fusion), channel_id=1, source_target_pairs={{0,2},{1,5},{2,0},{3,7},{4,6},{5,1},{6,4},{7,3},{8,10},{9,13},{10,... | collective-permute-start | bytes 1769480 | tf_op jit(solution)/shard_map/ppermute | solution.py:30
  77.8 5.1 %collective-permute-start.24 = (bf16[32,1536]{1,0:T(8,128)(2,1)S(1)}, bf16[32,1536]{1,0:T(8,128)(2,1)S(1)}, u32[]{:S(2)}, u32[]{:S(2)}) collective-permute-start(bf16[32,1536]{1,0:T(8,128)(2,1)S(1)} %get-tuple-element.98), channel_id=1, source_target_pairs={{0,8},{1,9},{2,10},{3,11},{4,12},{5,13},{6,14},{7,15},{8,0},{9,1},... | collective-permute-start | bytes 294920 | tf_op jit(solution)/shard_map/ppermute | solution.py:30
  81.0 7.8 %collective-permute-start.23 = (bf16[128,1536]{1,0:T(8,128)(2,1)S(1)}, bf16[128,1536]{1,0:T(8,128)(2,1)S(1)}, u32[]{:S(2)}, u32[]{:S(2)}) collective-permute-start(bf16[128,1536]{1,0:T(8,128)(2,1)S(1)} %get-tuple-element.88), channel_id=1, source_target_pairs={{0,4},{1,3},{2,6},{3,1},{4,0},{5,7},{6,2},{7,5},{8,12},{9,11},{10,... | collective-permute-start | bytes 1179656 | tf_op jit(solution)/shard_map/ppermute | solution.py:30
  89.0 6.1 %collective-permute-start.27 = (bf16[32,1536]{1,0:T(8,128)(2,1)S(1)}, bf16[32,1536]{1,0:T(8,128)(2,1)S(1)}, u32[]{:S(2)}, u32[]{:S(2)}) collective-permute-start(bf16[32,1536]{1,0:T(8,128)(2,1)S(1)} %get-tuple-element.100), channel_id=1, source_target_pairs={{0,8},{1,9},{2,10},{3,11},{4,12},{5,13},{6,14},{7,15},{8,0},{9,1},... | collective-permute-start | bytes 294920 | tf_op jit(solution)/shard_map/ppermute | solution.py:30
  89.5 9.5 %collective-permute-start.17 = (bf16[32,1536]{1,0:T(8,128)(2,1)S(1)}, bf16[32,1536]{1,0:T(8,128)(2,1)S(1)}, u32[]{:S(2)}, u32[]{:S(2)}) collective-permute-start(bf16[32,1536]{1,0:T(8,128)(2,1)S(1)} %get-tuple-element.97), channel_id=1, source_target_pairs={{0,8},{1,9},{2,10},{3,11},{4,12},{5,13},{6,14},{7,15},{8,0},{9,1},... | collective-permute-start | bytes 294920 | tf_op jit(solution)/shard_map/ppermute | solution.py:30
  91.1 7.9 %collective-permute-start.25 = (bf16[32,1536]{1,0:T(8,128)(2,1)S(1)}, bf16[32,1536]{1,0:T(8,128)(2,1)S(1)}, u32[]{:S(2)}, u32[]{:S(2)}) collective-permute-start(bf16[32,1536]{1,0:T(8,128)(2,1)S(1)} %fusion.2), channel_id=1, source_target_pairs={{0,16},{1,17},{2,18},{3,19},{4,20},{5,21},{6,22},{7,23},{8,24},{9,... | collective-permute-start | bytes 294920 | tf_op jit(solution)/shard_map/ppermute | solution.py:30
  92.9 7.9 %collective-permute-start.26 = (bf16[32,1536]{1,0:T(8,128)(2,1)S(1)}, bf16[32,1536]{1,0:T(8,128)(2,1)S(1)}, u32[]{:S(2)}, u32[]{:S(2)}) collective-permute-start(bf16[32,1536]{1,0:T(8,128)(2,1)S(1)} %get-tuple-element.99), channel_id=1, source_target_pairs={{0,8},{1,9},{2,10},{3,11},{4,12},{5,13},{6,14},{7,15},{8,0},{9,1},... | collective-permute-start | bytes 294920 | tf_op jit(solution)/shard_map/ppermute | solution.py:30
  95.1 6.5 %collective-permute-start.28 = (bf16[32,1536]{1,0:T(8,128)(2,1)S(1)}, bf16[32,1536]{1,0:T(8,128)(2,1)S(1)}, u32[]{:S(2)}, u32[]{:S(2)}) collective-permute-start(bf16[32,1536]{1,0:T(8,128)(2,1)S(1)} %fusion.5), channel_id=1, source_target_pairs={{0,16},{1,17},{2,18},{3,19},{4,20},{5,21},{6,22},{7,23},{8,24},{9,... | collective-permute-start | bytes 294920 | tf_op jit(solution)/shard_map/ppermute | solution.py:30
  101.7 1.5 %copy-start.2 = (bf16[2,16,2880]{2,1,0:T(8,128)(2,1)S(1)}, bf16[2,16,2880]{2,1,0:T(8,128)(2,1)}, u32[]{:S(2)}) copy-start(bf16[2,16,2880]{2,1,0:T(8,128)(2,1)} %hidden_ref.1) | copy-start | bytes 552964
  101.7 1.4 %collective-permute-start.29 = (bf16[2,16,1536]{2,1,0:T(8,128)(2,1)S(1)}, bf16[2,16,1536]{2,1,0:T(8,128)(2,1)S(1)}, u32[]{:S(2)}, u32[]{:S(2)}) collective-permute-start(bf16[2,16,1536]{2,1,0:T(8,128)(2,1)S(1)} %select_convert_fusion), channel_id=1, source_target_pairs={{0,1},{1,0},{2,3},{3,2},{4,5},{5,4},{6,7},{7,6},{8,9},{9,8},{10,11... | collective-permute-start | bytes 294920 | tf_op jit(solution)/shard_map/ppermute | solution.py:30

commit v6 on v5

--- a/solution.py
+++ b/solution.py
@@ -53,9 +53,9 @@
 SCALARS = pl.BlockSpec(memory_space=pltpu.SMEM)
 
 
-def slots_of(tokens, capacity, base, places_ref, rows_ref):
-    total, held = rows_ref.shape
-    tile = rows_ref[:, held - LANES :].astype(jnp.float32)
+def slots_of(tokens, capacity, base, places_ref, tile):
+    total = tile.shape[0]
+    tile = tile.astype(jnp.float32)
     lane = lax.broadcasted_iota(jnp.int32, (total, LANES), 1)
     row = lax.broadcasted_iota(jnp.int32, (total, LANES), 0)
     listed = (lane >= LANES - ROUTING) & (lane < LANES - ROUTING // 2)
@@ -72,12 +72,12 @@
     return jnp.where(marks > 0.0, ahead + (base + row // tokens * capacity).astype(jnp.float32), -1.0)
 
 
-def select_body(tokens, capacity, wanted, places_ref, near_ref, next_ref, *out_refs):
-    rows = near_ref.shape[0]
+def select_body(tokens, capacity, wanted, places_ref, tile_ref, _, near_ref, next_ref, *out_refs):
+    rows, held = near_ref.shape
     compact = out_refs[0].shape[0]
     slots = [
-        slots_of(tokens, capacity, part * (rows // tokens * capacity), places_ref, ref)
-        for part, ref in enumerate((near_ref, next_ref))
+        slots_of(tokens, capacity, part * (rows // tokens * capacity), places_ref, tile)
+        for part, tile in enumerate((tile_ref[...], next_ref[:, held - LANES :]))
     ]
     for part, slots_ref in enumerate(out_refs[len(wanted) :]):
         slots_ref[...] = slots[part]
@@ -91,22 +91,24 @@
         rows_ref[...] = result.astype(jnp.bfloat16)
 
 
-def select(tokens, capacity, wanted, places, near, following):
-    located = 2 * int(0 in wanted)
+def select(tokens, capacity, wanted, places, near, following, tile=None, token=None):
+    tile = near[:, near.shape[1] - LANES :] if tile is None else tile
+    token = places if token is None else token
+    located = 1 + int(0 in wanted)
     rows, held = near.shape
     compact = 2 * rows // tokens * capacity
     block = jax.ShapeDtypeStruct((compact, held), jnp.bfloat16)
     return pl.pallas_call(
         functools.partial(select_body, tokens, capacity, wanted),
         out_shape=[block] * len(wanted) + [jax.ShapeDtypeStruct((rows, LANES), jnp.float32)] * located,
-        in_specs=[SCALARS] + whole_arrays(2),
+        in_specs=[SCALARS] + whole_arrays(1) + [pl.BlockSpec(memory_space=pl.ANY)] + whole_arrays(2),
         out_specs=whole_arrays(len(wanted) + located),
         compiler_params=pltpu.CompilerParams(vmem_limit_bytes=20 * 2**20),
         cost_estimate=pl.CostEstimate(flops=8 * rows * compact * held, bytes_accessed=8 * rows * held, transcendentals=0),
-    )(places, near, following)
-
-
-def merge_body(wanted, near_slots_ref, next_slots_ref, keep_ref, taken_ref, arrived_ref, *out_refs):
+    )(places, tile, token, near, following)
+
+
+def merge_body(wanted, _, near_slots_ref, next_slots_ref, keep_ref, taken_ref, arrived_ref, *out_refs):
     rows = out_refs[0].shape[0]
     compact = keep_ref.shape[0]
     column = lax.broadcasted_iota(jnp.int32, (rows, compact), 1).astype(jnp.float32)
@@ -120,17 +122,18 @@
         out_ref[...] = result.astype(out_ref.dtype)
 
 
-def merge(wanted, types, slots, keep, taken, arrived):
+def merge(wanted, types, slots, keep, taken, arrived, token=None):
+    token = slots[0] if token is None else token
     rows = slots[0].shape[0]
     compact, held = keep.shape
     return pl.pallas_call(
         functools.partial(merge_body, wanted),
         out_shape=[jax.ShapeDtypeStruct((rows, held), kind) for kind in types],
-        in_specs=whole_arrays(5),
+        in_specs=[pl.BlockSpec(memory_space=pl.ANY)] + whole_arrays(5),
         out_specs=whole_arrays(len(types)),
         compiler_params=pltpu.CompilerParams(vmem_limit_bytes=20 * 2**20),
         cost_estimate=pl.CostEstimate(flops=8 * rows * compact * held, bytes_accessed=8 * rows * held, transcendentals=0),
-    )(*slots, keep, taken, arrived)
+    )(token, *slots, keep, taken, arrived)
 
 
 def ffn_body(
@@ -364,95 +367,128 @@
     chosen = tokens, capacity
     states = []
 
+    side = 2 * tokens
+
     def second_hop(state, apart):
         near, following = state["near"], state["next"]
         if apart:
-            (send,) = select(*chosen, (1,), places, near, following)
+            send, state["places"] = select(*chosen, (1,), places, near, following)
         else:
             send, state["own"], *state["slots"] = select(*chosen, (1, 0), places, near, following)
         if len(states) > 1:
             send, states[-2]["arrived"] = tied(send, states[-2]["arrived"])
         state["arrived"] = moved(send, second_axis)
         if apart:
-            following, _ = tied(following, send)
-            state["own"], *state["slots"] = select(*chosen, (0,), places, near, following)
+            tile = state["twin"]
+            state["own"], near_slots, next_slots = select(*chosen, (0,), places, near, following, tile, send)
+            state["slots"] = state["places"], next_slots
+
+    def staged(block, load):
+        crossed, beside = moved(block, far(2)), moved(block, far(1))
+        crossed, first_loaded = tied(crossed, load(0, block))
+        passed = moved(crossed, far(1))
+        passed, second_loaded = tied(passed, load(1, crossed))
+        return [beside, crossed, passed], first_loaded, second_loaded
 
     pair = pairs[0]
-    (gate_v,) = preload(pair, w_gate.T)
+    asides = [moved(other, first_axis) for other in pairs[1:]]
+    weights_t = w_gate.T, w_up.T
     if distant == 4:
-        crossed, beside = moved(pair, far(2)), moved(pair, far(1))
-        crossed, gate_v = tied(crossed, gate_v)
-        (up_v,) = preload(crossed, w_up.T)
-        passed = moved(crossed, far(1))
-        passed, up_v = tied(passed, up_v)
-        blocks = [beside, crossed, passed]
+        blocks, gate_v, up_v = staged(pair, lambda index, token: preload(token, weights_t[index])[0])
     else:
-        (up_v,) = preload(pair, w_up.T)
         blocks = far_blocks(pair)
+        gate_v, up_v = preload(pair, *weights_t)
+    blocks[0], *asides = tied(blocks[0], *asides)
     column = join(pair, *blocks)
     states.append({"near": column, "next": moved(column, first_axis)})
     down_v = None
-    for pair in pairs[1:]:
+    for pair, aside in zip(pairs[1:], asides):
         last = states[-1]
-        pair, last["near"] = tied(pair, last["near"])
-        blocks = far_blocks(pair)
-        second_hop(last, True)
-        *blocks, last["own"] = tied(*blocks, last["own"])
-        column = join(pair, *blocks)
-        following = moved(column, first_axis)
+        both, last["twin"] = tied(join(pair, aside), moved(last["near"][:, held - LANES :], other_core))
+        if distant == 4:
+            crossed, beside = moved(both, far(2)), moved(both, far(1))
+            second_hop(last, True)
+            crossed, beside, last["own"] = tied(crossed, beside, last["own"])
+            blocks = [beside, crossed, moved(crossed, far(1))]
+        else:
+            blocks = far_blocks(both)
+            second_hop(last, True)
         if down_v is None:
             (down_v,) = preload(last["own"], w_down)
-            following, down_v = tied(following, down_v)
-        states.append({"near": column, "next": following})
+            blocks[-1], down_v = tied(blocks[-1], down_v)
+        blocks = [both] + blocks
+        states.append(
+            {"near": join(*[block[:side] for block in blocks]), "next": join(*[block[side:] for block in blocks])}
+        )
     second_hop(states[-1], False)
     if down_v is None:
         (down_v,) = preload(states[-1]["own"], w_down)
 
-    hops = []
-    before = None
-    for state in states:
-        own, arrived = state["own"], state["arrived"]
-        if before is not None:
-            arrived, *before = tied(arrived, *before)
-            hops.append(before)
-        before = ffn(places, own, arrived, moved(own, other_core), moved(arrived, other_core), gate_v, up_v, down_v)
-    hops.append(before)
-
     def rounded_sum(a, b):
         return (a + b.astype(jnp.float32)).astype(jnp.bfloat16)
 
-    def far_total(block, earlier):
+    hops = []
+    for b, state in enumerate(states):
+        own, arrived = state["own"], state["arrived"]
+        other_far = moved(arrived, other_core)
+        if b:
+            other_far, hops[-1]["give"] = tied(other_far, hops[-1]["give"])
+        keep_near, keep_far, send_near, send_far = ffn(
+            places, own, arrived, moved(own, other_core), other_far, gate_v, up_v, down_v
+        )
+        if b + 1 < micro_count:
+            send_far, states[b + 1]["arrived"] = tied(send_far, states[b + 1]["arrived"])
+        if b:
+            send_far, hops[-1]["arrived"] = tied(send_far, hops[-1]["arrived"])
+        give = rounded_sum(keep_far, moved(send_far, other_core))
+        hops.append(
+            {"keep": keep_near, "taken": moved(send_near, other_core), "give": give, "arrived": moved(give, second_axis)}
+        )
+    for b in range(1, micro_count):
+        hops[b - 1]["taken"], hops[b]["give"] = tied(hops[b - 1]["taken"], hops[b]["give"])
+
+    def far_hop(block):
         block = block.reshape(distant, -1, held)
         if distant == 4:
-            if earlier:
-                block, earlier[-1]["crossing"] = tied(block, earlier[-1]["crossing"])
             through = moved(block[3].astype(jnp.bfloat16), far(1))
             beside = moved(block[1].astype(jnp.bfloat16), far(1))
-            return {"kept": block[0], "arrivals": [beside], "crossing": rounded_sum(block[2], through)}
-        return {
-            "kept": block[0],
-            "arrivals": [moved(block[j].astype(jnp.bfloat16), far(j)) for j in range(1, distant)],
-            "crossing": None,
-        }
-
-    def settled(total):
-        kept, arrivals = total["kept"], list(total["arrivals"])
-        if total["crossing"] is not None:
-            arrivals.append(moved(total["crossing"], far(2)))
+            return block[0], [beside], rounded_sum(block[2], through)
+        return block[0], [moved(block[j].astype(jnp.bfloat16), far(j)) for j in range(1, distant)], None
+
+    def crossing(total):
+        kept, arrivals, cross = total
+        return kept, arrivals + ([] if cross is None else [moved(cross, far(2))])
+
+    def settled(kept, arrivals):
         for arrival in arrivals:
             kept = kept + arrival.astype(jnp.float32)
         return kept
 
     sums = []
-    for state, (keep_near, keep_far, send_near, send_far) in zip(states, hops):
-        give = rounded_sum(keep_far, moved(send_far, other_core))
-        near, following = merge(
-            (0, 1), (jnp.float32, jnp.bfloat16), state["slots"], keep_near, moved(send_near, other_core),
-            moved(give, second_axis),
-        )
+    waiting = None
+    for b, (state, hop) in enumerate(zip(states, hops)):
+        final = b == micro_count - 1
+        parts = state["slots"], hop["keep"], hop["taken"], hop["arrived"]
+        if not final:
+            near, following = merge((0, 1), (jnp.float32, jnp.float32), *parts)
+            both = jnp.concatenate([near.reshape(distant, side, held), following.reshape(distant, side, held)], axis=1)
+            total = far_hop(both)
+            if total[2] is not None and b + 1 < micro_count:
+                cross, hops[b + 1]["arrived"] = tied(total[2], hops[b + 1]["arrived"])
+                total = total[0], total[1], cross
+            waiting = crossing(total)
+            continue
+        (following,) = merge((1,), (jnp.bfloat16,), *parts)
+        (near,) = merge((0,), (jnp.float32,), *parts, following)
+        if waiting is not None:
+            *earlier, near = tied(*waiting[1], near)
         near = near + moved(following, first_axis).astype(jnp.float32)
-        sums.append(far_total(near, sums))
-    sums = jnp.stack([settled(total) for total in sums])
+        kept, arrivals = crossing(far_hop(near))
+        if waiting is not None:
+            before = settled(waiting[0], earlier)
+            sums.append(before[:side] + moved(before[side:].astype(jnp.bfloat16), first_axis).astype(jnp.float32))
+        sums.append(settled(kept, arrivals))
+    sums = jnp.stack(sums)
     own = jnp.where(lower, sums[:, :tokens], sums[:, tokens:])
     give = jnp.where(lower, sums[:, tokens:], sums[:, :tokens]).astype(jnp.bfloat16)
     taken = moved(give, other_core).astype(jnp.float32)

time: 104 us -> 108 us (1.038)
  waiting for transfers between devices: 42.7 us -> 50.4 us
  starting transfers between devices: 32.3 us -> 27.6 us
    ppermute x30 -> x31, waiting for transfers between devices: 42.7 us -> 50.4 us  [moved(): return lax.ppermute(block, 'req', [(i, partner(i)) for i in range(count)])]
    ppermute x30 -> x31, starting transfers between devices: 32.3 us -> 27.6 us  [moved(): return lax.ppermute(block, 'req', [(i, partner(i)) for i in range(count)])]
    unnamed x19 -> x16, local copies, waits for them, and re-layouts: 3.19 us -> 3.17 us
  transfers between devices with their start and end apart: 30 -> 31, of which waited for: 20 -> 21; matrix products, arithmetic and copies ran while one was open for 1% -> 1% of each run, Pallas kernels for 20% -> 19%
where the time goes in v6:
time: 108 us
  waiting for transfers between devices  50.4 us (47%)
  starting transfers between devices  27.6 us (26%)
  Pallas kernels  21.8 us (20%)
  local copies, waits for them, and re-layouts  4.16 us (4%)
  other arithmetic  3.08 us (3%)
    ppermute x31, waiting for transfers between devices, moved(): return lax.ppermute(block, 'req', [(i, partner(i)) for i in range(count)])  50.4 us
    ppermute x31, starting transfers between devices, moved(): return lax.ppermute(block, 'req', [(i, partner(i)) for i in range(count)])  27.6 us
    pallas_call x2, Pallas kernels, ffn(): pl.pallas_call(ffn_body, out_shape=[jax.ShapeDtypeStruct((pair, held), jn...  14 us
    pallas_call x3, Pallas kernels, select(): pl.pallas_call(functools.partial(select_body, tokens, capacity, wanted),...  4.45 us
    unnamed x16, local copies, waits for them, and re-layouts  3.17 us
  transfers between devices with their start and end apart: 31, of which 21 were waited for; matrix products, arithmetic and copies ran while one was open for 1% of the time, Pallas kernels for 19%

profile of v6, /device:TPU:0, one launch (start us, length us, event | category | flops | bytes accessed | tf_op | source)
XLA Modules:
  0.0 107.5 jit_solution(888561040079443300)
XLA Ops:
  0.0 0.8 reshape.33
  0.8 0.7 convert_bitcast_fusion
  1.5 0.7 pad_convert_fusion
  2.4 0.9 copy-done.1
  3.3 0.8 shard_map.73
  4.6 0.9 collective-permute-done
  5.6 2.9 %collective-permute-start.2 = (bf16[32,1536]{1,0:T(8,128)(2,1)S(1)}, bf16[32,1536]{1,0:T(8,128)(2,1)S(1)}, u32[]{:S(2)}, u32[]{:S(2)}) collective-permute-start(bf16[32,1536]{1,0:T(8,128)(2,1)S(1)} %pad_maximum_fusion.6), channel_id=1, source_target_pairs={{0,4},{1,3},{2,6},{3,1},{4,0},{5,7},{6,2},{7,5},{8,12},{9,11},{10,... | collective-permute-start | bytes 294920 | tf_op jit(solution)/shard_map/ppermute | solution.py:30
  8.6 1.6 %collective-permute-start.1 = (bf16[32,1536]{1,0:T(8,128)(2,1)S(1)}, bf16[32,1536]{1,0:T(8,128)(2,1)S(1)}, u32[]{:S(2)}, u32[]{:S(2)}) collective-permute-start(bf16[32,1536]{1,0:T(8,128)(2,1)S(1)} %pad_maximum_fusion.5._), channel_id=1, source_target_pairs={{0,8},{1,9},{2,10},{3,11},{4,12},{5,13},{6,14},{7,15},{8,0},{9,1},... | collective-permute-start | bytes 294920 | tf_op jit(solution)/shard_map/ppermute | solution.py:30
  10.3 2.6 %collective-permute-start.3 = (bf16[32,1536]{1,0:T(8,128)(2,1)S(1)}, bf16[32,1536]{1,0:T(8,128)(2,1)S(1)}, u32[]{:S(2)}, u32[]{:S(2)}) collective-permute-start(bf16[32,1536]{1,0:T(8,128)(2,1)S(1)} %pad_maximum_fusion.5._), channel_id=1, source_target_pairs={{0,16},{1,17},{2,18},{3,19},{4,20},{5,21},{6,22},{7,23},{8,24},{9,... | collective-permute-start | bytes 294920 | tf_op jit(solution)/shard_map/ppermute | solution.py:30
  12.9 2.2 %copy-done = bf16[2880,720]{0,1:T(8,128)(2,1)S(1)} copy-done((bf16[2880,720]{0,1:T(8,128)(2,1)S(1)}, bf16[2880,720]{0,1:T(8,128)(2,1)}, u32[]{:S(2)}) %copy-start) | copy-done | bytes 4147224
  15.4 2.2 %collective-permute-done.3._ = bf16[32,1536]{1,0:T(8,128)(2,1)S(1)} collective-permute-done((bf16[32,1536]{1,0:T(8,128)(2,1)S(1)}, bf16[32,1536]{1,0:T(8,128)(2,1)S(1)}, u32[]{:S(2)}, u32[]{:S(2)}) %collective-permute-start.3) | collective-permute-done | bytes 98336 | tf_op jit(solution)/shard_map/ppermute | solution.py:30
  18.4 3.8 %collective-permute-done.4 = bf16[32,1536]{1,0:T(8,128)(2,1)S(1)} collective-permute-done((bf16[32,1536]{1,0:T(8,128)(2,1)S(1)}, bf16[32,1536]{1,0:T(8,128)(2,1)S(1)}, u32[]{:S(2)}, u32[]{:S(2)}) %collective-permute-start.4) | collective-permute-done | bytes 98336 | tf_op jit(solution)/shard_map/ppermute | solution.py:30
  22.3 1.5 %collective-permute-start.5 = (bf16[128,1536]{1,0:T(8,128)(2,1)S(1)}, bf16[128,1536]{1,0:T(8,128)(2,1)S(1)}, u32[]{:S(2)}, u32[]{:S(2)}) collective-permute-start(bf16[128,1536]{1,0:T(8,128)(2,1)S(1)} %constant_dynamic-update-slice_fusion.near_ref), channel_id=1, source_target_pairs={{0,4},{1,3},{2,6},{3,1},{4,0},{5,7},{6,2},{7,5},{8,12},{9,11},{10,... | collective-permute-start | bytes 1179656 | tf_op jit(solution)/shard_map/ppermute | solution.py:30
  24.4 2.6 %collective-permute-start.7 = (bf16[64,1536]{1,0:T(8,128)(2,1)S(1)}, bf16[64,1536]{1,0:T(8,128)(2,1)S(1)}, u32[]{:S(2)}, u32[]{:S(2)}) collective-permute-start(bf16[64,1536]{1,0:T(8,128)(2,1)S(1)} %pad_maximum_fusion.4), channel_id=1, source_target_pairs={{0,16},{1,17},{2,18},{3,19},{4,20},{5,21},{6,22},{7,23},{8,24},{9,... | collective-permute-start | bytes 589832 | tf_op jit(solution)/shard_map/ppermute | solution.py:30
  27.0 3.2 %collective-permute-done.5.next_ref = bf16[128,1536]{1,0:T(8,128)(2,1)S(1)} collective-permute-done((bf16[128,1536]{1,0:T(8,128)(2,1)S(1)}, bf16[128,1536]{1,0:T(8,128)(2,1)S(1)}, u32[]{:S(2)}, u32[]{:S(2)}) %collective-permute-start.5) | collective-permute-done | bytes 393248 | tf_op jit(solution)/shard_map/ppermute | solution.py:30
  30.2 1.3 %shard_map.76 = (bf16[192,1536]{1,0:T(8,128)(2,1)S(1)}, f32[128,128]{1,0:T(8,128)S(1)}) custom-call(s32[3]{0:T(128)S(1)} %pad_add_fusion.places_ref._, bf16[128,128]{1,0:T(8,128)(2,1)S(1)} %slice.130.tile_ref, s32[3]{0:T(128)S(1)} %pad_add_fusion.places_ref._, bf16[128,1536]{1,0:T(8,128)(2,1)S(1)} %constant_dynamic-update-slice_fusion.near_ref, ...), custom_call_target="tpu_custom_call" | custom-call | flops 301989888 | bytes 1572864 | tf_op jit(solution)/shard_map/pallas_call | solution.py:101
  31.5 0.8 collective-permute-start.10
  32.3 1.5 %shard_map.77 = (bf16[192,1536]{1,0:T(8,128)(2,1)S(1)}, f32[128,128]{1,0:T(8,128)}, f32[128,128]{1,0:T(8,128)S(1)}) custom-call(s32[3]{0:T(128)S(1)} %pad_add_fusion.places_ref._, bf16[128,128]{1,0:T(8,128)(2,1)S(1)} %collective-permute-done.6.tile_ref, bf16[192,1536]{1,0:T(8,128)(2,1)S(1)} %get-tuple-element.59._, ...), custom_call_target="tpu_custom_call" | custom-call | flops 301989888 | bytes 1572864 | tf_op jit(solution)/shard_map/pallas_call | solution.py:101
  33.8 0.7 collective-permute-done.8
  34.5 1.4 %collective-permute-done.7 = bf16[64,1536]{1,0:T(8,128)(2,1)S(1)} collective-permute-done((bf16[64,1536]{1,0:T(8,128)(2,1)S(1)}, bf16[64,1536]{1,0:T(8,128)(2,1)S(1)}, u32[]{:S(2)}, u32[]{:S(2)}) %collective-permute-start.7) | collective-permute-done | bytes 196640 | tf_op jit(solution)/shard_map/ppermute | solution.py:30
  36.7 4.8 %collective-permute-done.9 = bf16[64,1536]{1,0:T(8,128)(2,1)S(1)} collective-permute-done((bf16[64,1536]{1,0:T(8,128)(2,1)S(1)}, bf16[64,1536]{1,0:T(8,128)(2,1)S(1)}, u32[]{:S(2)}, u32[]{:S(2)}) %collective-permute-start.9) | collective-permute-done | bytes 196640 | tf_op jit(solution)/shard_map/ppermute | solution.py:30
  41.6 1.7 %shard_map.79 = (bf16[192,1536]{1,0:T(8,128)(2,1)S(1)}, bf16[192,1536]{1,0:T(8,128)(2,1)S(1)}, f32[128,128]{1,0:T(8,128)S(1)}, f32[128,128]{1,0:T(8,128)S(1)}) custom-call(s32[3]{0:T(128)S(1)} %pad_add_fusion.places_ref._, bf16[128,128]{1,0:T(8,128)(2,1)S(1)} %slice.131.tile_ref, s32[3]{0:T(128)S(1)} %pad_add_fusion.places_ref._, ...), custom_call_target="tpu_custom_call" | custom-call | flops 301989888 | bytes 1572864 | tf_op jit(solution)/shard_map/pallas_call | solution.py:101
  43.4 1.1 %collective-permute-start.14 = (bf16[192,1536]{1,0:T(8,128)(2,1)S(1)}, bf16[192,1536]{1,0:T(8,128)(2,1)S(1)}, u32[]{:S(2)}, u32[]{:S(2)}) collective-permute-start(bf16[192,1536]{1,0:T(8,128)(2,1)S(1)} %get-tuple-element.76), channel_id=1, source_target_pairs={{0,2},{1,5},{2,0},{3,7},{4,6},{5,1},{6,4},{7,3},{8,10},{9,13},{10,... | collective-permute-start | bytes 1769480 | tf_op jit(solution)/shard_map/ppermute | solution.py:30
  44.5 0.9 collective-permute-done.12.other_far_ref
  45.4 6.9 %shard_map.80 = (f32[192,1536]{1,0:T(8,128)S(1)}, f32[192,1536]{1,0:T(8,128)S(1)}, bf16[192,1536]{1,0:T(8,128)(2,1)S(1)}, bf16[192,1536]{1,0:T(8,128)(2,1)S(1)}) custom-call(s32[3]{0:T(128)S(1)} %pad_add_fusion.places_ref._, bf16[192,1536]{1,0:T(8,128)(2,1)S(1)} %get-tuple-element.63._.mine_near_ref, ...), custom_call_target="tpu_custom_call" | custom-call | flops 4777574400 | bytes 17160192 | tf_op jit(solution)/shard_map/pallas_call | solution.py:224
  52.3 1.1 collective-permute-done.14.mine_far_ref
  53.8 1.5 %collective-permute-done.17 = bf16[192,1536]{1,0:T(8,128)(2,1)S(1)} collective-permute-done((bf16[192,1536]{1,0:T(8,128)(2,1)S(1)}, bf16[192,1536]{1,0:T(8,128)(2,1)S(1)}, u32[]{:S(2)}, u32[]{:S(2)}) %collective-permute-start.17) | collective-permute-done | bytes 589856 | tf_op jit(solution)/shard_map/ppermute | solution.py:30
  55.5 1.1 %collective-permute-start.18 = (bf16[192,1536]{1,0:T(8,128)(2,1)S(1)}, bf16[192,1536]{1,0:T(8,128)(2,1)S(1)}, u32[]{:S(2)}, u32[]{:S(2)}) collective-permute-start(bf16[192,1536]{1,0:T(8,128)(2,1)S(1)} %add_convert_fusion.1), channel_id=1, source_target_pairs={{0,2},{1,5},{2,0},{3,7},{4,6},{5,1},{6,4},{7,3},{8,10},{9,13},{10,... | collective-permute-start | bytes 1769480 | tf_op jit(solution)/shard_map/ppermute | solution.py:30
  57.0 7.1 %shard_map.81 = (f32[192,1536]{1,0:T(8,128)S(1)}, f32[192,1536]{1,0:T(8,128)S(1)}, bf16[192,1536]{1,0:T(8,128)(2,1)S(1)}, bf16[192,1536]{1,0:T(8,128)(2,1)S(1)}) custom-call(s32[3]{0:T(128)S(1)} %pad_add_fusion.places_ref._, bf16[192,1536]{1,0:T(8,128)(2,1)S(1)} %get-tuple-element.74.mine_near_ref, ...), custom_call_target="tpu_custom_call" | custom-call | flops 4777574400 | bytes 17160192 | tf_op jit(solution)/shard_map/pallas_call | solution.py:224
  64.1 1.3 %collective-permute-done.18.arrived_ref = bf16[192,1536]{1,0:T(8,128)(2,1)S(1)} collective-permute-done((bf16[192,1536]{1,0:T(8,128)(2,1)S(1)}, bf16[192,1536]{1,0:T(8,128)(2,1)S(1)}, u32[]{:S(2)}, u32[]{:S(2)}) %collective-permute-start.18) | collective-permute-done | bytes 589856 | tf_op jit(solution)/shard_map/ppermute | solution.py:30
  65.9 1.5 %collective-permute-done.19 = bf16[192,1536]{1,0:T(8,128)(2,1)S(1)} collective-permute-done((bf16[192,1536]{1,0:T(8,128)(2,1)S(1)}, bf16[192,1536]{1,0:T(8,128)(2,1)S(1)}, u32[]{:S(2)}, u32[]{:S(2)}) %collective-permute-start.19) | collective-permute-done | bytes 589856 | tf_op jit(solution)/shard_map/ppermute | solution.py:30
  67.6 0.7 collective-permute-done.13.taken_ref
  68.3 0.6 shard_map.82
  69.0 0.6 collective-permute-start.21
  69.6 1.4 %collective-permute-start.22 = (bf16[192,1536]{1,0:T(8,128)(2,1)S(1)}, bf16[192,1536]{1,0:T(8,128)(2,1)S(1)}, u32[]{:S(2)}, u32[]{:S(2)}) collective-permute-start(bf16[192,1536]{1,0:T(8,128)(2,1)S(1)} %add_convert_fusion), channel_id=1, source_target_pairs={{0,2},{1,5},{2,0},{3,7},{4,6},{5,1},{6,4},{7,3},{8,10},{9,13},{10,... | collective-permute-start | bytes 1769480 | tf_op jit(solution)/shard_map/ppermute | solution.py:30
  71.0 5.0 %collective-permute-done.21 = bf16[64,1536]{1,0:T(8,128)(2,1)S(1)} collective-permute-done((bf16[64,1536]{1,0:T(8,128)(2,1)S(1)}, bf16[64,1536]{1,0:T(8,128)(2,1)S(1)}, u32[]{:S(2)}, u32[]{:S(2)}) %collective-permute-start.21) | collective-permute-done | bytes 196640 | tf_op jit(solution)/shard_map/ppermute | solution.py:30
  76.1 3.5 %collective-permute-done.22.arrived_ref = bf16[192,1536]{1,0:T(8,128)(2,1)S(1)} collective-permute-done((bf16[192,1536]{1,0:T(8,128)(2,1)S(1)}, bf16[192,1536]{1,0:T(8,128)(2,1)S(1)}, u32[]{:S(2)}, u32[]{:S(2)}) %collective-permute-start.22) | collective-permute-done | bytes 589856 | tf_op jit(solution)/shard_map/ppermute | solution.py:30
  80.0 1.8 %collective-permute-start.26 = (bf16[128,1536]{1,0:T(8,128)(2,1)S(1)}, bf16[128,1536]{1,0:T(8,128)(2,1)S(1)}, u32[]{:S(2)}, u32[]{:S(2)}) collective-permute-start(bf16[128,1536]{1,0:T(8,128)(2,1)S(1)} %shard_map.83._), channel_id=1, source_target_pairs={{0,4},{1,3},{2,6},{3,1},{4,0},{5,7},{6,2},{7,5},{8,12},{9,11},{10,... | collective-permute-start | bytes 1179656 | tf_op jit(solution)/shard_map/ppermute | solution.py:30
  81.8 1.2 %collective-permute-start.20 = (bf16[64,1536]{1,0:T(8,128)(2,1)S(1)}, bf16[64,1536]{1,0:T(8,128)(2,1)S(1)}, u32[]{:S(2)}, u32[]{:S(2)}) collective-permute-start(bf16[64,1536]{1,0:T(8,128)(2,1)S(1)} %get-tuple-element.104), channel_id=1, source_target_pairs={{0,8},{1,9},{2,10},{3,11},{4,12},{5,13},{6,14},{7,15},{8,0},{9,1},... | collective-permute-start | bytes 589832 | tf_op jit(solution)/shard_map/ppermute | solution.py:30
  83.0 1.4 %collective-permute-start.23 = (bf16[64,1536]{1,0:T(8,128)(2,1)S(1)}, bf16[64,1536]{1,0:T(8,128)(2,1)S(1)}, u32[]{:S(2)}, u32[]{:S(2)}) collective-permute-start(bf16[64,1536]{1,0:T(8,128)(2,1)S(1)} %fusion.8), channel_id=1, source_target_pairs={{0,16},{1,17},{2,18},{3,19},{4,20},{5,21},{6,22},{7,23},{8,24},{9,... | collective-permute-start | bytes 589832 | tf_op jit(solution)/shard_map/ppermute | solution.py:30
  84.9 6.3 %collective-permute-done.20 = bf16[64,1536]{1,0:T(8,128)(2,1)S(1)} collective-permute-done((bf16[64,1536]{1,0:T(8,128)(2,1)S(1)}, bf16[64,1536]{1,0:T(8,128)(2,1)S(1)}, u32[]{:S(2)}, u32[]{:S(2)}) %collective-permute-start.20) | collective-permute-done | bytes 196640 | tf_op jit(solution)/shard_map/ppermute | solution.py:30
  91.1 2.0 %collective-permute-done.23 = bf16[64,1536]{1,0:T(8,128)(2,1)S(1)} collective-permute-done((bf16[64,1536]{1,0:T(8,128)(2,1)S(1)}, bf16[64,1536]{1,0:T(8,128)(2,1)S(1)}, u32[]{:S(2)}, u32[]{:S(2)}) %collective-permute-start.23) | collective-permute-done | bytes 196640 | tf_op jit(solution)/shard_map/ppermute | solution.py:30
  93.9 1.7 %collective-permute-start.25 = (bf16[32,1536]{1,0:T(8,128)(2,1)S(1)}, bf16[32,1536]{1,0:T(8,128)(2,1)S(1)}, u32[]{:S(2)}, u32[]{:S(2)}) collective-permute-start(bf16[32,1536]{1,0:T(8,128)(2,1)S(1)} %slice.214), channel_id=1, source_target_pairs={{0,4},{1,3},{2,6},{3,1},{4,0},{5,7},{6,2},{7,5},{8,12},{9,11},{10,... | collective-permute-start | bytes 294920 | tf_op jit(solution)/shard_map/ppermute | solution.py:30
  95.6 3.0 %collective-permute-done.28 = bf16[32,1536]{1,0:T(8,128)(2,1)S(1)} collective-permute-done((bf16[32,1536]{1,0:T(8,128)(2,1)S(1)}, bf16[32,1536]{1,0:T(8,128)(2,1)S(1)}, u32[]{:S(2)}, u32[]{:S(2)}) %collective-permute-start.28) | collective-permute-done | bytes 98336 | tf_op jit(solution)/shard_map/ppermute | solution.py:30
  98.6 1.6 %collective-permute-start.29 = (bf16[32,1536]{1,0:T(8,128)(2,1)S(1)}, bf16[32,1536]{1,0:T(8,128)(2,1)S(1)}, u32[]{:S(2)}, u32[]{:S(2)}) collective-permute-start(bf16[32,1536]{1,0:T(8,128)(2,1)S(1)} %fusion.11), channel_id=1, source_target_pairs={{0,16},{1,17},{2,18},{3,19},{4,20},{5,21},{6,22},{7,23},{8,24},{9,... | collective-permute-start | bytes 294920 | tf_op jit(solution)/shard_map/ppermute | solution.py:30
  100.2 5.0 %collective-permute-done.29 = bf16[32,1536]{1,0:T(8,128)(2,1)S(1)} collective-permute-done((bf16[32,1536]{1,0:T(8,128)(2,1)S(1)}, bf16[32,1536]{1,0:T(8,128)(2,1)S(1)}, u32[]{:S(2)}, u32[]{:S(2)}) %collective-permute-start.29) | collective-permute-done | bytes 98336 | tf_op jit(solution)/shard_map/ppermute | solution.py:30
  105.4 1.3 %collective-permute-done.30 = bf16[2,16,1536]{2,1,0:T(8,128)(2,1)S(1)} collective-permute-done((bf16[2,16,1536]{2,1,0:T(8,128)(2,1)S(1)}, bf16[2,16,1536]{2,1,0:T(8,128)(2,1)S(1)}, u32[]{:S(2)}, u32[]{:S(2)}) %collective-permute-start.30) | collective-permute-done | bytes 98336 | tf_op jit(solution)/shard_map/ppermute | solution.py:30
  106.8 0.7 fusion.9
  (83 shorter events, 7.3 us)
Async XLA Ops:
  2.4 0.9 copy-start.1
  3.3 14.7 %slice-start.2 = ((s8[4239360]{0:T(1024)(128)(4,1)}), s8[45056]{0:T(1024)(128)(4,1)S(1)}, s32[]{:S(2)}) async-start(s8[4239360]{0:T(1024)(128)(4,1)} %bitcast.49), calls=%async_computation.2 | async-start | bytes 90112
  4.1 1.5 %collective-permute-start = (bf16[2,16,1536]{2,1,0:T(8,128)(2,1)S(1)}, bf16[2,16,1536]{2,1,0:T(8,128)(2,1)S(1)}, u32[]{:S(2)}, u32[]{:S(2)}) collective-permute-start(bf16[2,16,1536]{2,1,0:T(8,128)(2,1)S(1)} %get-tuple-element.52), channel_id=1, source_target_pairs={{0,1},{1,0},{2,3},{3,2},{4,5},{5,4},{6,7},{7,6},{8,9},{9,8},{10,11... | collective-permute-start | bytes 294920 | tf_op jit(solution)/shard_map/ppermute | solution.py:30
  5.6 9.8 %collective-permute-start.2 = (bf16[32,1536]{1,0:T(8,128)(2,1)S(1)}, bf16[32,1536]{1,0:T(8,128)(2,1)S(1)}, u32[]{:S(2)}, u32[]{:S(2)}) collective-permute-start(bf16[32,1536]{1,0:T(8,128)(2,1)S(1)} %pad_maximum_fusion.6), channel_id=1, source_target_pairs={{0,4},{1,3},{2,6},{3,1},{4,0},{5,7},{6,2},{7,5},{8,12},{9,11},{10,... | collective-permute-start | bytes 294920 | tf_op jit(solution)/shard_map/ppermute | solution.py:30
  8.6 6.8 %collective-permute-start.1 = (bf16[32,1536]{1,0:T(8,128)(2,1)S(1)}, bf16[32,1536]{1,0:T(8,128)(2,1)S(1)}, u32[]{:S(2)}, u32[]{:S(2)}) collective-permute-start(bf16[32,1536]{1,0:T(8,128)(2,1)S(1)} %pad_maximum_fusion.5._), channel_id=1, source_target_pairs={{0,8},{1,9},{2,10},{3,11},{4,12},{5,13},{6,14},{7,15},{8,0},{9,1},... | collective-permute-start | bytes 294920 | tf_op jit(solution)/shard_map/ppermute | solution.py:30
  10.3 7.3 %collective-permute-start.3 = (bf16[32,1536]{1,0:T(8,128)(2,1)S(1)}, bf16[32,1536]{1,0:T(8,128)(2,1)S(1)}, u32[]{:S(2)}, u32[]{:S(2)}) collective-permute-start(bf16[32,1536]{1,0:T(8,128)(2,1)S(1)} %pad_maximum_fusion.5._), channel_id=1, source_target_pairs={{0,16},{1,17},{2,18},{3,19},{4,20},{5,21},{6,22},{7,23},{8,24},{9,... | collective-permute-start | bytes 294920 | tf_op jit(solution)/shard_map/ppermute | solution.py:30
  12.8 2.2 %copy-start = (bf16[2880,720]{0,1:T(8,128)(2,1)S(1)}, bf16[2880,720]{0,1:T(8,128)(2,1)}, u32[]{:S(2)}) copy-start(bf16[2880,720]{0,1:T(8,128)(2,1)} %param.9) | copy-start | bytes 12441604
  15.1 2.9 %slice-start.3 = ((s8[4239360]{0:T(1024)(128)(4,1)}), s8[4194304]{0:T(1024)(128)(4,1)S(1)}, s32[]{:S(2)}) async-start(s8[4239360]{0:T(1024)(128)(4,1)} %bitcast.49), calls=%async_computation.3 | async-start | bytes 8388608
  17.6 4.6 %collective-permute-start.4 = (bf16[32,1536]{1,0:T(8,128)(2,1)S(1)}, bf16[32,1536]{1,0:T(8,128)(2,1)S(1)}, u32[]{:S(2)}, u32[]{:S(2)}) collective-permute-start(bf16[32,1536]{1,0:T(8,128)(2,1)S(1)} %collective-permute-done.3._), channel_id=1, source_target_pairs={{0,8},{1,9},{2,10},{3,11},{4,12},{5,13},{6,14},{7,15},{8,0},{9,1},... | collective-permute-start | bytes 294920 | tf_op jit(solution)/shard_map/ppermute | solution.py:30
  17.9 18.4 %slice-start = ((s8[4239360]{0:T(1024)(128)(4,1)}), s8[4194304]{0:T(1024)(128)(4,1)S(1)}, s32[]{:S(2)}) async-start(s8[4239360]{0:T(1024)(128)(4,1)} %bitcast.46), calls=%async_computation | async-start | bytes 8388608
  18.0 18.3 %slice-start.1 = ((s8[4239360]{0:T(1024)(128)(4,1)}), s8[45056]{0:T(1024)(128)(4,1)S(1)}, s32[]{:S(2)}) async-start(s8[4239360]{0:T(1024)(128)(4,1)} %bitcast.46), calls=%async_computation.1 | async-start | bytes 90112
  22.2 1.6 %collective-permute-start.6 = (bf16[128,128]{1,0:T(8,128)(2,1)S(1)}, bf16[128,128]{1,0:T(8,128)(2,1)S(1)}, u32[]{:S(2)}, u32[]{:S(2)}) collective-permute-start(bf16[128,128]{1,0:T(8,128)(2,1)S(1)} %slice.130.tile_ref), channel_id=1, source_target_pairs={{0,1},{1,0},{2,3},{3,2},{4,5},{5,4},{6,7},{7,6},{8,9},{9,8},{10,11... | collective-permute-start | bytes 98312 | tf_op jit(solution)/shard_map/ppermute | solution.py:30
  22.3 7.8 %collective-permute-start.5 = (bf16[128,1536]{1,0:T(8,128)(2,1)S(1)}, bf16[128,1536]{1,0:T(8,128)(2,1)S(1)}, u32[]{:S(2)}, u32[]{:S(2)}) collective-permute-start(bf16[128,1536]{1,0:T(8,128)(2,1)S(1)} %constant_dynamic-update-slice_fusion.near_ref), channel_id=1, source_target_pairs={{0,4},{1,3},{2,6},{3,1},{4,0},{5,7},{6,2},{7,5},{8,12},{9,11},{10,... | collective-permute-start | bytes 1179656 | tf_op jit(solution)/shard_map/ppermute | solution.py:30
  23.9 10.6 %collective-permute-start.8 = (bf16[64,1536]{1,0:T(8,128)(2,1)S(1)}, bf16[64,1536]{1,0:T(8,128)(2,1)S(1)}, u32[]{:S(2)}, u32[]{:S(2)}) collective-permute-start(bf16[64,1536]{1,0:T(8,128)(2,1)S(1)} %pad_maximum_fusion.4), channel_id=1, source_target_pairs={{0,8},{1,9},{2,10},{3,11},{4,12},{5,13},{6,14},{7,15},{8,0},{9,1},... | collective-permute-start | bytes 589832 | tf_op jit(solution)/shard_map/ppermute | solution.py:30
  24.4 11.5 %collective-permute-start.7 = (bf16[64,1536]{1,0:T(8,128)(2,1)S(1)}, bf16[64,1536]{1,0:T(8,128)(2,1)S(1)}, u32[]{:S(2)}, u32[]{:S(2)}) collective-permute-start(bf16[64,1536]{1,0:T(8,128)(2,1)S(1)} %pad_maximum_fusion.4), channel_id=1, source_target_pairs={{0,16},{1,17},{2,18},{3,19},{4,20},{5,21},{6,22},{7,23},{8,24},{9,... | collective-permute-start | bytes 589832 | tf_op jit(solution)/shard_map/ppermute | solution.py:30
  31.5 11.8 %collective-permute-start.10 = (bf16[192,1536]{1,0:T(8,128)(2,1)S(1)}, bf16[192,1536]{1,0:T(8,128)(2,1)S(1)}, u32[]{:S(2)}, u32[]{:S(2)}) collective-permute-start(bf16[192,1536]{1,0:T(8,128)(2,1)S(1)} %get-tuple-element.59._), channel_id=1, source_target_pairs={{0,2},{1,5},{2,0},{3,7},{4,6},{5,1},{6,4},{7,3},{8,10},{9,13},{10,... | collective-permute-start | bytes 1769480 | tf_op jit(solution)/shard_map/ppermute | solution.py:30
  35.9 5.7 %collective-permute-start.9 = (bf16[64,1536]{1,0:T(8,128)(2,1)S(1)}, bf16[64,1536]{1,0:T(8,128)(2,1)S(1)}, u32[]{:S(2)}, u32[]{:S(2)}) collective-permute-start(bf16[64,1536]{1,0:T(8,128)(2,1)S(1)} %collective-permute-done.7), channel_id=1, source_target_pairs={{0,8},{1,9},{2,10},{3,11},{4,12},{5,13},{6,14},{7,15},{8,0},{9,1},... | collective-permute-start | bytes 589832 | tf_op jit(solution)/shard_map/ppermute | solution.py:30
  36.2 8.3 %collective-permute-start.11 = (bf16[192,1536]{1,0:T(8,128)(2,1)S(1)}, bf16[192,1536]{1,0:T(8,128)(2,1)S(1)}, u32[]{:S(2)}, u32[]{:S(2)}) collective-permute-start(bf16[192,1536]{1,0:T(8,128)(2,1)S(1)} %get-tuple-element.63._.mine_near_ref), channel_id=1, source_target_pairs={{0,1},{1,0},{2,3},{3,2},{4,5},{5,4},{6,7},{7,6},{8,9},{9,8},{10,11... | collective-permute-start | bytes 1769480 | tf_op jit(solution)/shard_map/ppermute | solution.py:30
  43.3 2.1 %collective-permute-start.12 = (bf16[192,1536]{1,0:T(8,128)(2,1)S(1)}, bf16[192,1536]{1,0:T(8,128)(2,1)S(1)}, u32[]{:S(2)}, u32[]{:S(2)}) collective-permute-start(bf16[192,1536]{1,0:T(8,128)(2,1)S(1)} %collective-permute-done.10.mine_far_ref), channel_id=1, source_target_pairs={{0,1},{1,0},{2,3},{3,2},{4,5},{5,4},{6,7},{7,6},{8,9},{9,8},{10,11... | collective-permute-start | bytes 1769480 | tf_op jit(solution)/shard_map/ppermute | solution.py:30
  43.4 9.9 %collective-permute-start.14 = (bf16[192,1536]{1,0:T(8,128)(2,1)S(1)}, bf16[192,1536]{1,0:T(8,128)(2,1)S(1)}, u32[]{:S(2)}, u32[]{:S(2)}) collective-permute-start(bf16[192,1536]{1,0:T(8,128)(2,1)S(1)} %get-tuple-element.76), channel_id=1, source_target_pairs={{0,2},{1,5},{2,0},{3,7},{4,6},{5,1},{6,4},{7,3},{8,10},{9,13},{10,... | collective-permute-start | bytes 1769480 | tf_op jit(solution)/shard_map/ppermute | solution.py:30
  53.3 2.0 %collective-permute-start.17 = (bf16[192,1536]{1,0:T(8,128)(2,1)S(1)}, bf16[192,1536]{1,0:T(8,128)(2,1)S(1)}, u32[]{:S(2)}, u32[]{:S(2)}) collective-permute-start(bf16[192,1536]{1,0:T(8,128)(2,1)S(1)} %get-tuple-element.79), channel_id=1, source_target_pairs={{0,1},{1,0},{2,3},{3,2},{4,5},{5,4},{6,7},{7,6},{8,9},{9,8},{10,11... | collective-permute-start | bytes 1769480 | tf_op jit(solution)/shard_map/ppermute | solution.py:30
  53.3 3.7 %collective-permute-start.15 = (bf16[192,1536]{1,0:T(8,128)(2,1)S(1)}, bf16[192,1536]{1,0:T(8,128)(2,1)S(1)}, u32[]{:S(2)}, u32[]{:S(2)}) collective-permute-start(bf16[192,1536]{1,0:T(8,128)(2,1)S(1)} %get-tuple-element.74.mine_near_ref), channel_id=1, source_target_pairs={{0,1},{1,0},{2,3},{3,2},{4,5},{5,4},{6,7},{7,6},{8,9},{9,8},{10,11... | collective-permute-start | bytes 1769480 | tf_op jit(solution)/shard_map/ppermute | solution.py:30
  53.8 3.2 %collective-permute-start.16 = (bf16[192,1536]{1,0:T(8,128)(2,1)S(1)}, bf16[192,1536]{1,0:T(8,128)(2,1)S(1)}, u32[]{:S(2)}, u32[]{:S(2)}) collective-permute-start(bf16[192,1536]{1,0:T(8,128)(2,1)S(1)} %collective-permute-done.14.mine_far_ref), channel_id=1, source_target_pairs={{0,1},{1,0},{2,3},{3,2},{4,5},{5,4},{6,7},{7,6},{8,9},{9,8},{10,11... | collective-permute-start | bytes 1769480 | tf_op jit(solution)/shard_map/ppermute | solution.py:30
  55.5 9.9 %collective-permute-start.18 = (bf16[192,1536]{1,0:T(8,128)(2,1)S(1)}, bf16[192,1536]{1,0:T(8,128)(2,1)S(1)}, u32[]{:S(2)}, u32[]{:S(2)}) collective-permute-start(bf16[192,1536]{1,0:T(8,128)(2,1)S(1)} %add_convert_fusion.1), channel_id=1, source_target_pairs={{0,2},{1,5},{2,0},{3,7},{4,6},{5,1},{6,4},{7,3},{8,10},{9,13},{10,... | collective-permute-start | bytes 1769480 | tf_op jit(solution)/shard_map/ppermute | solution.py:30
  65.4 2.0 %collective-permute-start.19 = (bf16[192,1536]{1,0:T(8,128)(2,1)S(1)}, bf16[192,1536]{1,0:T(8,128)(2,1)S(1)}, u32[]{:S(2)}, u32[]{:S(2)}) collective-permute-start(bf16[192,1536]{1,0:T(8,128)(2,1)S(1)} %get-tuple-element.83), channel_id=1, source_target_pairs={{0,1},{1,0},{2,3},{3,2},{4,5},{5,4},{6,7},{7,6},{8,9},{9,8},{10,11... | collective-permute-start | bytes 1769480 | tf_op jit(solution)/shard_map/ppermute | solution.py:30
  65.4 2.8 %collective-permute-start.13 = (bf16[192,1536]{1,0:T(8,128)(2,1)S(1)}, bf16[192,1536]{1,0:T(8,128)(2,1)S(1)}, u32[]{:S(2)}, u32[]{:S(2)}) collective-permute-start(bf16[192,1536]{1,0:T(8,128)(2,1)S(1)} %get-tuple-element.73), channel_id=1, source_target_pairs={{0,1},{1,0},{2,3},{3,2},{4,5},{5,4},{6,7},{7,6},{8,9},{9,8},{10,11... | collective-permute-start | bytes 1769480 | tf_op jit(solution)/shard_map/ppermute | solution.py:30
  69.0 7.0 %collective-permute-start.21 = (bf16[64,1536]{1,0:T(8,128)(2,1)S(1)}, bf16[64,1536]{1,0:T(8,128)(2,1)S(1)}, u32[]{:S(2)}, u32[]{:S(2)}) collective-permute-start(bf16[64,1536]{1,0:T(8,128)(2,1)S(1)} %get-tuple-element.103), channel_id=1, source_target_pairs={{0,8},{1,9},{2,10},{3,11},{4,12},{5,13},{6,14},{7,15},{8,0},{9,1},... | collective-permute-start | bytes 589832 | tf_op jit(solution)/shard_map/ppermute | solution.py:30
  69.6 9.9 %collective-permute-start.22 = (bf16[192,1536]{1,0:T(8,128)(2,1)S(1)}, bf16[192,1536]{1,0:T(8,128)(2,1)S(1)}, u32[]{:S(2)}, u32[]{:S(2)}) collective-permute-start(bf16[192,1536]{1,0:T(8,128)(2,1)S(1)} %add_convert_fusion), channel_id=1, source_target_pairs={{0,2},{1,5},{2,0},{3,7},{4,6},{5,1},{6,4},{7,3},{8,10},{9,13},{10,... | collective-permute-start | bytes 1769480 | tf_op jit(solution)/shard_map/ppermute | solution.py:30
  71.0 8.5 %collective-permute-start.24 = (bf16[192,1536]{1,0:T(8,128)(2,1)S(1)}, bf16[192,1536]{1,0:T(8,128)(2,1)S(1)}, u32[]{:S(2)}, u32[]{:S(2)}) collective-permute-start(bf16[192,1536]{1,0:T(8,128)(2,1)S(1)} %get-tuple-element.92), channel_id=1, source_target_pairs={{0,1},{1,0},{2,3},{3,2},{4,5},{5,4},{6,7},{7,6},{8,9},{9,8},{10,11... | collective-permute-start | bytes 1769480 | tf_op jit(solution)/shard_map/ppermute | solution.py:30
  80.0 13.1 %collective-permute-start.26 = (bf16[128,1536]{1,0:T(8,128)(2,1)S(1)}, bf16[128,1536]{1,0:T(8,128)(2,1)S(1)}, u32[]{:S(2)}, u32[]{:S(2)}) collective-permute-start(bf16[128,1536]{1,0:T(8,128)(2,1)S(1)} %shard_map.83._), channel_id=1, source_target_pairs={{0,4},{1,3},{2,6},{3,1},{4,0},{5,7},{6,2},{7,5},{8,12},{9,11},{10,... | collective-permute-start | bytes 1179656 | tf_op jit(solution)/shard_map/ppermute | solution.py:30
  81.8 9.4 %collective-permute-start.20 = (bf16[64,1536]{1,0:T(8,128)(2,1)S(1)}, bf16[64,1536]{1,0:T(8,128)(2,1)S(1)}, u32[]{:S(2)}, u32[]{:S(2)}) collective-permute-start(bf16[64,1536]{1,0:T(8,128)(2,1)S(1)} %get-tuple-element.104), channel_id=1, source_target_pairs={{0,8},{1,9},{2,10},{3,11},{4,12},{5,13},{6,14},{7,15},{8,0},{9,1},... | collective-permute-start | bytes 589832 | tf_op jit(solution)/shard_map/ppermute | solution.py:30
  83.0 10.1 %collective-permute-start.23 = (bf16[64,1536]{1,0:T(8,128)(2,1)S(1)}, bf16[64,1536]{1,0:T(8,128)(2,1)S(1)}, u32[]{:S(2)}, u32[]{:S(2)}) collective-permute-start(bf16[64,1536]{1,0:T(8,128)(2,1)S(1)} %fusion.8), channel_id=1, source_target_pairs={{0,16},{1,17},{2,18},{3,19},{4,20},{5,21},{6,22},{7,23},{8,24},{9,... | collective-permute-start | bytes 589832 | tf_op jit(solution)/shard_map/ppermute | solution.py:30
  93.2 5.4 %collective-permute-start.28 = (bf16[32,1536]{1,0:T(8,128)(2,1)S(1)}, bf16[32,1536]{1,0:T(8,128)(2,1)S(1)}, u32[]{:S(2)}, u32[]{:S(2)}) collective-permute-start(bf16[32,1536]{1,0:T(8,128)(2,1)S(1)} %get-tuple-element.106), channel_id=1, source_target_pairs={{0,8},{1,9},{2,10},{3,11},{4,12},{5,13},{6,14},{7,15},{8,0},{9,1},... | collective-permute-start | bytes 294920 | tf_op jit(solution)/shard_map/ppermute | solution.py:30
  93.9 6.3 %collective-permute-start.25 = (bf16[32,1536]{1,0:T(8,128)(2,1)S(1)}, bf16[32,1536]{1,0:T(8,128)(2,1)S(1)}, u32[]{:S(2)}, u32[]{:S(2)}) collective-permute-start(bf16[32,1536]{1,0:T(8,128)(2,1)S(1)} %slice.214), channel_id=1, source_target_pairs={{0,4},{1,3},{2,6},{3,1},{4,0},{5,7},{6,2},{7,5},{8,12},{9,11},{10,... | collective-permute-start | bytes 294920 | tf_op jit(solution)/shard_map/ppermute | solution.py:30
  95.6 4.6 %collective-permute-start.27 = (bf16[32,1536]{1,0:T(8,128)(2,1)S(1)}, bf16[32,1536]{1,0:T(8,128)(2,1)S(1)}, u32[]{:S(2)}, u32[]{:S(2)}) collective-permute-start(bf16[32,1536]{1,0:T(8,128)(2,1)S(1)} %get-tuple-element.105), channel_id=1, source_target_pairs={{0,8},{1,9},{2,10},{3,11},{4,12},{5,13},{6,14},{7,15},{8,0},{9,1},... | collective-permute-start | bytes 294920 | tf_op jit(solution)/shard_map/ppermute | solution.py:30
  98.6 6.6 %collective-permute-start.29 = (bf16[32,1536]{1,0:T(8,128)(2,1)S(1)}, bf16[32,1536]{1,0:T(8,128)(2,1)S(1)}, u32[]{:S(2)}, u32[]{:S(2)}) collective-permute-start(bf16[32,1536]{1,0:T(8,128)(2,1)S(1)} %fusion.11), channel_id=1, source_target_pairs={{0,16},{1,17},{2,18},{3,19},{4,20},{5,21},{6,22},{7,23},{8,24},{9,... | collective-permute-start | bytes 294920 | tf_op jit(solution)/shard_map/ppermute | solution.py:30
  100.2 6.6 %copy-start.2 = (bf16[2,16,2880]{2,1,0:T(8,128)(2,1)S(1)}, bf16[2,16,2880]{2,1,0:T(8,128)(2,1)}, u32[]{:S(2)}) copy-start(bf16[2,16,2880]{2,1,0:T(8,128)(2,1)} %hidden_ref.1) | copy-start | bytes 552964
  105.3 1.4 %collective-permute-start.30 = (bf16[2,16,1536]{2,1,0:T(8,128)(2,1)S(1)}, bf16[2,16,1536]{2,1,0:T(8,128)(2,1)S(1)}, u32[]{:S(2)}, u32[]{:S(2)}) collective-permute-start(bf16[2,16,1536]{2,1,0:T(8,128)(2,1)S(1)} %select_convert_fusion), channel_id=1, source_target_pairs={{0,1},{1,0},{2,3},{3,2},{4,5},{5,4},{6,7},{7,6},{8,9},{9,8},{10,11... | collective-permute-start | bytes 294920 | tf_op jit(solution)/shard_map/ppermute | solution.py:30

commit v7 on v6

--- a/solution.py
+++ b/solution.py
@@ -383,22 +383,25 @@
             state["own"], near_slots, next_slots = select(*chosen, (0,), places, near, following, tile, send)
             state["slots"] = state["places"], next_slots
 
-    def staged(block, load):
-        crossed, beside = moved(block, far(2)), moved(block, far(1))
-        crossed, first_loaded = tied(crossed, load(0, block))
-        passed = moved(crossed, far(1))
-        passed, second_loaded = tied(passed, load(1, crossed))
-        return [beside, crossed, passed], first_loaded, second_loaded
-
     pair = pairs[0]
-    asides = [moved(other, first_axis) for other in pairs[1:]]
     weights_t = w_gate.T, w_up.T
     if distant == 4:
-        blocks, gate_v, up_v = staged(pair, lambda index, token: preload(token, weights_t[index])[0])
+        (gate_v,) = preload(pair, weights_t[0])
+        crossed = moved(pair, far(2))
+        again, pairs[-1] = tied(pair, pairs[-1])
+        beside = moved(again, far(1))
+        crossed, gate_v = tied(crossed, gate_v)
+        (up_v,) = preload(crossed, weights_t[1])
+        passed = moved(crossed, far(1))
+        passed, up_v = tied(passed, up_v)
+        blocks = [beside, crossed, passed]
+        *rest, gate_v = tied(*pairs[1:], gate_v)
     else:
         blocks = far_blocks(pair)
         gate_v, up_v = preload(pair, *weights_t)
-    blocks[0], *asides = tied(blocks[0], *asides)
+        rest = pairs[1:]
+    asides = [moved(other, first_axis) for other in rest]
+    blocks[-1], *asides = tied(blocks[-1], *asides)
     column = join(pair, *blocks)
     states.append({"near": column, "next": moved(column, first_axis)})
     down_v = None
@@ -415,7 +418,7 @@
             second_hop(last, True)
         if down_v is None:
             (down_v,) = preload(last["own"], w_down)
-            blocks[-1], down_v = tied(blocks[-1], down_v)
+            blocks[-1], down_v, last["arrived"] = tied(blocks[-1], down_v, last["arrived"])
         blocks = [both] + blocks
         states.append(
             {"near": join(*[block[:side] for block in blocks]), "next": join(*[block[side:] for block in blocks])}
@@ -444,51 +447,34 @@
         hops.append(
             {"keep": keep_near, "taken": moved(send_near, other_core), "give": give, "arrived": moved(give, second_axis)}
         )
-    for b in range(1, micro_count):
-        hops[b - 1]["taken"], hops[b]["give"] = tied(hops[b - 1]["taken"], hops[b]["give"])
-
     def far_hop(block):
         block = block.reshape(distant, -1, held)
         if distant == 4:
             through = moved(block[3].astype(jnp.bfloat16), far(1))
             beside = moved(block[1].astype(jnp.bfloat16), far(1))
-            return block[0], [beside], rounded_sum(block[2], through)
-        return block[0], [moved(block[j].astype(jnp.bfloat16), far(j)) for j in range(1, distant)], None
-
-    def crossing(total):
-        kept, arrivals, cross = total
-        return kept, arrivals + ([] if cross is None else [moved(cross, far(2))])
-
-    def settled(kept, arrivals):
-        for arrival in arrivals:
+            return [block[0], [beside], rounded_sum(block[2], through)]
+        return [block[0], [moved(block[j].astype(jnp.bfloat16), far(j)) for j in range(1, distant)], None]
+
+    def settled(kept, arrivals, cross):
+        for arrival in arrivals if cross is None else arrivals + [moved(cross, far(2))]:
             kept = kept + arrival.astype(jnp.float32)
         return kept
 
-    sums = []
-    waiting = None
+    totals = []
+    near = None
     for b, (state, hop) in enumerate(zip(states, hops)):
-        final = b == micro_count - 1
+        token = hops[b + 1]["give"] if b + 1 < micro_count else None
         parts = state["slots"], hop["keep"], hop["taken"], hop["arrived"]
-        if not final:
-            near, following = merge((0, 1), (jnp.float32, jnp.float32), *parts)
-            both = jnp.concatenate([near.reshape(distant, side, held), following.reshape(distant, side, held)], axis=1)
-            total = far_hop(both)
-            if total[2] is not None and b + 1 < micro_count:
-                cross, hops[b + 1]["arrived"] = tied(total[2], hops[b + 1]["arrived"])
-                total = total[0], total[1], cross
-            waiting = crossing(total)
-            continue
-        (following,) = merge((1,), (jnp.bfloat16,), *parts)
-        (near,) = merge((0,), (jnp.float32,), *parts, following)
-        if waiting is not None:
-            *earlier, near = tied(*waiting[1], near)
-        near = near + moved(following, first_axis).astype(jnp.float32)
-        kept, arrivals = crossing(far_hop(near))
-        if waiting is not None:
-            before = settled(waiting[0], earlier)
-            sums.append(before[:side] + moved(before[side:].astype(jnp.bfloat16), first_axis).astype(jnp.float32))
-        sums.append(settled(kept, arrivals))
-    sums = jnp.stack(sums)
+        if near is None:
+            kept, following = merge((0, 1), (jnp.float32, jnp.bfloat16), *parts, token)
+        else:
+            (following,) = merge((1,), (jnp.bfloat16,), *parts, token)
+            (kept,) = merge((0,), (jnp.float32,), *parts, following)
+            near, kept = tied(near, kept)
+            totals.append(far_hop(near))
+        near = kept + moved(following, first_axis).astype(jnp.float32)
+    totals.append(far_hop(near))
+    sums = jnp.stack([settled(*total) for total in totals])
     own = jnp.where(lower, sums[:, :tokens], sums[:, tokens:])
     give = jnp.where(lower, sums[:, tokens:], sums[:, :tokens]).astype(jnp.bfloat16)
     taken = moved(give, other_core).astype(jnp.float32)

time: 108 us -> 106 us (0.981)
  waiting for transfers between devices: 50.4 us -> 47.8 us
  starting transfers between devices: 27.6 us -> 29.1 us
    ppermute x31, waiting for transfers between devices: 50.4 us -> 47.8 us  [moved(): return lax.ppermute(block, 'req', [(i, partner(i)) for i in range(count)])]
    ppermute x31, starting transfers between devices: 27.6 us -> 29.1 us  [moved(): return lax.ppermute(block, 'req', [(i, partner(i)) for i in range(count)])]
  transfers between devices with their start and end apart: 31 -> 31, of which waited for: 21 -> 23; matrix products, arithmetic and copies ran while one was open for 1% -> 1% of each run, Pallas kernels for 19% -> 19%
where the time goes in v7:
time: 106 us
  waiting for transfers between devices  47.8 us (45%)
  starting transfers between devices  29.1 us (27%)
  Pallas kernels  21.8 us (21%)
  local copies, waits for them, and re-layouts  4.14 us (4%)
  other arithmetic  3.04 us (3%)
    ppermute x31, waiting for transfers between devices, moved(): return lax.ppermute(block, 'req', [(i, partner(i)) for i in range(count)])  47.8 us
    ppermute x31, starting transfers between devices, moved(): return lax.ppermute(block, 'req', [(i, partner(i)) for i in range(count)])  29.1 us
    pallas_call x2, Pallas kernels, ffn(): pl.pallas_call(ffn_body, out_shape=[jax.ShapeDtypeStruct((pair, held), jn...  14 us
    pallas_call x3, Pallas kernels, select(): pl.pallas_call(functools.partial(select_body, tokens, capacity, wanted),...  4.45 us
    unnamed x16, local copies, waits for them, and re-layouts  3.17 us
  transfers between devices with their start and end apart: 31, of which 23 were waited for; matrix products, arithmetic and copies ran while one was open for 1% of the time, Pallas kernels for 19%

profile of v7, /device:TPU:0, one launch (start us, length us, event | category | flops | bytes accessed | tf_op | source)
XLA Modules:
  0.0 106.2 jit_solution(6909888641803908097)
XLA Ops:
  0.0 0.8 reshape.34
  1.5 0.7 pad_convert_fusion
  2.4 0.9 copy-done.1
  3.3 0.8 shard_map.73
  4.6 0.9 collective-permute-done
  5.7 4.0 %collective-permute-start.1 = (bf16[32,1536]{1,0:T(8,128)(2,1)S(1)}, bf16[32,1536]{1,0:T(8,128)(2,1)S(1)}, u32[]{:S(2)}, u32[]{:S(2)}) collective-permute-start(bf16[32,1536]{1,0:T(8,128)(2,1)S(1)} %get-tuple-element.119._), channel_id=1, source_target_pairs={{0,16},{1,17},{2,18},{3,19},{4,20},{5,21},{6,22},{7,23},{8,24},{9,... | collective-permute-start | bytes 294920 | tf_op jit(solution)/shard_map/ppermute | solution.py:30
  9.7 1.6 %collective-permute-start.4 = (bf16[32,1536]{1,0:T(8,128)(2,1)S(1)}, bf16[32,1536]{1,0:T(8,128)(2,1)S(1)}, u32[]{:S(2)}, u32[]{:S(2)}) collective-permute-start(bf16[32,1536]{1,0:T(8,128)(2,1)S(1)} %get-tuple-element.119._), channel_id=1, source_target_pairs={{0,8},{1,9},{2,10},{3,11},{4,12},{5,13},{6,14},{7,15},{8,0},{9,1},... | collective-permute-start | bytes 294920 | tf_op jit(solution)/shard_map/ppermute | solution.py:30
  11.3 2.2 %copy-done = bf16[2880,720]{0,1:T(8,128)(2,1)S(1)} copy-done((bf16[2880,720]{0,1:T(8,128)(2,1)S(1)}, bf16[2880,720]{0,1:T(8,128)(2,1)}, u32[]{:S(2)}) %copy-start) | copy-done | bytes 4147224
  13.8 1.2 %collective-permute-done.1._ = bf16[32,1536]{1,0:T(8,128)(2,1)S(1)} collective-permute-done((bf16[32,1536]{1,0:T(8,128)(2,1)S(1)}, bf16[32,1536]{1,0:T(8,128)(2,1)S(1)}, u32[]{:S(2)}, u32[]{:S(2)}) %collective-permute-start.1) | collective-permute-done | bytes 98336 | tf_op jit(solution)/shard_map/ppermute | solution.py:30
  15.0 1.6 %collective-permute-start.3 = (bf16[32,1536]{1,0:T(8,128)(2,1)S(1)}, bf16[32,1536]{1,0:T(8,128)(2,1)S(1)}, u32[]{:S(2)}, u32[]{:S(2)}) collective-permute-start(bf16[32,1536]{1,0:T(8,128)(2,1)S(1)} %get-tuple-element.58), channel_id=1, source_target_pairs={{0,4},{1,3},{2,6},{3,1},{4,0},{5,7},{6,2},{7,5},{8,12},{9,11},{10,... | collective-permute-start | bytes 294920 | tf_op jit(solution)/shard_map/ppermute | solution.py:30
  17.6 3.6 %collective-permute-done.2 = bf16[32,1536]{1,0:T(8,128)(2,1)S(1)} collective-permute-done((bf16[32,1536]{1,0:T(8,128)(2,1)S(1)}, bf16[32,1536]{1,0:T(8,128)(2,1)S(1)}, u32[]{:S(2)}, u32[]{:S(2)}) %collective-permute-start.2) | collective-permute-done | bytes 98336 | tf_op jit(solution)/shard_map/ppermute | solution.py:30
  21.8 1.2 %collective-permute-done.5.tile_ref = bf16[128,128]{1,0:T(8,128)(2,1)S(1)} collective-permute-done((bf16[128,128]{1,0:T(8,128)(2,1)S(1)}, bf16[128,128]{1,0:T(8,128)(2,1)S(1)}, u32[]{:S(2)}, u32[]{:S(2)}) %collective-permute-start.5) | collective-permute-done | bytes 32800 | tf_op jit(solution)/shard_map/ppermute | solution.py:30
  23.0 1.4 %collective-permute-start.7 = (bf16[64,1536]{1,0:T(8,128)(2,1)S(1)}, bf16[64,1536]{1,0:T(8,128)(2,1)S(1)}, u32[]{:S(2)}, u32[]{:S(2)}) collective-permute-start(bf16[64,1536]{1,0:T(8,128)(2,1)S(1)} %pad_maximum_fusion.3), channel_id=1, source_target_pairs={{0,8},{1,9},{2,10},{3,11},{4,12},{5,13},{6,14},{7,15},{8,0},{9,1},... | collective-permute-start | bytes 589832 | tf_op jit(solution)/shard_map/ppermute | solution.py:30
  24.4 3.4 %collective-permute-start.6 = (bf16[64,1536]{1,0:T(8,128)(2,1)S(1)}, bf16[64,1536]{1,0:T(8,128)(2,1)S(1)}, u32[]{:S(2)}, u32[]{:S(2)}) collective-permute-start(bf16[64,1536]{1,0:T(8,128)(2,1)S(1)} %pad_maximum_fusion.3), channel_id=1, source_target_pairs={{0,16},{1,17},{2,18},{3,19},{4,20},{5,21},{6,22},{7,23},{8,24},{9,... | collective-permute-start | bytes 589832 | tf_op jit(solution)/shard_map/ppermute | solution.py:30
  27.8 1.3 %collective-permute-done.8.next_ref = bf16[128,1536]{1,0:T(8,128)(2,1)S(1)} collective-permute-done((bf16[128,1536]{1,0:T(8,128)(2,1)S(1)}, bf16[128,1536]{1,0:T(8,128)(2,1)S(1)}, u32[]{:S(2)}, u32[]{:S(2)}) %collective-permute-start.8) | collective-permute-done | bytes 393248 | tf_op jit(solution)/shard_map/ppermute | solution.py:30
  29.1 1.3 %shard_map.76 = (bf16[192,1536]{1,0:T(8,128)(2,1)S(1)}, f32[128,128]{1,0:T(8,128)S(1)}) custom-call(s32[3]{0:T(128)S(1)} %pad_add_fusion.places_ref._, bf16[128,128]{1,0:T(8,128)(2,1)S(1)} %slice.125.tile_ref, s32[3]{0:T(128)S(1)} %pad_add_fusion.places_ref._, bf16[128,1536]{1,0:T(8,128)(2,1)S(1)} %constant_dynamic-update-slice_fusion.near_ref, ...), custom_call_target="tpu_custom_call" | custom-call | flops 301989888 | bytes 1572864 | tf_op jit(solution)/shard_map/pallas_call | solution.py:101
  30.4 1.6 %collective-permute-start.10 = (bf16[192,1536]{1,0:T(8,128)(2,1)S(1)}, bf16[192,1536]{1,0:T(8,128)(2,1)S(1)}, u32[]{:S(2)}, u32[]{:S(2)}) collective-permute-start(bf16[192,1536]{1,0:T(8,128)(2,1)S(1)} %get-tuple-element.64._), channel_id=1, source_target_pairs={{0,2},{1,5},{2,0},{3,7},{4,6},{5,1},{6,4},{7,3},{8,10},{9,13},{10,... | collective-permute-start | bytes 1769480 | tf_op jit(solution)/shard_map/ppermute | solution.py:30
  32.0 1.5 %shard_map.77 = (bf16[192,1536]{1,0:T(8,128)(2,1)S(1)}, f32[128,128]{1,0:T(8,128)}, f32[128,128]{1,0:T(8,128)S(1)}) custom-call(s32[3]{0:T(128)S(1)} %pad_add_fusion.places_ref._, bf16[128,128]{1,0:T(8,128)(2,1)S(1)} %collective-permute-done.5.tile_ref, bf16[192,1536]{1,0:T(8,128)(2,1)S(1)} %get-tuple-element.64._, ...), custom_call_target="tpu_custom_call" | custom-call | flops 301989888 | bytes 1572864 | tf_op jit(solution)/shard_map/pallas_call | solution.py:101
  33.9 3.1 %collective-permute-done.6 = bf16[64,1536]{1,0:T(8,128)(2,1)S(1)} collective-permute-done((bf16[64,1536]{1,0:T(8,128)(2,1)S(1)}, bf16[64,1536]{1,0:T(8,128)(2,1)S(1)}, u32[]{:S(2)}, u32[]{:S(2)}) %collective-permute-start.6) | collective-permute-done | bytes 196640 | tf_op jit(solution)/shard_map/ppermute | solution.py:30
  37.9 4.8 %collective-permute-done.9 = bf16[64,1536]{1,0:T(8,128)(2,1)S(1)} collective-permute-done((bf16[64,1536]{1,0:T(8,128)(2,1)S(1)}, bf16[64,1536]{1,0:T(8,128)(2,1)S(1)}, u32[]{:S(2)}, u32[]{:S(2)}) %collective-permute-start.9) | collective-permute-done | bytes 196640 | tf_op jit(solution)/shard_map/ppermute | solution.py:30
  42.8 1.7 %shard_map.79 = (bf16[192,1536]{1,0:T(8,128)(2,1)S(1)}, bf16[192,1536]{1,0:T(8,128)(2,1)S(1)}, f32[128,128]{1,0:T(8,128)S(1)}, f32[128,128]{1,0:T(8,128)S(1)}) custom-call(s32[3]{0:T(128)S(1)} %pad_add_fusion.places_ref._, bf16[128,128]{1,0:T(8,128)(2,1)S(1)} %slice.126.tile_ref, s32[3]{0:T(128)S(1)} %pad_add_fusion.places_ref._, ...), custom_call_target="tpu_custom_call" | custom-call | flops 301989888 | bytes 1572864 | tf_op jit(solution)/shard_map/pallas_call | solution.py:101
  44.6 0.7 collective-permute-start.13
  45.3 1.3 %collective-permute-done.12.other_far_ref = bf16[192,1536]{1,0:T(8,128)(2,1)S(1)} collective-permute-done((bf16[192,1536]{1,0:T(8,128)(2,1)S(1)}, bf16[192,1536]{1,0:T(8,128)(2,1)S(1)}, u32[]{:S(2)}, u32[]{:S(2)}) %collective-permute-start.12) | collective-permute-done | bytes 589856 | tf_op jit(solution)/shard_map/ppermute | solution.py:30
  46.6 6.9 %shard_map.80 = (f32[192,1536]{1,0:T(8,128)S(1)}, f32[192,1536]{1,0:T(8,128)S(1)}, bf16[192,1536]{1,0:T(8,128)(2,1)S(1)}, bf16[192,1536]{1,0:T(8,128)(2,1)S(1)}) custom-call(s32[3]{0:T(128)S(1)} %pad_add_fusion.places_ref._, bf16[192,1536]{1,0:T(8,128)(2,1)S(1)} %get-tuple-element.68._.mine_near_ref, ...), custom_call_target="tpu_custom_call" | custom-call | flops 4777574400 | bytes 17160192 | tf_op jit(solution)/shard_map/pallas_call | solution.py:224
  53.5 1.1 collective-permute-done.13.mine_far_ref
  55.1 1.5 %collective-permute-done.16 = bf16[192,1536]{1,0:T(8,128)(2,1)S(1)} collective-permute-done((bf16[192,1536]{1,0:T(8,128)(2,1)S(1)}, bf16[192,1536]{1,0:T(8,128)(2,1)S(1)}, u32[]{:S(2)}, u32[]{:S(2)}) %collective-permute-start.16) | collective-permute-done | bytes 589856 | tf_op jit(solution)/shard_map/ppermute | solution.py:30
  56.7 0.7 collective-permute-start.17
  57.4 0.8 collective-permute-done.15.other_far_ref
  58.2 7.1 %shard_map.81 = (f32[192,1536]{1,0:T(8,128)S(1)}, f32[192,1536]{1,0:T(8,128)S(1)}, bf16[192,1536]{1,0:T(8,128)(2,1)S(1)}, bf16[192,1536]{1,0:T(8,128)(2,1)S(1)}) custom-call(s32[3]{0:T(128)S(1)} %pad_add_fusion.places_ref._, bf16[192,1536]{1,0:T(8,128)(2,1)S(1)} %get-tuple-element.70.mine_near_ref, ...), custom_call_target="tpu_custom_call" | custom-call | flops 4777574400 | bytes 17160192 | tf_op jit(solution)/shard_map/pallas_call | solution.py:224
  65.3 1.3 %collective-permute-done.17.arrived_ref = bf16[192,1536]{1,0:T(8,128)(2,1)S(1)} collective-permute-done((bf16[192,1536]{1,0:T(8,128)(2,1)S(1)}, bf16[192,1536]{1,0:T(8,128)(2,1)S(1)}, u32[]{:S(2)}, u32[]{:S(2)}) %collective-permute-start.17) | collective-permute-done | bytes 589856 | tf_op jit(solution)/shard_map/ppermute | solution.py:30
  67.1 1.5 %collective-permute-done.18 = bf16[192,1536]{1,0:T(8,128)(2,1)S(1)} collective-permute-done((bf16[192,1536]{1,0:T(8,128)(2,1)S(1)}, bf16[192,1536]{1,0:T(8,128)(2,1)S(1)}, u32[]{:S(2)}, u32[]{:S(2)}) %collective-permute-start.18) | collective-permute-done | bytes 589856 | tf_op jit(solution)/shard_map/ppermute | solution.py:30
  68.8 0.7 collective-permute-done.19.taken_ref
  70.1 0.8 collective-permute-start.20
  70.9 1.5 %collective-permute-start.22 = (bf16[192,1536]{1,0:T(8,128)(2,1)S(1)}, bf16[192,1536]{1,0:T(8,128)(2,1)S(1)}, u32[]{:S(2)}, u32[]{:S(2)}) collective-permute-start(bf16[192,1536]{1,0:T(8,128)(2,1)S(1)} %add_convert_fusion._), channel_id=1, source_target_pairs={{0,2},{1,5},{2,0},{3,7},{4,6},{5,1},{6,4},{7,3},{8,10},{9,13},{10,... | collective-permute-start | bytes 1769480 | tf_op jit(solution)/shard_map/ppermute | solution.py:30
  72.4 9.6 %collective-permute-done.20 = bf16[128,1536]{1,0:T(8,128)(2,1)S(1)} collective-permute-done((bf16[128,1536]{1,0:T(8,128)(2,1)S(1)}, bf16[128,1536]{1,0:T(8,128)(2,1)S(1)}, u32[]{:S(2)}, u32[]{:S(2)}) %collective-permute-start.20) | collective-permute-done | bytes 393248 | tf_op jit(solution)/shard_map/ppermute | solution.py:30
  82.0 1.4 %collective-permute-done.22.arrived_ref = bf16[192,1536]{1,0:T(8,128)(2,1)S(1)} collective-permute-done((bf16[192,1536]{1,0:T(8,128)(2,1)S(1)}, bf16[192,1536]{1,0:T(8,128)(2,1)S(1)}, u32[]{:S(2)}, u32[]{:S(2)}) %collective-permute-start.22) | collective-permute-done | bytes 589856 | tf_op jit(solution)/shard_map/ppermute | solution.py:30
  83.9 0.8 collective-permute-start.26
  85.2 1.0 collective-permute-start.23
  86.2 1.1 %collective-permute-start.24 = (bf16[32,1536]{1,0:T(8,128)(2,1)S(1)}, bf16[32,1536]{1,0:T(8,128)(2,1)S(1)}, u32[]{:S(2)}, u32[]{:S(2)}) collective-permute-start(bf16[32,1536]{1,0:T(8,128)(2,1)S(1)} %get-tuple-element.106), channel_id=1, source_target_pairs={{0,8},{1,9},{2,10},{3,11},{4,12},{5,13},{6,14},{7,15},{8,0},{9,1},... | collective-permute-start | bytes 294920 | tf_op jit(solution)/shard_map/ppermute | solution.py:30
  87.3 4.5 %collective-permute-done.26 = bf16[128,1536]{1,0:T(8,128)(2,1)S(1)} collective-permute-done((bf16[128,1536]{1,0:T(8,128)(2,1)S(1)}, bf16[128,1536]{1,0:T(8,128)(2,1)S(1)}, u32[]{:S(2)}, u32[]{:S(2)}) %collective-permute-start.26) | collective-permute-done | bytes 393248 | tf_op jit(solution)/shard_map/ppermute | solution.py:30
  91.9 0.9 collective-permute-start.28
  92.8 2.4 %collective-permute-start.25 = (bf16[32,1536]{1,0:T(8,128)(2,1)S(1)}, bf16[32,1536]{1,0:T(8,128)(2,1)S(1)}, u32[]{:S(2)}, u32[]{:S(2)}) collective-permute-start(bf16[32,1536]{1,0:T(8,128)(2,1)S(1)} %add_convert_fusion.2), channel_id=1, source_target_pairs={{0,16},{1,17},{2,18},{3,19},{4,20},{5,21},{6,22},{7,23},{8,24},{9,... | collective-permute-start | bytes 294920 | tf_op jit(solution)/shard_map/ppermute | solution.py:30
  95.7 2.6 %collective-permute-done.28 = bf16[32,1536]{1,0:T(8,128)(2,1)S(1)} collective-permute-done((bf16[32,1536]{1,0:T(8,128)(2,1)S(1)}, bf16[32,1536]{1,0:T(8,128)(2,1)S(1)}, u32[]{:S(2)}, u32[]{:S(2)}) %collective-permute-start.28) | collective-permute-done | bytes 98336 | tf_op jit(solution)/shard_map/ppermute | solution.py:30
  98.4 1.9 %collective-permute-start.29 = (bf16[32,1536]{1,0:T(8,128)(2,1)S(1)}, bf16[32,1536]{1,0:T(8,128)(2,1)S(1)}, u32[]{:S(2)}, u32[]{:S(2)}) collective-permute-start(bf16[32,1536]{1,0:T(8,128)(2,1)S(1)} %fusion.2), channel_id=1, source_target_pairs={{0,16},{1,17},{2,18},{3,19},{4,20},{5,21},{6,22},{7,23},{8,24},{9,... | collective-permute-start | bytes 294920 | tf_op jit(solution)/shard_map/ppermute | solution.py:30
  100.5 1.3 %collective-permute-done.27 = bf16[32,1536]{1,0:T(8,128)(2,1)S(1)} collective-permute-done((bf16[32,1536]{1,0:T(8,128)(2,1)S(1)}, bf16[32,1536]{1,0:T(8,128)(2,1)S(1)}, u32[]{:S(2)}, u32[]{:S(2)}) %collective-permute-start.27) | collective-permute-done | bytes 98336 | tf_op jit(solution)/shard_map/ppermute | solution.py:30
  101.8 2.1 %collective-permute-done.29 = bf16[32,1536]{1,0:T(8,128)(2,1)S(1)} collective-permute-done((bf16[32,1536]{1,0:T(8,128)(2,1)S(1)}, bf16[32,1536]{1,0:T(8,128)(2,1)S(1)}, u32[]{:S(2)}, u32[]{:S(2)}) %collective-permute-start.29) | collective-permute-done | bytes 98336 | tf_op jit(solution)/shard_map/ppermute | solution.py:30
  104.2 1.3 %collective-permute-done.30 = bf16[2,16,1536]{2,1,0:T(8,128)(2,1)S(1)} collective-permute-done((bf16[2,16,1536]{2,1,0:T(8,128)(2,1)S(1)}, bf16[2,16,1536]{2,1,0:T(8,128)(2,1)S(1)}, u32[]{:S(2)}, u32[]{:S(2)}) %collective-permute-start.30) | collective-permute-done | bytes 98336 | tf_op jit(solution)/shard_map/ppermute | solution.py:30
  105.5 0.7 fusion
  (82 shorter events, 8.9 us)
Async XLA Ops:
  2.4 0.9 copy-start.1
  3.3 13.9 %slice-start.2 = ((s8[4239360]{0:T(1024)(128)(4,1)}), s8[45056]{0:T(1024)(128)(4,1)S(1)}, s32[]{:S(2)}) async-start(s8[4239360]{0:T(1024)(128)(4,1)} %bitcast.25), calls=%async_computation.2 | async-start | bytes 90112
  4.1 1.5 %collective-permute-start = (bf16[2,16,1536]{2,1,0:T(8,128)(2,1)S(1)}, bf16[2,16,1536]{2,1,0:T(8,128)(2,1)S(1)}, u32[]{:S(2)}, u32[]{:S(2)}) collective-permute-start(bf16[2,16,1536]{2,1,0:T(8,128)(2,1)S(1)} %get-tuple-element.53), channel_id=1, source_target_pairs={{0,1},{1,0},{2,3},{3,2},{4,5},{5,4},{6,7},{7,6},{8,9},{9,8},{10,11... | collective-permute-start | bytes 294920 | tf_op jit(solution)/shard_map/ppermute | solution.py:30
  5.7 9.3 %collective-permute-start.1 = (bf16[32,1536]{1,0:T(8,128)(2,1)S(1)}, bf16[32,1536]{1,0:T(8,128)(2,1)S(1)}, u32[]{:S(2)}, u32[]{:S(2)}) collective-permute-start(bf16[32,1536]{1,0:T(8,128)(2,1)S(1)} %get-tuple-element.119._), channel_id=1, source_target_pairs={{0,16},{1,17},{2,18},{3,19},{4,20},{5,21},{6,22},{7,23},{8,24},{9,... | collective-permute-start | bytes 294920 | tf_op jit(solution)/shard_map/ppermute | solution.py:30
  9.7 7.5 %collective-permute-start.4 = (bf16[32,1536]{1,0:T(8,128)(2,1)S(1)}, bf16[32,1536]{1,0:T(8,128)(2,1)S(1)}, u32[]{:S(2)}, u32[]{:S(2)}) collective-permute-start(bf16[32,1536]{1,0:T(8,128)(2,1)S(1)} %get-tuple-element.119._), channel_id=1, source_target_pairs={{0,8},{1,9},{2,10},{3,11},{4,12},{5,13},{6,14},{7,15},{8,0},{9,1},... | collective-permute-start | bytes 294920 | tf_op jit(solution)/shard_map/ppermute | solution.py:30
  11.3 2.2 %copy-start = (bf16[2880,720]{0,1:T(8,128)(2,1)S(1)}, bf16[2880,720]{0,1:T(8,128)(2,1)}, u32[]{:S(2)}) copy-start(bf16[2880,720]{0,1:T(8,128)(2,1)} %param.9) | copy-start | bytes 12441604
  13.5 3.7 %slice-start.3 = ((s8[4239360]{0:T(1024)(128)(4,1)}), s8[4194304]{0:T(1024)(128)(4,1)S(1)}, s32[]{:S(2)}) async-start(s8[4239360]{0:T(1024)(128)(4,1)} %bitcast.25), calls=%async_computation.3 | async-start | bytes 8388608
  15.0 6.2 %collective-permute-start.3 = (bf16[32,1536]{1,0:T(8,128)(2,1)S(1)}, bf16[32,1536]{1,0:T(8,128)(2,1)S(1)}, u32[]{:S(2)}, u32[]{:S(2)}) collective-permute-start(bf16[32,1536]{1,0:T(8,128)(2,1)S(1)} %get-tuple-element.58), channel_id=1, source_target_pairs={{0,4},{1,3},{2,6},{3,1},{4,0},{5,7},{6,2},{7,5},{8,12},{9,11},{10,... | collective-permute-start | bytes 294920 | tf_op jit(solution)/shard_map/ppermute | solution.py:30
  16.6 4.6 %collective-permute-start.2 = (bf16[32,1536]{1,0:T(8,128)(2,1)S(1)}, bf16[32,1536]{1,0:T(8,128)(2,1)S(1)}, u32[]{:S(2)}, u32[]{:S(2)}) collective-permute-start(bf16[32,1536]{1,0:T(8,128)(2,1)S(1)} %collective-permute-done.1._), channel_id=1, source_target_pairs={{0,8},{1,9},{2,10},{3,11},{4,12},{5,13},{6,14},{7,15},{8,0},{9,1},... | collective-permute-start | bytes 294920 | tf_op jit(solution)/shard_map/ppermute | solution.py:30
  17.2 20.3 %slice-start = ((s8[4239360]{0:T(1024)(128)(4,1)}), s8[4194304]{0:T(1024)(128)(4,1)S(1)}, s32[]{:S(2)}) async-start(s8[4239360]{0:T(1024)(128)(4,1)} %bitcast.22), calls=%async_computation | async-start | bytes 8388608
  17.2 20.3 %slice-start.1 = ((s8[4239360]{0:T(1024)(128)(4,1)}), s8[45056]{0:T(1024)(128)(4,1)S(1)}, s32[]{:S(2)}) async-start(s8[4239360]{0:T(1024)(128)(4,1)} %bitcast.22), calls=%async_computation.1 | async-start | bytes 90112
  21.2 7.8 %collective-permute-start.8 = (bf16[128,1536]{1,0:T(8,128)(2,1)S(1)}, bf16[128,1536]{1,0:T(8,128)(2,1)S(1)}, u32[]{:S(2)}, u32[]{:S(2)}) collective-permute-start(bf16[128,1536]{1,0:T(8,128)(2,1)S(1)} %constant_dynamic-update-slice_fusion.near_ref), channel_id=1, source_target_pairs={{0,4},{1,3},{2,6},{3,1},{4,0},{5,7},{6,2},{7,5},{8,12},{9,11},{10,... | collective-permute-start | bytes 1179656 | tf_op jit(solution)/shard_map/ppermute | solution.py:30
  21.7 1.2 %collective-permute-start.5 = (bf16[128,128]{1,0:T(8,128)(2,1)S(1)}, bf16[128,128]{1,0:T(8,128)(2,1)S(1)}, u32[]{:S(2)}, u32[]{:S(2)}) collective-permute-start(bf16[128,128]{1,0:T(8,128)(2,1)S(1)} %slice.125.tile_ref), channel_id=1, source_target_pairs={{0,1},{1,0},{2,3},{3,2},{4,5},{5,4},{6,7},{7,6},{8,9},{9,8},{10,11... | collective-permute-start | bytes 98312 | tf_op jit(solution)/shard_map/ppermute | solution.py:30
  23.0 11.0 %collective-permute-start.7 = (bf16[64,1536]{1,0:T(8,128)(2,1)S(1)}, bf16[64,1536]{1,0:T(8,128)(2,1)S(1)}, u32[]{:S(2)}, u32[]{:S(2)}) collective-permute-start(bf16[64,1536]{1,0:T(8,128)(2,1)S(1)} %pad_maximum_fusion.3), channel_id=1, source_target_pairs={{0,8},{1,9},{2,10},{3,11},{4,12},{5,13},{6,14},{7,15},{8,0},{9,1},... | collective-permute-start | bytes 589832 | tf_op jit(solution)/shard_map/ppermute | solution.py:30
  24.4 12.6 %collective-permute-start.6 = (bf16[64,1536]{1,0:T(8,128)(2,1)S(1)}, bf16[64,1536]{1,0:T(8,128)(2,1)S(1)}, u32[]{:S(2)}, u32[]{:S(2)}) collective-permute-start(bf16[64,1536]{1,0:T(8,128)(2,1)S(1)} %pad_maximum_fusion.3), channel_id=1, source_target_pairs={{0,16},{1,17},{2,18},{3,19},{4,20},{5,21},{6,22},{7,23},{8,24},{9,... | collective-permute-start | bytes 589832 | tf_op jit(solution)/shard_map/ppermute | solution.py:30
  30.4 12.3 %collective-permute-start.10 = (bf16[192,1536]{1,0:T(8,128)(2,1)S(1)}, bf16[192,1536]{1,0:T(8,128)(2,1)S(1)}, u32[]{:S(2)}, u32[]{:S(2)}) collective-permute-start(bf16[192,1536]{1,0:T(8,128)(2,1)S(1)} %get-tuple-element.64._), channel_id=1, source_target_pairs={{0,2},{1,5},{2,0},{3,7},{4,6},{5,1},{6,4},{7,3},{8,10},{9,13},{10,... | collective-permute-start | bytes 1769480 | tf_op jit(solution)/shard_map/ppermute | solution.py:30
  37.0 5.7 %collective-permute-start.9 = (bf16[64,1536]{1,0:T(8,128)(2,1)S(1)}, bf16[64,1536]{1,0:T(8,128)(2,1)S(1)}, u32[]{:S(2)}, u32[]{:S(2)}) collective-permute-start(bf16[64,1536]{1,0:T(8,128)(2,1)S(1)} %collective-permute-done.6), channel_id=1, source_target_pairs={{0,8},{1,9},{2,10},{3,11},{4,12},{5,13},{6,14},{7,15},{8,0},{9,1},... | collective-permute-start | bytes 589832 | tf_op jit(solution)/shard_map/ppermute | solution.py:30
  37.4 7.9 %collective-permute-start.11 = (bf16[192,1536]{1,0:T(8,128)(2,1)S(1)}, bf16[192,1536]{1,0:T(8,128)(2,1)S(1)}, u32[]{:S(2)}, u32[]{:S(2)}) collective-permute-start(bf16[192,1536]{1,0:T(8,128)(2,1)S(1)} %get-tuple-element.68._.mine_near_ref), channel_id=1, source_target_pairs={{0,1},{1,0},{2,3},{3,2},{4,5},{5,4},{6,7},{7,6},{8,9},{9,8},{10,11... | collective-permute-start | bytes 1769480 | tf_op jit(solution)/shard_map/ppermute | solution.py:30
  44.5 2.1 %collective-permute-start.12 = (bf16[192,1536]{1,0:T(8,128)(2,1)S(1)}, bf16[192,1536]{1,0:T(8,128)(2,1)S(1)}, u32[]{:S(2)}, u32[]{:S(2)}) collective-permute-start(bf16[192,1536]{1,0:T(8,128)(2,1)S(1)} %collective-permute-done.10.mine_far_ref), channel_id=1, source_target_pairs={{0,1},{1,0},{2,3},{3,2},{4,5},{5,4},{6,7},{7,6},{8,9},{9,8},{10,11... | collective-permute-start | bytes 1769480 | tf_op jit(solution)/shard_map/ppermute | solution.py:30
  44.6 9.9 %collective-permute-start.13 = (bf16[192,1536]{1,0:T(8,128)(2,1)S(1)}, bf16[192,1536]{1,0:T(8,128)(2,1)S(1)}, u32[]{:S(2)}, u32[]{:S(2)}) collective-permute-start(bf16[192,1536]{1,0:T(8,128)(2,1)S(1)} %get-tuple-element.78), channel_id=1, source_target_pairs={{0,2},{1,5},{2,0},{3,7},{4,6},{5,1},{6,4},{7,3},{8,10},{9,13},{10,... | collective-permute-start | bytes 1769480 | tf_op jit(solution)/shard_map/ppermute | solution.py:30
  54.5 2.0 %collective-permute-start.16 = (bf16[192,1536]{1,0:T(8,128)(2,1)S(1)}, bf16[192,1536]{1,0:T(8,128)(2,1)S(1)}, u32[]{:S(2)}, u32[]{:S(2)}) collective-permute-start(bf16[192,1536]{1,0:T(8,128)(2,1)S(1)} %get-tuple-element.81), channel_id=1, source_target_pairs={{0,1},{1,0},{2,3},{3,2},{4,5},{5,4},{6,7},{7,6},{8,9},{9,8},{10,11... | collective-permute-start | bytes 1769480 | tf_op jit(solution)/shard_map/ppermute | solution.py:30
  54.5 3.7 %collective-permute-start.14 = (bf16[192,1536]{1,0:T(8,128)(2,1)S(1)}, bf16[192,1536]{1,0:T(8,128)(2,1)S(1)}, u32[]{:S(2)}, u32[]{:S(2)}) collective-permute-start(bf16[192,1536]{1,0:T(8,128)(2,1)S(1)} %get-tuple-element.70.mine_near_ref), channel_id=1, source_target_pairs={{0,1},{1,0},{2,3},{3,2},{4,5},{5,4},{6,7},{7,6},{8,9},{9,8},{10,11... | collective-permute-start | bytes 1769480 | tf_op jit(solution)/shard_map/ppermute | solution.py:30
  55.0 3.2 %collective-permute-start.15 = (bf16[192,1536]{1,0:T(8,128)(2,1)S(1)}, bf16[192,1536]{1,0:T(8,128)(2,1)S(1)}, u32[]{:S(2)}, u32[]{:S(2)}) collective-permute-start(bf16[192,1536]{1,0:T(8,128)(2,1)S(1)} %collective-permute-done.13.mine_far_ref), channel_id=1, source_target_pairs={{0,1},{1,0},{2,3},{3,2},{4,5},{5,4},{6,7},{7,6},{8,9},{9,8},{10,11... | collective-permute-start | bytes 1769480 | tf_op jit(solution)/shard_map/ppermute | solution.py:30
  56.7 9.9 %collective-permute-start.17 = (bf16[192,1536]{1,0:T(8,128)(2,1)S(1)}, bf16[192,1536]{1,0:T(8,128)(2,1)S(1)}, u32[]{:S(2)}, u32[]{:S(2)}) collective-permute-start(bf16[192,1536]{1,0:T(8,128)(2,1)S(1)} %add_convert_fusion.1), channel_id=1, source_target_pairs={{0,2},{1,5},{2,0},{3,7},{4,6},{5,1},{6,4},{7,3},{8,10},{9,13},{10,... | collective-permute-start | bytes 1769480 | tf_op jit(solution)/shard_map/ppermute | solution.py:30
  66.6 2.0 %collective-permute-start.18 = (bf16[192,1536]{1,0:T(8,128)(2,1)S(1)}, bf16[192,1536]{1,0:T(8,128)(2,1)S(1)}, u32[]{:S(2)}, u32[]{:S(2)}) collective-permute-start(bf16[192,1536]{1,0:T(8,128)(2,1)S(1)} %get-tuple-element.85), channel_id=1, source_target_pairs={{0,1},{1,0},{2,3},{3,2},{4,5},{5,4},{6,7},{7,6},{8,9},{9,8},{10,11... | collective-permute-start | bytes 1769480 | tf_op jit(solution)/shard_map/ppermute | solution.py:30
  66.6 2.8 %collective-permute-start.19 = (bf16[192,1536]{1,0:T(8,128)(2,1)S(1)}, bf16[192,1536]{1,0:T(8,128)(2,1)S(1)}, u32[]{:S(2)}, u32[]{:S(2)}) collective-permute-start(bf16[192,1536]{1,0:T(8,128)(2,1)S(1)} %get-tuple-element.89), channel_id=1, source_target_pairs={{0,1},{1,0},{2,3},{3,2},{4,5},{5,4},{6,7},{7,6},{8,9},{9,8},{10,11... | collective-permute-start | bytes 1769480 | tf_op jit(solution)/shard_map/ppermute | solution.py:30
  70.1 11.8 %collective-permute-start.20 = (bf16[128,1536]{1,0:T(8,128)(2,1)S(1)}, bf16[128,1536]{1,0:T(8,128)(2,1)S(1)}, u32[]{:S(2)}, u32[]{:S(2)}) collective-permute-start(bf16[128,1536]{1,0:T(8,128)(2,1)S(1)} %get-tuple-element.92), channel_id=1, source_target_pairs={{0,4},{1,3},{2,6},{3,1},{4,0},{5,7},{6,2},{7,5},{8,12},{9,11},{10,... | collective-permute-start | bytes 1179656 | tf_op jit(solution)/shard_map/ppermute | solution.py:30
  70.9 11.1 %collective-permute-start.21 = (bf16[192,1536]{1,0:T(8,128)(2,1)S(1)}, bf16[192,1536]{1,0:T(8,128)(2,1)S(1)}, u32[]{:S(2)}, u32[]{:S(2)}) collective-permute-start(bf16[192,1536]{1,0:T(8,128)(2,1)S(1)} %get-tuple-element.96), channel_id=1, source_target_pairs={{0,1},{1,0},{2,3},{3,2},{4,5},{5,4},{6,7},{7,6},{8,9},{9,8},{10,11... | collective-permute-start | bytes 1769480 | tf_op jit(solution)/shard_map/ppermute | solution.py:30
  70.9 12.6 %collective-permute-start.22 = (bf16[192,1536]{1,0:T(8,128)(2,1)S(1)}, bf16[192,1536]{1,0:T(8,128)(2,1)S(1)}, u32[]{:S(2)}, u32[]{:S(2)}) collective-permute-start(bf16[192,1536]{1,0:T(8,128)(2,1)S(1)} %add_convert_fusion._), channel_id=1, source_target_pairs={{0,2},{1,5},{2,0},{3,7},{4,6},{5,1},{6,4},{7,3},{8,10},{9,13},{10,... | collective-permute-start | bytes 1769480 | tf_op jit(solution)/shard_map/ppermute | solution.py:30
  83.9 7.8 %collective-permute-start.26 = (bf16[128,1536]{1,0:T(8,128)(2,1)S(1)}, bf16[128,1536]{1,0:T(8,128)(2,1)S(1)}, u32[]{:S(2)}, u32[]{:S(2)}) collective-permute-start(bf16[128,1536]{1,0:T(8,128)(2,1)S(1)} %shard_map.83._), channel_id=1, source_target_pairs={{0,4},{1,3},{2,6},{3,1},{4,0},{5,7},{6,2},{7,5},{8,12},{9,11},{10,... | collective-permute-start | bytes 1179656 | tf_op jit(solution)/shard_map/ppermute | solution.py:30
  85.2 15.1 %collective-permute-start.23 = (bf16[32,1536]{1,0:T(8,128)(2,1)S(1)}, bf16[32,1536]{1,0:T(8,128)(2,1)S(1)}, u32[]{:S(2)}, u32[]{:S(2)}) collective-permute-start(bf16[32,1536]{1,0:T(8,128)(2,1)S(1)} %get-tuple-element.105), channel_id=1, source_target_pairs={{0,8},{1,9},{2,10},{3,11},{4,12},{5,13},{6,14},{7,15},{8,0},{9,1},... | collective-permute-start | bytes 294920 | tf_op jit(solution)/shard_map/ppermute | solution.py:30
  86.2 6.6 %collective-permute-start.24 = (bf16[32,1536]{1,0:T(8,128)(2,1)S(1)}, bf16[32,1536]{1,0:T(8,128)(2,1)S(1)}, u32[]{:S(2)}, u32[]{:S(2)}) collective-permute-start(bf16[32,1536]{1,0:T(8,128)(2,1)S(1)} %get-tuple-element.106), channel_id=1, source_target_pairs={{0,8},{1,9},{2,10},{3,11},{4,12},{5,13},{6,14},{7,15},{8,0},{9,1},... | collective-permute-start | bytes 294920 | tf_op jit(solution)/shard_map/ppermute | solution.py:30
  91.9 6.5 %collective-permute-start.28 = (bf16[32,1536]{1,0:T(8,128)(2,1)S(1)}, bf16[32,1536]{1,0:T(8,128)(2,1)S(1)}, u32[]{:S(2)}, u32[]{:S(2)}) collective-permute-start(bf16[32,1536]{1,0:T(8,128)(2,1)S(1)} %get-tuple-element.108), channel_id=1, source_target_pairs={{0,8},{1,9},{2,10},{3,11},{4,12},{5,13},{6,14},{7,15},{8,0},{9,1},... | collective-permute-start | bytes 294920 | tf_op jit(solution)/shard_map/ppermute | solution.py:30
  92.8 7.7 %collective-permute-start.25 = (bf16[32,1536]{1,0:T(8,128)(2,1)S(1)}, bf16[32,1536]{1,0:T(8,128)(2,1)S(1)}, u32[]{:S(2)}, u32[]{:S(2)}) collective-permute-start(bf16[32,1536]{1,0:T(8,128)(2,1)S(1)} %add_convert_fusion.2), channel_id=1, source_target_pairs={{0,16},{1,17},{2,18},{3,19},{4,20},{5,21},{6,22},{7,23},{8,24},{9,... | collective-permute-start | bytes 294920 | tf_op jit(solution)/shard_map/ppermute | solution.py:30
  95.2 6.6 %collective-permute-start.27 = (bf16[32,1536]{1,0:T(8,128)(2,1)S(1)}, bf16[32,1536]{1,0:T(8,128)(2,1)S(1)}, u32[]{:S(2)}, u32[]{:S(2)}) collective-permute-start(bf16[32,1536]{1,0:T(8,128)(2,1)S(1)} %get-tuple-element.107), channel_id=1, source_target_pairs={{0,8},{1,9},{2,10},{3,11},{4,12},{5,13},{6,14},{7,15},{8,0},{9,1},... | collective-permute-start | bytes 294920 | tf_op jit(solution)/shard_map/ppermute | solution.py:30
  98.4 5.6 %collective-permute-start.29 = (bf16[32,1536]{1,0:T(8,128)(2,1)S(1)}, bf16[32,1536]{1,0:T(8,128)(2,1)S(1)}, u32[]{:S(2)}, u32[]{:S(2)}) collective-permute-start(bf16[32,1536]{1,0:T(8,128)(2,1)S(1)} %fusion.2), channel_id=1, source_target_pairs={{0,16},{1,17},{2,18},{3,19},{4,20},{5,21},{6,22},{7,23},{8,24},{9,... | collective-permute-start | bytes 294920 | tf_op jit(solution)/shard_map/ppermute | solution.py:30
  104.0 1.5 %copy-start.2 = (bf16[2,16,2880]{2,1,0:T(8,128)(2,1)S(1)}, bf16[2,16,2880]{2,1,0:T(8,128)(2,1)}, u32[]{:S(2)}) copy-start(bf16[2,16,2880]{2,1,0:T(8,128)(2,1)} %hidden_ref.1) | copy-start | bytes 552964
  104.0 1.4 %collective-permute-start.30 = (bf16[2,16,1536]{2,1,0:T(8,128)(2,1)S(1)}, bf16[2,16,1536]{2,1,0:T(8,128)(2,1)S(1)}, u32[]{:S(2)}, u32[]{:S(2)}) collective-permute-start(bf16[2,16,1536]{2,1,0:T(8,128)(2,1)S(1)} %select_convert_fusion), channel_id=1, source_target_pairs={{0,1},{1,0},{2,3},{3,2},{4,5},{5,4},{6,7},{7,6},{8,9},{9,8},{10,11... | collective-permute-start | bytes 294920 | tf_op jit(solution)/shard_map/ppermute | solution.py:30

commit v8 on v5

--- a/solution.py
+++ b/solution.py
@@ -106,7 +106,7 @@
     )(places, near, following)
 
 
-def merge_body(wanted, near_slots_ref, next_slots_ref, keep_ref, taken_ref, arrived_ref, *out_refs):
+def merge_body(wanted, _, near_slots_ref, next_slots_ref, keep_ref, taken_ref, arrived_ref, *out_refs):
     rows = out_refs[0].shape[0]
     compact = keep_ref.shape[0]
     column = lax.broadcasted_iota(jnp.int32, (rows, compact), 1).astype(jnp.float32)
@@ -120,47 +120,81 @@
         out_ref[...] = result.astype(out_ref.dtype)
 
 
-def merge(wanted, types, slots, keep, taken, arrived):
+def merge(wanted, types, slots, keep, taken, arrived, token=None):
+    token = slots[0] if token is None else token
     rows = slots[0].shape[0]
     compact, held = keep.shape
     return pl.pallas_call(
         functools.partial(merge_body, wanted),
         out_shape=[jax.ShapeDtypeStruct((rows, held), kind) for kind in types],
-        in_specs=whole_arrays(5),
+        in_specs=[pl.BlockSpec(memory_space=pl.ANY)] + whole_arrays(5),
         out_specs=whole_arrays(len(types)),
         compiler_params=pltpu.CompilerParams(vmem_limit_bytes=20 * 2**20),
         cost_estimate=pl.CostEstimate(flops=8 * rows * compact * held, bytes_accessed=8 * rows * held, transcendentals=0),
-    )(*slots, keep, taken, arrived)
+    )(token, *slots, keep, taken, arrived)
+
+
+def add_products(places_ref, mine_ref, other_ref, weights_ref, mine_to, other_to, total_ref, fresh):
+    width = weights_ref.shape[1]
+    first, second, _ = split_widths(width)
+    quad = mine_ref.shape[0] // 2
+
+    def add(mine_columns, other_columns):
+        pieces = []
+        for ref, (start, size), places in (
+            (mine_ref, mine_columns, mine_to), (other_ref, other_columns, other_to)
+        ):
+            product = lax.dot_general(
+                ref[:, :size], weights_ref[:, start : start + size], across, preferred_element_type=jnp.float32
+            )
+            pieces += [(place, product[block * quad : (block + 1) * quad]) for block, place in enumerate(places)]
+        seen = set()
+        for place, piece in pieces:
+            there = pl.ds(place * quad, quad)
+            if place in fresh and place not in seen:
+                total_ref[there, :] = piece
+            else:
+                total_ref[there, :] += piece
+            seen.add(place)
+
+    lower = places_ref[0] == 0
+
+    @pl.when(lower)
+    def _():
+        add((0, first), (first, second))
+
+    @pl.when(jnp.logical_not(lower))
+    def _():
+        add((first, second), (0, first))
+
+
+def start_body(places_ref, _, mine_ref, other_ref, gate_v, up_v, gate_ref, up_ref):
+    for weights_ref, total_ref in ((gate_v, gate_ref), (up_v, up_ref)):
+        add_products(places_ref, mine_ref, other_ref, weights_ref, (0, 1), (0, 2), total_ref, (0, 1, 2))
+
+
+def ffn_start(places, mine, other, gate_v, up_v, token=None):
+    pair = mine.shape[0]
+    hidden, width = gate_v.shape
+    return pl.pallas_call(
+        start_body,
+        out_shape=[jax.ShapeDtypeStruct((pair // 2 * 3, hidden), jnp.float32)] * 2,
+        in_specs=[SCALARS, pl.BlockSpec(memory_space=pl.ANY)] + whole_arrays(4),
+        out_specs=whole_arrays(2),
+        compiler_params=pltpu.CompilerParams(vmem_limit_bytes=20 * 2**20),
+        cost_estimate=pl.CostEstimate(flops=4 * pair * width * hidden, bytes_accessed=4 * width * hidden, transcendentals=0),
+    )(places, places if token is None else token, mine, other, gate_v, up_v)
 
 
 def ffn_body(
-    places_ref, mine_near_ref, mine_far_ref, other_near_ref, other_far_ref, gate_v, up_v, down_v,
-    keep_near_ref, keep_far_ref, send_near_ref, send_far_ref, rows_v, act_v,
+    places_ref, gate_part_ref, up_part_ref, mine_near_ref, mine_far_ref, other_far_ref, gate_v, up_v, down_v,
+    keep_near_ref, keep_far_ref, send_near_ref, send_far_ref, gate_acc, up_acc, act_v,
 ):
     hidden, width = gate_v.shape
     first, second, held = split_widths(width)
     pair = mine_near_ref.shape[0]
     quad = pair // 2
-    chunk = hidden // 3
-    def lay(near, far_ref, swapped, start, size):
-        for place in range(4):
-            if swapped:
-                source, block = (near, far_ref)[place % 2], place // 2
-            else:
-                source, block = (near, far_ref)[place // 2], place % 2
-            rows_v[pl.ds(place * quad, quad), start : start + size] = source[pl.ds(block * quad, quad), :size]
-
     lower = places_ref[0] == 0
-
-    @pl.when(lower)
-    def _():
-        lay(mine_near_ref, mine_far_ref, False, 0, first)
-        lay(other_near_ref, other_far_ref, True, first, second)
-
-    @pl.when(jnp.logical_not(lower))
-    def _():
-        lay(other_near_ref, other_far_ref, True, 0, first)
-        lay(mine_near_ref, mine_far_ref, False, first, second)
 
     tile = jnp.concatenate([mine_near_ref[:, held - LANES :], mine_far_ref[:, held - LANES :]], axis=0)
     tile = tile.astype(jnp.float32)
@@ -171,11 +205,11 @@
         jnp.where(chosen, pltpu.roll(tile, LANES - ROUTING // 2, 1), 0.0), axis=1, keepdims=True
     )
 
-    for part in range(3):
-        there = slice(part * chunk, (part + 1) * chunk)
-        gate = lax.dot_general(rows_v[...], gate_v[there, :], across, preferred_element_type=jnp.float32)
-        up = lax.dot_general(rows_v[...], up_v[there, :], across, preferred_element_type=jnp.float32)
-        act_v[:, there] = ((up + 1.0) * gate * jax.nn.sigmoid(swish_scale * gate)).astype(jnp.bfloat16)
+    for part_ref, weights_ref, total_ref in ((gate_part_ref, gate_v, gate_acc), (up_part_ref, up_v, up_acc)):
+        total_ref[pl.ds(0, 3 * quad), :] = part_ref[...]
+        add_products(places_ref, mine_far_ref, other_far_ref, weights_ref, (2, 3), (1, 3), total_ref, (3,))
+    gate = gate_acc[...]
+    act_v[...] = ((up_acc[...] + 1.0) * gate * jax.nn.sigmoid(swish_scale * gate)).astype(jnp.bfloat16)
 
     def keep_half(result, size):
         keep_near_ref[:, :size] = result[:pair]
@@ -214,27 +248,28 @@
         keep_half(high, second)
 
 
-def ffn(places, mine_near, mine_far, other_near, other_far, gate_t, up_t, w_down):
+def ffn(places, parts, mine_near, mine_far, other_far, gate_v, up_v, down_v):
     pair, held = mine_near.shape
-    hidden, width = gate_t.shape
+    hidden, width = gate_v.shape
     total = 2 * pair
     return pl.pallas_call(
         ffn_body,
         out_shape=[jax.ShapeDtypeStruct((pair, held), jnp.float32)] * 2
         + [jax.ShapeDtypeStruct((pair, held), jnp.bfloat16)] * 2,
-        in_specs=[SCALARS] + whole_arrays(7),
+        in_specs=[SCALARS] + whole_arrays(8),
         out_specs=whole_arrays(4),
         scratch_shapes=[
-            pltpu.VMEM((total, width), jnp.bfloat16),
+            pltpu.VMEM((total, hidden), jnp.float32),
+            pltpu.VMEM((total, hidden), jnp.float32),
             pltpu.VMEM((total, hidden), jnp.bfloat16),
         ],
         compiler_params=pltpu.CompilerParams(vmem_limit_bytes=20 * 2**20),
         cost_estimate=pl.CostEstimate(
-            flops=6 * total * width * hidden,
+            flops=4 * total * width * hidden,
             bytes_accessed=6 * width * hidden + 8 * total * held,
             transcendentals=total * hidden,
         ),
-    )(places, mine_near, mine_far, other_near, other_far, gate_t, up_t, w_down)
+    )(places, *parts, mine_near, mine_far, other_far, gate_v, up_v, down_v)
 
 
 def preload_body(_, *refs):
@@ -400,8 +435,9 @@
         *blocks, last["own"] = tied(*blocks, last["own"])
         column = join(pair, *blocks)
         following = moved(column, first_axis)
+        last["parts"] = ffn_start(places, last["own"], moved(last["own"], other_core), gate_v, up_v)
         if down_v is None:
-            (down_v,) = preload(last["own"], w_down)
+            (down_v,) = preload(last["parts"][0], w_down)
             following, down_v = tied(following, down_v)
         states.append({"near": column, "next": following})
     second_hop(states[-1], False)
@@ -409,50 +445,48 @@
         (down_v,) = preload(states[-1]["own"], w_down)
 
     hops = []
-    before = None
     for state in states:
         own, arrived = state["own"], state["arrived"]
-        if before is not None:
-            arrived, *before = tied(arrived, *before)
-            hops.append(before)
-        before = ffn(places, own, arrived, moved(own, other_core), moved(arrived, other_core), gate_v, up_v, down_v)
-    hops.append(before)
+        if "parts" not in state:
+            token = hops[-1][1] if hops else None
+            state["parts"] = ffn_start(places, own, moved(own, other_core), gate_v, up_v, token)
+        if hops:
+            arrived, *state["parts"] = tied(arrived, *state["parts"])
+        hops.append(
+            ffn(places, state["parts"], own, arrived, moved(arrived, other_core), gate_v, up_v, down_v)
+        )
 
     def rounded_sum(a, b):
         return (a + b.astype(jnp.float32)).astype(jnp.bfloat16)
 
-    def far_total(block, earlier):
+    def far_hop(block):
         block = block.reshape(distant, -1, held)
         if distant == 4:
-            if earlier:
-                block, earlier[-1]["crossing"] = tied(block, earlier[-1]["crossing"])
             through = moved(block[3].astype(jnp.bfloat16), far(1))
             beside = moved(block[1].astype(jnp.bfloat16), far(1))
-            return {"kept": block[0], "arrivals": [beside], "crossing": rounded_sum(block[2], through)}
-        return {
-            "kept": block[0],
-            "arrivals": [moved(block[j].astype(jnp.bfloat16), far(j)) for j in range(1, distant)],
-            "crossing": None,
-        }
-
-    def settled(total):
-        kept, arrivals = total["kept"], list(total["arrivals"])
-        if total["crossing"] is not None:
-            arrivals.append(moved(total["crossing"], far(2)))
-        for arrival in arrivals:
+            return [block[0], [beside], rounded_sum(block[2], through)]
+        return [block[0], [moved(block[j].astype(jnp.bfloat16), far(j)) for j in range(1, distant)], None]
+
+    def settled(kept, arrivals, cross):
+        for arrival in arrivals if cross is None else arrivals + [moved(cross, far(2))]:
             kept = kept + arrival.astype(jnp.float32)
         return kept
 
-    sums = []
+    totals = []
+    near = None
     for state, (keep_near, keep_far, send_near, send_far) in zip(states, hops):
         give = rounded_sum(keep_far, moved(send_far, other_core))
-        near, following = merge(
-            (0, 1), (jnp.float32, jnp.bfloat16), state["slots"], keep_near, moved(send_near, other_core),
-            moved(give, second_axis),
-        )
-        near = near + moved(following, first_axis).astype(jnp.float32)
-        sums.append(far_total(near, sums))
-    sums = jnp.stack([settled(total) for total in sums])
+        parts = state["slots"], keep_near, moved(send_near, other_core), moved(give, second_axis)
+        if near is None:
+            kept, following = merge((0, 1), (jnp.float32, jnp.bfloat16), *parts)
+        else:
+            (following,) = merge((1,), (jnp.bfloat16,), *parts)
+            (kept,) = merge((0,), (jnp.float32,), *parts, following)
+            near, kept = tied(near, kept)
+            totals.append(far_hop(near))
+        near = kept + moved(following, first_axis).astype(jnp.float32)
+    totals.append(far_hop(near))
+    sums = jnp.stack([settled(*total) for total in totals])
     own = jnp.where(lower, sums[:, :tokens], sums[:, tokens:])
     give = jnp.where(lower, sums[:, tokens:], sums[:, :tokens]).astype(jnp.bfloat16)
     taken = moved(give, other_core).astype(jnp.float32)

time: 104 us -> 105 us (level)
  waiting for transfers between devices: 42.7 us -> 33.9 us
  Pallas kernels: 21.5 us -> 27.2 us
  starting transfers between devices: 32.3 us -> 36.2 us
    ppermute x30, waiting for transfers between devices: 42.7 us -> 33.9 us  [moved(): return lax.ppermute(block, 'req', [(i, partner(i)) for i in range(count)])]
    pallas_call x0 -> x2, Pallas kernels: none -> 6.85 us  [ffn_start(): pl.pallas_call(start_body, out_shape=[jax.ShapeDtypeStruct((pair // 2 * 3...]
    ppermute x30, starting transfers between devices: 32.3 us -> 36.2 us  [moved(): return lax.ppermute(block, 'req', [(i, partner(i)) for i in range(count)])]
    pallas_call x2, Pallas kernels: 14 us -> 12.6 us  [ffn(): pl.pallas_call(ffn_body, out_shape=[jax.ShapeDtypeStruct((pair, held), jn...]
  transfers between devices with their start and end apart: 30 -> 30, of which waited for: 20 -> 18; matrix products, arithmetic and copies ran while one was open for 1% -> 1% of each run, Pallas kernels for 20% -> 25%
where the time goes in v8:
time: 105 us
  starting transfers between devices  36.2 us (34%)
  waiting for transfers between devices  33.9 us (32%)
  Pallas kernels  27.2 us (26%)
  local copies, waits for them, and re-layouts  4.09 us (4%)
  other arithmetic  2.98 us (3%)
    ppermute x30, starting transfers between devices, moved(): return lax.ppermute(block, 'req', [(i, partner(i)) for i in range(count)])  36.2 us
    ppermute x30, waiting for transfers between devices, moved(): return lax.ppermute(block, 'req', [(i, partner(i)) for i in range(count)])  33.9 us
    pallas_call x2, Pallas kernels, ffn(): pl.pallas_call(ffn_body, out_shape=[jax.ShapeDtypeStruct((pair, held), jn...  12.6 us
    pallas_call x2, Pallas kernels, ffn_start(): pl.pallas_call(start_body, out_shape=[jax.ShapeDtypeStruct((pair // 2 * 3...  6.85 us
    pallas_call x3, Pallas kernels, select(): pl.pallas_call(functools.partial(select_body, tokens, capacity, wanted),...  4.33 us
    unnamed x19, local copies, waits for them, and re-layouts  3.19 us
  transfers between devices with their start and end apart: 30, of which 18 were waited for; matrix products, arithmetic and copies ran while one was open for 1% of the time, Pallas kernels for 25%

profile of v8, /device:TPU:0, one launch (start us, length us, event | category | flops | bytes accessed | tf_op | source)
XLA Modules:
  0.0 104.8 jit_solution(4652550124253036350)
XLA Ops:
  0.0 0.8 reshape.34
  0.8 0.7 convert_bitcast_fusion
  1.5 0.7 pad_convert_fusion
  2.4 0.9 copy-done.1
  3.3 0.8 shard_map.73
  4.6 0.9 collective-permute-done
  5.6 4.0 %collective-permute-start.2 = (bf16[32,1536]{1,0:T(8,128)(2,1)S(1)}, bf16[32,1536]{1,0:T(8,128)(2,1)S(1)}, u32[]{:S(2)}, u32[]{:S(2)}) collective-permute-start(bf16[32,1536]{1,0:T(8,128)(2,1)S(1)} %pad_maximum_fusion.2._), channel_id=1, source_target_pairs={{0,16},{1,17},{2,18},{3,19},{4,20},{5,21},{6,22},{7,23},{8,24},{9,... | collective-permute-start | bytes 294920 | tf_op jit(solution)/shard_map/ppermute | solution.py:30
  9.7 1.6 %collective-permute-start.1 = (bf16[32,1536]{1,0:T(8,128)(2,1)S(1)}, bf16[32,1536]{1,0:T(8,128)(2,1)S(1)}, u32[]{:S(2)}, u32[]{:S(2)}) collective-permute-start(bf16[32,1536]{1,0:T(8,128)(2,1)S(1)} %pad_maximum_fusion.2._), channel_id=1, source_target_pairs={{0,8},{1,9},{2,10},{3,11},{4,12},{5,13},{6,14},{7,15},{8,0},{9,1},... | collective-permute-start | bytes 294920 | tf_op jit(solution)/shard_map/ppermute | solution.py:30
  11.3 2.2 %copy-done = bf16[2880,720]{0,1:T(8,128)(2,1)S(1)} copy-done((bf16[2880,720]{0,1:T(8,128)(2,1)S(1)}, bf16[2880,720]{0,1:T(8,128)(2,1)}, u32[]{:S(2)}) %copy-start) | copy-done | bytes 4147224
  13.8 1.2 %collective-permute-done.2._ = bf16[32,1536]{1,0:T(8,128)(2,1)S(1)} collective-permute-done((bf16[32,1536]{1,0:T(8,128)(2,1)S(1)}, bf16[32,1536]{1,0:T(8,128)(2,1)S(1)}, u32[]{:S(2)}, u32[]{:S(2)}) %collective-permute-start.2) | collective-permute-done | bytes 98336 | tf_op jit(solution)/shard_map/ppermute | solution.py:30
  15.0 0.6 collective-permute-start.3
  16.0 3.6 %collective-permute-done.3 = bf16[32,1536]{1,0:T(8,128)(2,1)S(1)} collective-permute-done((bf16[32,1536]{1,0:T(8,128)(2,1)S(1)}, bf16[32,1536]{1,0:T(8,128)(2,1)S(1)}, u32[]{:S(2)}, u32[]{:S(2)}) %collective-permute-start.3) | collective-permute-done | bytes 98336 | tf_op jit(solution)/shard_map/ppermute | solution.py:30
  19.6 1.6 %collective-permute-start.4 = (bf16[128,1536]{1,0:T(8,128)(2,1)S(1)}, bf16[128,1536]{1,0:T(8,128)(2,1)S(1)}, u32[]{:S(2)}, u32[]{:S(2)}) collective-permute-start(bf16[128,1536]{1,0:T(8,128)(2,1)S(1)} %get-tuple-element.104), channel_id=1, source_target_pairs={{0,4},{1,3},{2,6},{3,1},{4,0},{5,7},{6,2},{7,5},{8,12},{9,11},{10,... | collective-permute-start | bytes 1179656 | tf_op jit(solution)/shard_map/ppermute | solution.py:30
  21.2 3.5 %collective-permute-start.7 = (bf16[32,1536]{1,0:T(8,128)(2,1)S(1)}, bf16[32,1536]{1,0:T(8,128)(2,1)S(1)}, u32[]{:S(2)}, u32[]{:S(2)}) collective-permute-start(bf16[32,1536]{1,0:T(8,128)(2,1)S(1)} %get-tuple-element.56), channel_id=1, source_target_pairs={{0,24},{1,25},{2,26},{3,27},{4,28},{5,29},{6,30},{7,31},{8,16},{9,... | collective-permute-start | bytes 294920 | tf_op jit(solution)/shard_map/ppermute | solution.py:30
  24.8 0.9 collective-permute-start.5
  25.6 1.8 %collective-permute-done.4.next_ref = bf16[128,1536]{1,0:T(8,128)(2,1)S(1)} collective-permute-done((bf16[128,1536]{1,0:T(8,128)(2,1)S(1)}, bf16[128,1536]{1,0:T(8,128)(2,1)S(1)}, u32[]{:S(2)}, u32[]{:S(2)}) %collective-permute-start.4) | collective-permute-done | bytes 393248 | tf_op jit(solution)/shard_map/ppermute | solution.py:30
  27.5 1.3 %shard_map.76 = bf16[192,1536]{1,0:T(8,128)(2,1)S(1)} custom-call(s32[3]{0:T(128)S(1)} %pad_add_fusion.places_ref._, bf16[128,1536]{1,0:T(8,128)(2,1)S(1)} %get-tuple-element.104, bf16[128,1536]{1,0:T(8,128)(2,1)S(1)} %collective-permute-done.4.next_ref), custom_call_target="tpu_custom_call" | custom-call | flops 301989888 | bytes 1572864 | tf_op jit(solution)/shard_map/pallas_call | solution.py:99
  28.8 1.6 %collective-permute-start.10 = (bf16[192,1536]{1,0:T(8,128)(2,1)S(1)}, bf16[192,1536]{1,0:T(8,128)(2,1)S(1)}, u32[]{:S(2)}, u32[]{:S(2)}) collective-permute-start(bf16[192,1536]{1,0:T(8,128)(2,1)S(1)} %shard_map.76), channel_id=1, source_target_pairs={{0,2},{1,5},{2,0},{3,7},{4,6},{5,1},{6,4},{7,3},{8,10},{9,13},{10,... | collective-permute-start | bytes 1769480 | tf_op jit(solution)/shard_map/ppermute | solution.py:30
  30.4 1.3 %shard_map.77 = (bf16[192,1536]{1,0:T(8,128)(2,1)S(1)}, f32[128,128]{1,0:T(8,128)S(1)}, f32[128,128]{1,0:T(8,128)S(1)}) custom-call(s32[3]{0:T(128)S(1)} %pad_add_fusion.places_ref._, bf16[128,1536]{1,0:T(8,128)(2,1)S(1)} %get-tuple-element.104, bf16[128,1536]{1,0:T(8,128)(2,1)S(1)} %collective-permute-done.4.next_ref), custom_call_target="tpu_custom_call" | custom-call | flops 301989888 | bytes 1572864 | tf_op jit(solution)/shard_map/pallas_call | solution.py:99
  32.1 1.6 %collective-permute-start.9 = (bf16[128,1536]{1,0:T(8,128)(2,1)S(1)}, bf16[128,1536]{1,0:T(8,128)(2,1)S(1)}, u32[]{:S(2)}, u32[]{:S(2)}) collective-permute-start(bf16[128,1536]{1,0:T(8,128)(2,1)S(1)} %constant_dynamic-update-slice_fusion.5.near_ref), channel_id=1, source_target_pairs={{0,4},{1,3},{2,6},{3,1},{4,0},{5,7},{6,2},{7,5},{8,12},{9,11},{10,... | collective-permute-start | bytes 1179656 | tf_op jit(solution)/shard_map/ppermute | solution.py:30
  34.1 3.4 %shard_map.78 = (f32[288,720]{1,0:T(8,128)S(1)}, f32[288,720]{1,0:T(8,128)S(1)}) custom-call(s32[3]{0:T(128)S(1)} %pad_add_fusion.places_ref._, s32[3]{0:T(128)S(1)} %pad_add_fusion.places_ref._, bf16[192,1536]{1,0:T(8,128)(2,1)S(1)} %get-tuple-element.58.mine_ref.mine_near_ref, bf16[192,1536]{1,0:T(8,128)(2,1)S(1)} %collective-permute-done.8.other_ref, ...), custom_call_target="tpu_custom_call" | custom-call | flops 1592524800 | bytes 8294400 | tf_op jit(solution)/shard_map/pallas_call | solution.py:179
  37.9 2.1 %collective-permute-done.9.next_ref = bf16[128,1536]{1,0:T(8,128)(2,1)S(1)} collective-permute-done((bf16[128,1536]{1,0:T(8,128)(2,1)S(1)}, bf16[128,1536]{1,0:T(8,128)(2,1)S(1)}, u32[]{:S(2)}, u32[]{:S(2)}) %collective-permute-start.9) | collective-permute-done | bytes 393248 | tf_op jit(solution)/shard_map/ppermute | solution.py:30
  40.0 1.7 %shard_map.80 = (bf16[192,1536]{1,0:T(8,128)(2,1)S(1)}, bf16[192,1536]{1,0:T(8,128)(2,1)S(1)}, f32[128,128]{1,0:T(8,128)S(1)}, f32[128,128]{1,0:T(8,128)S(1)}) custom-call(s32[3]{0:T(128)S(1)} %pad_add_fusion.places_ref._, bf16[128,1536]{1,0:T(8,128)(2,1)S(1)} %constant_dynamic-update-slice_fusion.5.near_ref, ...), custom_call_target="tpu_custom_call" | custom-call | flops 301989888 | bytes 1572864 | tf_op jit(solution)/shard_map/pallas_call | solution.py:99
  42.1 2.4 %collective-permute-start.11 = (bf16[192,1536]{1,0:T(8,128)(2,1)S(1)}, bf16[192,1536]{1,0:T(8,128)(2,1)S(1)}, u32[]{:S(2)}, u32[]{:S(2)}) collective-permute-start(bf16[192,1536]{1,0:T(8,128)(2,1)S(1)} %collective-permute-done.10.mine_far_ref), channel_id=1, source_target_pairs={{0,1},{1,0},{2,3},{3,2},{4,5},{5,4},{6,7},{7,6},{8,9},{9,8},{10,11... | collective-permute-start | bytes 1769480 | tf_op jit(solution)/shard_map/ppermute | solution.py:30
  44.5 1.8 %collective-permute-start.16 = (bf16[192,1536]{1,0:T(8,128)(2,1)S(1)}, bf16[192,1536]{1,0:T(8,128)(2,1)S(1)}, u32[]{:S(2)}, u32[]{:S(2)}) collective-permute-start(bf16[192,1536]{1,0:T(8,128)(2,1)S(1)} %get-tuple-element.78), channel_id=1, source_target_pairs={{0,2},{1,5},{2,0},{3,7},{4,6},{5,1},{6,4},{7,3},{8,10},{9,13},{10,... | collective-permute-start | bytes 1769480 | tf_op jit(solution)/shard_map/ppermute | solution.py:30
  46.3 6.3 %shard_map.81 = (f32[192,1536]{1,0:T(8,128)S(1)}, f32[192,1536]{1,0:T(8,128)S(1)}, bf16[192,1536]{1,0:T(8,128)(2,1)S(1)}, bf16[192,1536]{1,0:T(8,128)(2,1)S(1)}) custom-call(s32[3]{0:T(128)S(1)} %pad_add_fusion.places_ref._, f32[288,720]{1,0:T(8,128)S(1)} %get-tuple-element.61._.gate_part_ref, f32[288,720]{1,0:T(8,128)S(1)} %get-tuple-element.62.up_part_ref, ...), custom_call_target="tpu_custom_call" | custom-call | flops 3185049600 | bytes 17160192 | tf_op jit(solution)/shard_map/pallas_call | solution.py:255
  52.6 0.7 collective-permute-start.13
  53.2 3.4 %shard_map.83 = (f32[288,720]{1,0:T(8,128)S(1)}, f32[288,720]{1,0:T(8,128)S(1)}) custom-call(s32[3]{0:T(128)S(1)} %pad_add_fusion.places_ref._, f32[192,1536]{1,0:T(8,128)S(1)} %get-tuple-element.72._, bf16[192,1536]{1,0:T(8,128)(2,1)S(1)} %get-tuple-element.79.mine_ref.mine_near_ref, bf16[192,1536]{1,0:T(8,128)(2,1)S(1)} %collective-permute-done.17.other_ref, ...), custom_call_target="tpu_custom_call" | custom-call | flops 1592524800 | bytes 8294400 | tf_op jit(solution)/shard_map/pallas_call | solution.py:179
  57.4 1.6 %collective-permute-start.14 = (bf16[192,1536]{1,0:T(8,128)(2,1)S(1)}, bf16[192,1536]{1,0:T(8,128)(2,1)S(1)}, u32[]{:S(2)}, u32[]{:S(2)}) collective-permute-start(bf16[192,1536]{1,0:T(8,128)(2,1)S(1)} %add_convert_fusion.1), channel_id=1, source_target_pairs={{0,2},{1,5},{2,0},{3,7},{4,6},{5,1},{6,4},{7,3},{8,10},{9,13},{10,... | collective-permute-start | bytes 1769480 | tf_op jit(solution)/shard_map/ppermute | solution.py:30
  58.9 6.3 %shard_map.84 = (f32[192,1536]{1,0:T(8,128)S(1)}, f32[192,1536]{1,0:T(8,128)S(1)}, bf16[192,1536]{1,0:T(8,128)(2,1)S(1)}, bf16[192,1536]{1,0:T(8,128)(2,1)S(1)}) custom-call(s32[3]{0:T(128)S(1)} %pad_add_fusion.places_ref._, f32[288,720]{1,0:T(8,128)S(1)} %get-tuple-element.82.gate_part_ref, f32[288,720]{1,0:T(8,128)S(1)} %get-tuple-element.83.up_part_ref, ...), custom_call_target="tpu_custom_call" | custom-call | flops 3185049600 | bytes 17160192 | tf_op jit(solution)/shard_map/pallas_call | solution.py:255
  65.8 1.5 %collective-permute-done.14.arrived_ref = bf16[192,1536]{1,0:T(8,128)(2,1)S(1)} collective-permute-done((bf16[192,1536]{1,0:T(8,128)(2,1)S(1)}, bf16[192,1536]{1,0:T(8,128)(2,1)S(1)}, u32[]{:S(2)}, u32[]{:S(2)}) %collective-permute-start.14) | collective-permute-done | bytes 589856 | tf_op jit(solution)/shard_map/ppermute | solution.py:30
  67.3 0.6 shard_map.82
  68.0 1.5 %collective-permute-start.15 = (bf16[128,1536]{1,0:T(8,128)(2,1)S(1)}, bf16[128,1536]{1,0:T(8,128)(2,1)S(1)}, u32[]{:S(2)}, u32[]{:S(2)}) collective-permute-start(bf16[128,1536]{1,0:T(8,128)(2,1)S(1)} %get-tuple-element.75), channel_id=1, source_target_pairs={{0,4},{1,3},{2,6},{3,1},{4,0},{5,7},{6,2},{7,5},{8,12},{9,11},{10,... | collective-permute-start | bytes 1179656 | tf_op jit(solution)/shard_map/ppermute | solution.py:30
  69.6 1.6 %collective-permute-start.21 = (bf16[192,1536]{1,0:T(8,128)(2,1)S(1)}, bf16[192,1536]{1,0:T(8,128)(2,1)S(1)}, u32[]{:S(2)}, u32[]{:S(2)}) collective-permute-start(bf16[192,1536]{1,0:T(8,128)(2,1)S(1)} %add_convert_fusion), channel_id=1, source_target_pairs={{0,2},{1,5},{2,0},{3,7},{4,6},{5,1},{6,4},{7,3},{8,10},{9,13},{10,... | collective-permute-start | bytes 1769480 | tf_op jit(solution)/shard_map/ppermute | solution.py:30
  71.1 8.9 %collective-permute-done.15 = bf16[128,1536]{1,0:T(8,128)(2,1)S(1)} collective-permute-done((bf16[128,1536]{1,0:T(8,128)(2,1)S(1)}, bf16[128,1536]{1,0:T(8,128)(2,1)S(1)}, u32[]{:S(2)}, u32[]{:S(2)}) %collective-permute-start.15) | collective-permute-done | bytes 393248 | tf_op jit(solution)/shard_map/ppermute | solution.py:30
  80.8 1.5 %collective-permute-start.25 = (bf16[128,1536]{1,0:T(8,128)(2,1)S(1)}, bf16[128,1536]{1,0:T(8,128)(2,1)S(1)}, u32[]{:S(2)}, u32[]{:S(2)}) collective-permute-start(bf16[128,1536]{1,0:T(8,128)(2,1)S(1)} %shard_map.85._), channel_id=1, source_target_pairs={{0,4},{1,3},{2,6},{3,1},{4,0},{5,7},{6,2},{7,5},{8,12},{9,11},{10,... | collective-permute-start | bytes 1179656 | tf_op jit(solution)/shard_map/ppermute | solution.py:30
  82.8 0.6 collective-permute-start.22
  83.5 1.5 %collective-permute-start.23 = (bf16[32,1536]{1,0:T(8,128)(2,1)S(1)}, bf16[32,1536]{1,0:T(8,128)(2,1)S(1)}, u32[]{:S(2)}, u32[]{:S(2)}) collective-permute-start(bf16[32,1536]{1,0:T(8,128)(2,1)S(1)} %get-tuple-element.98), channel_id=1, source_target_pairs={{0,8},{1,9},{2,10},{3,11},{4,12},{5,13},{6,14},{7,15},{8,0},{9,1},... | collective-permute-start | bytes 294920 | tf_op jit(solution)/shard_map/ppermute | solution.py:30
  84.9 3.8 %collective-permute-done.25 = bf16[128,1536]{1,0:T(8,128)(2,1)S(1)} collective-permute-done((bf16[128,1536]{1,0:T(8,128)(2,1)S(1)}, bf16[128,1536]{1,0:T(8,128)(2,1)S(1)}, u32[]{:S(2)}, u32[]{:S(2)}) %collective-permute-start.25) | collective-permute-done | bytes 393248 | tf_op jit(solution)/shard_map/ppermute | solution.py:30
  89.8 3.0 %collective-permute-start.24 = (bf16[32,1536]{1,0:T(8,128)(2,1)S(1)}, bf16[32,1536]{1,0:T(8,128)(2,1)S(1)}, u32[]{:S(2)}, u32[]{:S(2)}) collective-permute-start(bf16[32,1536]{1,0:T(8,128)(2,1)S(1)} %add_convert_fusion.2), channel_id=1, source_target_pairs={{0,16},{1,17},{2,18},{3,19},{4,20},{5,21},{6,22},{7,23},{8,24},{9,... | collective-permute-start | bytes 294920 | tf_op jit(solution)/shard_map/ppermute | solution.py:30
  92.8 0.9 collective-permute-start.26
  93.7 1.5 %collective-permute-done.27 = bf16[32,1536]{1,0:T(8,128)(2,1)S(1)} collective-permute-done((bf16[32,1536]{1,0:T(8,128)(2,1)S(1)}, bf16[32,1536]{1,0:T(8,128)(2,1)S(1)}, u32[]{:S(2)}, u32[]{:S(2)}) %collective-permute-start.27) | collective-permute-done | bytes 98336 | tf_op jit(solution)/shard_map/ppermute | solution.py:30
  95.3 1.7 %collective-permute-start.28 = (bf16[32,1536]{1,0:T(8,128)(2,1)S(1)}, bf16[32,1536]{1,0:T(8,128)(2,1)S(1)}, u32[]{:S(2)}, u32[]{:S(2)}) collective-permute-start(bf16[32,1536]{1,0:T(8,128)(2,1)S(1)} %fusion.2), channel_id=1, source_target_pairs={{0,16},{1,17},{2,18},{3,19},{4,20},{5,21},{6,22},{7,23},{8,24},{9,... | collective-permute-start | bytes 294920 | tf_op jit(solution)/shard_map/ppermute | solution.py:30
  97.0 1.3 %collective-permute-done.24 = bf16[32,1536]{1,0:T(8,128)(2,1)S(1)} collective-permute-done((bf16[32,1536]{1,0:T(8,128)(2,1)S(1)}, bf16[32,1536]{1,0:T(8,128)(2,1)S(1)}, u32[]{:S(2)}, u32[]{:S(2)}) %collective-permute-start.24) | collective-permute-done | bytes 98336 | tf_op jit(solution)/shard_map/ppermute | solution.py:30
  98.3 0.9 collective-permute-done.26
  99.2 3.3 %collective-permute-done.28 = bf16[32,1536]{1,0:T(8,128)(2,1)S(1)} collective-permute-done((bf16[32,1536]{1,0:T(8,128)(2,1)S(1)}, bf16[32,1536]{1,0:T(8,128)(2,1)S(1)}, u32[]{:S(2)}, u32[]{:S(2)}) %collective-permute-start.28) | collective-permute-done | bytes 98336 | tf_op jit(solution)/shard_map/ppermute | solution.py:30
  102.8 1.3 %collective-permute-done.29 = bf16[2,16,1536]{2,1,0:T(8,128)(2,1)S(1)} collective-permute-done((bf16[2,16,1536]{2,1,0:T(8,128)(2,1)S(1)}, bf16[2,16,1536]{2,1,0:T(8,128)(2,1)S(1)}, u32[]{:S(2)}, u32[]{:S(2)}) %collective-permute-start.29) | collective-permute-done | bytes 98336 | tf_op jit(solution)/shard_map/ppermute | solution.py:30
  104.1 0.7 fusion
  (77 shorter events, 7.2 us)
Async XLA Ops:
  2.4 0.9 copy-start.1
  3.3 12.3 %slice-start = ((s8[4239360]{0:T(1024)(128)(4,1)}), s8[45056]{0:T(1024)(128)(4,1)S(1)}, s32[]{:S(2)}) async-start(s8[4239360]{0:T(1024)(128)(4,1)} %bitcast.23), calls=%async_computation | async-start | bytes 90112
  4.1 1.5 %collective-permute-start = (bf16[2,16,1536]{2,1,0:T(8,128)(2,1)S(1)}, bf16[2,16,1536]{2,1,0:T(8,128)(2,1)S(1)}, u32[]{:S(2)}, u32[]{:S(2)}) collective-permute-start(bf16[2,16,1536]{2,1,0:T(8,128)(2,1)S(1)} %get-tuple-element.49), channel_id=1, source_target_pairs={{0,1},{1,0},{2,3},{3,2},{4,5},{5,4},{6,7},{7,6},{8,9},{9,8},{10,11... | collective-permute-start | bytes 294920 | tf_op jit(solution)/shard_map/ppermute | solution.py:30
  5.6 9.3 %collective-permute-start.2 = (bf16[32,1536]{1,0:T(8,128)(2,1)S(1)}, bf16[32,1536]{1,0:T(8,128)(2,1)S(1)}, u32[]{:S(2)}, u32[]{:S(2)}) collective-permute-start(bf16[32,1536]{1,0:T(8,128)(2,1)S(1)} %pad_maximum_fusion.2._), channel_id=1, source_target_pairs={{0,16},{1,17},{2,18},{3,19},{4,20},{5,21},{6,22},{7,23},{8,24},{9,... | collective-permute-start | bytes 294920 | tf_op jit(solution)/shard_map/ppermute | solution.py:30
  9.7 6.0 %collective-permute-start.1 = (bf16[32,1536]{1,0:T(8,128)(2,1)S(1)}, bf16[32,1536]{1,0:T(8,128)(2,1)S(1)}, u32[]{:S(2)}, u32[]{:S(2)}) collective-permute-start(bf16[32,1536]{1,0:T(8,128)(2,1)S(1)} %pad_maximum_fusion.2._), channel_id=1, source_target_pairs={{0,8},{1,9},{2,10},{3,11},{4,12},{5,13},{6,14},{7,15},{8,0},{9,1},... | collective-permute-start | bytes 294920 | tf_op jit(solution)/shard_map/ppermute | solution.py:30
  11.2 2.2 %copy-start = (bf16[2880,720]{0,1:T(8,128)(2,1)S(1)}, bf16[2880,720]{0,1:T(8,128)(2,1)}, u32[]{:S(2)}) copy-start(bf16[2880,720]{0,1:T(8,128)(2,1)} %param.9) | copy-start | bytes 12441604
  13.5 2.2 %slice-start.1 = ((s8[4239360]{0:T(1024)(128)(4,1)}), s8[4194304]{0:T(1024)(128)(4,1)S(1)}, s32[]{:S(2)}) async-start(s8[4239360]{0:T(1024)(128)(4,1)} %bitcast.23), calls=%async_computation.1 | async-start | bytes 8388608
  15.0 4.6 %collective-permute-start.3 = (bf16[32,1536]{1,0:T(8,128)(2,1)S(1)}, bf16[32,1536]{1,0:T(8,128)(2,1)S(1)}, u32[]{:S(2)}, u32[]{:S(2)}) collective-permute-start(bf16[32,1536]{1,0:T(8,128)(2,1)S(1)} %collective-permute-done.2._), channel_id=1, source_target_pairs={{0,8},{1,9},{2,10},{3,11},{4,12},{5,13},{6,14},{7,15},{8,0},{9,1},... | collective-permute-start | bytes 294920 | tf_op jit(solution)/shard_map/ppermute | solution.py:30
  19.6 7.8 %collective-permute-start.4 = (bf16[128,1536]{1,0:T(8,128)(2,1)S(1)}, bf16[128,1536]{1,0:T(8,128)(2,1)S(1)}, u32[]{:S(2)}, u32[]{:S(2)}) collective-permute-start(bf16[128,1536]{1,0:T(8,128)(2,1)S(1)} %get-tuple-element.104), channel_id=1, source_target_pairs={{0,4},{1,3},{2,6},{3,1},{4,0},{5,7},{6,2},{7,5},{8,12},{9,11},{10,... | collective-permute-start | bytes 1179656 | tf_op jit(solution)/shard_map/ppermute | solution.py:30
  21.2 10.5 %collective-permute-start.7 = (bf16[32,1536]{1,0:T(8,128)(2,1)S(1)}, bf16[32,1536]{1,0:T(8,128)(2,1)S(1)}, u32[]{:S(2)}, u32[]{:S(2)}) collective-permute-start(bf16[32,1536]{1,0:T(8,128)(2,1)S(1)} %get-tuple-element.56), channel_id=1, source_target_pairs={{0,24},{1,25},{2,26},{3,27},{4,28},{5,29},{6,30},{7,31},{8,16},{9,... | collective-permute-start | bytes 294920 | tf_op jit(solution)/shard_map/ppermute | solution.py:30
  24.8 7.3 %collective-permute-start.6 = (bf16[32,1536]{1,0:T(8,128)(2,1)S(1)}, bf16[32,1536]{1,0:T(8,128)(2,1)S(1)}, u32[]{:S(2)}, u32[]{:S(2)}) collective-permute-start(bf16[32,1536]{1,0:T(8,128)(2,1)S(1)} %get-tuple-element.56), channel_id=1, source_target_pairs={{0,16},{1,17},{2,18},{3,19},{4,20},{5,21},{6,22},{7,23},{8,24},{9,... | collective-permute-start | bytes 294920 | tf_op jit(solution)/shard_map/ppermute | solution.py:30
  24.8 7.3 %collective-permute-start.5 = (bf16[32,1536]{1,0:T(8,128)(2,1)S(1)}, bf16[32,1536]{1,0:T(8,128)(2,1)S(1)}, u32[]{:S(2)}, u32[]{:S(2)}) collective-permute-start(bf16[32,1536]{1,0:T(8,128)(2,1)S(1)} %get-tuple-element.56), channel_id=1, source_target_pairs={{0,8},{1,9},{2,10},{3,11},{4,12},{5,13},{6,14},{7,15},{8,0},{9,1},... | collective-permute-start | bytes 294920 | tf_op jit(solution)/shard_map/ppermute | solution.py:30
  28.8 13.3 %collective-permute-start.10 = (bf16[192,1536]{1,0:T(8,128)(2,1)S(1)}, bf16[192,1536]{1,0:T(8,128)(2,1)S(1)}, u32[]{:S(2)}, u32[]{:S(2)}) collective-permute-start(bf16[192,1536]{1,0:T(8,128)(2,1)S(1)} %shard_map.76), channel_id=1, source_target_pairs={{0,2},{1,5},{2,0},{3,7},{4,6},{5,1},{6,4},{7,3},{8,10},{9,13},{10,... | collective-permute-start | bytes 1769480 | tf_op jit(solution)/shard_map/ppermute | solution.py:30
  32.1 2.0 %collective-permute-start.8 = (bf16[192,1536]{1,0:T(8,128)(2,1)S(1)}, bf16[192,1536]{1,0:T(8,128)(2,1)S(1)}, u32[]{:S(2)}, u32[]{:S(2)}) collective-permute-start(bf16[192,1536]{1,0:T(8,128)(2,1)S(1)} %get-tuple-element.58.mine_ref.mine_near_ref), channel_id=1, source_target_pairs={{0,1},{1,0},{2,3},{3,2},{4,5},{5,4},{6,7},{7,6},{8,9},{9,8},{10,11... | collective-permute-start | bytes 1769480 | tf_op jit(solution)/shard_map/ppermute | solution.py:30
  32.1 5.4 %slice-start.2 = ((s8[4239360]{0:T(1024)(128)(4,1)}), s8[4194304]{0:T(1024)(128)(4,1)S(1)}, s32[]{:S(2)}) async-start(s8[4239360]{0:T(1024)(128)(4,1)} %bitcast.26), calls=%async_computation.2 | async-start | bytes 8388608
  32.1 5.4 %slice-start.3 = ((s8[4239360]{0:T(1024)(128)(4,1)}), s8[45056]{0:T(1024)(128)(4,1)S(1)}, s32[]{:S(2)}) async-start(s8[4239360]{0:T(1024)(128)(4,1)} %bitcast.26), calls=%async_computation.3 | async-start | bytes 90112
  32.1 7.8 %collective-permute-start.9 = (bf16[128,1536]{1,0:T(8,128)(2,1)S(1)}, bf16[128,1536]{1,0:T(8,128)(2,1)S(1)}, u32[]{:S(2)}, u32[]{:S(2)}) collective-permute-start(bf16[128,1536]{1,0:T(8,128)(2,1)S(1)} %constant_dynamic-update-slice_fusion.5.near_ref), channel_id=1, source_target_pairs={{0,4},{1,3},{2,6},{3,1},{4,0},{5,7},{6,2},{7,5},{8,12},{9,11},{10,... | collective-permute-start | bytes 1179656 | tf_op jit(solution)/shard_map/ppermute | solution.py:30
  42.1 4.2 %collective-permute-start.11 = (bf16[192,1536]{1,0:T(8,128)(2,1)S(1)}, bf16[192,1536]{1,0:T(8,128)(2,1)S(1)}, u32[]{:S(2)}, u32[]{:S(2)}) collective-permute-start(bf16[192,1536]{1,0:T(8,128)(2,1)S(1)} %collective-permute-done.10.mine_far_ref), channel_id=1, source_target_pairs={{0,1},{1,0},{2,3},{3,2},{4,5},{5,4},{6,7},{7,6},{8,9},{9,8},{10,11... | collective-permute-start | bytes 1769480 | tf_op jit(solution)/shard_map/ppermute | solution.py:30
  44.5 12.2 %collective-permute-start.16 = (bf16[192,1536]{1,0:T(8,128)(2,1)S(1)}, bf16[192,1536]{1,0:T(8,128)(2,1)S(1)}, u32[]{:S(2)}, u32[]{:S(2)}) collective-permute-start(bf16[192,1536]{1,0:T(8,128)(2,1)S(1)} %get-tuple-element.78), channel_id=1, source_target_pairs={{0,2},{1,5},{2,0},{3,7},{4,6},{5,1},{6,4},{7,3},{8,10},{9,13},{10,... | collective-permute-start | bytes 1769480 | tf_op jit(solution)/shard_map/ppermute | solution.py:30
  46.3 6.9 %collective-permute-start.17 = (bf16[192,1536]{1,0:T(8,128)(2,1)S(1)}, bf16[192,1536]{1,0:T(8,128)(2,1)S(1)}, u32[]{:S(2)}, u32[]{:S(2)}) collective-permute-start(bf16[192,1536]{1,0:T(8,128)(2,1)S(1)} %get-tuple-element.79.mine_ref.mine_near_ref), channel_id=1, source_target_pairs={{0,1},{1,0},{2,3},{3,2},{4,5},{5,4},{6,7},{7,6},{8,9},{9,8},{10,11... | collective-permute-start | bytes 1769480 | tf_op jit(solution)/shard_map/ppermute | solution.py:30
  52.6 4.7 %collective-permute-start.13 = (bf16[192,1536]{1,0:T(8,128)(2,1)S(1)}, bf16[192,1536]{1,0:T(8,128)(2,1)S(1)}, u32[]{:S(2)}, u32[]{:S(2)}) collective-permute-start(bf16[192,1536]{1,0:T(8,128)(2,1)S(1)} %get-tuple-element.73), channel_id=1, source_target_pairs={{0,1},{1,0},{2,3},{3,2},{4,5},{5,4},{6,7},{7,6},{8,9},{9,8},{10,11... | collective-permute-start | bytes 1769480 | tf_op jit(solution)/shard_map/ppermute | solution.py:30
  56.7 2.3 %collective-permute-start.18 = (bf16[192,1536]{1,0:T(8,128)(2,1)S(1)}, bf16[192,1536]{1,0:T(8,128)(2,1)S(1)}, u32[]{:S(2)}, u32[]{:S(2)}) collective-permute-start(bf16[192,1536]{1,0:T(8,128)(2,1)S(1)} %collective-permute-done.16.mine_far_ref), channel_id=1, source_target_pairs={{0,1},{1,0},{2,3},{3,2},{4,5},{5,4},{6,7},{7,6},{8,9},{9,8},{10,11... | collective-permute-start | bytes 1769480 | tf_op jit(solution)/shard_map/ppermute | solution.py:30
  56.8 9.1 %collective-permute-start.12 = (bf16[192,1536]{1,0:T(8,128)(2,1)S(1)}, bf16[192,1536]{1,0:T(8,128)(2,1)S(1)}, u32[]{:S(2)}, u32[]{:S(2)}) collective-permute-start(bf16[192,1536]{1,0:T(8,128)(2,1)S(1)} %get-tuple-element.71), channel_id=1, source_target_pairs={{0,1},{1,0},{2,3},{3,2},{4,5},{5,4},{6,7},{7,6},{8,9},{9,8},{10,11... | collective-permute-start | bytes 1769480 | tf_op jit(solution)/shard_map/ppermute | solution.py:30
  57.4 9.9 %collective-permute-start.14 = (bf16[192,1536]{1,0:T(8,128)(2,1)S(1)}, bf16[192,1536]{1,0:T(8,128)(2,1)S(1)}, u32[]{:S(2)}, u32[]{:S(2)}) collective-permute-start(bf16[192,1536]{1,0:T(8,128)(2,1)S(1)} %add_convert_fusion.1), channel_id=1, source_target_pairs={{0,2},{1,5},{2,0},{3,7},{4,6},{5,1},{6,4},{7,3},{8,10},{9,13},{10,... | collective-permute-start | bytes 1769480 | tf_op jit(solution)/shard_map/ppermute | solution.py:30
  65.3 4.2 %collective-permute-start.20 = (bf16[192,1536]{1,0:T(8,128)(2,1)S(1)}, bf16[192,1536]{1,0:T(8,128)(2,1)S(1)}, u32[]{:S(2)}, u32[]{:S(2)}) collective-permute-start(bf16[192,1536]{1,0:T(8,128)(2,1)S(1)} %get-tuple-element.88), channel_id=1, source_target_pairs={{0,1},{1,0},{2,3},{3,2},{4,5},{5,4},{6,7},{7,6},{8,9},{9,8},{10,11... | collective-permute-start | bytes 1769480 | tf_op jit(solution)/shard_map/ppermute | solution.py:30
  65.4 14.7 %collective-permute-start.19 = (bf16[192,1536]{1,0:T(8,128)(2,1)S(1)}, bf16[192,1536]{1,0:T(8,128)(2,1)S(1)}, u32[]{:S(2)}, u32[]{:S(2)}) collective-permute-start(bf16[192,1536]{1,0:T(8,128)(2,1)S(1)} %get-tuple-element.86), channel_id=1, source_target_pairs={{0,1},{1,0},{2,3},{3,2},{4,5},{5,4},{6,7},{7,6},{8,9},{9,8},{10,11... | collective-permute-start | bytes 1769480 | tf_op jit(solution)/shard_map/ppermute | solution.py:30
  68.0 12.1 %collective-permute-start.15 = (bf16[128,1536]{1,0:T(8,128)(2,1)S(1)}, bf16[128,1536]{1,0:T(8,128)(2,1)S(1)}, u32[]{:S(2)}, u32[]{:S(2)}) collective-permute-start(bf16[128,1536]{1,0:T(8,128)(2,1)S(1)} %get-tuple-element.75), channel_id=1, source_target_pairs={{0,4},{1,3},{2,6},{3,1},{4,0},{5,7},{6,2},{7,5},{8,12},{9,11},{10,... | collective-permute-start | bytes 1179656 | tf_op jit(solution)/shard_map/ppermute | solution.py:30
  69.6 10.8 %collective-permute-start.21 = (bf16[192,1536]{1,0:T(8,128)(2,1)S(1)}, bf16[192,1536]{1,0:T(8,128)(2,1)S(1)}, u32[]{:S(2)}, u32[]{:S(2)}) collective-permute-start(bf16[192,1536]{1,0:T(8,128)(2,1)S(1)} %add_convert_fusion), channel_id=1, source_target_pairs={{0,2},{1,5},{2,0},{3,7},{4,6},{5,1},{6,4},{7,3},{8,10},{9,13},{10,... | collective-permute-start | bytes 1769480 | tf_op jit(solution)/shard_map/ppermute | solution.py:30
  80.8 7.8 %collective-permute-start.25 = (bf16[128,1536]{1,0:T(8,128)(2,1)S(1)}, bf16[128,1536]{1,0:T(8,128)(2,1)S(1)}, u32[]{:S(2)}, u32[]{:S(2)}) collective-permute-start(bf16[128,1536]{1,0:T(8,128)(2,1)S(1)} %shard_map.85._), channel_id=1, source_target_pairs={{0,4},{1,3},{2,6},{3,1},{4,0},{5,7},{6,2},{7,5},{8,12},{9,11},{10,... | collective-permute-start | bytes 1179656 | tf_op jit(solution)/shard_map/ppermute | solution.py:30
  82.8 14.1 %collective-permute-start.22 = (bf16[32,1536]{1,0:T(8,128)(2,1)S(1)}, bf16[32,1536]{1,0:T(8,128)(2,1)S(1)}, u32[]{:S(2)}, u32[]{:S(2)}) collective-permute-start(bf16[32,1536]{1,0:T(8,128)(2,1)S(1)} %get-tuple-element.97), channel_id=1, source_target_pairs={{0,8},{1,9},{2,10},{3,11},{4,12},{5,13},{6,14},{7,15},{8,0},{9,1},... | collective-permute-start | bytes 294920 | tf_op jit(solution)/shard_map/ppermute | solution.py:30
  83.5 6.3 %collective-permute-start.23 = (bf16[32,1536]{1,0:T(8,128)(2,1)S(1)}, bf16[32,1536]{1,0:T(8,128)(2,1)S(1)}, u32[]{:S(2)}, u32[]{:S(2)}) collective-permute-start(bf16[32,1536]{1,0:T(8,128)(2,1)S(1)} %get-tuple-element.98), channel_id=1, source_target_pairs={{0,8},{1,9},{2,10},{3,11},{4,12},{5,13},{6,14},{7,15},{8,0},{9,1},... | collective-permute-start | bytes 294920 | tf_op jit(solution)/shard_map/ppermute | solution.py:30
  88.8 6.4 %collective-permute-start.27 = (bf16[32,1536]{1,0:T(8,128)(2,1)S(1)}, bf16[32,1536]{1,0:T(8,128)(2,1)S(1)}, u32[]{:S(2)}, u32[]{:S(2)}) collective-permute-start(bf16[32,1536]{1,0:T(8,128)(2,1)S(1)} %get-tuple-element.100), channel_id=1, source_target_pairs={{0,8},{1,9},{2,10},{3,11},{4,12},{5,13},{6,14},{7,15},{8,0},{9,1},... | collective-permute-start | bytes 294920 | tf_op jit(solution)/shard_map/ppermute | solution.py:30
  89.8 8.5 %collective-permute-start.24 = (bf16[32,1536]{1,0:T(8,128)(2,1)S(1)}, bf16[32,1536]{1,0:T(8,128)(2,1)S(1)}, u32[]{:S(2)}, u32[]{:S(2)}) collective-permute-start(bf16[32,1536]{1,0:T(8,128)(2,1)S(1)} %add_convert_fusion.2), channel_id=1, source_target_pairs={{0,16},{1,17},{2,18},{3,19},{4,20},{5,21},{6,22},{7,23},{8,24},{9,... | collective-permute-start | bytes 294920 | tf_op jit(solution)/shard_map/ppermute | solution.py:30
  92.8 6.4 %collective-permute-start.26 = (bf16[32,1536]{1,0:T(8,128)(2,1)S(1)}, bf16[32,1536]{1,0:T(8,128)(2,1)S(1)}, u32[]{:S(2)}, u32[]{:S(2)}) collective-permute-start(bf16[32,1536]{1,0:T(8,128)(2,1)S(1)} %get-tuple-element.99), channel_id=1, source_target_pairs={{0,8},{1,9},{2,10},{3,11},{4,12},{5,13},{6,14},{7,15},{8,0},{9,1},... | collective-permute-start | bytes 294920 | tf_op jit(solution)/shard_map/ppermute | solution.py:30
  95.3 7.3 %collective-permute-start.28 = (bf16[32,1536]{1,0:T(8,128)(2,1)S(1)}, bf16[32,1536]{1,0:T(8,128)(2,1)S(1)}, u32[]{:S(2)}, u32[]{:S(2)}) collective-permute-start(bf16[32,1536]{1,0:T(8,128)(2,1)S(1)} %fusion.2), channel_id=1, source_target_pairs={{0,16},{1,17},{2,18},{3,19},{4,20},{5,21},{6,22},{7,23},{8,24},{9,... | collective-permute-start | bytes 294920 | tf_op jit(solution)/shard_map/ppermute | solution.py:30
  102.6 1.5 %copy-start.2 = (bf16[2,16,2880]{2,1,0:T(8,128)(2,1)S(1)}, bf16[2,16,2880]{2,1,0:T(8,128)(2,1)}, u32[]{:S(2)}) copy-start(bf16[2,16,2880]{2,1,0:T(8,128)(2,1)} %hidden_ref.1) | copy-start | bytes 552964
  102.7 1.4 %collective-permute-start.29 = (bf16[2,16,1536]{2,1,0:T(8,128)(2,1)S(1)}, bf16[2,16,1536]{2,1,0:T(8,128)(2,1)S(1)}, u32[]{:S(2)}, u32[]{:S(2)}) collective-permute-start(bf16[2,16,1536]{2,1,0:T(8,128)(2,1)S(1)} %select_convert_fusion), channel_id=1, source_target_pairs={{0,1},{1,0},{2,3},{3,2},{4,5},{5,4},{6,7},{7,6},{8,9},{9,8},{10,11... | collective-permute-start | bytes 294920 | tf_op jit(solution)/shard_map/ppermute | solution.py:30

commit v9 on v5

--- a/solution.py
+++ b/solution.py
@@ -106,7 +106,7 @@
     )(places, near, following)
 
 
-def merge_body(wanted, near_slots_ref, next_slots_ref, keep_ref, taken_ref, arrived_ref, *out_refs):
+def merge_body(wanted, _, near_slots_ref, next_slots_ref, keep_ref, taken_ref, arrived_ref, *out_refs):
     rows = out_refs[0].shape[0]
     compact = keep_ref.shape[0]
     column = lax.broadcasted_iota(jnp.int32, (rows, compact), 1).astype(jnp.float32)
@@ -120,17 +120,18 @@
         out_ref[...] = result.astype(out_ref.dtype)
 
 
-def merge(wanted, types, slots, keep, taken, arrived):
+def merge(wanted, types, slots, keep, taken, arrived, token=None):
+    token = slots[0] if token is None else token
     rows = slots[0].shape[0]
     compact, held = keep.shape
     return pl.pallas_call(
         functools.partial(merge_body, wanted),
         out_shape=[jax.ShapeDtypeStruct((rows, held), kind) for kind in types],
-        in_specs=whole_arrays(5),
+        in_specs=[pl.BlockSpec(memory_space=pl.ANY)] + whole_arrays(5),
         out_specs=whole_arrays(len(types)),
         compiler_params=pltpu.CompilerParams(vmem_limit_bytes=20 * 2**20),
         cost_estimate=pl.CostEstimate(flops=8 * rows * compact * held, bytes_accessed=8 * rows * held, transcendentals=0),
-    )(*slots, keep, taken, arrived)
+    )(token, *slots, keep, taken, arrived)
 
 
 def ffn_body(
@@ -193,25 +194,18 @@
             send_near_ref[:, size:] = jnp.zeros((pair, held - size), jnp.bfloat16)
             send_far_ref[:, size:] = jnp.zeros((pair, held - size), jnp.bfloat16)
 
-    low = weight * jnp.dot(act_v[...], down_v[:, :first], preferred_element_type=jnp.float32)
+    def product(start, size):
+        return weight * jnp.dot(act_v[...], down_v[:, start : start + size], preferred_element_type=jnp.float32)
 
     @pl.when(lower)
     def _():
-        keep_half(low, first)
+        send_half(product(first, second), second)
+        keep_half(product(0, first), first)
 
     @pl.when(jnp.logical_not(lower))
     def _():
-        send_half(low, first)
-
-    high = weight * jnp.dot(act_v[...], down_v[:, first:], preferred_element_type=jnp.float32)
-
-    @pl.when(lower)
-    def _():
-        send_half(high, second)
-
-    @pl.when(jnp.logical_not(lower))
-    def _():
-        keep_half(high, second)
+        send_half(product(0, first), first)
+        keep_half(product(first, second), second)
 
 
 def ffn(places, mine_near, mine_far, other_near, other_far, gate_t, up_t, w_down):
@@ -328,6 +322,35 @@
         out_specs=whole_arrays(2),
         compiler_params=pltpu.CompilerParams(vmem_limit_bytes=20 * 2**20),
     )(places, hidden, packed)
+
+
+def finish_body(places_ref, hidden_ref, own_ref, taken_ref, mixed_ref):
+    first, second, _ = split_widths(hidden_ref.shape[2])
+    lower = places_ref[0] == 0
+
+    def add(low_ref, high_ref):
+        for ref, (start, size) in ((low_ref, (0, first)), (high_ref, (first, second))):
+            columns = slice(start, start + size)
+            total = hidden_ref[:, :, columns].astype(jnp.float32) + ref[:, :, :size].astype(jnp.float32)
+            mixed_ref[:, :, columns] = total.astype(jnp.bfloat16)
+
+    @pl.when(lower)
+    def _():
+        add(own_ref, taken_ref)
+
+    @pl.when(jnp.logical_not(lower))
+    def _():
+        add(taken_ref, own_ref)
+
+
+def finish(places, hidden, own, taken):
+    return pl.pallas_call(
+        finish_body,
+        out_shape=jax.ShapeDtypeStruct(hidden.shape, jnp.bfloat16),
+        in_specs=[SCALARS] + whole_arrays(3),
+        out_specs=pl.BlockSpec(memory_space=pltpu.VMEM),
+        compiler_params=pltpu.CompilerParams(vmem_limit_bytes=20 * 2**20),
+    )(places, hidden, own, taken)
 
 
 def local(hidden, norm_gain, w_gate, w_up, w_down, expert_ids, route_weight):
@@ -421,45 +444,38 @@
     def rounded_sum(a, b):
         return (a + b.astype(jnp.float32)).astype(jnp.bfloat16)
 
-    def far_total(block, earlier):
+    def far_hop(block):
         block = block.reshape(distant, -1, held)
         if distant == 4:
-            if earlier:
-                block, earlier[-1]["crossing"] = tied(block, earlier[-1]["crossing"])
             through = moved(block[3].astype(jnp.bfloat16), far(1))
             beside = moved(block[1].astype(jnp.bfloat16), far(1))
-            return {"kept": block[0], "arrivals": [beside], "crossing": rounded_sum(block[2], through)}
-        return {
-            "kept": block[0],
-            "arrivals": [moved(block[j].astype(jnp.bfloat16), far(j)) for j in range(1, distant)],
-            "crossing": None,
-        }
-
-    def settled(total):
-        kept, arrivals = total["kept"], list(total["arrivals"])
-        if total["crossing"] is not None:
-            arrivals.append(moved(total["crossing"], far(2)))
-        for arrival in arrivals:
+            return [block[0], [beside], rounded_sum(block[2], through)]
+        return [block[0], [moved(block[j].astype(jnp.bfloat16), far(j)) for j in range(1, distant)], None]
+
+    def settled(kept, arrivals, cross):
+        for arrival in arrivals if cross is None else arrivals + [moved(cross, far(2))]:
             kept = kept + arrival.astype(jnp.float32)
         return kept
 
-    sums = []
+    totals = []
+    near = None
     for state, (keep_near, keep_far, send_near, send_far) in zip(states, hops):
         give = rounded_sum(keep_far, moved(send_far, other_core))
-        near, following = merge(
-            (0, 1), (jnp.float32, jnp.bfloat16), state["slots"], keep_near, moved(send_near, other_core),
-            moved(give, second_axis),
-        )
-        near = near + moved(following, first_axis).astype(jnp.float32)
-        sums.append(far_total(near, sums))
-    sums = jnp.stack([settled(total) for total in sums])
+        parts = state["slots"], keep_near, moved(send_near, other_core), moved(give, second_axis)
+        if near is None:
+            kept, following = merge((0, 1), (jnp.float32, jnp.bfloat16), *parts)
+        else:
+            (following,) = merge((1,), (jnp.bfloat16,), *parts)
+            (kept,) = merge((0,), (jnp.float32,), *parts, following)
+            near, kept = tied(near, kept)
+            totals.append(far_hop(near))
+        near = kept + moved(following, first_axis).astype(jnp.float32)
+    totals.append(far_hop(near))
+    sums = jnp.stack([settled(*total) for total in totals])
     own = jnp.where(lower, sums[:, :tokens], sums[:, tokens:])
     give = jnp.where(lower, sums[:, tokens:], sums[:, :tokens]).astype(jnp.bfloat16)
-    taken = moved(give, other_core).astype(jnp.float32)
-    mixture = jnp.concatenate(
-        [jnp.where(lower, own, taken)[:, :, :first], jnp.where(lower, taken, own)[:, :, :second]], axis=2
-    )
-    return (hidden.astype(jnp.float32) + mixture).astype(jnp.bfloat16)
+    taken = moved(give, other_core)
+    return finish(places, hidden, own, taken)
 
 
 def solution(mesh):

time: 104 us -> 106 us (1.019)
  starting transfers between devices: 32.3 us -> 39.6 us
  waiting for transfers between devices: 42.7 us -> 36.6 us
    ppermute x30, starting transfers between devices: 32.3 us -> 39.6 us  [moved(): return lax.ppermute(block, 'req', [(i, partner(i)) for i in range(count)])]
    ppermute x30, waiting for transfers between devices: 42.7 us -> 36.6 us  [moved(): return lax.ppermute(block, 'req', [(i, partner(i)) for i in range(count)])]
    pallas_call x0 -> x1, Pallas kernels: none -> 1.27 us  [finish(): pl.pallas_call(finish_body, out_shape=jax.ShapeDtypeStruct(hidden.shape,...]
  transfers between devices with their start and end apart: 30 -> 30, of which waited for: 20 -> 15; matrix products, arithmetic and copies ran while one was open for 1% -> 1% of each run, Pallas kernels for 20% -> 19%
where the time goes in v9:
time: 106 us; the launch traced here: 105 us
  starting transfers between devices  39.6 us (37%)
  waiting for transfers between devices  36.6 us (35%)
  Pallas kernels  22.5 us (21%)
  local copies, waits for them, and re-layouts  4.09 us (4%)
  other arithmetic  2.2 us (2%)
    ppermute x30, starting transfers between devices, moved(): return lax.ppermute(block, 'req', [(i, partner(i)) for i in range(count)])  39.6 us
    ppermute x30, waiting for transfers between devices, moved(): return lax.ppermute(block, 'req', [(i, partner(i)) for i in range(count)])  36.6 us
    pallas_call x2, Pallas kernels, ffn(): pl.pallas_call(ffn_body, out_shape=[jax.ShapeDtypeStruct((pair, held), jn...  13.5 us
    pallas_call x3, Pallas kernels, select(): pl.pallas_call(functools.partial(select_body, tokens, capacity, wanted),...  4.33 us
    unnamed x19, local copies, waits for them, and re-layouts  3.19 us
  transfers between devices with their start and end apart: 30, of which 15 were waited for; matrix products, arithmetic and copies ran while one was open for 1% of the time, Pallas kernels for 19%

profile of v9, /device:TPU:0, one launch (start us, length us, event | category | flops | bytes accessed | tf_op | source)
XLA Modules:
  0.0 105.4 jit_solution(14827844670014908208)
XLA Ops:
  0.0 0.8 reshape.34
  0.8 0.7 convert_bitcast_fusion
  1.5 0.7 pad_convert_fusion
  2.4 0.9 copy-done.1
  3.3 0.8 shard_map.73
  4.1 0.5 collective-permute-start
  4.6 0.9 collective-permute-done
  5.6 3.0 %collective-permute-start.1 = (bf16[32,1536]{1,0:T(8,128)(2,1)S(1)}, bf16[32,1536]{1,0:T(8,128)(2,1)S(1)}, u32[]{:S(2)}, u32[]{:S(2)}) collective-permute-start(bf16[32,1536]{1,0:T(8,128)(2,1)S(1)} %pad_maximum_fusion.2._), channel_id=1, source_target_pairs={{0,8},{1,9},{2,10},{3,11},{4,12},{5,13},{6,14},{7,15},{8,0},{9,1},... | collective-permute-start | bytes 294920 | tf_op jit(solution)/shard_map/ppermute | solution.py:30
  8.6 2.6 %collective-permute-start.2 = (bf16[32,1536]{1,0:T(8,128)(2,1)S(1)}, bf16[32,1536]{1,0:T(8,128)(2,1)S(1)}, u32[]{:S(2)}, u32[]{:S(2)}) collective-permute-start(bf16[32,1536]{1,0:T(8,128)(2,1)S(1)} %pad_maximum_fusion.2._), channel_id=1, source_target_pairs={{0,16},{1,17},{2,18},{3,19},{4,20},{5,21},{6,22},{7,23},{8,24},{9,... | collective-permute-start | bytes 294920 | tf_op jit(solution)/shard_map/ppermute | solution.py:30
  11.3 2.2 %copy-done = bf16[2880,720]{0,1:T(8,128)(2,1)S(1)} copy-done((bf16[2880,720]{0,1:T(8,128)(2,1)S(1)}, bf16[2880,720]{0,1:T(8,128)(2,1)}, u32[]{:S(2)}) %copy-start) | copy-done | bytes 4147224
  13.8 2.5 %collective-permute-done.2._ = bf16[32,1536]{1,0:T(8,128)(2,1)S(1)} collective-permute-done((bf16[32,1536]{1,0:T(8,128)(2,1)S(1)}, bf16[32,1536]{1,0:T(8,128)(2,1)S(1)}, u32[]{:S(2)}, u32[]{:S(2)}) %collective-permute-start.2) | collective-permute-done | bytes 98336 | tf_op jit(solution)/shard_map/ppermute | solution.py:30
  16.3 0.4 collective-permute-start.3
  17.2 3.7 %collective-permute-done.3 = bf16[32,1536]{1,0:T(8,128)(2,1)S(1)} collective-permute-done((bf16[32,1536]{1,0:T(8,128)(2,1)S(1)}, bf16[32,1536]{1,0:T(8,128)(2,1)S(1)}, u32[]{:S(2)}, u32[]{:S(2)}) %collective-permute-start.3) | collective-permute-done | bytes 98336 | tf_op jit(solution)/shard_map/ppermute | solution.py:30
  20.9 1.6 %collective-permute-start.4 = (bf16[128,1536]{1,0:T(8,128)(2,1)S(1)}, bf16[128,1536]{1,0:T(8,128)(2,1)S(1)}, u32[]{:S(2)}, u32[]{:S(2)}) collective-permute-start(bf16[128,1536]{1,0:T(8,128)(2,1)S(1)} %get-tuple-element.100), channel_id=1, source_target_pairs={{0,4},{1,3},{2,6},{3,1},{4,0},{5,7},{6,2},{7,5},{8,12},{9,11},{10,... | collective-permute-start | bytes 1179656 | tf_op jit(solution)/shard_map/ppermute | solution.py:30
  22.5 0.4 collective-permute-start.5
  22.9 2.7 %collective-permute-start.6 = (bf16[32,1536]{1,0:T(8,128)(2,1)S(1)}, bf16[32,1536]{1,0:T(8,128)(2,1)S(1)}, u32[]{:S(2)}, u32[]{:S(2)}) collective-permute-start(bf16[32,1536]{1,0:T(8,128)(2,1)S(1)} %get-tuple-element.54), channel_id=1, source_target_pairs={{0,16},{1,17},{2,18},{3,19},{4,20},{5,21},{6,22},{7,23},{8,24},{9,... | collective-permute-start | bytes 294920 | tf_op jit(solution)/shard_map/ppermute | solution.py:30
  25.6 1.3 %collective-permute-start.7 = (bf16[32,1536]{1,0:T(8,128)(2,1)S(1)}, bf16[32,1536]{1,0:T(8,128)(2,1)S(1)}, u32[]{:S(2)}, u32[]{:S(2)}) collective-permute-start(bf16[32,1536]{1,0:T(8,128)(2,1)S(1)} %get-tuple-element.54), channel_id=1, source_target_pairs={{0,24},{1,25},{2,26},{3,27},{4,28},{5,29},{6,30},{7,31},{8,16},{9,... | collective-permute-start | bytes 294920 | tf_op jit(solution)/shard_map/ppermute | solution.py:30
  26.9 1.9 %collective-permute-done.4.next_ref = bf16[128,1536]{1,0:T(8,128)(2,1)S(1)} collective-permute-done((bf16[128,1536]{1,0:T(8,128)(2,1)S(1)}, bf16[128,1536]{1,0:T(8,128)(2,1)S(1)}, u32[]{:S(2)}, u32[]{:S(2)}) %collective-permute-start.4) | collective-permute-done | bytes 393248 | tf_op jit(solution)/shard_map/ppermute | solution.py:30
  28.7 1.3 %shard_map.76 = bf16[192,1536]{1,0:T(8,128)(2,1)S(1)} custom-call(s32[3]{0:T(128)S(1)} %pad_add_fusion.places_ref, bf16[128,1536]{1,0:T(8,128)(2,1)S(1)} %get-tuple-element.100, bf16[128,1536]{1,0:T(8,128)(2,1)S(1)} %collective-permute-done.4.next_ref), custom_call_target="tpu_custom_call" | custom-call | flops 301989888 | bytes 1572864 | tf_op jit(solution)/shard_map/pallas_call | solution.py:99
  30.1 2.5 %collective-permute-start.9 = (bf16[192,1536]{1,0:T(8,128)(2,1)S(1)}, bf16[192,1536]{1,0:T(8,128)(2,1)S(1)}, u32[]{:S(2)}, u32[]{:S(2)}) collective-permute-start(bf16[192,1536]{1,0:T(8,128)(2,1)S(1)} %shard_map.76), channel_id=1, source_target_pairs={{0,2},{1,5},{2,0},{3,7},{4,6},{5,1},{6,4},{7,3},{8,10},{9,13},{10,... | collective-permute-start | bytes 1769480 | tf_op jit(solution)/shard_map/ppermute | solution.py:30
  32.6 1.3 %shard_map.77 = (bf16[192,1536]{1,0:T(8,128)(2,1)S(1)}, f32[128,128]{1,0:T(8,128)S(1)}, f32[128,128]{1,0:T(8,128)S(1)}) custom-call(s32[3]{0:T(128)S(1)} %pad_add_fusion.places_ref, bf16[128,1536]{1,0:T(8,128)(2,1)S(1)} %get-tuple-element.100, bf16[128,1536]{1,0:T(8,128)(2,1)S(1)} %collective-permute-done.4.next_ref), custom_call_target="tpu_custom_call" | custom-call | flops 301989888 | bytes 1572864 | tf_op jit(solution)/shard_map/pallas_call | solution.py:99
  34.0 1.6 %collective-permute-start.8 = (bf16[128,1536]{1,0:T(8,128)(2,1)S(1)}, bf16[128,1536]{1,0:T(8,128)(2,1)S(1)}, u32[]{:S(2)}, u32[]{:S(2)}) collective-permute-start(bf16[128,1536]{1,0:T(8,128)(2,1)S(1)} %constant_dynamic-update-slice_fusion.5.near_ref), channel_id=1, source_target_pairs={{0,4},{1,3},{2,6},{3,1},{4,0},{5,7},{6,2},{7,5},{8,12},{9,11},{10,... | collective-permute-start | bytes 1179656 | tf_op jit(solution)/shard_map/ppermute | solution.py:30
  36.0 5.9 %collective-permute-done.8.next_ref = bf16[128,1536]{1,0:T(8,128)(2,1)S(1)} collective-permute-done((bf16[128,1536]{1,0:T(8,128)(2,1)S(1)}, bf16[128,1536]{1,0:T(8,128)(2,1)S(1)}, u32[]{:S(2)}, u32[]{:S(2)}) %collective-permute-start.8) | collective-permute-done | bytes 393248 | tf_op jit(solution)/shard_map/ppermute | solution.py:30
  41.8 1.6 %shard_map.79 = (bf16[192,1536]{1,0:T(8,128)(2,1)S(1)}, bf16[192,1536]{1,0:T(8,128)(2,1)S(1)}, f32[128,128]{1,0:T(8,128)S(1)}, f32[128,128]{1,0:T(8,128)S(1)}) custom-call(s32[3]{0:T(128)S(1)} %pad_add_fusion.places_ref, bf16[128,1536]{1,0:T(8,128)(2,1)S(1)} %constant_dynamic-update-slice_fusion.5.near_ref, bf16[128,1536]{1,0:T(8,128)(2,1)S(1)} %collective-permute-done.8.next_ref), custom_call_target="tpu_custom_call" | custom-call | flops 301989888 | bytes 1572864 | tf_op jit(solution)/shard_map/pallas_call | solution.py:99
  43.6 1.5 %collective-permute-start.10 = (bf16[192,1536]{1,0:T(8,128)(2,1)S(1)}, bf16[192,1536]{1,0:T(8,128)(2,1)S(1)}, u32[]{:S(2)}, u32[]{:S(2)}) collective-permute-start(bf16[192,1536]{1,0:T(8,128)(2,1)S(1)} %get-tuple-element.62), channel_id=1, source_target_pairs={{0,2},{1,5},{2,0},{3,7},{4,6},{5,1},{6,4},{7,3},{8,10},{9,13},{10,... | collective-permute-start | bytes 1769480 | tf_op jit(solution)/shard_map/ppermute | solution.py:30
  45.1 0.4 collective-permute-done.12.other_far_ref
  45.6 6.7 %shard_map.80 = (f32[192,1536]{1,0:T(8,128)S(1)}, f32[192,1536]{1,0:T(8,128)S(1)}, bf16[192,1536]{1,0:T(8,128)(2,1)S(1)}, bf16[192,1536]{1,0:T(8,128)(2,1)S(1)}) custom-call(s32[3]{0:T(128)S(1)} %pad_add_fusion.places_ref, bf16[192,1536]{1,0:T(8,128)(2,1)S(1)} %get-tuple-element.59._.mine_near_ref, ...), custom_call_target="tpu_custom_call" | custom-call | flops 4777574400 | bytes 17160192 | tf_op jit(solution)/shard_map/pallas_call | solution.py:215
  52.3 1.3 %collective-permute-done.10.mine_far_ref = bf16[192,1536]{1,0:T(8,128)(2,1)S(1)} collective-permute-done((bf16[192,1536]{1,0:T(8,128)(2,1)S(1)}, bf16[192,1536]{1,0:T(8,128)(2,1)S(1)}, u32[]{:S(2)}, u32[]{:S(2)}) %collective-permute-start.10) | collective-permute-done | bytes 589856 | tf_op jit(solution)/shard_map/ppermute | solution.py:30
  53.5 0.5 collective-permute-start.17
  54.1 0.5 collective-permute-start.13
  54.6 1.0 collective-permute-done.14
  55.7 1.5 %collective-permute-start.15 = (bf16[192,1536]{1,0:T(8,128)(2,1)S(1)}, bf16[192,1536]{1,0:T(8,128)(2,1)S(1)}, u32[]{:S(2)}, u32[]{:S(2)}) collective-permute-start(bf16[192,1536]{1,0:T(8,128)(2,1)S(1)} %add_convert_fusion.1), channel_id=1, source_target_pairs={{0,2},{1,5},{2,0},{3,7},{4,6},{5,1},{6,4},{7,3},{8,10},{9,13},{10,... | collective-permute-start | bytes 1769480 | tf_op jit(solution)/shard_map/ppermute | solution.py:30
  57.2 6.8 %shard_map.82 = (f32[192,1536]{1,0:T(8,128)S(1)}, f32[192,1536]{1,0:T(8,128)S(1)}, bf16[192,1536]{1,0:T(8,128)(2,1)S(1)}, bf16[192,1536]{1,0:T(8,128)(2,1)S(1)}) custom-call(s32[3]{0:T(128)S(1)} %pad_add_fusion.places_ref, bf16[192,1536]{1,0:T(8,128)(2,1)S(1)} %get-tuple-element.79.mine_near_ref, bf16[192,1536]{1,0:T(8,128)(2,1)S(1)} %collective-permute-done.10.mine_far_ref, ...), custom_call_target="tpu_custom_call" | custom-call | flops 4777574400 | bytes 17160192 | tf_op jit(solution)/shard_map/pallas_call | solution.py:215
  64.7 0.9 collective-permute-done.15.arrived_ref
  65.6 0.6 shard_map.81
  66.2 1.6 %collective-permute-start.16 = (bf16[128,1536]{1,0:T(8,128)(2,1)S(1)}, bf16[128,1536]{1,0:T(8,128)(2,1)S(1)}, u32[]{:S(2)}, u32[]{:S(2)}) collective-permute-start(bf16[128,1536]{1,0:T(8,128)(2,1)S(1)} %get-tuple-element.76), channel_id=1, source_target_pairs={{0,4},{1,3},{2,6},{3,1},{4,0},{5,7},{6,2},{7,5},{8,12},{9,11},{10,... | collective-permute-start | bytes 1179656 | tf_op jit(solution)/shard_map/ppermute | solution.py:30
  68.0 0.5 collective-permute-start.21
  68.5 9.8 %collective-permute-done.16 = bf16[128,1536]{1,0:T(8,128)(2,1)S(1)} collective-permute-done((bf16[128,1536]{1,0:T(8,128)(2,1)S(1)}, bf16[128,1536]{1,0:T(8,128)(2,1)S(1)}, u32[]{:S(2)}, u32[]{:S(2)}) %collective-permute-start.16) | collective-permute-done | bytes 393248 | tf_op jit(solution)/shard_map/ppermute | solution.py:30
  78.7 0.4 shard_map.83._
  79.2 1.6 %collective-permute-start.25 = (bf16[128,1536]{1,0:T(8,128)(2,1)S(1)}, bf16[128,1536]{1,0:T(8,128)(2,1)S(1)}, u32[]{:S(2)}, u32[]{:S(2)}) collective-permute-start(bf16[128,1536]{1,0:T(8,128)(2,1)S(1)} %shard_map.83._), channel_id=1, source_target_pairs={{0,4},{1,3},{2,6},{3,1},{4,0},{5,7},{6,2},{7,5},{8,12},{9,11},{10,... | collective-permute-start | bytes 1179656 | tf_op jit(solution)/shard_map/ppermute | solution.py:30
  81.3 2.0 %collective-permute-start.22 = (bf16[32,1536]{1,0:T(8,128)(2,1)S(1)}, bf16[32,1536]{1,0:T(8,128)(2,1)S(1)}, u32[]{:S(2)}, u32[]{:S(2)}) collective-permute-start(bf16[32,1536]{1,0:T(8,128)(2,1)S(1)} %get-tuple-element.93), channel_id=1, source_target_pairs={{0,8},{1,9},{2,10},{3,11},{4,12},{5,13},{6,14},{7,15},{8,0},{9,1},... | collective-permute-start | bytes 294920 | tf_op jit(solution)/shard_map/ppermute | solution.py:30
  83.3 3.7 %collective-permute-done.25 = bf16[128,1536]{1,0:T(8,128)(2,1)S(1)} collective-permute-done((bf16[128,1536]{1,0:T(8,128)(2,1)S(1)}, bf16[128,1536]{1,0:T(8,128)(2,1)S(1)}, u32[]{:S(2)}, u32[]{:S(2)}) %collective-permute-start.25) | collective-permute-done | bytes 393248 | tf_op jit(solution)/shard_map/ppermute | solution.py:30
  87.3 6.9 %collective-permute-start.24 = (bf16[32,1536]{1,0:T(8,128)(2,1)S(1)}, bf16[32,1536]{1,0:T(8,128)(2,1)S(1)}, u32[]{:S(2)}, u32[]{:S(2)}) collective-permute-start(bf16[32,1536]{1,0:T(8,128)(2,1)S(1)} %add_convert_fusion.2), channel_id=1, source_target_pairs={{0,16},{1,17},{2,18},{3,19},{4,20},{5,21},{6,22},{7,23},{8,24},{9,... | collective-permute-start | bytes 294920 | tf_op jit(solution)/shard_map/ppermute | solution.py:30
  94.3 5.4 %collective-permute-start.28 = (bf16[32,1536]{1,0:T(8,128)(2,1)S(1)}, bf16[32,1536]{1,0:T(8,128)(2,1)S(1)}, u32[]{:S(2)}, u32[]{:S(2)}) collective-permute-start(bf16[32,1536]{1,0:T(8,128)(2,1)S(1)} %fusion.1), channel_id=1, source_target_pairs={{0,16},{1,17},{2,18},{3,19},{4,20},{5,21},{6,22},{7,23},{8,24},{9,... | collective-permute-start | bytes 294920 | tf_op jit(solution)/shard_map/ppermute | solution.py:30
  99.7 0.5 collective-permute-done.26
  100.2 2.4 %collective-permute-done.28 = bf16[32,1536]{1,0:T(8,128)(2,1)S(1)} collective-permute-done((bf16[32,1536]{1,0:T(8,128)(2,1)S(1)}, bf16[32,1536]{1,0:T(8,128)(2,1)S(1)}, u32[]{:S(2)}, u32[]{:S(2)}) %collective-permute-start.28) | collective-permute-done | bytes 98336 | tf_op jit(solution)/shard_map/ppermute | solution.py:30
  102.9 1.3 %collective-permute-done.29.taken_ref = bf16[2,16,1536]{2,1,0:T(8,128)(2,1)S(1)} collective-permute-done((bf16[2,16,1536]{2,1,0:T(8,128)(2,1)S(1)}, bf16[2,16,1536]{2,1,0:T(8,128)(2,1)S(1)}, u32[]{:S(2)}, u32[]{:S(2)}) %collective-permute-start.29) | collective-permute-done | bytes 98336 | tf_op jit(solution)/shard_map/ppermute | solution.py:30
  104.1 1.3 %shard_map.85 = bf16[2,16,2880]{2,1,0:T(8,128)(2,1)} custom-call(s32[3]{0:T(128)S(1)} %pad_add_fusion.places_ref, bf16[2,16,2880]{2,1,0:T(8,128)(2,1)S(1)} %copy-done.2, f32[2,16,1536]{2,1,0:T(8,128)S(1)} %broadcast_select_fusion.own_ref, bf16[2,16,1536]{2,1,0:T(8,128)(2,1)S(1)} %collective-permute-done.29.taken_ref), custom_call_target="tpu_custom_call" | custom-call | tf_op jit(solution)/shard_map/pallas_call | solution.py:347
  (72 shorter events, 3.9 us)
Async XLA Ops:
  2.4 0.9 copy-start.1
  3.3 13.5 %slice-start.2 = ((s8[4239360]{0:T(1024)(128)(4,1)}), s8[45056]{0:T(1024)(128)(4,1)S(1)}, s32[]{:S(2)}) async-start(s8[4239360]{0:T(1024)(128)(4,1)} %bitcast.25), calls=%async_computation.2 | async-start | bytes 90112
  4.1 1.5 %collective-permute-start = (bf16[2,16,1536]{2,1,0:T(8,128)(2,1)S(1)}, bf16[2,16,1536]{2,1,0:T(8,128)(2,1)S(1)}, u32[]{:S(2)}, u32[]{:S(2)}) collective-permute-start(bf16[2,16,1536]{2,1,0:T(8,128)(2,1)S(1)} %get-tuple-element.47), channel_id=1, source_target_pairs={{0,1},{1,0},{2,3},{3,2},{4,5},{5,4},{6,7},{7,6},{8,9},{9,8},{10,11... | collective-permute-start | bytes 294920 | tf_op jit(solution)/shard_map/ppermute | solution.py:30
  5.6 11.1 %collective-permute-start.1 = (bf16[32,1536]{1,0:T(8,128)(2,1)S(1)}, bf16[32,1536]{1,0:T(8,128)(2,1)S(1)}, u32[]{:S(2)}, u32[]{:S(2)}) collective-permute-start(bf16[32,1536]{1,0:T(8,128)(2,1)S(1)} %pad_maximum_fusion.2._), channel_id=1, source_target_pairs={{0,8},{1,9},{2,10},{3,11},{4,12},{5,13},{6,14},{7,15},{8,0},{9,1},... | collective-permute-start | bytes 294920 | tf_op jit(solution)/shard_map/ppermute | solution.py:30
  8.6 7.6 %collective-permute-start.2 = (bf16[32,1536]{1,0:T(8,128)(2,1)S(1)}, bf16[32,1536]{1,0:T(8,128)(2,1)S(1)}, u32[]{:S(2)}, u32[]{:S(2)}) collective-permute-start(bf16[32,1536]{1,0:T(8,128)(2,1)S(1)} %pad_maximum_fusion.2._), channel_id=1, source_target_pairs={{0,16},{1,17},{2,18},{3,19},{4,20},{5,21},{6,22},{7,23},{8,24},{9,... | collective-permute-start | bytes 294920 | tf_op jit(solution)/shard_map/ppermute | solution.py:30
  11.2 2.2 %copy-start = (bf16[2880,720]{0,1:T(8,128)(2,1)S(1)}, bf16[2880,720]{0,1:T(8,128)(2,1)}, u32[]{:S(2)}) copy-start(bf16[2880,720]{0,1:T(8,128)(2,1)} %param.9) | copy-start | bytes 12441604
  13.5 3.3 %slice-start.3 = ((s8[4239360]{0:T(1024)(128)(4,1)}), s8[4194304]{0:T(1024)(128)(4,1)S(1)}, s32[]{:S(2)}) async-start(s8[4239360]{0:T(1024)(128)(4,1)} %bitcast.25), calls=%async_computation.3 | async-start | bytes 8388608
  16.3 4.6 %collective-permute-start.3 = (bf16[32,1536]{1,0:T(8,128)(2,1)S(1)}, bf16[32,1536]{1,0:T(8,128)(2,1)S(1)}, u32[]{:S(2)}, u32[]{:S(2)}) collective-permute-start(bf16[32,1536]{1,0:T(8,128)(2,1)S(1)} %collective-permute-done.2._), channel_id=1, source_target_pairs={{0,8},{1,9},{2,10},{3,11},{4,12},{5,13},{6,14},{7,15},{8,0},{9,1},... | collective-permute-start | bytes 294920 | tf_op jit(solution)/shard_map/ppermute | solution.py:30
  16.7 18.9 %slice-start = ((s8[4239360]{0:T(1024)(128)(4,1)}), s8[4194304]{0:T(1024)(128)(4,1)S(1)}, s32[]{:S(2)}) async-start(s8[4239360]{0:T(1024)(128)(4,1)} %bitcast.22), calls=%async_computation | async-start | bytes 8388608
  16.8 18.8 %slice-start.1 = ((s8[4239360]{0:T(1024)(128)(4,1)}), s8[45056]{0:T(1024)(128)(4,1)S(1)}, s32[]{:S(2)}) async-start(s8[4239360]{0:T(1024)(128)(4,1)} %bitcast.22), calls=%async_computation.1 | async-start | bytes 90112
  20.9 7.8 %collective-permute-start.4 = (bf16[128,1536]{1,0:T(8,128)(2,1)S(1)}, bf16[128,1536]{1,0:T(8,128)(2,1)S(1)}, u32[]{:S(2)}, u32[]{:S(2)}) collective-permute-start(bf16[128,1536]{1,0:T(8,128)(2,1)S(1)} %get-tuple-element.100), channel_id=1, source_target_pairs={{0,4},{1,3},{2,6},{3,1},{4,0},{5,7},{6,2},{7,5},{8,12},{9,11},{10,... | collective-permute-start | bytes 1179656 | tf_op jit(solution)/shard_map/ppermute | solution.py:30
  22.5 11.4 %collective-permute-start.5 = (bf16[32,1536]{1,0:T(8,128)(2,1)S(1)}, bf16[32,1536]{1,0:T(8,128)(2,1)S(1)}, u32[]{:S(2)}, u32[]{:S(2)}) collective-permute-start(bf16[32,1536]{1,0:T(8,128)(2,1)S(1)} %get-tuple-element.54), channel_id=1, source_target_pairs={{0,8},{1,9},{2,10},{3,11},{4,12},{5,13},{6,14},{7,15},{8,0},{9,1},... | collective-permute-start | bytes 294920 | tf_op jit(solution)/shard_map/ppermute | solution.py:30
  22.9 11.0 %collective-permute-start.6 = (bf16[32,1536]{1,0:T(8,128)(2,1)S(1)}, bf16[32,1536]{1,0:T(8,128)(2,1)S(1)}, u32[]{:S(2)}, u32[]{:S(2)}) collective-permute-start(bf16[32,1536]{1,0:T(8,128)(2,1)S(1)} %get-tuple-element.54), channel_id=1, source_target_pairs={{0,16},{1,17},{2,18},{3,19},{4,20},{5,21},{6,22},{7,23},{8,24},{9,... | collective-permute-start | bytes 294920 | tf_op jit(solution)/shard_map/ppermute | solution.py:30
  25.6 8.3 %collective-permute-start.7 = (bf16[32,1536]{1,0:T(8,128)(2,1)S(1)}, bf16[32,1536]{1,0:T(8,128)(2,1)S(1)}, u32[]{:S(2)}, u32[]{:S(2)}) collective-permute-start(bf16[32,1536]{1,0:T(8,128)(2,1)S(1)} %get-tuple-element.54), channel_id=1, source_target_pairs={{0,24},{1,25},{2,26},{3,27},{4,28},{5,29},{6,30},{7,31},{8,16},{9,... | collective-permute-start | bytes 294920 | tf_op jit(solution)/shard_map/ppermute | solution.py:30
  30.1 13.4 %collective-permute-start.9 = (bf16[192,1536]{1,0:T(8,128)(2,1)S(1)}, bf16[192,1536]{1,0:T(8,128)(2,1)S(1)}, u32[]{:S(2)}, u32[]{:S(2)}) collective-permute-start(bf16[192,1536]{1,0:T(8,128)(2,1)S(1)} %shard_map.76), channel_id=1, source_target_pairs={{0,2},{1,5},{2,0},{3,7},{4,6},{5,1},{6,4},{7,3},{8,10},{9,13},{10,... | collective-permute-start | bytes 1769480 | tf_op jit(solution)/shard_map/ppermute | solution.py:30
  34.0 7.8 %collective-permute-start.8 = (bf16[128,1536]{1,0:T(8,128)(2,1)S(1)}, bf16[128,1536]{1,0:T(8,128)(2,1)S(1)}, u32[]{:S(2)}, u32[]{:S(2)}) collective-permute-start(bf16[128,1536]{1,0:T(8,128)(2,1)S(1)} %constant_dynamic-update-slice_fusion.5.near_ref), channel_id=1, source_target_pairs={{0,4},{1,3},{2,6},{3,1},{4,0},{5,7},{6,2},{7,5},{8,12},{9,11},{10,... | collective-permute-start | bytes 1179656 | tf_op jit(solution)/shard_map/ppermute | solution.py:30
  35.6 9.5 %collective-permute-start.11 = (bf16[192,1536]{1,0:T(8,128)(2,1)S(1)}, bf16[192,1536]{1,0:T(8,128)(2,1)S(1)}, u32[]{:S(2)}, u32[]{:S(2)}) collective-permute-start(bf16[192,1536]{1,0:T(8,128)(2,1)S(1)} %get-tuple-element.59._.mine_near_ref), channel_id=1, source_target_pairs={{0,1},{1,0},{2,3},{3,2},{4,5},{5,4},{6,7},{7,6},{8,9},{9,8},{10,11... | collective-permute-start | bytes 1769480 | tf_op jit(solution)/shard_map/ppermute | solution.py:30
  43.5 2.1 %collective-permute-start.12 = (bf16[192,1536]{1,0:T(8,128)(2,1)S(1)}, bf16[192,1536]{1,0:T(8,128)(2,1)S(1)}, u32[]{:S(2)}, u32[]{:S(2)}) collective-permute-start(bf16[192,1536]{1,0:T(8,128)(2,1)S(1)} %collective-permute-done.9.mine_far_ref), channel_id=1, source_target_pairs={{0,1},{1,0},{2,3},{3,2},{4,5},{5,4},{6,7},{7,6},{8,9},{9,8},{10,11... | collective-permute-start | bytes 1769480 | tf_op jit(solution)/shard_map/ppermute | solution.py:30
  43.6 9.9 %collective-permute-start.10 = (bf16[192,1536]{1,0:T(8,128)(2,1)S(1)}, bf16[192,1536]{1,0:T(8,128)(2,1)S(1)}, u32[]{:S(2)}, u32[]{:S(2)}) collective-permute-start(bf16[192,1536]{1,0:T(8,128)(2,1)S(1)} %get-tuple-element.62), channel_id=1, source_target_pairs={{0,2},{1,5},{2,0},{3,7},{4,6},{5,1},{6,4},{7,3},{8,10},{9,13},{10,... | collective-permute-start | bytes 1769480 | tf_op jit(solution)/shard_map/ppermute | solution.py:30
  53.5 2.0 %collective-permute-start.14 = (bf16[192,1536]{1,0:T(8,128)(2,1)S(1)}, bf16[192,1536]{1,0:T(8,128)(2,1)S(1)}, u32[]{:S(2)}, u32[]{:S(2)}) collective-permute-start(bf16[192,1536]{1,0:T(8,128)(2,1)S(1)} %get-tuple-element.74), channel_id=1, source_target_pairs={{0,1},{1,0},{2,3},{3,2},{4,5},{5,4},{6,7},{7,6},{8,9},{9,8},{10,11... | collective-permute-start | bytes 1769480 | tf_op jit(solution)/shard_map/ppermute | solution.py:30
  53.5 3.7 %collective-permute-start.17 = (bf16[192,1536]{1,0:T(8,128)(2,1)S(1)}, bf16[192,1536]{1,0:T(8,128)(2,1)S(1)}, u32[]{:S(2)}, u32[]{:S(2)}) collective-permute-start(bf16[192,1536]{1,0:T(8,128)(2,1)S(1)} %get-tuple-element.79.mine_near_ref), channel_id=1, source_target_pairs={{0,1},{1,0},{2,3},{3,2},{4,5},{5,4},{6,7},{7,6},{8,9},{9,8},{10,11... | collective-permute-start | bytes 1769480 | tf_op jit(solution)/shard_map/ppermute | solution.py:30
  54.1 3.2 %collective-permute-start.18 = (bf16[192,1536]{1,0:T(8,128)(2,1)S(1)}, bf16[192,1536]{1,0:T(8,128)(2,1)S(1)}, u32[]{:S(2)}, u32[]{:S(2)}) collective-permute-start(bf16[192,1536]{1,0:T(8,128)(2,1)S(1)} %collective-permute-done.10.mine_far_ref), channel_id=1, source_target_pairs={{0,1},{1,0},{2,3},{3,2},{4,5},{5,4},{6,7},{7,6},{8,9},{9,8},{10,11... | collective-permute-start | bytes 1769480 | tf_op jit(solution)/shard_map/ppermute | solution.py:30
  54.1 10.6 %collective-permute-start.13 = (bf16[192,1536]{1,0:T(8,128)(2,1)S(1)}, bf16[192,1536]{1,0:T(8,128)(2,1)S(1)}, u32[]{:S(2)}, u32[]{:S(2)}) collective-permute-start(bf16[192,1536]{1,0:T(8,128)(2,1)S(1)} %get-tuple-element.72), channel_id=1, source_target_pairs={{0,1},{1,0},{2,3},{3,2},{4,5},{5,4},{6,7},{7,6},{8,9},{9,8},{10,11... | collective-permute-start | bytes 1769480 | tf_op jit(solution)/shard_map/ppermute | solution.py:30
  55.7 9.9 %collective-permute-start.15 = (bf16[192,1536]{1,0:T(8,128)(2,1)S(1)}, bf16[192,1536]{1,0:T(8,128)(2,1)S(1)}, u32[]{:S(2)}, u32[]{:S(2)}) collective-permute-start(bf16[192,1536]{1,0:T(8,128)(2,1)S(1)} %add_convert_fusion.1), channel_id=1, source_target_pairs={{0,2},{1,5},{2,0},{3,7},{4,6},{5,1},{6,4},{7,3},{8,10},{9,13},{10,... | collective-permute-start | bytes 1769480 | tf_op jit(solution)/shard_map/ppermute | solution.py:30
  64.1 3.7 %collective-permute-start.20 = (bf16[192,1536]{1,0:T(8,128)(2,1)S(1)}, bf16[192,1536]{1,0:T(8,128)(2,1)S(1)}, u32[]{:S(2)}, u32[]{:S(2)}) collective-permute-start(bf16[192,1536]{1,0:T(8,128)(2,1)S(1)} %get-tuple-element.84), channel_id=1, source_target_pairs={{0,1},{1,0},{2,3},{3,2},{4,5},{5,4},{6,7},{7,6},{8,9},{9,8},{10,11... | collective-permute-start | bytes 1769480 | tf_op jit(solution)/shard_map/ppermute | solution.py:30
  64.3 14.1 %collective-permute-start.19 = (bf16[192,1536]{1,0:T(8,128)(2,1)S(1)}, bf16[192,1536]{1,0:T(8,128)(2,1)S(1)}, u32[]{:S(2)}, u32[]{:S(2)}) collective-permute-start(bf16[192,1536]{1,0:T(8,128)(2,1)S(1)} %get-tuple-element.82), channel_id=1, source_target_pairs={{0,1},{1,0},{2,3},{3,2},{4,5},{5,4},{6,7},{7,6},{8,9},{9,8},{10,11... | collective-permute-start | bytes 1769480 | tf_op jit(solution)/shard_map/ppermute | solution.py:30
  66.2 12.1 %collective-permute-start.16 = (bf16[128,1536]{1,0:T(8,128)(2,1)S(1)}, bf16[128,1536]{1,0:T(8,128)(2,1)S(1)}, u32[]{:S(2)}, u32[]{:S(2)}) collective-permute-start(bf16[128,1536]{1,0:T(8,128)(2,1)S(1)} %get-tuple-element.76), channel_id=1, source_target_pairs={{0,4},{1,3},{2,6},{3,1},{4,0},{5,7},{6,2},{7,5},{8,12},{9,11},{10,... | collective-permute-start | bytes 1179656 | tf_op jit(solution)/shard_map/ppermute | solution.py:30
  68.0 10.7 %collective-permute-start.21 = (bf16[192,1536]{1,0:T(8,128)(2,1)S(1)}, bf16[192,1536]{1,0:T(8,128)(2,1)S(1)}, u32[]{:S(2)}, u32[]{:S(2)}) collective-permute-start(bf16[192,1536]{1,0:T(8,128)(2,1)S(1)} %add_convert_fusion), channel_id=1, source_target_pairs={{0,2},{1,5},{2,0},{3,7},{4,6},{5,1},{6,4},{7,3},{8,10},{9,13},{10,... | collective-permute-start | bytes 1769480 | tf_op jit(solution)/shard_map/ppermute | solution.py:30
  79.2 7.8 %collective-permute-start.25 = (bf16[128,1536]{1,0:T(8,128)(2,1)S(1)}, bf16[128,1536]{1,0:T(8,128)(2,1)S(1)}, u32[]{:S(2)}, u32[]{:S(2)}) collective-permute-start(bf16[128,1536]{1,0:T(8,128)(2,1)S(1)} %shard_map.83._), channel_id=1, source_target_pairs={{0,4},{1,3},{2,6},{3,1},{4,0},{5,7},{6,2},{7,5},{8,12},{9,11},{10,... | collective-permute-start | bytes 1179656 | tf_op jit(solution)/shard_map/ppermute | solution.py:30
  81.2 6.1 %collective-permute-start.23 = (bf16[32,1536]{1,0:T(8,128)(2,1)S(1)}, bf16[32,1536]{1,0:T(8,128)(2,1)S(1)}, u32[]{:S(2)}, u32[]{:S(2)}) collective-permute-start(bf16[32,1536]{1,0:T(8,128)(2,1)S(1)} %get-tuple-element.94), channel_id=1, source_target_pairs={{0,8},{1,9},{2,10},{3,11},{4,12},{5,13},{6,14},{7,15},{8,0},{9,1},... | collective-permute-start | bytes 294920 | tf_op jit(solution)/shard_map/ppermute | solution.py:30
  81.3 18.4 %collective-permute-start.22 = (bf16[32,1536]{1,0:T(8,128)(2,1)S(1)}, bf16[32,1536]{1,0:T(8,128)(2,1)S(1)}, u32[]{:S(2)}, u32[]{:S(2)}) collective-permute-start(bf16[32,1536]{1,0:T(8,128)(2,1)S(1)} %get-tuple-element.93), channel_id=1, source_target_pairs={{0,8},{1,9},{2,10},{3,11},{4,12},{5,13},{6,14},{7,15},{8,0},{9,1},... | collective-permute-start | bytes 294920 | tf_op jit(solution)/shard_map/ppermute | solution.py:30
  87.1 7.1 %collective-permute-start.27 = (bf16[32,1536]{1,0:T(8,128)(2,1)S(1)}, bf16[32,1536]{1,0:T(8,128)(2,1)S(1)}, u32[]{:S(2)}, u32[]{:S(2)}) collective-permute-start(bf16[32,1536]{1,0:T(8,128)(2,1)S(1)} %get-tuple-element.96), channel_id=1, source_target_pairs={{0,8},{1,9},{2,10},{3,11},{4,12},{5,13},{6,14},{7,15},{8,0},{9,1},... | collective-permute-start | bytes 294920 | tf_op jit(solution)/shard_map/ppermute | solution.py:30
  87.3 12.4 %collective-permute-start.24 = (bf16[32,1536]{1,0:T(8,128)(2,1)S(1)}, bf16[32,1536]{1,0:T(8,128)(2,1)S(1)}, u32[]{:S(2)}, u32[]{:S(2)}) collective-permute-start(bf16[32,1536]{1,0:T(8,128)(2,1)S(1)} %add_convert_fusion.2), channel_id=1, source_target_pairs={{0,16},{1,17},{2,18},{3,19},{4,20},{5,21},{6,22},{7,23},{8,24},{9,... | collective-permute-start | bytes 294920 | tf_op jit(solution)/shard_map/ppermute | solution.py:30
  94.3 6.0 %collective-permute-start.26 = (bf16[32,1536]{1,0:T(8,128)(2,1)S(1)}, bf16[32,1536]{1,0:T(8,128)(2,1)S(1)}, u32[]{:S(2)}, u32[]{:S(2)}) collective-permute-start(bf16[32,1536]{1,0:T(8,128)(2,1)S(1)} %get-tuple-element.95), channel_id=1, source_target_pairs={{0,8},{1,9},{2,10},{3,11},{4,12},{5,13},{6,14},{7,15},{8,0},{9,1},... | collective-permute-start | bytes 294920 | tf_op jit(solution)/shard_map/ppermute | solution.py:30
  94.3 9.8 %copy-start.2 = (bf16[2,16,2880]{2,1,0:T(8,128)(2,1)S(1)}, bf16[2,16,2880]{2,1,0:T(8,128)(2,1)}, u32[]{:S(2)}) copy-start(bf16[2,16,2880]{2,1,0:T(8,128)(2,1)} %hidden_ref.3) | copy-start | bytes 552964
  94.3 8.4 %collective-permute-start.28 = (bf16[32,1536]{1,0:T(8,128)(2,1)S(1)}, bf16[32,1536]{1,0:T(8,128)(2,1)S(1)}, u32[]{:S(2)}, u32[]{:S(2)}) collective-permute-start(bf16[32,1536]{1,0:T(8,128)(2,1)S(1)} %fusion.1), channel_id=1, source_target_pairs={{0,16},{1,17},{2,18},{3,19},{4,20},{5,21},{6,22},{7,23},{8,24},{9,... | collective-permute-start | bytes 294920 | tf_op jit(solution)/shard_map/ppermute | solution.py:30
  102.7 1.4 %collective-permute-start.29 = (bf16[2,16,1536]{2,1,0:T(8,128)(2,1)S(1)}, bf16[2,16,1536]{2,1,0:T(8,128)(2,1)S(1)}, u32[]{:S(2)}, u32[]{:S(2)}) collective-permute-start(bf16[2,16,1536]{2,1,0:T(8,128)(2,1)S(1)} %select_convert_fusion), channel_id=1, source_target_pairs={{0,1},{1,0},{2,3},{3,2},{4,5},{5,4},{6,7},{7,6},{8,9},{9,8},{10,11... | collective-permute-start | bytes 294920 | tf_op jit(solution)/shard_map/ppermute | solution.py:30

commit v10 on v9

--- a/solution.py
+++ b/solution.py
@@ -403,7 +403,9 @@
     pair = pairs[0]
     (gate_v,) = preload(pair, w_gate.T)
     if distant == 4:
-        crossed, beside = moved(pair, far(2)), moved(pair, far(1))
+        crossed = moved(pair, far(2))
+        again, pairs[-1] = tied(pair, pairs[-1])
+        beside = moved(again, far(1))
         crossed, gate_v = tied(crossed, gate_v)
         (up_v,) = preload(crossed, w_up.T)
         passed = moved(crossed, far(1))
@@ -447,9 +449,8 @@
     def far_hop(block):
         block = block.reshape(distant, -1, held)
         if distant == 4:
-            through = moved(block[3].astype(jnp.bfloat16), far(1))
-            beside = moved(block[1].astype(jnp.bfloat16), far(1))
-            return [block[0], [beside], rounded_sum(block[2], through)]
+            odd = moved(jnp.stack([block[1], block[3]]).astype(jnp.bfloat16), far(1))
+            return [block[0], [odd[0]], rounded_sum(block[2], odd[1])]
         return [block[0], [moved(block[j].astype(jnp.bfloat16), far(j)) for j in range(1, distant)], None]
 
     def settled(kept, arrivals, cross):

time: 106 us -> 106 us (level)
  waiting for transfers between devices: 36.6 us -> 45 us
  starting transfers between devices: 39.6 us -> 31.9 us
    ppermute x30 -> x28, waiting for transfers between devices: 36.6 us -> 45 us  [moved(): return lax.ppermute(block, 'req', [(i, partner(i)) for i in range(count)])]
    ppermute x30 -> x28, starting transfers between devices: 39.6 us -> 31.9 us  [moved(): return lax.ppermute(block, 'req', [(i, partner(i)) for i in range(count)])]
  transfers between devices with their start and end apart: 30 -> 28, of which waited for: 15 -> 18; matrix products, arithmetic and copies ran while one was open for 1% -> 1% of each run, Pallas kernels for 19% -> 19%
where the time goes in v10:
time: 106 us
  waiting for transfers between devices  45 us (42%)
  starting transfers between devices  31.9 us (30%)
  Pallas kernels  22.5 us (21%)
  local copies, waits for them, and re-layouts  4.1 us (4%)
  other arithmetic  2.23 us (2%)
    ppermute x28, waiting for transfers between devices, moved(): return lax.ppermute(block, 'req', [(i, partner(i)) for i in range(count)])  45 us
    ppermute x28, starting transfers between devices, moved(): return lax.ppermute(block, 'req', [(i, partner(i)) for i in range(count)])  31.9 us
    pallas_call x2, Pallas kernels, ffn(): pl.pallas_call(ffn_body, out_shape=[jax.ShapeDtypeStruct((pair, held), jn...  13.5 us
    pallas_call x3, Pallas kernels, select(): pl.pallas_call(functools.partial(select_body, tokens, capacity, wanted),...  4.33 us
    unnamed x19, local copies, waits for them, and re-layouts  3.19 us
  transfers between devices with their start and end apart: 28, of which 18 were waited for; matrix products, arithmetic and copies ran while one was open for 1% of the time, Pallas kernels for 19%

profile of v10, /device:TPU:0, one launch (start us, length us, event | category | flops | bytes accessed | tf_op | source)
XLA Modules:
  0.0 106.0 jit_solution(15390050757083245707)
XLA Ops:
  0.0 0.8 reshape.42
  0.8 0.7 convert_bitcast_fusion
  1.5 0.7 pad_convert_fusion
  2.4 0.9 copy-done.1
  3.3 0.8 shard_map.73
  4.1 0.5 collective-permute-start
  4.6 0.9 collective-permute-done
  5.7 4.0 %collective-permute-start.2 = (bf16[32,1536]{1,0:T(8,128)(2,1)S(1)}, bf16[32,1536]{1,0:T(8,128)(2,1)S(1)}, u32[]{:S(2)}, u32[]{:S(2)}) collective-permute-start(bf16[32,1536]{1,0:T(8,128)(2,1)S(1)} %get-tuple-element.103._), channel_id=1, source_target_pairs={{0,16},{1,17},{2,18},{3,19},{4,20},{5,21},{6,22},{7,23},{8,24},{9,... | collective-permute-start | bytes 294920 | tf_op jit(solution)/shard_map/ppermute | solution.py:30
  9.7 1.6 %collective-permute-start.1 = (bf16[32,1536]{1,0:T(8,128)(2,1)S(1)}, bf16[32,1536]{1,0:T(8,128)(2,1)S(1)}, u32[]{:S(2)}, u32[]{:S(2)}) collective-permute-start(bf16[32,1536]{1,0:T(8,128)(2,1)S(1)} %get-tuple-element.103._), channel_id=1, source_target_pairs={{0,8},{1,9},{2,10},{3,11},{4,12},{5,13},{6,14},{7,15},{8,0},{9,1},... | collective-permute-start | bytes 294920 | tf_op jit(solution)/shard_map/ppermute | solution.py:30
  11.3 2.2 %copy-done = bf16[2880,720]{0,1:T(8,128)(2,1)S(1)} copy-done((bf16[2880,720]{0,1:T(8,128)(2,1)S(1)}, bf16[2880,720]{0,1:T(8,128)(2,1)}, u32[]{:S(2)}) %copy-start) | copy-done | bytes 4147224
  13.8 1.2 %collective-permute-done.2._ = bf16[32,1536]{1,0:T(8,128)(2,1)S(1)} collective-permute-done((bf16[32,1536]{1,0:T(8,128)(2,1)S(1)}, bf16[32,1536]{1,0:T(8,128)(2,1)S(1)}, u32[]{:S(2)}, u32[]{:S(2)}) %collective-permute-start.2) | collective-permute-done | bytes 98336 | tf_op jit(solution)/shard_map/ppermute | solution.py:30
  15.0 0.6 collective-permute-start.3
  16.1 3.5 %collective-permute-done.3 = bf16[32,1536]{1,0:T(8,128)(2,1)S(1)} collective-permute-done((bf16[32,1536]{1,0:T(8,128)(2,1)S(1)}, bf16[32,1536]{1,0:T(8,128)(2,1)S(1)}, u32[]{:S(2)}, u32[]{:S(2)}) %collective-permute-start.3) | collective-permute-done | bytes 98336 | tf_op jit(solution)/shard_map/ppermute | solution.py:30
  19.6 1.6 %collective-permute-start.4 = (bf16[128,1536]{1,0:T(8,128)(2,1)S(1)}, bf16[128,1536]{1,0:T(8,128)(2,1)S(1)}, u32[]{:S(2)}, u32[]{:S(2)}) collective-permute-start(bf16[128,1536]{1,0:T(8,128)(2,1)S(1)} %constant_dynamic-update-slice_fusion.near_ref), channel_id=1, source_target_pairs={{0,4},{1,3},{2,6},{3,1},{4,0},{5,7},{6,2},{7,5},{8,12},{9,11},{10,... | collective-permute-start | bytes 1179656 | tf_op jit(solution)/shard_map/ppermute | solution.py:30
  21.3 0.7 collective-permute-start.5
  22.0 3.4 %collective-permute-start.6 = (bf16[32,1536]{1,0:T(8,128)(2,1)S(1)}, bf16[32,1536]{1,0:T(8,128)(2,1)S(1)}, u32[]{:S(2)}, u32[]{:S(2)}) collective-permute-start(bf16[32,1536]{1,0:T(8,128)(2,1)S(1)} %get-tuple-element.58), channel_id=1, source_target_pairs={{0,16},{1,17},{2,18},{3,19},{4,20},{5,21},{6,22},{7,23},{8,24},{9,... | collective-permute-start | bytes 294920 | tf_op jit(solution)/shard_map/ppermute | solution.py:30
  25.7 1.8 %collective-permute-done.4.next_ref = bf16[128,1536]{1,0:T(8,128)(2,1)S(1)} collective-permute-done((bf16[128,1536]{1,0:T(8,128)(2,1)S(1)}, bf16[128,1536]{1,0:T(8,128)(2,1)S(1)}, u32[]{:S(2)}, u32[]{:S(2)}) %collective-permute-start.4) | collective-permute-done | bytes 393248 | tf_op jit(solution)/shard_map/ppermute | solution.py:30
  27.5 1.3 %shard_map.76 = bf16[192,1536]{1,0:T(8,128)(2,1)S(1)} custom-call(s32[3]{0:T(128)S(1)} %pad_add_fusion.places_ref, bf16[128,1536]{1,0:T(8,128)(2,1)S(1)} %constant_dynamic-update-slice_fusion.near_ref, bf16[128,1536]{1,0:T(8,128)(2,1)S(1)} %collective-permute-done.4.next_ref), custom_call_target="tpu_custom_call" | custom-call | flops 301989888 | bytes 1572864 | tf_op jit(solution)/shard_map/pallas_call | solution.py:99
  28.8 1.6 %collective-permute-start.9 = (bf16[192,1536]{1,0:T(8,128)(2,1)S(1)}, bf16[192,1536]{1,0:T(8,128)(2,1)S(1)}, u32[]{:S(2)}, u32[]{:S(2)}) collective-permute-start(bf16[192,1536]{1,0:T(8,128)(2,1)S(1)} %shard_map.76), channel_id=1, source_target_pairs={{0,2},{1,5},{2,0},{3,7},{4,6},{5,1},{6,4},{7,3},{8,10},{9,13},{10,... | collective-permute-start | bytes 1769480 | tf_op jit(solution)/shard_map/ppermute | solution.py:30
  30.4 1.3 %shard_map.77 = (bf16[192,1536]{1,0:T(8,128)(2,1)S(1)}, f32[128,128]{1,0:T(8,128)S(1)}, f32[128,128]{1,0:T(8,128)S(1)}) custom-call(s32[3]{0:T(128)S(1)} %pad_add_fusion.places_ref, bf16[128,1536]{1,0:T(8,128)(2,1)S(1)} %constant_dynamic-update-slice_fusion.near_ref, bf16[128,1536]{1,0:T(8,128)(2,1)S(1)} %collective-permute-done.4.next_ref), custom_call_target="tpu_custom_call" | custom-call | flops 301989888 | bytes 1572864 | tf_op jit(solution)/shard_map/pallas_call | solution.py:99
  32.3 1.3 %collective-permute-start.8 = (bf16[128,1536]{1,0:T(8,128)(2,1)S(1)}, bf16[128,1536]{1,0:T(8,128)(2,1)S(1)}, u32[]{:S(2)}, u32[]{:S(2)}) collective-permute-start(bf16[128,1536]{1,0:T(8,128)(2,1)S(1)} %constant_dynamic-update-slice_fusion.5.near_ref), channel_id=1, source_target_pairs={{0,4},{1,3},{2,6},{3,1},{4,0},{5,7},{6,2},{7,5},{8,12},{9,11},{10,... | collective-permute-start | bytes 1179656 | tf_op jit(solution)/shard_map/ppermute | solution.py:30
  33.9 6.2 %collective-permute-done.8.next_ref = bf16[128,1536]{1,0:T(8,128)(2,1)S(1)} collective-permute-done((bf16[128,1536]{1,0:T(8,128)(2,1)S(1)}, bf16[128,1536]{1,0:T(8,128)(2,1)S(1)}, u32[]{:S(2)}, u32[]{:S(2)}) %collective-permute-start.8) | collective-permute-done | bytes 393248 | tf_op jit(solution)/shard_map/ppermute | solution.py:30
  40.1 1.6 %shard_map.79 = (bf16[192,1536]{1,0:T(8,128)(2,1)S(1)}, bf16[192,1536]{1,0:T(8,128)(2,1)S(1)}, f32[128,128]{1,0:T(8,128)S(1)}, f32[128,128]{1,0:T(8,128)S(1)}) custom-call(s32[3]{0:T(128)S(1)} %pad_add_fusion.places_ref, bf16[128,1536]{1,0:T(8,128)(2,1)S(1)} %constant_dynamic-update-slice_fusion.5.near_ref, bf16[128,1536]{1,0:T(8,128)(2,1)S(1)} %collective-permute-done.8.next_ref), custom_call_target="tpu_custom_call" | custom-call | flops 301989888 | bytes 1572864 | tf_op jit(solution)/shard_map/pallas_call | solution.py:99
  41.8 1.2 %collective-permute-done.9.mine_far_ref = bf16[192,1536]{1,0:T(8,128)(2,1)S(1)} collective-permute-done((bf16[192,1536]{1,0:T(8,128)(2,1)S(1)}, bf16[192,1536]{1,0:T(8,128)(2,1)S(1)}, u32[]{:S(2)}, u32[]{:S(2)}) %collective-permute-start.9) | collective-permute-done | bytes 589856 | tf_op jit(solution)/shard_map/ppermute | solution.py:30
  43.0 0.7 collective-permute-start.10
  43.7 1.3 %collective-permute-done.12.other_far_ref = bf16[192,1536]{1,0:T(8,128)(2,1)S(1)} collective-permute-done((bf16[192,1536]{1,0:T(8,128)(2,1)S(1)}, bf16[192,1536]{1,0:T(8,128)(2,1)S(1)}, u32[]{:S(2)}, u32[]{:S(2)}) %collective-permute-start.12) | collective-permute-done | bytes 589856 | tf_op jit(solution)/shard_map/ppermute | solution.py:30
  45.0 6.7 %shard_map.80 = (f32[192,1536]{1,0:T(8,128)S(1)}, f32[192,1536]{1,0:T(8,128)S(1)}, bf16[192,1536]{1,0:T(8,128)(2,1)S(1)}, bf16[192,1536]{1,0:T(8,128)(2,1)S(1)}) custom-call(s32[3]{0:T(128)S(1)} %pad_add_fusion.places_ref, bf16[192,1536]{1,0:T(8,128)(2,1)S(1)} %get-tuple-element.63._.mine_near_ref, ...), custom_call_target="tpu_custom_call" | custom-call | flops 4777574400 | bytes 17160192 | tf_op jit(solution)/shard_map/pallas_call | solution.py:215
  51.7 1.2 %collective-permute-done.10.mine_far_ref = bf16[192,1536]{1,0:T(8,128)(2,1)S(1)} collective-permute-done((bf16[192,1536]{1,0:T(8,128)(2,1)S(1)}, bf16[192,1536]{1,0:T(8,128)(2,1)S(1)}, u32[]{:S(2)}, u32[]{:S(2)}) %collective-permute-start.10) | collective-permute-done | bytes 589856 | tf_op jit(solution)/shard_map/ppermute | solution.py:30
  53.9 1.0 collective-permute-done.14
  55.0 0.8 collective-permute-start.15
  55.8 0.8 collective-permute-done.18.other_far_ref
  56.6 6.8 %shard_map.82 = (f32[192,1536]{1,0:T(8,128)S(1)}, f32[192,1536]{1,0:T(8,128)S(1)}, bf16[192,1536]{1,0:T(8,128)(2,1)S(1)}, bf16[192,1536]{1,0:T(8,128)(2,1)S(1)}) custom-call(s32[3]{0:T(128)S(1)} %pad_add_fusion.places_ref, bf16[192,1536]{1,0:T(8,128)(2,1)S(1)} %get-tuple-element.83.mine_near_ref, bf16[192,1536]{1,0:T(8,128)(2,1)S(1)} %collective-permute-done.10.mine_far_ref, ...), custom_call_target="tpu_custom_call" | custom-call | flops 4777574400 | bytes 17160192 | tf_op jit(solution)/shard_map/pallas_call | solution.py:215
  64.0 0.9 collective-permute-done.15.arrived_ref
  64.9 0.6 shard_map.81
  65.6 2.1 %collective-permute-start.16 = (bf16[128,1536]{1,0:T(8,128)(2,1)S(1)}, bf16[128,1536]{1,0:T(8,128)(2,1)S(1)}, u32[]{:S(2)}, u32[]{:S(2)}) collective-permute-start(bf16[128,1536]{1,0:T(8,128)(2,1)S(1)} %get-tuple-element.80), channel_id=1, source_target_pairs={{0,4},{1,3},{2,6},{3,1},{4,0},{5,7},{6,2},{7,5},{8,12},{9,11},{10,... | collective-permute-start | bytes 1179656 | tf_op jit(solution)/shard_map/ppermute | solution.py:30
  67.9 0.7 collective-permute-start.21
  68.5 9.1 %collective-permute-done.16 = bf16[128,1536]{1,0:T(8,128)(2,1)S(1)} collective-permute-done((bf16[128,1536]{1,0:T(8,128)(2,1)S(1)}, bf16[128,1536]{1,0:T(8,128)(2,1)S(1)}, u32[]{:S(2)}, u32[]{:S(2)}) %collective-permute-start.16) | collective-permute-done | bytes 393248 | tf_op jit(solution)/shard_map/ppermute | solution.py:30
  77.7 0.7 collective-permute-done.21.arrived_ref
  78.8 1.8 %collective-permute-start.24 = (bf16[128,1536]{1,0:T(8,128)(2,1)S(1)}, bf16[128,1536]{1,0:T(8,128)(2,1)S(1)}, u32[]{:S(2)}, u32[]{:S(2)}) collective-permute-start(bf16[128,1536]{1,0:T(8,128)(2,1)S(1)} %shard_map.83._), channel_id=1, source_target_pairs={{0,4},{1,3},{2,6},{3,1},{4,0},{5,7},{6,2},{7,5},{8,12},{9,11},{10,... | collective-permute-start | bytes 1179656 | tf_op jit(solution)/shard_map/ppermute | solution.py:30
  81.2 1.8 %collective-permute-start.22 = (bf16[2,32,1536]{2,1,0:T(8,128)(2,1)S(1)}, bf16[2,32,1536]{2,1,0:T(8,128)(2,1)S(1)}, u32[]{:S(2)}, u32[]{:S(2)}) collective-permute-start(bf16[2,32,1536]{2,1,0:T(8,128)(2,1)S(1)} %pad_maximum_fusion.1), channel_id=1, source_target_pairs={{0,8},{1,9},{2,10},{3,11},{4,12},{5,13},{6,14},{7,15},{8,0},{9,1},... | collective-permute-start | bytes 589832 | tf_op jit(solution)/shard_map/ppermute | solution.py:30
  83.0 3.7 %collective-permute-done.24 = bf16[128,1536]{1,0:T(8,128)(2,1)S(1)} collective-permute-done((bf16[128,1536]{1,0:T(8,128)(2,1)S(1)}, bf16[128,1536]{1,0:T(8,128)(2,1)S(1)}, u32[]{:S(2)}, u32[]{:S(2)}) %collective-permute-start.24) | collective-permute-done | bytes 393248 | tf_op jit(solution)/shard_map/ppermute | solution.py:30
  86.8 2.3 %collective-permute-start.25 = (bf16[2,32,1536]{2,1,0:T(8,128)(2,1)S(1)}, bf16[2,32,1536]{2,1,0:T(8,128)(2,1)S(1)}, u32[]{:S(2)}, u32[]{:S(2)}) collective-permute-start(bf16[2,32,1536]{2,1,0:T(8,128)(2,1)S(1)} %pad_maximum_fusion.2), channel_id=1, source_target_pairs={{0,8},{1,9},{2,10},{3,11},{4,12},{5,13},{6,14},{7,15},{8,0},{9,1},... | collective-permute-start | bytes 589832 | tf_op jit(solution)/shard_map/ppermute | solution.py:30
  89.1 2.3 %collective-permute-start.23 = (bf16[32,1536]{1,0:T(8,128)(2,1)S(1)}, bf16[32,1536]{1,0:T(8,128)(2,1)S(1)}, u32[]{:S(2)}, u32[]{:S(2)}) collective-permute-start(bf16[32,1536]{1,0:T(8,128)(2,1)S(1)} %fusion.4), channel_id=1, source_target_pairs={{0,16},{1,17},{2,18},{3,19},{4,20},{5,21},{6,22},{7,23},{8,24},{9,... | collective-permute-start | bytes 294920 | tf_op jit(solution)/shard_map/ppermute | solution.py:30
  91.4 4.8 %collective-permute-done.25 = bf16[2,32,1536]{2,1,0:T(8,128)(2,1)S(1)} collective-permute-done((bf16[2,32,1536]{2,1,0:T(8,128)(2,1)S(1)}, bf16[2,32,1536]{2,1,0:T(8,128)(2,1)S(1)}, u32[]{:S(2)}, u32[]{:S(2)}) %collective-permute-start.25) | collective-permute-done | bytes 196640 | tf_op jit(solution)/shard_map/ppermute | solution.py:30
  96.2 2.2 %collective-permute-start.26 = (bf16[32,1536]{1,0:T(8,128)(2,1)S(1)}, bf16[32,1536]{1,0:T(8,128)(2,1)S(1)}, u32[]{:S(2)}, u32[]{:S(2)}) collective-permute-start(bf16[32,1536]{1,0:T(8,128)(2,1)S(1)} %fusion.1), channel_id=1, source_target_pairs={{0,16},{1,17},{2,18},{3,19},{4,20},{5,21},{6,22},{7,23},{8,24},{9,... | collective-permute-start | bytes 294920 | tf_op jit(solution)/shard_map/ppermute | solution.py:30
  98.5 4.9 %collective-permute-done.26 = bf16[32,1536]{1,0:T(8,128)(2,1)S(1)} collective-permute-done((bf16[32,1536]{1,0:T(8,128)(2,1)S(1)}, bf16[32,1536]{1,0:T(8,128)(2,1)S(1)}, u32[]{:S(2)}, u32[]{:S(2)}) %collective-permute-start.26) | collective-permute-done | bytes 98336 | tf_op jit(solution)/shard_map/ppermute | solution.py:30
  103.5 1.3 %collective-permute-done.27.taken_ref = bf16[2,16,1536]{2,1,0:T(8,128)(2,1)S(1)} collective-permute-done((bf16[2,16,1536]{2,1,0:T(8,128)(2,1)S(1)}, bf16[2,16,1536]{2,1,0:T(8,128)(2,1)S(1)}, u32[]{:S(2)}, u32[]{:S(2)}) %collective-permute-start.27) | collective-permute-done | bytes 98336 | tf_op jit(solution)/shard_map/ppermute | solution.py:30
  104.8 1.3 %shard_map.85 = bf16[2,16,2880]{2,1,0:T(8,128)(2,1)} custom-call(s32[3]{0:T(128)S(1)} %pad_add_fusion.places_ref, bf16[2,16,2880]{2,1,0:T(8,128)(2,1)S(1)} %copy-done.2, f32[2,16,1536]{2,1,0:T(8,128)S(1)} %broadcast_select_fusion.own_ref, bf16[2,16,1536]{2,1,0:T(8,128)(2,1)S(1)} %collective-permute-done.27.taken_ref), custom_call_target="tpu_custom_call" | custom-call | tf_op jit(solution)/shard_map/pallas_call | solution.py:347
  (70 shorter events, 5.4 us)
Async XLA Ops:
  2.4 0.9 copy-start.1
  3.3 12.4 %slice-start.2 = ((s8[4239360]{0:T(1024)(128)(4,1)}), s8[45056]{0:T(1024)(128)(4,1)S(1)}, s32[]{:S(2)}) async-start(s8[4239360]{0:T(1024)(128)(4,1)} %bitcast.53), calls=%async_computation.2 | async-start | bytes 90112
  4.1 1.5 %collective-permute-start = (bf16[2,16,1536]{2,1,0:T(8,128)(2,1)S(1)}, bf16[2,16,1536]{2,1,0:T(8,128)(2,1)S(1)}, u32[]{:S(2)}, u32[]{:S(2)}) collective-permute-start(bf16[2,16,1536]{2,1,0:T(8,128)(2,1)S(1)} %get-tuple-element.49), channel_id=1, source_target_pairs={{0,1},{1,0},{2,3},{3,2},{4,5},{5,4},{6,7},{7,6},{8,9},{9,8},{10,11... | collective-permute-start | bytes 294920 | tf_op jit(solution)/shard_map/ppermute | solution.py:30
  5.7 9.3 %collective-permute-start.2 = (bf16[32,1536]{1,0:T(8,128)(2,1)S(1)}, bf16[32,1536]{1,0:T(8,128)(2,1)S(1)}, u32[]{:S(2)}, u32[]{:S(2)}) collective-permute-start(bf16[32,1536]{1,0:T(8,128)(2,1)S(1)} %get-tuple-element.103._), channel_id=1, source_target_pairs={{0,16},{1,17},{2,18},{3,19},{4,20},{5,21},{6,22},{7,23},{8,24},{9,... | collective-permute-start | bytes 294920 | tf_op jit(solution)/shard_map/ppermute | solution.py:30
  9.7 6.0 %collective-permute-start.1 = (bf16[32,1536]{1,0:T(8,128)(2,1)S(1)}, bf16[32,1536]{1,0:T(8,128)(2,1)S(1)}, u32[]{:S(2)}, u32[]{:S(2)}) collective-permute-start(bf16[32,1536]{1,0:T(8,128)(2,1)S(1)} %get-tuple-element.103._), channel_id=1, source_target_pairs={{0,8},{1,9},{2,10},{3,11},{4,12},{5,13},{6,14},{7,15},{8,0},{9,1},... | collective-permute-start | bytes 294920 | tf_op jit(solution)/shard_map/ppermute | solution.py:30
  11.3 2.2 %copy-start = (bf16[2880,720]{0,1:T(8,128)(2,1)S(1)}, bf16[2880,720]{0,1:T(8,128)(2,1)}, u32[]{:S(2)}) copy-start(bf16[2880,720]{0,1:T(8,128)(2,1)} %param.9) | copy-start | bytes 12441604
  13.5 2.2 %slice-start.3 = ((s8[4239360]{0:T(1024)(128)(4,1)}), s8[4194304]{0:T(1024)(128)(4,1)S(1)}, s32[]{:S(2)}) async-start(s8[4239360]{0:T(1024)(128)(4,1)} %bitcast.53), calls=%async_computation.3 | async-start | bytes 8388608
  15.0 4.6 %collective-permute-start.3 = (bf16[32,1536]{1,0:T(8,128)(2,1)S(1)}, bf16[32,1536]{1,0:T(8,128)(2,1)S(1)}, u32[]{:S(2)}, u32[]{:S(2)}) collective-permute-start(bf16[32,1536]{1,0:T(8,128)(2,1)S(1)} %collective-permute-done.2._), channel_id=1, source_target_pairs={{0,8},{1,9},{2,10},{3,11},{4,12},{5,13},{6,14},{7,15},{8,0},{9,1},... | collective-permute-start | bytes 294920 | tf_op jit(solution)/shard_map/ppermute | solution.py:30
  15.6 17.9 %slice-start = ((s8[4239360]{0:T(1024)(128)(4,1)}), s8[4194304]{0:T(1024)(128)(4,1)S(1)}, s32[]{:S(2)}) async-start(s8[4239360]{0:T(1024)(128)(4,1)} %bitcast.50), calls=%async_computation | async-start | bytes 8388608
  15.7 17.8 %slice-start.1 = ((s8[4239360]{0:T(1024)(128)(4,1)}), s8[45056]{0:T(1024)(128)(4,1)S(1)}, s32[]{:S(2)}) async-start(s8[4239360]{0:T(1024)(128)(4,1)} %bitcast.50), calls=%async_computation.1 | async-start | bytes 90112
  19.6 7.8 %collective-permute-start.4 = (bf16[128,1536]{1,0:T(8,128)(2,1)S(1)}, bf16[128,1536]{1,0:T(8,128)(2,1)S(1)}, u32[]{:S(2)}, u32[]{:S(2)}) collective-permute-start(bf16[128,1536]{1,0:T(8,128)(2,1)S(1)} %constant_dynamic-update-slice_fusion.near_ref), channel_id=1, source_target_pairs={{0,4},{1,3},{2,6},{3,1},{4,0},{5,7},{6,2},{7,5},{8,12},{9,11},{10,... | collective-permute-start | bytes 1179656 | tf_op jit(solution)/shard_map/ppermute | solution.py:30
  21.3 10.5 %collective-permute-start.5 = (bf16[32,1536]{1,0:T(8,128)(2,1)S(1)}, bf16[32,1536]{1,0:T(8,128)(2,1)S(1)}, u32[]{:S(2)}, u32[]{:S(2)}) collective-permute-start(bf16[32,1536]{1,0:T(8,128)(2,1)S(1)} %get-tuple-element.58), channel_id=1, source_target_pairs={{0,8},{1,9},{2,10},{3,11},{4,12},{5,13},{6,14},{7,15},{8,0},{9,1},... | collective-permute-start | bytes 294920 | tf_op jit(solution)/shard_map/ppermute | solution.py:30
  22.0 10.2 %collective-permute-start.6 = (bf16[32,1536]{1,0:T(8,128)(2,1)S(1)}, bf16[32,1536]{1,0:T(8,128)(2,1)S(1)}, u32[]{:S(2)}, u32[]{:S(2)}) collective-permute-start(bf16[32,1536]{1,0:T(8,128)(2,1)S(1)} %get-tuple-element.58), channel_id=1, source_target_pairs={{0,16},{1,17},{2,18},{3,19},{4,20},{5,21},{6,22},{7,23},{8,24},{9,... | collective-permute-start | bytes 294920 | tf_op jit(solution)/shard_map/ppermute | solution.py:30
  25.3 6.9 %collective-permute-start.7 = (bf16[32,1536]{1,0:T(8,128)(2,1)S(1)}, bf16[32,1536]{1,0:T(8,128)(2,1)S(1)}, u32[]{:S(2)}, u32[]{:S(2)}) collective-permute-start(bf16[32,1536]{1,0:T(8,128)(2,1)S(1)} %get-tuple-element.58), channel_id=1, source_target_pairs={{0,24},{1,25},{2,26},{3,27},{4,28},{5,29},{6,30},{7,31},{8,16},{9,... | collective-permute-start | bytes 294920 | tf_op jit(solution)/shard_map/ppermute | solution.py:30
  28.8 14.2 %collective-permute-start.9 = (bf16[192,1536]{1,0:T(8,128)(2,1)S(1)}, bf16[192,1536]{1,0:T(8,128)(2,1)S(1)}, u32[]{:S(2)}, u32[]{:S(2)}) collective-permute-start(bf16[192,1536]{1,0:T(8,128)(2,1)S(1)} %shard_map.76), channel_id=1, source_target_pairs={{0,2},{1,5},{2,0},{3,7},{4,6},{5,1},{6,4},{7,3},{8,10},{9,13},{10,... | collective-permute-start | bytes 1769480 | tf_op jit(solution)/shard_map/ppermute | solution.py:30
  32.3 7.8 %collective-permute-start.8 = (bf16[128,1536]{1,0:T(8,128)(2,1)S(1)}, bf16[128,1536]{1,0:T(8,128)(2,1)S(1)}, u32[]{:S(2)}, u32[]{:S(2)}) collective-permute-start(bf16[128,1536]{1,0:T(8,128)(2,1)S(1)} %constant_dynamic-update-slice_fusion.5.near_ref), channel_id=1, source_target_pairs={{0,4},{1,3},{2,6},{3,1},{4,0},{5,7},{6,2},{7,5},{8,12},{9,11},{10,... | collective-permute-start | bytes 1179656 | tf_op jit(solution)/shard_map/ppermute | solution.py:30
  33.5 10.2 %collective-permute-start.11 = (bf16[192,1536]{1,0:T(8,128)(2,1)S(1)}, bf16[192,1536]{1,0:T(8,128)(2,1)S(1)}, u32[]{:S(2)}, u32[]{:S(2)}) collective-permute-start(bf16[192,1536]{1,0:T(8,128)(2,1)S(1)} %get-tuple-element.63._.mine_near_ref), channel_id=1, source_target_pairs={{0,1},{1,0},{2,3},{3,2},{4,5},{5,4},{6,7},{7,6},{8,9},{9,8},{10,11... | collective-permute-start | bytes 1769480 | tf_op jit(solution)/shard_map/ppermute | solution.py:30
  43.0 2.0 %collective-permute-start.12 = (bf16[192,1536]{1,0:T(8,128)(2,1)S(1)}, bf16[192,1536]{1,0:T(8,128)(2,1)S(1)}, u32[]{:S(2)}, u32[]{:S(2)}) collective-permute-start(bf16[192,1536]{1,0:T(8,128)(2,1)S(1)} %collective-permute-done.9.mine_far_ref), channel_id=1, source_target_pairs={{0,1},{1,0},{2,3},{3,2},{4,5},{5,4},{6,7},{7,6},{8,9},{9,8},{10,11... | collective-permute-start | bytes 1769480 | tf_op jit(solution)/shard_map/ppermute | solution.py:30
  43.0 9.9 %collective-permute-start.10 = (bf16[192,1536]{1,0:T(8,128)(2,1)S(1)}, bf16[192,1536]{1,0:T(8,128)(2,1)S(1)}, u32[]{:S(2)}, u32[]{:S(2)}) collective-permute-start(bf16[192,1536]{1,0:T(8,128)(2,1)S(1)} %get-tuple-element.66), channel_id=1, source_target_pairs={{0,2},{1,5},{2,0},{3,7},{4,6},{5,1},{6,4},{7,3},{8,10},{9,13},{10,... | collective-permute-start | bytes 1769480 | tf_op jit(solution)/shard_map/ppermute | solution.py:30
  52.9 2.0 %collective-permute-start.14 = (bf16[192,1536]{1,0:T(8,128)(2,1)S(1)}, bf16[192,1536]{1,0:T(8,128)(2,1)S(1)}, u32[]{:S(2)}, u32[]{:S(2)}) collective-permute-start(bf16[192,1536]{1,0:T(8,128)(2,1)S(1)} %get-tuple-element.78), channel_id=1, source_target_pairs={{0,1},{1,0},{2,3},{3,2},{4,5},{5,4},{6,7},{7,6},{8,9},{9,8},{10,11... | collective-permute-start | bytes 1769480 | tf_op jit(solution)/shard_map/ppermute | solution.py:30
  52.9 2.9 %collective-permute-start.17 = (bf16[192,1536]{1,0:T(8,128)(2,1)S(1)}, bf16[192,1536]{1,0:T(8,128)(2,1)S(1)}, u32[]{:S(2)}, u32[]{:S(2)}) collective-permute-start(bf16[192,1536]{1,0:T(8,128)(2,1)S(1)} %get-tuple-element.83.mine_near_ref), channel_id=1, source_target_pairs={{0,1},{1,0},{2,3},{3,2},{4,5},{5,4},{6,7},{7,6},{8,9},{9,8},{10,11... | collective-permute-start | bytes 1769480 | tf_op jit(solution)/shard_map/ppermute | solution.py:30
  53.4 3.2 %collective-permute-start.18 = (bf16[192,1536]{1,0:T(8,128)(2,1)S(1)}, bf16[192,1536]{1,0:T(8,128)(2,1)S(1)}, u32[]{:S(2)}, u32[]{:S(2)}) collective-permute-start(bf16[192,1536]{1,0:T(8,128)(2,1)S(1)} %collective-permute-done.10.mine_far_ref), channel_id=1, source_target_pairs={{0,1},{1,0},{2,3},{3,2},{4,5},{5,4},{6,7},{7,6},{8,9},{9,8},{10,11... | collective-permute-start | bytes 1769480 | tf_op jit(solution)/shard_map/ppermute | solution.py:30
  53.4 10.6 %collective-permute-start.13 = (bf16[192,1536]{1,0:T(8,128)(2,1)S(1)}, bf16[192,1536]{1,0:T(8,128)(2,1)S(1)}, u32[]{:S(2)}, u32[]{:S(2)}) collective-permute-start(bf16[192,1536]{1,0:T(8,128)(2,1)S(1)} %get-tuple-element.76), channel_id=1, source_target_pairs={{0,1},{1,0},{2,3},{3,2},{4,5},{5,4},{6,7},{7,6},{8,9},{9,8},{10,11... | collective-permute-start | bytes 1769480 | tf_op jit(solution)/shard_map/ppermute | solution.py:30
  55.0 9.9 %collective-permute-start.15 = (bf16[192,1536]{1,0:T(8,128)(2,1)S(1)}, bf16[192,1536]{1,0:T(8,128)(2,1)S(1)}, u32[]{:S(2)}, u32[]{:S(2)}) collective-permute-start(bf16[192,1536]{1,0:T(8,128)(2,1)S(1)} %add_convert_fusion.1), channel_id=1, source_target_pairs={{0,2},{1,5},{2,0},{3,7},{4,6},{5,1},{6,4},{7,3},{8,10},{9,13},{10,... | collective-permute-start | bytes 1769480 | tf_op jit(solution)/shard_map/ppermute | solution.py:30
  63.4 4.3 %collective-permute-start.20 = (bf16[192,1536]{1,0:T(8,128)(2,1)S(1)}, bf16[192,1536]{1,0:T(8,128)(2,1)S(1)}, u32[]{:S(2)}, u32[]{:S(2)}) collective-permute-start(bf16[192,1536]{1,0:T(8,128)(2,1)S(1)} %get-tuple-element.88), channel_id=1, source_target_pairs={{0,1},{1,0},{2,3},{3,2},{4,5},{5,4},{6,7},{7,6},{8,9},{9,8},{10,11... | collective-permute-start | bytes 1769480 | tf_op jit(solution)/shard_map/ppermute | solution.py:30
  63.9 13.8 %collective-permute-start.19 = (bf16[192,1536]{1,0:T(8,128)(2,1)S(1)}, bf16[192,1536]{1,0:T(8,128)(2,1)S(1)}, u32[]{:S(2)}, u32[]{:S(2)}) collective-permute-start(bf16[192,1536]{1,0:T(8,128)(2,1)S(1)} %get-tuple-element.86), channel_id=1, source_target_pairs={{0,1},{1,0},{2,3},{3,2},{4,5},{5,4},{6,7},{7,6},{8,9},{9,8},{10,11... | collective-permute-start | bytes 1769480 | tf_op jit(solution)/shard_map/ppermute | solution.py:30
  65.6 12.0 %collective-permute-start.16 = (bf16[128,1536]{1,0:T(8,128)(2,1)S(1)}, bf16[128,1536]{1,0:T(8,128)(2,1)S(1)}, u32[]{:S(2)}, u32[]{:S(2)}) collective-permute-start(bf16[128,1536]{1,0:T(8,128)(2,1)S(1)} %get-tuple-element.80), channel_id=1, source_target_pairs={{0,4},{1,3},{2,6},{3,1},{4,0},{5,7},{6,2},{7,5},{8,12},{9,11},{10,... | collective-permute-start | bytes 1179656 | tf_op jit(solution)/shard_map/ppermute | solution.py:30
  67.9 10.5 %collective-permute-start.21 = (bf16[192,1536]{1,0:T(8,128)(2,1)S(1)}, bf16[192,1536]{1,0:T(8,128)(2,1)S(1)}, u32[]{:S(2)}, u32[]{:S(2)}) collective-permute-start(bf16[192,1536]{1,0:T(8,128)(2,1)S(1)} %add_convert_fusion), channel_id=1, source_target_pairs={{0,2},{1,5},{2,0},{3,7},{4,6},{5,1},{6,4},{7,3},{8,10},{9,13},{10,... | collective-permute-start | bytes 1769480 | tf_op jit(solution)/shard_map/ppermute | solution.py:30
  78.8 7.8 %collective-permute-start.24 = (bf16[128,1536]{1,0:T(8,128)(2,1)S(1)}, bf16[128,1536]{1,0:T(8,128)(2,1)S(1)}, u32[]{:S(2)}, u32[]{:S(2)}) collective-permute-start(bf16[128,1536]{1,0:T(8,128)(2,1)S(1)} %shard_map.83._), channel_id=1, source_target_pairs={{0,4},{1,3},{2,6},{3,1},{4,0},{5,7},{6,2},{7,5},{8,12},{9,11},{10,... | collective-permute-start | bytes 1179656 | tf_op jit(solution)/shard_map/ppermute | solution.py:30
  81.2 7.9 %collective-permute-start.22 = (bf16[2,32,1536]{2,1,0:T(8,128)(2,1)S(1)}, bf16[2,32,1536]{2,1,0:T(8,128)(2,1)S(1)}, u32[]{:S(2)}, u32[]{:S(2)}) collective-permute-start(bf16[2,32,1536]{2,1,0:T(8,128)(2,1)S(1)} %pad_maximum_fusion.1), channel_id=1, source_target_pairs={{0,8},{1,9},{2,10},{3,11},{4,12},{5,13},{6,14},{7,15},{8,0},{9,1},... | collective-permute-start | bytes 589832 | tf_op jit(solution)/shard_map/ppermute | solution.py:30
  86.8 9.3 %collective-permute-start.25 = (bf16[2,32,1536]{2,1,0:T(8,128)(2,1)S(1)}, bf16[2,32,1536]{2,1,0:T(8,128)(2,1)S(1)}, u32[]{:S(2)}, u32[]{:S(2)}) collective-permute-start(bf16[2,32,1536]{2,1,0:T(8,128)(2,1)S(1)} %pad_maximum_fusion.2), channel_id=1, source_target_pairs={{0,8},{1,9},{2,10},{3,11},{4,12},{5,13},{6,14},{7,15},{8,0},{9,1},... | collective-permute-start | bytes 589832 | tf_op jit(solution)/shard_map/ppermute | solution.py:30
  89.1 9.3 %collective-permute-start.23 = (bf16[32,1536]{1,0:T(8,128)(2,1)S(1)}, bf16[32,1536]{1,0:T(8,128)(2,1)S(1)}, u32[]{:S(2)}, u32[]{:S(2)}) collective-permute-start(bf16[32,1536]{1,0:T(8,128)(2,1)S(1)} %fusion.4), channel_id=1, source_target_pairs={{0,16},{1,17},{2,18},{3,19},{4,20},{5,21},{6,22},{7,23},{8,24},{9,... | collective-permute-start | bytes 294920 | tf_op jit(solution)/shard_map/ppermute | solution.py:30
  96.2 8.6 %copy-start.2 = (bf16[2,16,2880]{2,1,0:T(8,128)(2,1)S(1)}, bf16[2,16,2880]{2,1,0:T(8,128)(2,1)}, u32[]{:S(2)}) copy-start(bf16[2,16,2880]{2,1,0:T(8,128)(2,1)} %hidden_ref.3) | copy-start | bytes 552964
  96.2 7.1 %collective-permute-start.26 = (bf16[32,1536]{1,0:T(8,128)(2,1)S(1)}, bf16[32,1536]{1,0:T(8,128)(2,1)S(1)}, u32[]{:S(2)}, u32[]{:S(2)}) collective-permute-start(bf16[32,1536]{1,0:T(8,128)(2,1)S(1)} %fusion.1), channel_id=1, source_target_pairs={{0,16},{1,17},{2,18},{3,19},{4,20},{5,21},{6,22},{7,23},{8,24},{9,... | collective-permute-start | bytes 294920 | tf_op jit(solution)/shard_map/ppermute | solution.py:30
  103.4 1.4 %collective-permute-start.27 = (bf16[2,16,1536]{2,1,0:T(8,128)(2,1)S(1)}, bf16[2,16,1536]{2,1,0:T(8,128)(2,1)S(1)}, u32[]{:S(2)}, u32[]{:S(2)}) collective-permute-start(bf16[2,16,1536]{2,1,0:T(8,128)(2,1)S(1)} %select_convert_fusion), channel_id=1, source_target_pairs={{0,1},{1,0},{2,3},{3,2},{4,5},{5,4},{6,7},{7,6},{8,9},{9,8},{10,11... | collective-permute-start | bytes 294920 | tf_op jit(solution)/shard_map/ppermute | solution.py:30

commit v11 on v9

--- a/solution.py
+++ b/solution.py
@@ -324,35 +324,6 @@
     )(places, hidden, packed)
 
 
-def finish_body(places_ref, hidden_ref, own_ref, taken_ref, mixed_ref):
-    first, second, _ = split_widths(hidden_ref.shape[2])
-    lower = places_ref[0] == 0
-
-    def add(low_ref, high_ref):
-        for ref, (start, size) in ((low_ref, (0, first)), (high_ref, (first, second))):
-            columns = slice(start, start + size)
-            total = hidden_ref[:, :, columns].astype(jnp.float32) + ref[:, :, :size].astype(jnp.float32)
-            mixed_ref[:, :, columns] = total.astype(jnp.bfloat16)
-
-    @pl.when(lower)
-    def _():
-        add(own_ref, taken_ref)
-
-    @pl.when(jnp.logical_not(lower))
-    def _():
-        add(taken_ref, own_ref)
-
-
-def finish(places, hidden, own, taken):
-    return pl.pallas_call(
-        finish_body,
-        out_shape=jax.ShapeDtypeStruct(hidden.shape, jnp.bfloat16),
-        in_specs=[SCALARS] + whole_arrays(3),
-        out_specs=pl.BlockSpec(memory_space=pltpu.VMEM),
-        compiler_params=pltpu.CompilerParams(vmem_limit_bytes=20 * 2**20),
-    )(places, hidden, own, taken)
-
-
 def local(hidden, norm_gain, w_gate, w_up, w_down, expert_ids, route_weight):
     micro_count, tokens, width = hidden.shape
     top_count = expert_ids.shape[2]
@@ -403,7 +374,9 @@
     pair = pairs[0]
     (gate_v,) = preload(pair, w_gate.T)
     if distant == 4:
-        crossed, beside = moved(pair, far(2)), moved(pair, far(1))
+        crossed = moved(pair, far(2))
+        again, pairs[-1] = tied(pair, pairs[-1])
+        beside = moved(again, far(1))
         crossed, gate_v = tied(crossed, gate_v)
         (up_v,) = preload(crossed, w_up.T)
         passed = moved(crossed, far(1))
@@ -474,8 +447,11 @@
     sums = jnp.stack([settled(*total) for total in totals])
     own = jnp.where(lower, sums[:, :tokens], sums[:, tokens:])
     give = jnp.where(lower, sums[:, tokens:], sums[:, :tokens]).astype(jnp.bfloat16)
-    taken = moved(give, other_core)
-    return finish(places, hidden, own, taken)
+    taken = moved(give, other_core).astype(jnp.float32)
+    mixture = jnp.concatenate(
+        [jnp.where(lower, own, taken)[:, :, :first], jnp.where(lower, taken, own)[:, :, :second]], axis=2
+    )
+    return (hidden.astype(jnp.float32) + mixture).astype(jnp.bfloat16)
 
 
 def solution(mesh):

time: 106 us -> 103 us (0.972)
  starting transfers between devices: 39.6 us -> 34.9 us
  waiting for transfers between devices: 36.6 us -> 39.6 us
  Pallas kernels: 22.5 us -> 21.2 us
    ppermute x30, starting transfers between devices: 39.6 us -> 34.9 us  [moved(): return lax.ppermute(block, 'req', [(i, partner(i)) for i in range(count)])]
    ppermute x30, waiting for transfers between devices: 36.6 us -> 39.6 us  [moved(): return lax.ppermute(block, 'req', [(i, partner(i)) for i in range(count)])]
    pallas_call x1 -> x0, Pallas kernels: 1.27 us -> none  [finish(): pl.pallas_call(finish_body, out_shape=jax.ShapeDtypeStruct(hidden.shape,...]
  transfers between devices with their start and end apart: 30 -> 30, of which waited for: 15 -> 18; matrix products, arithmetic and copies ran while one was open for 1% -> 1% of each run, Pallas kernels for 19% -> 19%
where the time goes in v11:
time: 103 us
  waiting for transfers between devices  39.6 us (38%)
  starting transfers between devices  34.9 us (34%)
  Pallas kernels  21.2 us (21%)
  local copies, waits for them, and re-layouts  4.1 us (4%)
  other arithmetic  2.98 us (3%)
    ppermute x30, waiting for transfers between devices, moved(): return lax.ppermute(block, 'req', [(i, partner(i)) for i in range(count)])  39.6 us
    ppermute x30, starting transfers between devices, moved(): return lax.ppermute(block, 'req', [(i, partner(i)) for i in range(count)])  34.9 us
    pallas_call x2, Pallas kernels, ffn(): pl.pallas_call(ffn_body, out_shape=[jax.ShapeDtypeStruct((pair, held), jn...  13.5 us
    pallas_call x3, Pallas kernels, select(): pl.pallas_call(functools.partial(select_body, tokens, capacity, wanted),...  4.33 us
    unnamed x19, local copies, waits for them, and re-layouts  3.19 us
  transfers between devices with their start and end apart: 30, of which 18 were waited for; matrix products, arithmetic and copies ran while one was open for 1% of the time, Pallas kernels for 19%

profile of v11, /device:TPU:0, one launch (start us, length us, event | category | flops | bytes accessed | tf_op | source)
XLA Modules:
  0.0 103.2 jit_solution(14202692022065529504)
XLA Ops:
  0.0 0.8 reshape.34
  0.8 0.7 convert_bitcast_fusion
  1.5 0.7 pad_convert_fusion
  2.4 0.9 copy-done.1
  3.3 0.8 shard_map.73
  4.6 0.9 collective-permute-done
  5.7 4.0 %collective-permute-start.2 = (bf16[32,1536]{1,0:T(8,128)(2,1)S(1)}, bf16[32,1536]{1,0:T(8,128)(2,1)S(1)}, u32[]{:S(2)}, u32[]{:S(2)}) collective-permute-start(bf16[32,1536]{1,0:T(8,128)(2,1)S(1)} %get-tuple-element.103._), channel_id=1, source_target_pairs={{0,16},{1,17},{2,18},{3,19},{4,20},{5,21},{6,22},{7,23},{8,24},{9,... | collective-permute-start | bytes 294920 | tf_op jit(solution)/shard_map/ppermute | solution.py:30
  9.7 1.6 %collective-permute-start.1 = (bf16[32,1536]{1,0:T(8,128)(2,1)S(1)}, bf16[32,1536]{1,0:T(8,128)(2,1)S(1)}, u32[]{:S(2)}, u32[]{:S(2)}) collective-permute-start(bf16[32,1536]{1,0:T(8,128)(2,1)S(1)} %get-tuple-element.103._), channel_id=1, source_target_pairs={{0,8},{1,9},{2,10},{3,11},{4,12},{5,13},{6,14},{7,15},{8,0},{9,1},... | collective-permute-start | bytes 294920 | tf_op jit(solution)/shard_map/ppermute | solution.py:30
  11.3 2.2 %copy-done = bf16[2880,720]{0,1:T(8,128)(2,1)S(1)} copy-done((bf16[2880,720]{0,1:T(8,128)(2,1)S(1)}, bf16[2880,720]{0,1:T(8,128)(2,1)}, u32[]{:S(2)}) %copy-start) | copy-done | bytes 4147224
  13.8 1.2 %collective-permute-done.2._ = bf16[32,1536]{1,0:T(8,128)(2,1)S(1)} collective-permute-done((bf16[32,1536]{1,0:T(8,128)(2,1)S(1)}, bf16[32,1536]{1,0:T(8,128)(2,1)S(1)}, u32[]{:S(2)}, u32[]{:S(2)}) %collective-permute-start.2) | collective-permute-done | bytes 98336 | tf_op jit(solution)/shard_map/ppermute | solution.py:30
  15.0 0.6 collective-permute-start.3
  16.1 3.5 %collective-permute-done.3 = bf16[32,1536]{1,0:T(8,128)(2,1)S(1)} collective-permute-done((bf16[32,1536]{1,0:T(8,128)(2,1)S(1)}, bf16[32,1536]{1,0:T(8,128)(2,1)S(1)}, u32[]{:S(2)}, u32[]{:S(2)}) %collective-permute-start.3) | collective-permute-done | bytes 98336 | tf_op jit(solution)/shard_map/ppermute | solution.py:30
  19.6 1.6 %collective-permute-start.4 = (bf16[128,1536]{1,0:T(8,128)(2,1)S(1)}, bf16[128,1536]{1,0:T(8,128)(2,1)S(1)}, u32[]{:S(2)}, u32[]{:S(2)}) collective-permute-start(bf16[128,1536]{1,0:T(8,128)(2,1)S(1)} %constant_dynamic-update-slice_fusion.near_ref), channel_id=1, source_target_pairs={{0,4},{1,3},{2,6},{3,1},{4,0},{5,7},{6,2},{7,5},{8,12},{9,11},{10,... | collective-permute-start | bytes 1179656 | tf_op jit(solution)/shard_map/ppermute | solution.py:30
  21.3 0.7 collective-permute-start.5
  22.0 3.4 %collective-permute-start.6 = (bf16[32,1536]{1,0:T(8,128)(2,1)S(1)}, bf16[32,1536]{1,0:T(8,128)(2,1)S(1)}, u32[]{:S(2)}, u32[]{:S(2)}) collective-permute-start(bf16[32,1536]{1,0:T(8,128)(2,1)S(1)} %get-tuple-element.58), channel_id=1, source_target_pairs={{0,16},{1,17},{2,18},{3,19},{4,20},{5,21},{6,22},{7,23},{8,24},{9,... | collective-permute-start | bytes 294920 | tf_op jit(solution)/shard_map/ppermute | solution.py:30
  25.7 1.8 %collective-permute-done.4.next_ref = bf16[128,1536]{1,0:T(8,128)(2,1)S(1)} collective-permute-done((bf16[128,1536]{1,0:T(8,128)(2,1)S(1)}, bf16[128,1536]{1,0:T(8,128)(2,1)S(1)}, u32[]{:S(2)}, u32[]{:S(2)}) %collective-permute-start.4) | collective-permute-done | bytes 393248 | tf_op jit(solution)/shard_map/ppermute | solution.py:30
  27.5 1.3 %shard_map.76 = bf16[192,1536]{1,0:T(8,128)(2,1)S(1)} custom-call(s32[3]{0:T(128)S(1)} %pad_add_fusion.places_ref, bf16[128,1536]{1,0:T(8,128)(2,1)S(1)} %constant_dynamic-update-slice_fusion.near_ref, bf16[128,1536]{1,0:T(8,128)(2,1)S(1)} %collective-permute-done.4.next_ref), custom_call_target="tpu_custom_call" | custom-call | flops 301989888 | bytes 1572864 | tf_op jit(solution)/shard_map/pallas_call | solution.py:99
  28.8 1.6 %collective-permute-start.9 = (bf16[192,1536]{1,0:T(8,128)(2,1)S(1)}, bf16[192,1536]{1,0:T(8,128)(2,1)S(1)}, u32[]{:S(2)}, u32[]{:S(2)}) collective-permute-start(bf16[192,1536]{1,0:T(8,128)(2,1)S(1)} %shard_map.76), channel_id=1, source_target_pairs={{0,2},{1,5},{2,0},{3,7},{4,6},{5,1},{6,4},{7,3},{8,10},{9,13},{10,... | collective-permute-start | bytes 1769480 | tf_op jit(solution)/shard_map/ppermute | solution.py:30
  30.4 1.3 %shard_map.77 = (bf16[192,1536]{1,0:T(8,128)(2,1)S(1)}, f32[128,128]{1,0:T(8,128)S(1)}, f32[128,128]{1,0:T(8,128)S(1)}) custom-call(s32[3]{0:T(128)S(1)} %pad_add_fusion.places_ref, bf16[128,1536]{1,0:T(8,128)(2,1)S(1)} %constant_dynamic-update-slice_fusion.near_ref, bf16[128,1536]{1,0:T(8,128)(2,1)S(1)} %collective-permute-done.4.next_ref), custom_call_target="tpu_custom_call" | custom-call | flops 301989888 | bytes 1572864 | tf_op jit(solution)/shard_map/pallas_call | solution.py:99
  32.3 1.3 %collective-permute-start.8 = (bf16[128,1536]{1,0:T(8,128)(2,1)S(1)}, bf16[128,1536]{1,0:T(8,128)(2,1)S(1)}, u32[]{:S(2)}, u32[]{:S(2)}) collective-permute-start(bf16[128,1536]{1,0:T(8,128)(2,1)S(1)} %constant_dynamic-update-slice_fusion.5.near_ref), channel_id=1, source_target_pairs={{0,4},{1,3},{2,6},{3,1},{4,0},{5,7},{6,2},{7,5},{8,12},{9,11},{10,... | collective-permute-start | bytes 1179656 | tf_op jit(solution)/shard_map/ppermute | solution.py:30
  33.9 6.2 %collective-permute-done.8.next_ref = bf16[128,1536]{1,0:T(8,128)(2,1)S(1)} collective-permute-done((bf16[128,1536]{1,0:T(8,128)(2,1)S(1)}, bf16[128,1536]{1,0:T(8,128)(2,1)S(1)}, u32[]{:S(2)}, u32[]{:S(2)}) %collective-permute-start.8) | collective-permute-done | bytes 393248 | tf_op jit(solution)/shard_map/ppermute | solution.py:30
  40.1 1.6 %shard_map.79 = (bf16[192,1536]{1,0:T(8,128)(2,1)S(1)}, bf16[192,1536]{1,0:T(8,128)(2,1)S(1)}, f32[128,128]{1,0:T(8,128)S(1)}, f32[128,128]{1,0:T(8,128)S(1)}) custom-call(s32[3]{0:T(128)S(1)} %pad_add_fusion.places_ref, bf16[128,1536]{1,0:T(8,128)(2,1)S(1)} %constant_dynamic-update-slice_fusion.5.near_ref, bf16[128,1536]{1,0:T(8,128)(2,1)S(1)} %collective-permute-done.8.next_ref), custom_call_target="tpu_custom_call" | custom-call | flops 301989888 | bytes 1572864 | tf_op jit(solution)/shard_map/pallas_call | solution.py:99
  41.8 1.2 %collective-permute-done.9.mine_far_ref = bf16[192,1536]{1,0:T(8,128)(2,1)S(1)} collective-permute-done((bf16[192,1536]{1,0:T(8,128)(2,1)S(1)}, bf16[192,1536]{1,0:T(8,128)(2,1)S(1)}, u32[]{:S(2)}, u32[]{:S(2)}) %collective-permute-start.9) | collective-permute-done | bytes 589856 | tf_op jit(solution)/shard_map/ppermute | solution.py:30
  43.0 0.7 collective-permute-start.10
  43.7 1.3 %collective-permute-done.12.other_far_ref = bf16[192,1536]{1,0:T(8,128)(2,1)S(1)} collective-permute-done((bf16[192,1536]{1,0:T(8,128)(2,1)S(1)}, bf16[192,1536]{1,0:T(8,128)(2,1)S(1)}, u32[]{:S(2)}, u32[]{:S(2)}) %collective-permute-start.12) | collective-permute-done | bytes 589856 | tf_op jit(solution)/shard_map/ppermute | solution.py:30
  45.0 6.7 %shard_map.80 = (f32[192,1536]{1,0:T(8,128)S(1)}, f32[192,1536]{1,0:T(8,128)S(1)}, bf16[192,1536]{1,0:T(8,128)(2,1)S(1)}, bf16[192,1536]{1,0:T(8,128)(2,1)S(1)}) custom-call(s32[3]{0:T(128)S(1)} %pad_add_fusion.places_ref, bf16[192,1536]{1,0:T(8,128)(2,1)S(1)} %get-tuple-element.63._.mine_near_ref, ...), custom_call_target="tpu_custom_call" | custom-call | flops 4777574400 | bytes 17160192 | tf_op jit(solution)/shard_map/pallas_call | solution.py:215
  51.7 1.2 %collective-permute-done.10.mine_far_ref = bf16[192,1536]{1,0:T(8,128)(2,1)S(1)} collective-permute-done((bf16[192,1536]{1,0:T(8,128)(2,1)S(1)}, bf16[192,1536]{1,0:T(8,128)(2,1)S(1)}, u32[]{:S(2)}, u32[]{:S(2)}) %collective-permute-start.10) | collective-permute-done | bytes 589856 | tf_op jit(solution)/shard_map/ppermute | solution.py:30
  53.9 1.0 collective-permute-done.14
  55.0 0.8 collective-permute-start.15
  55.8 0.8 collective-permute-done.18.other_far_ref
  56.6 6.8 %shard_map.82 = (f32[192,1536]{1,0:T(8,128)S(1)}, f32[192,1536]{1,0:T(8,128)S(1)}, bf16[192,1536]{1,0:T(8,128)(2,1)S(1)}, bf16[192,1536]{1,0:T(8,128)(2,1)S(1)}) custom-call(s32[3]{0:T(128)S(1)} %pad_add_fusion.places_ref, bf16[192,1536]{1,0:T(8,128)(2,1)S(1)} %get-tuple-element.83.mine_near_ref, bf16[192,1536]{1,0:T(8,128)(2,1)S(1)} %collective-permute-done.10.mine_far_ref, ...), custom_call_target="tpu_custom_call" | custom-call | flops 4777574400 | bytes 17160192 | tf_op jit(solution)/shard_map/pallas_call | solution.py:215
  64.0 0.9 collective-permute-done.15.arrived_ref
  64.9 0.6 shard_map.81
  65.6 2.1 %collective-permute-start.16 = (bf16[128,1536]{1,0:T(8,128)(2,1)S(1)}, bf16[128,1536]{1,0:T(8,128)(2,1)S(1)}, u32[]{:S(2)}, u32[]{:S(2)}) collective-permute-start(bf16[128,1536]{1,0:T(8,128)(2,1)S(1)} %get-tuple-element.80), channel_id=1, source_target_pairs={{0,4},{1,3},{2,6},{3,1},{4,0},{5,7},{6,2},{7,5},{8,12},{9,11},{10,... | collective-permute-start | bytes 1179656 | tf_op jit(solution)/shard_map/ppermute | solution.py:30
  67.9 0.7 collective-permute-start.21
  68.5 9.1 %collective-permute-done.16 = bf16[128,1536]{1,0:T(8,128)(2,1)S(1)} collective-permute-done((bf16[128,1536]{1,0:T(8,128)(2,1)S(1)}, bf16[128,1536]{1,0:T(8,128)(2,1)S(1)}, u32[]{:S(2)}, u32[]{:S(2)}) %collective-permute-start.16) | collective-permute-done | bytes 393248 | tf_op jit(solution)/shard_map/ppermute | solution.py:30
  77.7 0.7 collective-permute-done.21.arrived_ref
  78.8 1.8 %collective-permute-start.25 = (bf16[128,1536]{1,0:T(8,128)(2,1)S(1)}, bf16[128,1536]{1,0:T(8,128)(2,1)S(1)}, u32[]{:S(2)}, u32[]{:S(2)}) collective-permute-start(bf16[128,1536]{1,0:T(8,128)(2,1)S(1)} %shard_map.83._), channel_id=1, source_target_pairs={{0,4},{1,3},{2,6},{3,1},{4,0},{5,7},{6,2},{7,5},{8,12},{9,11},{10,... | collective-permute-start | bytes 1179656 | tf_op jit(solution)/shard_map/ppermute | solution.py:30
  81.1 1.8 %collective-permute-start.23 = (bf16[32,1536]{1,0:T(8,128)(2,1)S(1)}, bf16[32,1536]{1,0:T(8,128)(2,1)S(1)}, u32[]{:S(2)}, u32[]{:S(2)}) collective-permute-start(bf16[32,1536]{1,0:T(8,128)(2,1)S(1)} %get-tuple-element.98), channel_id=1, source_target_pairs={{0,8},{1,9},{2,10},{3,11},{4,12},{5,13},{6,14},{7,15},{8,0},{9,1},... | collective-permute-start | bytes 294920 | tf_op jit(solution)/shard_map/ppermute | solution.py:30
  83.2 3.4 %collective-permute-done.25 = bf16[128,1536]{1,0:T(8,128)(2,1)S(1)} collective-permute-done((bf16[128,1536]{1,0:T(8,128)(2,1)S(1)}, bf16[128,1536]{1,0:T(8,128)(2,1)S(1)}, u32[]{:S(2)}, u32[]{:S(2)}) %collective-permute-start.25) | collective-permute-done | bytes 393248 | tf_op jit(solution)/shard_map/ppermute | solution.py:30
  86.8 2.3 %collective-permute-start.27 = (bf16[32,1536]{1,0:T(8,128)(2,1)S(1)}, bf16[32,1536]{1,0:T(8,128)(2,1)S(1)}, u32[]{:S(2)}, u32[]{:S(2)}) collective-permute-start(bf16[32,1536]{1,0:T(8,128)(2,1)S(1)} %get-tuple-element.100), channel_id=1, source_target_pairs={{0,8},{1,9},{2,10},{3,11},{4,12},{5,13},{6,14},{7,15},{8,0},{9,1},... | collective-permute-start | bytes 294920 | tf_op jit(solution)/shard_map/ppermute | solution.py:30
  89.1 1.7 %collective-permute-start.24 = (bf16[32,1536]{1,0:T(8,128)(2,1)S(1)}, bf16[32,1536]{1,0:T(8,128)(2,1)S(1)}, u32[]{:S(2)}, u32[]{:S(2)}) collective-permute-start(bf16[32,1536]{1,0:T(8,128)(2,1)S(1)} %add_convert_fusion.2), channel_id=1, source_target_pairs={{0,16},{1,17},{2,18},{3,19},{4,20},{5,21},{6,22},{7,23},{8,24},{9,... | collective-permute-start | bytes 294920 | tf_op jit(solution)/shard_map/ppermute | solution.py:30
  90.8 1.9 %collective-permute-start.26 = (bf16[32,1536]{1,0:T(8,128)(2,1)S(1)}, bf16[32,1536]{1,0:T(8,128)(2,1)S(1)}, u32[]{:S(2)}, u32[]{:S(2)}) collective-permute-start(bf16[32,1536]{1,0:T(8,128)(2,1)S(1)} %get-tuple-element.99), channel_id=1, source_target_pairs={{0,8},{1,9},{2,10},{3,11},{4,12},{5,13},{6,14},{7,15},{8,0},{9,1},... | collective-permute-start | bytes 294920 | tf_op jit(solution)/shard_map/ppermute | solution.py:30
  92.7 3.6 %collective-permute-start.28 = (bf16[32,1536]{1,0:T(8,128)(2,1)S(1)}, bf16[32,1536]{1,0:T(8,128)(2,1)S(1)}, u32[]{:S(2)}, u32[]{:S(2)}) collective-permute-start(bf16[32,1536]{1,0:T(8,128)(2,1)S(1)} %fusion.2), channel_id=1, source_target_pairs={{0,16},{1,17},{2,18},{3,19},{4,20},{5,21},{6,22},{7,23},{8,24},{9,... | collective-permute-start | bytes 294920 | tf_op jit(solution)/shard_map/ppermute | solution.py:30
  96.4 1.0 collective-permute-done.26
  97.3 3.6 %collective-permute-done.28 = bf16[32,1536]{1,0:T(8,128)(2,1)S(1)} collective-permute-done((bf16[32,1536]{1,0:T(8,128)(2,1)S(1)}, bf16[32,1536]{1,0:T(8,128)(2,1)S(1)}, u32[]{:S(2)}, u32[]{:S(2)}) %collective-permute-start.28) | collective-permute-done | bytes 98336 | tf_op jit(solution)/shard_map/ppermute | solution.py:30
  101.1 1.3 %collective-permute-done.29 = bf16[2,16,1536]{2,1,0:T(8,128)(2,1)S(1)} collective-permute-done((bf16[2,16,1536]{2,1,0:T(8,128)(2,1)S(1)}, bf16[2,16,1536]{2,1,0:T(8,128)(2,1)S(1)}, u32[]{:S(2)}, u32[]{:S(2)}) %collective-permute-start.29) | collective-permute-done | bytes 98336 | tf_op jit(solution)/shard_map/ppermute | solution.py:30
  102.5 0.7 fusion
  (75 shorter events, 6.2 us)
Async XLA Ops:
  2.4 0.9 copy-start.1
  3.3 12.4 %slice-start.2 = ((s8[4239360]{0:T(1024)(128)(4,1)}), s8[45056]{0:T(1024)(128)(4,1)S(1)}, s32[]{:S(2)}) async-start(s8[4239360]{0:T(1024)(128)(4,1)} %bitcast.25), calls=%async_computation.2 | async-start | bytes 90112
  4.1 1.5 %collective-permute-start = (bf16[2,16,1536]{2,1,0:T(8,128)(2,1)S(1)}, bf16[2,16,1536]{2,1,0:T(8,128)(2,1)S(1)}, u32[]{:S(2)}, u32[]{:S(2)}) collective-permute-start(bf16[2,16,1536]{2,1,0:T(8,128)(2,1)S(1)} %get-tuple-element.49), channel_id=1, source_target_pairs={{0,1},{1,0},{2,3},{3,2},{4,5},{5,4},{6,7},{7,6},{8,9},{9,8},{10,11... | collective-permute-start | bytes 294920 | tf_op jit(solution)/shard_map/ppermute | solution.py:30
  5.7 9.3 %collective-permute-start.2 = (bf16[32,1536]{1,0:T(8,128)(2,1)S(1)}, bf16[32,1536]{1,0:T(8,128)(2,1)S(1)}, u32[]{:S(2)}, u32[]{:S(2)}) collective-permute-start(bf16[32,1536]{1,0:T(8,128)(2,1)S(1)} %get-tuple-element.103._), channel_id=1, source_target_pairs={{0,16},{1,17},{2,18},{3,19},{4,20},{5,21},{6,22},{7,23},{8,24},{9,... | collective-permute-start | bytes 294920 | tf_op jit(solution)/shard_map/ppermute | solution.py:30
  9.7 6.0 %collective-permute-start.1 = (bf16[32,1536]{1,0:T(8,128)(2,1)S(1)}, bf16[32,1536]{1,0:T(8,128)(2,1)S(1)}, u32[]{:S(2)}, u32[]{:S(2)}) collective-permute-start(bf16[32,1536]{1,0:T(8,128)(2,1)S(1)} %get-tuple-element.103._), channel_id=1, source_target_pairs={{0,8},{1,9},{2,10},{3,11},{4,12},{5,13},{6,14},{7,15},{8,0},{9,1},... | collective-permute-start | bytes 294920 | tf_op jit(solution)/shard_map/ppermute | solution.py:30
  11.3 2.2 %copy-start = (bf16[2880,720]{0,1:T(8,128)(2,1)S(1)}, bf16[2880,720]{0,1:T(8,128)(2,1)}, u32[]{:S(2)}) copy-start(bf16[2880,720]{0,1:T(8,128)(2,1)} %param.9) | copy-start | bytes 12441604
  13.5 2.2 %slice-start.3 = ((s8[4239360]{0:T(1024)(128)(4,1)}), s8[4194304]{0:T(1024)(128)(4,1)S(1)}, s32[]{:S(2)}) async-start(s8[4239360]{0:T(1024)(128)(4,1)} %bitcast.25), calls=%async_computation.3 | async-start | bytes 8388608
  15.0 4.6 %collective-permute-start.3 = (bf16[32,1536]{1,0:T(8,128)(2,1)S(1)}, bf16[32,1536]{1,0:T(8,128)(2,1)S(1)}, u32[]{:S(2)}, u32[]{:S(2)}) collective-permute-start(bf16[32,1536]{1,0:T(8,128)(2,1)S(1)} %collective-permute-done.2._), channel_id=1, source_target_pairs={{0,8},{1,9},{2,10},{3,11},{4,12},{5,13},{6,14},{7,15},{8,0},{9,1},... | collective-permute-start | bytes 294920 | tf_op jit(solution)/shard_map/ppermute | solution.py:30
  15.6 17.9 %slice-start = ((s8[4239360]{0:T(1024)(128)(4,1)}), s8[4194304]{0:T(1024)(128)(4,1)S(1)}, s32[]{:S(2)}) async-start(s8[4239360]{0:T(1024)(128)(4,1)} %bitcast.22), calls=%async_computation | async-start | bytes 8388608
  15.7 17.8 %slice-start.1 = ((s8[4239360]{0:T(1024)(128)(4,1)}), s8[45056]{0:T(1024)(128)(4,1)S(1)}, s32[]{:S(2)}) async-start(s8[4239360]{0:T(1024)(128)(4,1)} %bitcast.22), calls=%async_computation.1 | async-start | bytes 90112
  19.6 7.8 %collective-permute-start.4 = (bf16[128,1536]{1,0:T(8,128)(2,1)S(1)}, bf16[128,1536]{1,0:T(8,128)(2,1)S(1)}, u32[]{:S(2)}, u32[]{:S(2)}) collective-permute-start(bf16[128,1536]{1,0:T(8,128)(2,1)S(1)} %constant_dynamic-update-slice_fusion.near_ref), channel_id=1, source_target_pairs={{0,4},{1,3},{2,6},{3,1},{4,0},{5,7},{6,2},{7,5},{8,12},{9,11},{10,... | collective-permute-start | bytes 1179656 | tf_op jit(solution)/shard_map/ppermute | solution.py:30
  21.3 10.5 %collective-permute-start.5 = (bf16[32,1536]{1,0:T(8,128)(2,1)S(1)}, bf16[32,1536]{1,0:T(8,128)(2,1)S(1)}, u32[]{:S(2)}, u32[]{:S(2)}) collective-permute-start(bf16[32,1536]{1,0:T(8,128)(2,1)S(1)} %get-tuple-element.58), channel_id=1, source_target_pairs={{0,8},{1,9},{2,10},{3,11},{4,12},{5,13},{6,14},{7,15},{8,0},{9,1},... | collective-permute-start | bytes 294920 | tf_op jit(solution)/shard_map/ppermute | solution.py:30
  22.0 10.2 %collective-permute-start.6 = (bf16[32,1536]{1,0:T(8,128)(2,1)S(1)}, bf16[32,1536]{1,0:T(8,128)(2,1)S(1)}, u32[]{:S(2)}, u32[]{:S(2)}) collective-permute-start(bf16[32,1536]{1,0:T(8,128)(2,1)S(1)} %get-tuple-element.58), channel_id=1, source_target_pairs={{0,16},{1,17},{2,18},{3,19},{4,20},{5,21},{6,22},{7,23},{8,24},{9,... | collective-permute-start | bytes 294920 | tf_op jit(solution)/shard_map/ppermute | solution.py:30
  25.3 6.9 %collective-permute-start.7 = (bf16[32,1536]{1,0:T(8,128)(2,1)S(1)}, bf16[32,1536]{1,0:T(8,128)(2,1)S(1)}, u32[]{:S(2)}, u32[]{:S(2)}) collective-permute-start(bf16[32,1536]{1,0:T(8,128)(2,1)S(1)} %get-tuple-element.58), channel_id=1, source_target_pairs={{0,24},{1,25},{2,26},{3,27},{4,28},{5,29},{6,30},{7,31},{8,16},{9,... | collective-permute-start | bytes 294920 | tf_op jit(solution)/shard_map/ppermute | solution.py:30
  28.8 14.2 %collective-permute-start.9 = (bf16[192,1536]{1,0:T(8,128)(2,1)S(1)}, bf16[192,1536]{1,0:T(8,128)(2,1)S(1)}, u32[]{:S(2)}, u32[]{:S(2)}) collective-permute-start(bf16[192,1536]{1,0:T(8,128)(2,1)S(1)} %shard_map.76), channel_id=1, source_target_pairs={{0,2},{1,5},{2,0},{3,7},{4,6},{5,1},{6,4},{7,3},{8,10},{9,13},{10,... | collective-permute-start | bytes 1769480 | tf_op jit(solution)/shard_map/ppermute | solution.py:30
  32.3 7.8 %collective-permute-start.8 = (bf16[128,1536]{1,0:T(8,128)(2,1)S(1)}, bf16[128,1536]{1,0:T(8,128)(2,1)S(1)}, u32[]{:S(2)}, u32[]{:S(2)}) collective-permute-start(bf16[128,1536]{1,0:T(8,128)(2,1)S(1)} %constant_dynamic-update-slice_fusion.5.near_ref), channel_id=1, source_target_pairs={{0,4},{1,3},{2,6},{3,1},{4,0},{5,7},{6,2},{7,5},{8,12},{9,11},{10,... | collective-permute-start | bytes 1179656 | tf_op jit(solution)/shard_map/ppermute | solution.py:30
  33.5 10.2 %collective-permute-start.11 = (bf16[192,1536]{1,0:T(8,128)(2,1)S(1)}, bf16[192,1536]{1,0:T(8,128)(2,1)S(1)}, u32[]{:S(2)}, u32[]{:S(2)}) collective-permute-start(bf16[192,1536]{1,0:T(8,128)(2,1)S(1)} %get-tuple-element.63._.mine_near_ref), channel_id=1, source_target_pairs={{0,1},{1,0},{2,3},{3,2},{4,5},{5,4},{6,7},{7,6},{8,9},{9,8},{10,11... | collective-permute-start | bytes 1769480 | tf_op jit(solution)/shard_map/ppermute | solution.py:30
  43.0 2.0 %collective-permute-start.12 = (bf16[192,1536]{1,0:T(8,128)(2,1)S(1)}, bf16[192,1536]{1,0:T(8,128)(2,1)S(1)}, u32[]{:S(2)}, u32[]{:S(2)}) collective-permute-start(bf16[192,1536]{1,0:T(8,128)(2,1)S(1)} %collective-permute-done.9.mine_far_ref), channel_id=1, source_target_pairs={{0,1},{1,0},{2,3},{3,2},{4,5},{5,4},{6,7},{7,6},{8,9},{9,8},{10,11... | collective-permute-start | bytes 1769480 | tf_op jit(solution)/shard_map/ppermute | solution.py:30
  43.0 9.9 %collective-permute-start.10 = (bf16[192,1536]{1,0:T(8,128)(2,1)S(1)}, bf16[192,1536]{1,0:T(8,128)(2,1)S(1)}, u32[]{:S(2)}, u32[]{:S(2)}) collective-permute-start(bf16[192,1536]{1,0:T(8,128)(2,1)S(1)} %get-tuple-element.66), channel_id=1, source_target_pairs={{0,2},{1,5},{2,0},{3,7},{4,6},{5,1},{6,4},{7,3},{8,10},{9,13},{10,... | collective-permute-start | bytes 1769480 | tf_op jit(solution)/shard_map/ppermute | solution.py:30
  52.9 2.0 %collective-permute-start.14 = (bf16[192,1536]{1,0:T(8,128)(2,1)S(1)}, bf16[192,1536]{1,0:T(8,128)(2,1)S(1)}, u32[]{:S(2)}, u32[]{:S(2)}) collective-permute-start(bf16[192,1536]{1,0:T(8,128)(2,1)S(1)} %get-tuple-element.78), channel_id=1, source_target_pairs={{0,1},{1,0},{2,3},{3,2},{4,5},{5,4},{6,7},{7,6},{8,9},{9,8},{10,11... | collective-permute-start | bytes 1769480 | tf_op jit(solution)/shard_map/ppermute | solution.py:30
  52.9 2.9 %collective-permute-start.17 = (bf16[192,1536]{1,0:T(8,128)(2,1)S(1)}, bf16[192,1536]{1,0:T(8,128)(2,1)S(1)}, u32[]{:S(2)}, u32[]{:S(2)}) collective-permute-start(bf16[192,1536]{1,0:T(8,128)(2,1)S(1)} %get-tuple-element.83.mine_near_ref), channel_id=1, source_target_pairs={{0,1},{1,0},{2,3},{3,2},{4,5},{5,4},{6,7},{7,6},{8,9},{9,8},{10,11... | collective-permute-start | bytes 1769480 | tf_op jit(solution)/shard_map/ppermute | solution.py:30
  53.4 3.2 %collective-permute-start.18 = (bf16[192,1536]{1,0:T(8,128)(2,1)S(1)}, bf16[192,1536]{1,0:T(8,128)(2,1)S(1)}, u32[]{:S(2)}, u32[]{:S(2)}) collective-permute-start(bf16[192,1536]{1,0:T(8,128)(2,1)S(1)} %collective-permute-done.10.mine_far_ref), channel_id=1, source_target_pairs={{0,1},{1,0},{2,3},{3,2},{4,5},{5,4},{6,7},{7,6},{8,9},{9,8},{10,11... | collective-permute-start | bytes 1769480 | tf_op jit(solution)/shard_map/ppermute | solution.py:30
  53.4 10.6 %collective-permute-start.13 = (bf16[192,1536]{1,0:T(8,128)(2,1)S(1)}, bf16[192,1536]{1,0:T(8,128)(2,1)S(1)}, u32[]{:S(2)}, u32[]{:S(2)}) collective-permute-start(bf16[192,1536]{1,0:T(8,128)(2,1)S(1)} %get-tuple-element.76), channel_id=1, source_target_pairs={{0,1},{1,0},{2,3},{3,2},{4,5},{5,4},{6,7},{7,6},{8,9},{9,8},{10,11... | collective-permute-start | bytes 1769480 | tf_op jit(solution)/shard_map/ppermute | solution.py:30
  55.0 9.9 %collective-permute-start.15 = (bf16[192,1536]{1,0:T(8,128)(2,1)S(1)}, bf16[192,1536]{1,0:T(8,128)(2,1)S(1)}, u32[]{:S(2)}, u32[]{:S(2)}) collective-permute-start(bf16[192,1536]{1,0:T(8,128)(2,1)S(1)} %add_convert_fusion.1), channel_id=1, source_target_pairs={{0,2},{1,5},{2,0},{3,7},{4,6},{5,1},{6,4},{7,3},{8,10},{9,13},{10,... | collective-permute-start | bytes 1769480 | tf_op jit(solution)/shard_map/ppermute | solution.py:30
  63.4 4.3 %collective-permute-start.20 = (bf16[192,1536]{1,0:T(8,128)(2,1)S(1)}, bf16[192,1536]{1,0:T(8,128)(2,1)S(1)}, u32[]{:S(2)}, u32[]{:S(2)}) collective-permute-start(bf16[192,1536]{1,0:T(8,128)(2,1)S(1)} %get-tuple-element.88), channel_id=1, source_target_pairs={{0,1},{1,0},{2,3},{3,2},{4,5},{5,4},{6,7},{7,6},{8,9},{9,8},{10,11... | collective-permute-start | bytes 1769480 | tf_op jit(solution)/shard_map/ppermute | solution.py:30
  63.9 13.8 %collective-permute-start.19 = (bf16[192,1536]{1,0:T(8,128)(2,1)S(1)}, bf16[192,1536]{1,0:T(8,128)(2,1)S(1)}, u32[]{:S(2)}, u32[]{:S(2)}) collective-permute-start(bf16[192,1536]{1,0:T(8,128)(2,1)S(1)} %get-tuple-element.86), channel_id=1, source_target_pairs={{0,1},{1,0},{2,3},{3,2},{4,5},{5,4},{6,7},{7,6},{8,9},{9,8},{10,11... | collective-permute-start | bytes 1769480 | tf_op jit(solution)/shard_map/ppermute | solution.py:30
  65.6 12.0 %collective-permute-start.16 = (bf16[128,1536]{1,0:T(8,128)(2,1)S(1)}, bf16[128,1536]{1,0:T(8,128)(2,1)S(1)}, u32[]{:S(2)}, u32[]{:S(2)}) collective-permute-start(bf16[128,1536]{1,0:T(8,128)(2,1)S(1)} %get-tuple-element.80), channel_id=1, source_target_pairs={{0,4},{1,3},{2,6},{3,1},{4,0},{5,7},{6,2},{7,5},{8,12},{9,11},{10,... | collective-permute-start | bytes 1179656 | tf_op jit(solution)/shard_map/ppermute | solution.py:30
  67.9 10.5 %collective-permute-start.21 = (bf16[192,1536]{1,0:T(8,128)(2,1)S(1)}, bf16[192,1536]{1,0:T(8,128)(2,1)S(1)}, u32[]{:S(2)}, u32[]{:S(2)}) collective-permute-start(bf16[192,1536]{1,0:T(8,128)(2,1)S(1)} %add_convert_fusion), channel_id=1, source_target_pairs={{0,2},{1,5},{2,0},{3,7},{4,6},{5,1},{6,4},{7,3},{8,10},{9,13},{10,... | collective-permute-start | bytes 1769480 | tf_op jit(solution)/shard_map/ppermute | solution.py:30
  78.8 7.8 %collective-permute-start.25 = (bf16[128,1536]{1,0:T(8,128)(2,1)S(1)}, bf16[128,1536]{1,0:T(8,128)(2,1)S(1)}, u32[]{:S(2)}, u32[]{:S(2)}) collective-permute-start(bf16[128,1536]{1,0:T(8,128)(2,1)S(1)} %shard_map.83._), channel_id=1, source_target_pairs={{0,4},{1,3},{2,6},{3,1},{4,0},{5,7},{6,2},{7,5},{8,12},{9,11},{10,... | collective-permute-start | bytes 1179656 | tf_op jit(solution)/shard_map/ppermute | solution.py:30
  81.1 7.9 %collective-permute-start.23 = (bf16[32,1536]{1,0:T(8,128)(2,1)S(1)}, bf16[32,1536]{1,0:T(8,128)(2,1)S(1)}, u32[]{:S(2)}, u32[]{:S(2)}) collective-permute-start(bf16[32,1536]{1,0:T(8,128)(2,1)S(1)} %get-tuple-element.98), channel_id=1, source_target_pairs={{0,8},{1,9},{2,10},{3,11},{4,12},{5,13},{6,14},{7,15},{8,0},{9,1},... | collective-permute-start | bytes 294920 | tf_op jit(solution)/shard_map/ppermute | solution.py:30
  82.9 13.4 %collective-permute-start.22 = (bf16[32,1536]{1,0:T(8,128)(2,1)S(1)}, bf16[32,1536]{1,0:T(8,128)(2,1)S(1)}, u32[]{:S(2)}, u32[]{:S(2)}) collective-permute-start(bf16[32,1536]{1,0:T(8,128)(2,1)S(1)} %get-tuple-element.97), channel_id=1, source_target_pairs={{0,8},{1,9},{2,10},{3,11},{4,12},{5,13},{6,14},{7,15},{8,0},{9,1},... | collective-permute-start | bytes 294920 | tf_op jit(solution)/shard_map/ppermute | solution.py:30
  86.8 5.9 %collective-permute-start.27 = (bf16[32,1536]{1,0:T(8,128)(2,1)S(1)}, bf16[32,1536]{1,0:T(8,128)(2,1)S(1)}, u32[]{:S(2)}, u32[]{:S(2)}) collective-permute-start(bf16[32,1536]{1,0:T(8,128)(2,1)S(1)} %get-tuple-element.100), channel_id=1, source_target_pairs={{0,8},{1,9},{2,10},{3,11},{4,12},{5,13},{6,14},{7,15},{8,0},{9,1},... | collective-permute-start | bytes 294920 | tf_op jit(solution)/shard_map/ppermute | solution.py:30
  89.1 7.2 %collective-permute-start.24 = (bf16[32,1536]{1,0:T(8,128)(2,1)S(1)}, bf16[32,1536]{1,0:T(8,128)(2,1)S(1)}, u32[]{:S(2)}, u32[]{:S(2)}) collective-permute-start(bf16[32,1536]{1,0:T(8,128)(2,1)S(1)} %add_convert_fusion.2), channel_id=1, source_target_pairs={{0,16},{1,17},{2,18},{3,19},{4,20},{5,21},{6,22},{7,23},{8,24},{9,... | collective-permute-start | bytes 294920 | tf_op jit(solution)/shard_map/ppermute | solution.py:30
  90.8 6.5 %collective-permute-start.26 = (bf16[32,1536]{1,0:T(8,128)(2,1)S(1)}, bf16[32,1536]{1,0:T(8,128)(2,1)S(1)}, u32[]{:S(2)}, u32[]{:S(2)}) collective-permute-start(bf16[32,1536]{1,0:T(8,128)(2,1)S(1)} %get-tuple-element.99), channel_id=1, source_target_pairs={{0,8},{1,9},{2,10},{3,11},{4,12},{5,13},{6,14},{7,15},{8,0},{9,1},... | collective-permute-start | bytes 294920 | tf_op jit(solution)/shard_map/ppermute | solution.py:30
  92.7 8.2 %collective-permute-start.28 = (bf16[32,1536]{1,0:T(8,128)(2,1)S(1)}, bf16[32,1536]{1,0:T(8,128)(2,1)S(1)}, u32[]{:S(2)}, u32[]{:S(2)}) collective-permute-start(bf16[32,1536]{1,0:T(8,128)(2,1)S(1)} %fusion.2), channel_id=1, source_target_pairs={{0,16},{1,17},{2,18},{3,19},{4,20},{5,21},{6,22},{7,23},{8,24},{9,... | collective-permute-start | bytes 294920 | tf_op jit(solution)/shard_map/ppermute | solution.py:30
  101.0 1.5 %copy-start.2 = (bf16[2,16,2880]{2,1,0:T(8,128)(2,1)S(1)}, bf16[2,16,2880]{2,1,0:T(8,128)(2,1)}, u32[]{:S(2)}) copy-start(bf16[2,16,2880]{2,1,0:T(8,128)(2,1)} %hidden_ref.1) | copy-start | bytes 552964
  101.0 1.4 %collective-permute-start.29 = (bf16[2,16,1536]{2,1,0:T(8,128)(2,1)S(1)}, bf16[2,16,1536]{2,1,0:T(8,128)(2,1)S(1)}, u32[]{:S(2)}, u32[]{:S(2)}) collective-permute-start(bf16[2,16,1536]{2,1,0:T(8,128)(2,1)S(1)} %select_convert_fusion), channel_id=1, source_target_pairs={{0,1},{1,0},{2,3},{3,2},{4,5},{5,4},{6,7},{7,6},{8,9},{9,8},{10,11... | collective-permute-start | bytes 294920 | tf_op jit(solution)/shard_map/ppermute | solution.py:30

commit v12 on v11

--- a/solution.py
+++ b/solution.py
@@ -142,7 +142,7 @@
     first, second, held = split_widths(width)
     pair = mine_near_ref.shape[0]
     quad = pair // 2
-    chunk = hidden // 3
+    chunk = 2 * LANES
     def lay(near, far_ref, swapped, start, size):
         for place in range(4):
             if swapped:
@@ -172,8 +172,8 @@
         jnp.where(chosen, pltpu.roll(tile, LANES - ROUTING // 2, 1), 0.0), axis=1, keepdims=True
     )
 
-    for part in range(3):
-        there = slice(part * chunk, (part + 1) * chunk)
+    for start in range(0, hidden, chunk):
+        there = slice(start, min(start + chunk, hidden))
         gate = lax.dot_general(rows_v[...], gate_v[there, :], across, preferred_element_type=jnp.float32)
         up = lax.dot_general(rows_v[...], up_v[there, :], across, preferred_element_type=jnp.float32)
         act_v[:, there] = ((up + 1.0) * gate * jax.nn.sigmoid(swish_scale * gate)).astype(jnp.bfloat16)

time: 103 us -> 103 us (level)
  no operation moved by 1% of the time
where the time goes in v12:
time: 103 us
  waiting for transfers between devices  39.7 us (39%)
  starting transfers between devices  34.9 us (34%)
  Pallas kernels  21.1 us (20%)
  local copies, waits for them, and re-layouts  4.1 us (4%)
  other arithmetic  2.98 us (3%)
    ppermute x30, waiting for transfers between devices, moved(): return lax.ppermute(block, 'req', [(i, partner(i)) for i in range(count)])  39.7 us
    ppermute x30, starting transfers between devices, moved(): return lax.ppermute(block, 'req', [(i, partner(i)) for i in range(count)])  34.9 us
    pallas_call x2, Pallas kernels, ffn(): pl.pallas_call(ffn_body, out_shape=[jax.ShapeDtypeStruct((pair, held), jn...  13.4 us
    pallas_call x3, Pallas kernels, select(): pl.pallas_call(functools.partial(select_body, tokens, capacity, wanted),...  4.33 us
    unnamed x19, local copies, waits for them, and re-layouts  3.19 us
  transfers between devices with their start and end apart: 30, of which 18 were waited for; matrix products, arithmetic and copies ran while one was open for 1% of the time, Pallas kernels for 19%

profile of v12, /device:TPU:0, one launch (start us, length us, event | category | flops | bytes accessed | tf_op | source)
XLA Modules:
  0.0 103.1 jit_solution(5598322939644481917)
XLA Ops:
  0.0 0.8 reshape.34
  0.8 0.7 convert_bitcast_fusion
  1.5 0.7 pad_convert_fusion
  2.4 0.9 copy-done.1
  3.3 0.8 shard_map.73
  4.6 0.9 collective-permute-done
  5.7 4.0 %collective-permute-start.2 = (bf16[32,1536]{1,0:T(8,128)(2,1)S(1)}, bf16[32,1536]{1,0:T(8,128)(2,1)S(1)}, u32[]{:S(2)}, u32[]{:S(2)}) collective-permute-start(bf16[32,1536]{1,0:T(8,128)(2,1)S(1)} %get-tuple-element.103._), channel_id=1, source_target_pairs={{0,16},{1,17},{2,18},{3,19},{4,20},{5,21},{6,22},{7,23},{8,24},{9,... | collective-permute-start | bytes 294920 | tf_op jit(solution)/shard_map/ppermute | solution.py:30
  9.7 1.6 %collective-permute-start.1 = (bf16[32,1536]{1,0:T(8,128)(2,1)S(1)}, bf16[32,1536]{1,0:T(8,128)(2,1)S(1)}, u32[]{:S(2)}, u32[]{:S(2)}) collective-permute-start(bf16[32,1536]{1,0:T(8,128)(2,1)S(1)} %get-tuple-element.103._), channel_id=1, source_target_pairs={{0,8},{1,9},{2,10},{3,11},{4,12},{5,13},{6,14},{7,15},{8,0},{9,1},... | collective-permute-start | bytes 294920 | tf_op jit(solution)/shard_map/ppermute | solution.py:30
  11.3 2.2 %copy-done = bf16[2880,720]{0,1:T(8,128)(2,1)S(1)} copy-done((bf16[2880,720]{0,1:T(8,128)(2,1)S(1)}, bf16[2880,720]{0,1:T(8,128)(2,1)}, u32[]{:S(2)}) %copy-start) | copy-done | bytes 4147224
  13.8 1.2 %collective-permute-done.2._ = bf16[32,1536]{1,0:T(8,128)(2,1)S(1)} collective-permute-done((bf16[32,1536]{1,0:T(8,128)(2,1)S(1)}, bf16[32,1536]{1,0:T(8,128)(2,1)S(1)}, u32[]{:S(2)}, u32[]{:S(2)}) %collective-permute-start.2) | collective-permute-done | bytes 98336 | tf_op jit(solution)/shard_map/ppermute | solution.py:30
  15.0 0.6 collective-permute-start.3
  16.1 3.5 %collective-permute-done.3 = bf16[32,1536]{1,0:T(8,128)(2,1)S(1)} collective-permute-done((bf16[32,1536]{1,0:T(8,128)(2,1)S(1)}, bf16[32,1536]{1,0:T(8,128)(2,1)S(1)}, u32[]{:S(2)}, u32[]{:S(2)}) %collective-permute-start.3) | collective-permute-done | bytes 98336 | tf_op jit(solution)/shard_map/ppermute | solution.py:30
  19.6 1.6 %collective-permute-start.4 = (bf16[128,1536]{1,0:T(8,128)(2,1)S(1)}, bf16[128,1536]{1,0:T(8,128)(2,1)S(1)}, u32[]{:S(2)}, u32[]{:S(2)}) collective-permute-start(bf16[128,1536]{1,0:T(8,128)(2,1)S(1)} %constant_dynamic-update-slice_fusion.near_ref), channel_id=1, source_target_pairs={{0,4},{1,3},{2,6},{3,1},{4,0},{5,7},{6,2},{7,5},{8,12},{9,11},{10,... | collective-permute-start | bytes 1179656 | tf_op jit(solution)/shard_map/ppermute | solution.py:30
  21.3 0.7 collective-permute-start.5
  22.0 3.4 %collective-permute-start.6 = (bf16[32,1536]{1,0:T(8,128)(2,1)S(1)}, bf16[32,1536]{1,0:T(8,128)(2,1)S(1)}, u32[]{:S(2)}, u32[]{:S(2)}) collective-permute-start(bf16[32,1536]{1,0:T(8,128)(2,1)S(1)} %get-tuple-element.58), channel_id=1, source_target_pairs={{0,16},{1,17},{2,18},{3,19},{4,20},{5,21},{6,22},{7,23},{8,24},{9,... | collective-permute-start | bytes 294920 | tf_op jit(solution)/shard_map/ppermute | solution.py:30
  25.7 1.8 %collective-permute-done.4.next_ref = bf16[128,1536]{1,0:T(8,128)(2,1)S(1)} collective-permute-done((bf16[128,1536]{1,0:T(8,128)(2,1)S(1)}, bf16[128,1536]{1,0:T(8,128)(2,1)S(1)}, u32[]{:S(2)}, u32[]{:S(2)}) %collective-permute-start.4) | collective-permute-done | bytes 393248 | tf_op jit(solution)/shard_map/ppermute | solution.py:30
  27.5 1.3 %shard_map.76 = bf16[192,1536]{1,0:T(8,128)(2,1)S(1)} custom-call(s32[3]{0:T(128)S(1)} %pad_add_fusion.places_ref, bf16[128,1536]{1,0:T(8,128)(2,1)S(1)} %constant_dynamic-update-slice_fusion.near_ref, bf16[128,1536]{1,0:T(8,128)(2,1)S(1)} %collective-permute-done.4.next_ref), custom_call_target="tpu_custom_call" | custom-call | flops 301989888 | bytes 1572864 | tf_op jit(solution)/shard_map/pallas_call | solution.py:99
  28.8 1.6 %collective-permute-start.9 = (bf16[192,1536]{1,0:T(8,128)(2,1)S(1)}, bf16[192,1536]{1,0:T(8,128)(2,1)S(1)}, u32[]{:S(2)}, u32[]{:S(2)}) collective-permute-start(bf16[192,1536]{1,0:T(8,128)(2,1)S(1)} %shard_map.76), channel_id=1, source_target_pairs={{0,2},{1,5},{2,0},{3,7},{4,6},{5,1},{6,4},{7,3},{8,10},{9,13},{10,... | collective-permute-start | bytes 1769480 | tf_op jit(solution)/shard_map/ppermute | solution.py:30
  30.4 1.3 %shard_map.77 = (bf16[192,1536]{1,0:T(8,128)(2,1)S(1)}, f32[128,128]{1,0:T(8,128)S(1)}, f32[128,128]{1,0:T(8,128)S(1)}) custom-call(s32[3]{0:T(128)S(1)} %pad_add_fusion.places_ref, bf16[128,1536]{1,0:T(8,128)(2,1)S(1)} %constant_dynamic-update-slice_fusion.near_ref, bf16[128,1536]{1,0:T(8,128)(2,1)S(1)} %collective-permute-done.4.next_ref), custom_call_target="tpu_custom_call" | custom-call | flops 301989888 | bytes 1572864 | tf_op jit(solution)/shard_map/pallas_call | solution.py:99
  32.3 1.3 %collective-permute-start.8 = (bf16[128,1536]{1,0:T(8,128)(2,1)S(1)}, bf16[128,1536]{1,0:T(8,128)(2,1)S(1)}, u32[]{:S(2)}, u32[]{:S(2)}) collective-permute-start(bf16[128,1536]{1,0:T(8,128)(2,1)S(1)} %constant_dynamic-update-slice_fusion.5.near_ref), channel_id=1, source_target_pairs={{0,4},{1,3},{2,6},{3,1},{4,0},{5,7},{6,2},{7,5},{8,12},{9,11},{10,... | collective-permute-start | bytes 1179656 | tf_op jit(solution)/shard_map/ppermute | solution.py:30
  33.9 6.2 %collective-permute-done.8.next_ref = bf16[128,1536]{1,0:T(8,128)(2,1)S(1)} collective-permute-done((bf16[128,1536]{1,0:T(8,128)(2,1)S(1)}, bf16[128,1536]{1,0:T(8,128)(2,1)S(1)}, u32[]{:S(2)}, u32[]{:S(2)}) %collective-permute-start.8) | collective-permute-done | bytes 393248 | tf_op jit(solution)/shard_map/ppermute | solution.py:30
  40.1 1.6 %shard_map.79 = (bf16[192,1536]{1,0:T(8,128)(2,1)S(1)}, bf16[192,1536]{1,0:T(8,128)(2,1)S(1)}, f32[128,128]{1,0:T(8,128)S(1)}, f32[128,128]{1,0:T(8,128)S(1)}) custom-call(s32[3]{0:T(128)S(1)} %pad_add_fusion.places_ref, bf16[128,1536]{1,0:T(8,128)(2,1)S(1)} %constant_dynamic-update-slice_fusion.5.near_ref, bf16[128,1536]{1,0:T(8,128)(2,1)S(1)} %collective-permute-done.8.next_ref), custom_call_target="tpu_custom_call" | custom-call | flops 301989888 | bytes 1572864 | tf_op jit(solution)/shard_map/pallas_call | solution.py:99
  41.8 1.2 %collective-permute-done.9.mine_far_ref = bf16[192,1536]{1,0:T(8,128)(2,1)S(1)} collective-permute-done((bf16[192,1536]{1,0:T(8,128)(2,1)S(1)}, bf16[192,1536]{1,0:T(8,128)(2,1)S(1)}, u32[]{:S(2)}, u32[]{:S(2)}) %collective-permute-start.9) | collective-permute-done | bytes 589856 | tf_op jit(solution)/shard_map/ppermute | solution.py:30
  43.0 0.7 collective-permute-start.10
  43.7 1.3 %collective-permute-done.12.other_far_ref = bf16[192,1536]{1,0:T(8,128)(2,1)S(1)} collective-permute-done((bf16[192,1536]{1,0:T(8,128)(2,1)S(1)}, bf16[192,1536]{1,0:T(8,128)(2,1)S(1)}, u32[]{:S(2)}, u32[]{:S(2)}) %collective-permute-start.12) | collective-permute-done | bytes 589856 | tf_op jit(solution)/shard_map/ppermute | solution.py:30
  45.0 6.6 %shard_map.80 = (f32[192,1536]{1,0:T(8,128)S(1)}, f32[192,1536]{1,0:T(8,128)S(1)}, bf16[192,1536]{1,0:T(8,128)(2,1)S(1)}, bf16[192,1536]{1,0:T(8,128)(2,1)S(1)}) custom-call(s32[3]{0:T(128)S(1)} %pad_add_fusion.places_ref, bf16[192,1536]{1,0:T(8,128)(2,1)S(1)} %get-tuple-element.63._.mine_near_ref, ...), custom_call_target="tpu_custom_call" | custom-call | flops 4777574400 | bytes 17160192 | tf_op jit(solution)/shard_map/pallas_call | solution.py:215
  51.6 1.3 %collective-permute-done.10.mine_far_ref = bf16[192,1536]{1,0:T(8,128)(2,1)S(1)} collective-permute-done((bf16[192,1536]{1,0:T(8,128)(2,1)S(1)}, bf16[192,1536]{1,0:T(8,128)(2,1)S(1)}, u32[]{:S(2)}, u32[]{:S(2)}) %collective-permute-start.10) | collective-permute-done | bytes 589856 | tf_op jit(solution)/shard_map/ppermute | solution.py:30
  53.9 1.0 collective-permute-done.14
  55.0 0.8 collective-permute-start.15
  55.8 0.8 collective-permute-done.18.other_far_ref
  56.6 6.8 %shard_map.82 = (f32[192,1536]{1,0:T(8,128)S(1)}, f32[192,1536]{1,0:T(8,128)S(1)}, bf16[192,1536]{1,0:T(8,128)(2,1)S(1)}, bf16[192,1536]{1,0:T(8,128)(2,1)S(1)}) custom-call(s32[3]{0:T(128)S(1)} %pad_add_fusion.places_ref, bf16[192,1536]{1,0:T(8,128)(2,1)S(1)} %get-tuple-element.83.mine_near_ref, bf16[192,1536]{1,0:T(8,128)(2,1)S(1)} %collective-permute-done.10.mine_far_ref, ...), custom_call_target="tpu_custom_call" | custom-call | flops 4777574400 | bytes 17160192 | tf_op jit(solution)/shard_map/pallas_call | solution.py:215
  63.9 1.0 collective-permute-done.15.arrived_ref
  64.9 0.6 shard_map.81
  65.6 2.1 %collective-permute-start.16 = (bf16[128,1536]{1,0:T(8,128)(2,1)S(1)}, bf16[128,1536]{1,0:T(8,128)(2,1)S(1)}, u32[]{:S(2)}, u32[]{:S(2)}) collective-permute-start(bf16[128,1536]{1,0:T(8,128)(2,1)S(1)} %get-tuple-element.80), channel_id=1, source_target_pairs={{0,4},{1,3},{2,6},{3,1},{4,0},{5,7},{6,2},{7,5},{8,12},{9,11},{10,... | collective-permute-start | bytes 1179656 | tf_op jit(solution)/shard_map/ppermute | solution.py:30
  67.9 0.7 collective-permute-start.21
  68.5 9.1 %collective-permute-done.16 = bf16[128,1536]{1,0:T(8,128)(2,1)S(1)} collective-permute-done((bf16[128,1536]{1,0:T(8,128)(2,1)S(1)}, bf16[128,1536]{1,0:T(8,128)(2,1)S(1)}, u32[]{:S(2)}, u32[]{:S(2)}) %collective-permute-start.16) | collective-permute-done | bytes 393248 | tf_op jit(solution)/shard_map/ppermute | solution.py:30
  77.7 0.7 collective-permute-done.21.arrived_ref
  78.8 1.8 %collective-permute-start.25 = (bf16[128,1536]{1,0:T(8,128)(2,1)S(1)}, bf16[128,1536]{1,0:T(8,128)(2,1)S(1)}, u32[]{:S(2)}, u32[]{:S(2)}) collective-permute-start(bf16[128,1536]{1,0:T(8,128)(2,1)S(1)} %shard_map.83._), channel_id=1, source_target_pairs={{0,4},{1,3},{2,6},{3,1},{4,0},{5,7},{6,2},{7,5},{8,12},{9,11},{10,... | collective-permute-start | bytes 1179656 | tf_op jit(solution)/shard_map/ppermute | solution.py:30
  81.1 1.8 %collective-permute-start.23 = (bf16[32,1536]{1,0:T(8,128)(2,1)S(1)}, bf16[32,1536]{1,0:T(8,128)(2,1)S(1)}, u32[]{:S(2)}, u32[]{:S(2)}) collective-permute-start(bf16[32,1536]{1,0:T(8,128)(2,1)S(1)} %get-tuple-element.98), channel_id=1, source_target_pairs={{0,8},{1,9},{2,10},{3,11},{4,12},{5,13},{6,14},{7,15},{8,0},{9,1},... | collective-permute-start | bytes 294920 | tf_op jit(solution)/shard_map/ppermute | solution.py:30
  83.2 3.4 %collective-permute-done.25 = bf16[128,1536]{1,0:T(8,128)(2,1)S(1)} collective-permute-done((bf16[128,1536]{1,0:T(8,128)(2,1)S(1)}, bf16[128,1536]{1,0:T(8,128)(2,1)S(1)}, u32[]{:S(2)}, u32[]{:S(2)}) %collective-permute-start.25) | collective-permute-done | bytes 393248 | tf_op jit(solution)/shard_map/ppermute | solution.py:30
  86.8 2.3 %collective-permute-start.27 = (bf16[32,1536]{1,0:T(8,128)(2,1)S(1)}, bf16[32,1536]{1,0:T(8,128)(2,1)S(1)}, u32[]{:S(2)}, u32[]{:S(2)}) collective-permute-start(bf16[32,1536]{1,0:T(8,128)(2,1)S(1)} %get-tuple-element.100), channel_id=1, source_target_pairs={{0,8},{1,9},{2,10},{3,11},{4,12},{5,13},{6,14},{7,15},{8,0},{9,1},... | collective-permute-start | bytes 294920 | tf_op jit(solution)/shard_map/ppermute | solution.py:30
  89.1 1.7 %collective-permute-start.24 = (bf16[32,1536]{1,0:T(8,128)(2,1)S(1)}, bf16[32,1536]{1,0:T(8,128)(2,1)S(1)}, u32[]{:S(2)}, u32[]{:S(2)}) collective-permute-start(bf16[32,1536]{1,0:T(8,128)(2,1)S(1)} %add_convert_fusion.2), channel_id=1, source_target_pairs={{0,16},{1,17},{2,18},{3,19},{4,20},{5,21},{6,22},{7,23},{8,24},{9,... | collective-permute-start | bytes 294920 | tf_op jit(solution)/shard_map/ppermute | solution.py:30
  90.8 1.9 %collective-permute-start.26 = (bf16[32,1536]{1,0:T(8,128)(2,1)S(1)}, bf16[32,1536]{1,0:T(8,128)(2,1)S(1)}, u32[]{:S(2)}, u32[]{:S(2)}) collective-permute-start(bf16[32,1536]{1,0:T(8,128)(2,1)S(1)} %get-tuple-element.99), channel_id=1, source_target_pairs={{0,8},{1,9},{2,10},{3,11},{4,12},{5,13},{6,14},{7,15},{8,0},{9,1},... | collective-permute-start | bytes 294920 | tf_op jit(solution)/shard_map/ppermute | solution.py:30
  92.7 3.6 %collective-permute-start.28 = (bf16[32,1536]{1,0:T(8,128)(2,1)S(1)}, bf16[32,1536]{1,0:T(8,128)(2,1)S(1)}, u32[]{:S(2)}, u32[]{:S(2)}) collective-permute-start(bf16[32,1536]{1,0:T(8,128)(2,1)S(1)} %fusion.2), channel_id=1, source_target_pairs={{0,16},{1,17},{2,18},{3,19},{4,20},{5,21},{6,22},{7,23},{8,24},{9,... | collective-permute-start | bytes 294920 | tf_op jit(solution)/shard_map/ppermute | solution.py:30
  96.4 1.0 collective-permute-done.26
  97.3 3.5 %collective-permute-done.28 = bf16[32,1536]{1,0:T(8,128)(2,1)S(1)} collective-permute-done((bf16[32,1536]{1,0:T(8,128)(2,1)S(1)}, bf16[32,1536]{1,0:T(8,128)(2,1)S(1)}, u32[]{:S(2)}, u32[]{:S(2)}) %collective-permute-start.28) | collective-permute-done | bytes 98336 | tf_op jit(solution)/shard_map/ppermute | solution.py:30
  101.1 1.3 %collective-permute-done.29 = bf16[2,16,1536]{2,1,0:T(8,128)(2,1)S(1)} collective-permute-done((bf16[2,16,1536]{2,1,0:T(8,128)(2,1)S(1)}, bf16[2,16,1536]{2,1,0:T(8,128)(2,1)S(1)}, u32[]{:S(2)}, u32[]{:S(2)}) %collective-permute-start.29) | collective-permute-done | bytes 98336 | tf_op jit(solution)/shard_map/ppermute | solution.py:30
  102.4 0.7 fusion
  (75 shorter events, 6.2 us)
Async XLA Ops:
  2.4 0.9 copy-start.1
  3.3 12.4 %slice-start.2 = ((s8[4239360]{0:T(1024)(128)(4,1)}), s8[45056]{0:T(1024)(128)(4,1)S(1)}, s32[]{:S(2)}) async-start(s8[4239360]{0:T(1024)(128)(4,1)} %bitcast.25), calls=%async_computation.2 | async-start | bytes 90112
  4.1 1.5 %collective-permute-start = (bf16[2,16,1536]{2,1,0:T(8,128)(2,1)S(1)}, bf16[2,16,1536]{2,1,0:T(8,128)(2,1)S(1)}, u32[]{:S(2)}, u32[]{:S(2)}) collective-permute-start(bf16[2,16,1536]{2,1,0:T(8,128)(2,1)S(1)} %get-tuple-element.49), channel_id=1, source_target_pairs={{0,1},{1,0},{2,3},{3,2},{4,5},{5,4},{6,7},{7,6},{8,9},{9,8},{10,11... | collective-permute-start | bytes 294920 | tf_op jit(solution)/shard_map/ppermute | solution.py:30
  5.7 9.3 %collective-permute-start.2 = (bf16[32,1536]{1,0:T(8,128)(2,1)S(1)}, bf16[32,1536]{1,0:T(8,128)(2,1)S(1)}, u32[]{:S(2)}, u32[]{:S(2)}) collective-permute-start(bf16[32,1536]{1,0:T(8,128)(2,1)S(1)} %get-tuple-element.103._), channel_id=1, source_target_pairs={{0,16},{1,17},{2,18},{3,19},{4,20},{5,21},{6,22},{7,23},{8,24},{9,... | collective-permute-start | bytes 294920 | tf_op jit(solution)/shard_map/ppermute | solution.py:30
  9.7 6.0 %collective-permute-start.1 = (bf16[32,1536]{1,0:T(8,128)(2,1)S(1)}, bf16[32,1536]{1,0:T(8,128)(2,1)S(1)}, u32[]{:S(2)}, u32[]{:S(2)}) collective-permute-start(bf16[32,1536]{1,0:T(8,128)(2,1)S(1)} %get-tuple-element.103._), channel_id=1, source_target_pairs={{0,8},{1,9},{2,10},{3,11},{4,12},{5,13},{6,14},{7,15},{8,0},{9,1},... | collective-permute-start | bytes 294920 | tf_op jit(solution)/shard_map/ppermute | solution.py:30
  11.3 2.2 %copy-start = (bf16[2880,720]{0,1:T(8,128)(2,1)S(1)}, bf16[2880,720]{0,1:T(8,128)(2,1)}, u32[]{:S(2)}) copy-start(bf16[2880,720]{0,1:T(8,128)(2,1)} %param.9) | copy-start | bytes 12441604
  13.5 2.2 %slice-start.3 = ((s8[4239360]{0:T(1024)(128)(4,1)}), s8[4194304]{0:T(1024)(128)(4,1)S(1)}, s32[]{:S(2)}) async-start(s8[4239360]{0:T(1024)(128)(4,1)} %bitcast.25), calls=%async_computation.3 | async-start | bytes 8388608
  15.0 4.6 %collective-permute-start.3 = (bf16[32,1536]{1,0:T(8,128)(2,1)S(1)}, bf16[32,1536]{1,0:T(8,128)(2,1)S(1)}, u32[]{:S(2)}, u32[]{:S(2)}) collective-permute-start(bf16[32,1536]{1,0:T(8,128)(2,1)S(1)} %collective-permute-done.2._), channel_id=1, source_target_pairs={{0,8},{1,9},{2,10},{3,11},{4,12},{5,13},{6,14},{7,15},{8,0},{9,1},... | collective-permute-start | bytes 294920 | tf_op jit(solution)/shard_map/ppermute | solution.py:30
  15.6 17.9 %slice-start = ((s8[4239360]{0:T(1024)(128)(4,1)}), s8[4194304]{0:T(1024)(128)(4,1)S(1)}, s32[]{:S(2)}) async-start(s8[4239360]{0:T(1024)(128)(4,1)} %bitcast.22), calls=%async_computation | async-start | bytes 8388608
  15.7 17.8 %slice-start.1 = ((s8[4239360]{0:T(1024)(128)(4,1)}), s8[45056]{0:T(1024)(128)(4,1)S(1)}, s32[]{:S(2)}) async-start(s8[4239360]{0:T(1024)(128)(4,1)} %bitcast.22), calls=%async_computation.1 | async-start | bytes 90112
  19.6 7.8 %collective-permute-start.4 = (bf16[128,1536]{1,0:T(8,128)(2,1)S(1)}, bf16[128,1536]{1,0:T(8,128)(2,1)S(1)}, u32[]{:S(2)}, u32[]{:S(2)}) collective-permute-start(bf16[128,1536]{1,0:T(8,128)(2,1)S(1)} %constant_dynamic-update-slice_fusion.near_ref), channel_id=1, source_target_pairs={{0,4},{1,3},{2,6},{3,1},{4,0},{5,7},{6,2},{7,5},{8,12},{9,11},{10,... | collective-permute-start | bytes 1179656 | tf_op jit(solution)/shard_map/ppermute | solution.py:30
  21.3 10.5 %collective-permute-start.5 = (bf16[32,1536]{1,0:T(8,128)(2,1)S(1)}, bf16[32,1536]{1,0:T(8,128)(2,1)S(1)}, u32[]{:S(2)}, u32[]{:S(2)}) collective-permute-start(bf16[32,1536]{1,0:T(8,128)(2,1)S(1)} %get-tuple-element.58), channel_id=1, source_target_pairs={{0,8},{1,9},{2,10},{3,11},{4,12},{5,13},{6,14},{7,15},{8,0},{9,1},... | collective-permute-start | bytes 294920 | tf_op jit(solution)/shard_map/ppermute | solution.py:30
  22.0 10.2 %collective-permute-start.6 = (bf16[32,1536]{1,0:T(8,128)(2,1)S(1)}, bf16[32,1536]{1,0:T(8,128)(2,1)S(1)}, u32[]{:S(2)}, u32[]{:S(2)}) collective-permute-start(bf16[32,1536]{1,0:T(8,128)(2,1)S(1)} %get-tuple-element.58), channel_id=1, source_target_pairs={{0,16},{1,17},{2,18},{3,19},{4,20},{5,21},{6,22},{7,23},{8,24},{9,... | collective-permute-start | bytes 294920 | tf_op jit(solution)/shard_map/ppermute | solution.py:30
  25.3 6.9 %collective-permute-start.7 = (bf16[32,1536]{1,0:T(8,128)(2,1)S(1)}, bf16[32,1536]{1,0:T(8,128)(2,1)S(1)}, u32[]{:S(2)}, u32[]{:S(2)}) collective-permute-start(bf16[32,1536]{1,0:T(8,128)(2,1)S(1)} %get-tuple-element.58), channel_id=1, source_target_pairs={{0,24},{1,25},{2,26},{3,27},{4,28},{5,29},{6,30},{7,31},{8,16},{9,... | collective-permute-start | bytes 294920 | tf_op jit(solution)/shard_map/ppermute | solution.py:30
  28.8 14.2 %collective-permute-start.9 = (bf16[192,1536]{1,0:T(8,128)(2,1)S(1)}, bf16[192,1536]{1,0:T(8,128)(2,1)S(1)}, u32[]{:S(2)}, u32[]{:S(2)}) collective-permute-start(bf16[192,1536]{1,0:T(8,128)(2,1)S(1)} %shard_map.76), channel_id=1, source_target_pairs={{0,2},{1,5},{2,0},{3,7},{4,6},{5,1},{6,4},{7,3},{8,10},{9,13},{10,... | collective-permute-start | bytes 1769480 | tf_op jit(solution)/shard_map/ppermute | solution.py:30
  32.3 7.8 %collective-permute-start.8 = (bf16[128,1536]{1,0:T(8,128)(2,1)S(1)}, bf16[128,1536]{1,0:T(8,128)(2,1)S(1)}, u32[]{:S(2)}, u32[]{:S(2)}) collective-permute-start(bf16[128,1536]{1,0:T(8,128)(2,1)S(1)} %constant_dynamic-update-slice_fusion.5.near_ref), channel_id=1, source_target_pairs={{0,4},{1,3},{2,6},{3,1},{4,0},{5,7},{6,2},{7,5},{8,12},{9,11},{10,... | collective-permute-start | bytes 1179656 | tf_op jit(solution)/shard_map/ppermute | solution.py:30
  33.5 10.2 %collective-permute-start.11 = (bf16[192,1536]{1,0:T(8,128)(2,1)S(1)}, bf16[192,1536]{1,0:T(8,128)(2,1)S(1)}, u32[]{:S(2)}, u32[]{:S(2)}) collective-permute-start(bf16[192,1536]{1,0:T(8,128)(2,1)S(1)} %get-tuple-element.63._.mine_near_ref), channel_id=1, source_target_pairs={{0,1},{1,0},{2,3},{3,2},{4,5},{5,4},{6,7},{7,6},{8,9},{9,8},{10,11... | collective-permute-start | bytes 1769480 | tf_op jit(solution)/shard_map/ppermute | solution.py:30
  43.0 2.0 %collective-permute-start.12 = (bf16[192,1536]{1,0:T(8,128)(2,1)S(1)}, bf16[192,1536]{1,0:T(8,128)(2,1)S(1)}, u32[]{:S(2)}, u32[]{:S(2)}) collective-permute-start(bf16[192,1536]{1,0:T(8,128)(2,1)S(1)} %collective-permute-done.9.mine_far_ref), channel_id=1, source_target_pairs={{0,1},{1,0},{2,3},{3,2},{4,5},{5,4},{6,7},{7,6},{8,9},{9,8},{10,11... | collective-permute-start | bytes 1769480 | tf_op jit(solution)/shard_map/ppermute | solution.py:30
  43.0 9.9 %collective-permute-start.10 = (bf16[192,1536]{1,0:T(8,128)(2,1)S(1)}, bf16[192,1536]{1,0:T(8,128)(2,1)S(1)}, u32[]{:S(2)}, u32[]{:S(2)}) collective-permute-start(bf16[192,1536]{1,0:T(8,128)(2,1)S(1)} %get-tuple-element.66), channel_id=1, source_target_pairs={{0,2},{1,5},{2,0},{3,7},{4,6},{5,1},{6,4},{7,3},{8,10},{9,13},{10,... | collective-permute-start | bytes 1769480 | tf_op jit(solution)/shard_map/ppermute | solution.py:30
  52.9 2.0 %collective-permute-start.14 = (bf16[192,1536]{1,0:T(8,128)(2,1)S(1)}, bf16[192,1536]{1,0:T(8,128)(2,1)S(1)}, u32[]{:S(2)}, u32[]{:S(2)}) collective-permute-start(bf16[192,1536]{1,0:T(8,128)(2,1)S(1)} %get-tuple-element.78), channel_id=1, source_target_pairs={{0,1},{1,0},{2,3},{3,2},{4,5},{5,4},{6,7},{7,6},{8,9},{9,8},{10,11... | collective-permute-start | bytes 1769480 | tf_op jit(solution)/shard_map/ppermute | solution.py:30
  52.9 2.9 %collective-permute-start.17 = (bf16[192,1536]{1,0:T(8,128)(2,1)S(1)}, bf16[192,1536]{1,0:T(8,128)(2,1)S(1)}, u32[]{:S(2)}, u32[]{:S(2)}) collective-permute-start(bf16[192,1536]{1,0:T(8,128)(2,1)S(1)} %get-tuple-element.83.mine_near_ref), channel_id=1, source_target_pairs={{0,1},{1,0},{2,3},{3,2},{4,5},{5,4},{6,7},{7,6},{8,9},{9,8},{10,11... | collective-permute-start | bytes 1769480 | tf_op jit(solution)/shard_map/ppermute | solution.py:30
  53.4 3.2 %collective-permute-start.18 = (bf16[192,1536]{1,0:T(8,128)(2,1)S(1)}, bf16[192,1536]{1,0:T(8,128)(2,1)S(1)}, u32[]{:S(2)}, u32[]{:S(2)}) collective-permute-start(bf16[192,1536]{1,0:T(8,128)(2,1)S(1)} %collective-permute-done.10.mine_far_ref), channel_id=1, source_target_pairs={{0,1},{1,0},{2,3},{3,2},{4,5},{5,4},{6,7},{7,6},{8,9},{9,8},{10,11... | collective-permute-start | bytes 1769480 | tf_op jit(solution)/shard_map/ppermute | solution.py:30
  53.4 10.6 %collective-permute-start.13 = (bf16[192,1536]{1,0:T(8,128)(2,1)S(1)}, bf16[192,1536]{1,0:T(8,128)(2,1)S(1)}, u32[]{:S(2)}, u32[]{:S(2)}) collective-permute-start(bf16[192,1536]{1,0:T(8,128)(2,1)S(1)} %get-tuple-element.76), channel_id=1, source_target_pairs={{0,1},{1,0},{2,3},{3,2},{4,5},{5,4},{6,7},{7,6},{8,9},{9,8},{10,11... | collective-permute-start | bytes 1769480 | tf_op jit(solution)/shard_map/ppermute | solution.py:30
  55.0 9.9 %collective-permute-start.15 = (bf16[192,1536]{1,0:T(8,128)(2,1)S(1)}, bf16[192,1536]{1,0:T(8,128)(2,1)S(1)}, u32[]{:S(2)}, u32[]{:S(2)}) collective-permute-start(bf16[192,1536]{1,0:T(8,128)(2,1)S(1)} %add_convert_fusion.1), channel_id=1, source_target_pairs={{0,2},{1,5},{2,0},{3,7},{4,6},{5,1},{6,4},{7,3},{8,10},{9,13},{10,... | collective-permute-start | bytes 1769480 | tf_op jit(solution)/shard_map/ppermute | solution.py:30
  63.4 4.3 %collective-permute-start.20 = (bf16[192,1536]{1,0:T(8,128)(2,1)S(1)}, bf16[192,1536]{1,0:T(8,128)(2,1)S(1)}, u32[]{:S(2)}, u32[]{:S(2)}) collective-permute-start(bf16[192,1536]{1,0:T(8,128)(2,1)S(1)} %get-tuple-element.88), channel_id=1, source_target_pairs={{0,1},{1,0},{2,3},{3,2},{4,5},{5,4},{6,7},{7,6},{8,9},{9,8},{10,11... | collective-permute-start | bytes 1769480 | tf_op jit(solution)/shard_map/ppermute | solution.py:30
  63.8 13.9 %collective-permute-start.19 = (bf16[192,1536]{1,0:T(8,128)(2,1)S(1)}, bf16[192,1536]{1,0:T(8,128)(2,1)S(1)}, u32[]{:S(2)}, u32[]{:S(2)}) collective-permute-start(bf16[192,1536]{1,0:T(8,128)(2,1)S(1)} %get-tuple-element.86), channel_id=1, source_target_pairs={{0,1},{1,0},{2,3},{3,2},{4,5},{5,4},{6,7},{7,6},{8,9},{9,8},{10,11... | collective-permute-start | bytes 1769480 | tf_op jit(solution)/shard_map/ppermute | solution.py:30
  65.6 12.0 %collective-permute-start.16 = (bf16[128,1536]{1,0:T(8,128)(2,1)S(1)}, bf16[128,1536]{1,0:T(8,128)(2,1)S(1)}, u32[]{:S(2)}, u32[]{:S(2)}) collective-permute-start(bf16[128,1536]{1,0:T(8,128)(2,1)S(1)} %get-tuple-element.80), channel_id=1, source_target_pairs={{0,4},{1,3},{2,6},{3,1},{4,0},{5,7},{6,2},{7,5},{8,12},{9,11},{10,... | collective-permute-start | bytes 1179656 | tf_op jit(solution)/shard_map/ppermute | solution.py:30
  67.9 10.5 %collective-permute-start.21 = (bf16[192,1536]{1,0:T(8,128)(2,1)S(1)}, bf16[192,1536]{1,0:T(8,128)(2,1)S(1)}, u32[]{:S(2)}, u32[]{:S(2)}) collective-permute-start(bf16[192,1536]{1,0:T(8,128)(2,1)S(1)} %add_convert_fusion), channel_id=1, source_target_pairs={{0,2},{1,5},{2,0},{3,7},{4,6},{5,1},{6,4},{7,3},{8,10},{9,13},{10,... | collective-permute-start | bytes 1769480 | tf_op jit(solution)/shard_map/ppermute | solution.py:30
  78.8 7.8 %collective-permute-start.25 = (bf16[128,1536]{1,0:T(8,128)(2,1)S(1)}, bf16[128,1536]{1,0:T(8,128)(2,1)S(1)}, u32[]{:S(2)}, u32[]{:S(2)}) collective-permute-start(bf16[128,1536]{1,0:T(8,128)(2,1)S(1)} %shard_map.83._), channel_id=1, source_target_pairs={{0,4},{1,3},{2,6},{3,1},{4,0},{5,7},{6,2},{7,5},{8,12},{9,11},{10,... | collective-permute-start | bytes 1179656 | tf_op jit(solution)/shard_map/ppermute | solution.py:30
  81.1 7.9 %collective-permute-start.23 = (bf16[32,1536]{1,0:T(8,128)(2,1)S(1)}, bf16[32,1536]{1,0:T(8,128)(2,1)S(1)}, u32[]{:S(2)}, u32[]{:S(2)}) collective-permute-start(bf16[32,1536]{1,0:T(8,128)(2,1)S(1)} %get-tuple-element.98), channel_id=1, source_target_pairs={{0,8},{1,9},{2,10},{3,11},{4,12},{5,13},{6,14},{7,15},{8,0},{9,1},... | collective-permute-start | bytes 294920 | tf_op jit(solution)/shard_map/ppermute | solution.py:30
  82.9 13.4 %collective-permute-start.22 = (bf16[32,1536]{1,0:T(8,128)(2,1)S(1)}, bf16[32,1536]{1,0:T(8,128)(2,1)S(1)}, u32[]{:S(2)}, u32[]{:S(2)}) collective-permute-start(bf16[32,1536]{1,0:T(8,128)(2,1)S(1)} %get-tuple-element.97), channel_id=1, source_target_pairs={{0,8},{1,9},{2,10},{3,11},{4,12},{5,13},{6,14},{7,15},{8,0},{9,1},... | collective-permute-start | bytes 294920 | tf_op jit(solution)/shard_map/ppermute | solution.py:30
  86.8 5.9 %collective-permute-start.27 = (bf16[32,1536]{1,0:T(8,128)(2,1)S(1)}, bf16[32,1536]{1,0:T(8,128)(2,1)S(1)}, u32[]{:S(2)}, u32[]{:S(2)}) collective-permute-start(bf16[32,1536]{1,0:T(8,128)(2,1)S(1)} %get-tuple-element.100), channel_id=1, source_target_pairs={{0,8},{1,9},{2,10},{3,11},{4,12},{5,13},{6,14},{7,15},{8,0},{9,1},... | collective-permute-start | bytes 294920 | tf_op jit(solution)/shard_map/ppermute | solution.py:30
  89.1 7.2 %collective-permute-start.24 = (bf16[32,1536]{1,0:T(8,128)(2,1)S(1)}, bf16[32,1536]{1,0:T(8,128)(2,1)S(1)}, u32[]{:S(2)}, u32[]{:S(2)}) collective-permute-start(bf16[32,1536]{1,0:T(8,128)(2,1)S(1)} %add_convert_fusion.2), channel_id=1, source_target_pairs={{0,16},{1,17},{2,18},{3,19},{4,20},{5,21},{6,22},{7,23},{8,24},{9,... | collective-permute-start | bytes 294920 | tf_op jit(solution)/shard_map/ppermute | solution.py:30
  90.8 6.6 %collective-permute-start.26 = (bf16[32,1536]{1,0:T(8,128)(2,1)S(1)}, bf16[32,1536]{1,0:T(8,128)(2,1)S(1)}, u32[]{:S(2)}, u32[]{:S(2)}) collective-permute-start(bf16[32,1536]{1,0:T(8,128)(2,1)S(1)} %get-tuple-element.99), channel_id=1, source_target_pairs={{0,8},{1,9},{2,10},{3,11},{4,12},{5,13},{6,14},{7,15},{8,0},{9,1},... | collective-permute-start | bytes 294920 | tf_op jit(solution)/shard_map/ppermute | solution.py:30
  92.7 8.2 %collective-permute-start.28 = (bf16[32,1536]{1,0:T(8,128)(2,1)S(1)}, bf16[32,1536]{1,0:T(8,128)(2,1)S(1)}, u32[]{:S(2)}, u32[]{:S(2)}) collective-permute-start(bf16[32,1536]{1,0:T(8,128)(2,1)S(1)} %fusion.2), channel_id=1, source_target_pairs={{0,16},{1,17},{2,18},{3,19},{4,20},{5,21},{6,22},{7,23},{8,24},{9,... | collective-permute-start | bytes 294920 | tf_op jit(solution)/shard_map/ppermute | solution.py:30
  100.9 1.5 %copy-start.2 = (bf16[2,16,2880]{2,1,0:T(8,128)(2,1)S(1)}, bf16[2,16,2880]{2,1,0:T(8,128)(2,1)}, u32[]{:S(2)}) copy-start(bf16[2,16,2880]{2,1,0:T(8,128)(2,1)} %hidden_ref.1) | copy-start | bytes 552964
  100.9 1.4 %collective-permute-start.29 = (bf16[2,16,1536]{2,1,0:T(8,128)(2,1)S(1)}, bf16[2,16,1536]{2,1,0:T(8,128)(2,1)S(1)}, u32[]{:S(2)}, u32[]{:S(2)}) collective-permute-start(bf16[2,16,1536]{2,1,0:T(8,128)(2,1)S(1)} %select_convert_fusion), channel_id=1, source_target_pairs={{0,1},{1,0},{2,3},{3,2},{4,5},{5,4},{6,7},{7,6},{8,9},{9,8},{10,11... | collective-permute-start | bytes 294920 | tf_op jit(solution)/shard_map/ppermute | solution.py:30
